TPU v7x, 32 devices: a whole 2x2x4 slice. The times are simulated.
32 devices in a mesh: seq: 8 (over z, core), fsdp: 4 (over y, x).
Axes of the slice: x: 2, y: 2, z: 4, core: 2. Of those that a mesh axis runs over, the one named last changes fastest.
Arguments:
- hidden_in: bfloat16 [5120, 2048], P(('seq', 'fsdp')), may hold values from -6 to 6
- w_input: bfloat16 [2, 2048, 2048], P(None, 'seq', 'fsdp'), may hold values from -0.125 to 0.125
- w_forget: bfloat16 [2, 2048, 2048], P(None, 'seq', 'fsdp'), may hold values from -0.125 to 0.125
- w_gate: bfloat16 [2, 2048, 2048], P(None, 'seq', 'fsdp'), may hold values from -0.125 to 0.125
- w_out: bfloat16 [2, 2048, 2048], P(None, 'fsdp', 'seq'), may hold values from -0.125 to 0.125
- w_up: bfloat16 [2, 2048, 5632], P(None, 'seq', 'fsdp'), may hold values from -0.125 to 0.125
- w_glu: bfloat16 [2, 2048, 5632], P(None, 'seq', 'fsdp'), may hold values from -0.125 to 0.125
- w_down: bfloat16 [2, 5632, 2048], P(None, 'fsdp', 'seq'), may hold values from -0.078125 to 0.078125
- lower_bound: float32 [2, 2048], replicated, may hold values from 0.9 to 0.99999609
- norm_mix: float32 [2, 2048], replicated, may hold values from 0.5 to 1.5
- norm_ffn: float32 [2, 2048], replicated, may hold values from 0.5 to 1.5
- out_gain: float32 [2, 2048], replicated, may hold values from 0.5 to 1.5
- lengths: int32 [5], replicated, may hold values from 1 to 4480, as said below
- cotangent: bfloat16 [5120, 2048], P(('seq', 'fsdp')), may hold values from -6 to 6
Outputs:
- hidden_out: bfloat16 [5120, 2048], P(('seq', 'fsdp'))
- grad_in: float32 [5120, 2048], P(('seq', 'fsdp'))
- grad_w_input: float32 [2, 2048, 2048], P(None, 'seq', 'fsdp')
- grad_w_forget: float32 [2, 2048, 2048], P(None, 'seq', 'fsdp')
- grad_w_gate: float32 [2, 2048, 2048], P(None, 'seq', 'fsdp')
- grad_w_out: float32 [2, 2048, 2048], P(None, 'fsdp', 'seq')
- grad_w_up: float32 [2, 2048, 5632], P(None, 'seq', 'fsdp')
- grad_w_glu: float32 [2, 2048, 5632], P(None, 'seq', 'fsdp')
- grad_w_down: float32 [2, 5632, 2048], P(None, 'fsdp', 'seq')
- grad_lower_bound: float32 [2, 2048], replicated
- grad_norm_mix: float32 [2, 2048], replicated
- grad_norm_ffn: float32 [2, 2048], replicated
- grad_out_gain: float32 [2, 2048], replicated
Inputs may be any that keep to these rules, and one draw needn't show every extreme that they name: `lengths`: one sequence, neither the first nor the last, has 4480 rows; the others share 640 rows.
All inputs are finite; a program needn't handle non-finite values.
Results may differ from a plain program's by a relative error of at most 0.025.
Values may be sent and summed in bfloat16 or wider, within the bound.
No kernel may reach another device: no remote copies, remote signals or barrier semaphores. Data moves between devices by JAX's collectives and lax.ppermute only.
A program may use at most 256 MiB of HBM per device.

v0:
```python
import jax
import jax.numpy as jnp
from jax import lax
from jax.sharding import PartitionSpec as P

LAYERS = 2


epsilon = 1e-06


def entering_2(array, axis, combine, identity, reverse):
    length, place = (lax.axis_size(axis), lax.axis_index(axis))
    everything = jax.tree.map(lambda part: lax.all_gather(part, axis), array)
    start = jax.tree.map(
        lambda part, zero: jnp.broadcast_to(jnp.asarray(zero, part.dtype), part.shape),
        array,
        identity,
    )

    def step(k, before):
        at = length - 1 - k if reverse else k
        reached = at > place if reverse else at < place
        new = combine(before, jax.tree.map(lambda part: part[at], everything))
        return jax.tree.map(lambda a, b: jnp.where(reached, a, b), new, before)

    return lax.fori_loop(0, length, step, start)


def combine(earlier, later_part):
    return (earlier[0] * later_part[0], later_part[0] * earlier[1] + later_part[1])


def plain_dot(operand, matrix):
    return jnp.dot(operand, matrix, preferred_element_type=jnp.float32)


def trans_dot(operand, matrix):
    return lax.dot_general(
        operand, matrix, (((1,), (1,)), ((), ())), preferred_element_type=jnp.float32
    )


def outer_dot(operand, other):
    return lax.dot_general(
        operand, other, (((0,), (0,)), ((), ())), preferred_element_type=jnp.float32
    )


def rms_parts(values):
    factor = lax.rsqrt(jnp.mean(values * values, axis=-1, keepdims=True) + epsilon)
    return (values * factor, factor)


def norm_back(grad_unit, unit_rows, factor):
    return factor * (
        grad_unit - unit_rows * jnp.mean(grad_unit * unit_rows, axis=-1, keepdims=True)
    )


def dsilu(values):
    sigma = jax.nn.sigmoid(values)
    return sigma * (1.0 + values * (1.0 - sigma))


def gather_rows(values):
    return lax.all_gather(values, "fsdp", axis=0, tiled=True)


def gather_grads(values):
    return lax.all_gather(values, "fsdp", axis=0, tiled=True)


def spread(operand, matrix, row_count):

    def term(first_row, row_span):
        return plain_dot(operand, matrix)

    return lax.psum_scatter(
        term(jnp.int32(0), lax.axis_size("fsdp") * row_count).astype(jnp.bfloat16),
        "fsdp",
        scatter_dimension=0,
        tiled=True,
    ).astype(jnp.float32)


def spread_back(grads, matrices, row_count):

    def term(first_row, row_span):
        result = trans_dot(grads[0], matrices[0])
        for position in range(1, len(grads)):
            result = result + trans_dot(grads[position], matrices[position])
        return result

    return lax.psum_scatter(
        term(jnp.int32(0), lax.axis_size("fsdp") * row_count).astype(jnp.bfloat16),
        "fsdp",
        scatter_dimension=0,
        tiled=True,
    ).astype(jnp.float32)


def local(
    hidden_in,
    w_input,
    w_forget,
    w_gate,
    w_out,
    w_up,
    w_glu,
    w_down,
    lower_bound,
    norm_mix,
    norm_ffn,
    out_gain,
    lengths,
    cotangent,
):
    row_count = hidden_in.shape[0]
    model_width = hidden_in.shape[1]
    channels = w_input.shape[2]
    block_rows = row_count * lax.axis_size("fsdp")
    first_channel = lax.axis_index("fsdp") * channels
    starts = jnp.cumsum(lengths) - lengths
    positions = lax.axis_index("seq") * block_rows + jnp.arange(block_rows, dtype=jnp.int32)
    keep_column = (
        1.0 - jnp.any(positions[:, None] == starts[None, :], axis=1).astype(jnp.float32)
    )[:, None]
    bounds = lax.dynamic_slice_in_dim(lower_bound, first_channel, channels, 1)
    out_gains = lax.dynamic_slice_in_dim(out_gain, first_channel, channels, 1)
    identity = (jnp.ones((channels,), jnp.float32), jnp.zeros((channels,), jnp.float32))
    stream = hidden_in.astype(jnp.float32)
    saved_layers = []
    for layer_index in range(LAYERS):
        fetched = (
            lax.all_gather(w_input[layer_index], "seq", axis=0, tiled=True),
            lax.all_gather(w_forget[layer_index], "seq", axis=0, tiled=True),
            lax.all_gather(w_gate[layer_index], "seq", axis=0, tiled=True),
            lax.all_gather(w_out[layer_index], "seq", axis=1, tiled=True),
            lax.all_gather(w_up[layer_index], "seq", axis=0, tiled=True),
            lax.all_gather(w_glu[layer_index], "seq", axis=0, tiled=True),
            lax.all_gather(w_down[layer_index], "seq", axis=1, tiled=True),
        )
        (
            input_matrix,
            forget_matrix,
            gate_matrix,
            output_matrix,
            up_matrix,
            glu_matrix,
            down_matrix,
        ) = fetched
        unit_one, factor_one = rms_parts(stream)
        normed = gather_rows((unit_one * norm_mix[layer_index]).astype(jnp.bfloat16))
        proj_input = plain_dot(normed, input_matrix)
        proj_forget = plain_dot(normed, forget_matrix)
        proj_gate = plain_dot(normed, gate_matrix)
        bound_row = bounds[layer_index]
        forget = bound_row + (1.0 - bound_row) * jax.nn.sigmoid(proj_forget)
        source = jax.nn.silu(proj_input) * (1.0 - forget)
        decay_all = forget * keep_column
        local_decay, local_state = lax.associative_scan(combine, (decay_all, source), axis=0)
        entering = entering_2((local_decay[-1], local_state[-1]), "seq", combine, identity, False)[
            1
        ]
        state_all = local_state + local_decay * entering[None, :]
        squares = lax.psum(jnp.sum(state_all * state_all, axis=1), "fsdp")
        inverse = lax.rsqrt(squares / model_width + epsilon)[:, None]
        scaled = state_all * inverse
        mixed_out = (scaled * out_gains[layer_index] * jax.nn.silu(proj_gate)).astype(jnp.bfloat16)
        middle = stream + spread(mixed_out, output_matrix, row_count)
        unit_two, factor_two = rms_parts(middle)
        normed_two = gather_rows((unit_two * norm_ffn[layer_index]).astype(jnp.bfloat16))
        upward = plain_dot(normed_two, up_matrix)
        gating = plain_dot(normed_two, glu_matrix)
        hidden = (jax.nn.silu(gating) * upward).astype(jnp.bfloat16)
        saved_layers.append(
            (
                fetched,
                unit_one,
                factor_one,
                normed,
                proj_input,
                proj_forget,
                proj_gate,
                forget,
                decay_all,
                entering,
                state_all,
                inverse,
                scaled,
                mixed_out,
                unit_two,
                factor_two,
                normed_two,
                upward,
                gating,
                hidden,
            )
        )
        stream = middle + spread(hidden, down_matrix, row_count)
    hidden_out = stream.astype(jnp.bfloat16)
    grad_x = cotangent.astype(jnp.float32)
    matrix_grads = []
    grad_mix_list = []
    grad_ffn_list = []
    grad_bound_list = []
    grad_gain_list = []
    zero_width = jnp.zeros((model_width,), jnp.float32)
    for layer_index in reversed(range(LAYERS)):
        (
            kept,
            unit_one,
            factor_one,
            normed,
            proj_input,
            proj_forget,
            proj_gate,
            forget,
            decay_all,
            entering,
            state_all,
            inverse,
            scaled,
            mixed_out,
            unit_two,
            factor_two,
            normed_two,
            upward,
            gating,
            hidden,
        ) = saved_layers[layer_index]
        fetched = (
            lax.all_gather(w_input[layer_index], "seq", axis=0, tiled=True),
            lax.all_gather(w_forget[layer_index], "seq", axis=0, tiled=True),
            lax.all_gather(w_gate[layer_index], "seq", axis=0, tiled=True),
            lax.all_gather(w_out[layer_index], "seq", axis=1, tiled=True),
            lax.all_gather(w_up[layer_index], "seq", axis=0, tiled=True),
            lax.all_gather(w_glu[layer_index], "seq", axis=0, tiled=True),
            lax.all_gather(w_down[layer_index], "seq", axis=1, tiled=True),
        )
        (
            input_matrix,
            forget_matrix,
            gate_matrix,
            output_matrix,
            up_matrix,
            glu_matrix,
            down_matrix,
        ) = fetched
        grad_y = gather_grads(grad_x.astype(jnp.bfloat16))
        grad_hidden = trans_dot(grad_y, down_matrix)
        grad_down = outer_dot(hidden, grad_y)
        grad_up = (grad_hidden * jax.nn.silu(gating)).astype(jnp.bfloat16)
        grad_glu = (grad_hidden * upward * dsilu(gating)).astype(jnp.bfloat16)
        grad_upw = outer_dot(normed_two, grad_up)
        grad_gluw = outer_dot(normed_two, grad_glu)
        grad_normed_two = spread_back((grad_up, grad_glu), (up_matrix, glu_matrix), row_count)
        grad_ffn_list.append(jnp.sum(grad_normed_two * unit_two, axis=0))
        grad_middle = grad_x + norm_back(
            grad_normed_two * norm_ffn[layer_index], unit_two, factor_two
        )
        grad_m = gather_grads(grad_middle.astype(jnp.bfloat16))
        grad_mixed = trans_dot(grad_m, output_matrix)
        grad_outw = outer_dot(mixed_out, grad_m)
        silu_gate = jax.nn.silu(proj_gate)
        gain_row = out_gains[layer_index]
        gain_piece = jnp.sum(grad_mixed * scaled * silu_gate, axis=0)
        grad_gate = (grad_mixed * scaled * gain_row * dsilu(proj_gate)).astype(jnp.bfloat16)
        grad_scaled = grad_mixed * gain_row * silu_gate
        projected = lax.psum(jnp.sum(grad_scaled * scaled, axis=1), "fsdp")
        grad_state = inverse * (grad_scaled - scaled * (projected / model_width)[:, None])
        next_decay = jnp.concatenate([decay_all[1:], jnp.ones((1, channels), jnp.float32)], axis=0)
        local_keep, local_adjoint = lax.associative_scan(
            combine, (next_decay, grad_state), axis=0, reverse=True
        )
        summary = (decay_all[0] * local_keep[0], decay_all[0] * local_adjoint[0])
        coming = entering_2(summary, "seq", combine, identity, True)[1]
        adjoint = local_adjoint + local_keep * coming[None, :]
        previous = jnp.concatenate([entering[None, :], state_all[:-1]], axis=0)
        silu_input = jax.nn.silu(proj_input)
        grad_forget = adjoint * (keep_column * previous - silu_input)
        bound_row = bounds[layer_index]
        sigma_forget = jax.nn.sigmoid(proj_forget)
        bound_piece = jnp.sum(grad_forget * (1.0 - sigma_forget), axis=0)
        grad_input = (adjoint * (1.0 - forget) * dsilu(proj_input)).astype(jnp.bfloat16)
        grad_fgate = (grad_forget * (1.0 - bound_row) * sigma_forget * (1.0 - sigma_forget)).astype(
            jnp.bfloat16
        )
        grad_inw = outer_dot(normed, grad_input)
        grad_fgw = outer_dot(normed, grad_fgate)
        grad_gtw = outer_dot(normed, grad_gate)
        grad_normed = spread_back(
            (grad_input, grad_fgate, grad_gate),
            (input_matrix, forget_matrix, gate_matrix),
            row_count,
        )
        grad_mix_list.append(jnp.sum(grad_normed * unit_one, axis=0))
        grad_x = grad_middle + norm_back(grad_normed * norm_mix[layer_index], unit_one, factor_one)
        grad_bound_list.append(
            lax.dynamic_update_slice_in_dim(zero_width, bound_piece, first_channel, 0)
        )
        grad_gain_list.append(
            lax.dynamic_update_slice_in_dim(zero_width, gain_piece, first_channel, 0)
        )
        shards = (
            lax.psum_scatter(
                grad_inw.astype(jnp.bfloat16), "seq", scatter_dimension=0, tiled=True
            ).astype(jnp.float32),
            lax.psum_scatter(
                grad_fgw.astype(jnp.bfloat16), "seq", scatter_dimension=0, tiled=True
            ).astype(jnp.float32),
            lax.psum_scatter(
                grad_gtw.astype(jnp.bfloat16), "seq", scatter_dimension=0, tiled=True
            ).astype(jnp.float32),
            lax.psum_scatter(
                grad_outw.astype(jnp.bfloat16), "seq", scatter_dimension=1, tiled=True
            ).astype(jnp.float32),
            lax.psum_scatter(
                grad_upw.astype(jnp.bfloat16), "seq", scatter_dimension=0, tiled=True
            ).astype(jnp.float32),
            lax.psum_scatter(
                grad_gluw.astype(jnp.bfloat16), "seq", scatter_dimension=0, tiled=True
            ).astype(jnp.float32),
            lax.psum_scatter(
                grad_down.astype(jnp.bfloat16), "seq", scatter_dimension=1, tiled=True
            ).astype(jnp.float32),
        )
        matrix_grads.append(shards)
    matrix_grads = matrix_grads[::-1]
    stacked = tuple(
        (jnp.stack([layer_grads[member] for layer_grads in matrix_grads]) for member in range(7))
    )
    small_totals = lax.psum(
        (
            jnp.stack(grad_mix_list[::-1]),
            jnp.stack(grad_ffn_list[::-1]),
            jnp.stack(grad_bound_list[::-1]),
            jnp.stack(grad_gain_list[::-1]),
        ),
        ("seq", "fsdp"),
    )
    return (
        hidden_out,
        grad_x,
        stacked[0],
        stacked[1],
        stacked[2],
        stacked[3],
        stacked[4],
        stacked[5],
        stacked[6],
        small_totals[2],
        small_totals[0],
        small_totals[1],
        small_totals[3],
    )


def solution(mesh):
    placed = (
        P(("seq", "fsdp"), None),
        P(None, "seq", "fsdp"),
        P(None, "seq", "fsdp"),
        P(None, "seq", "fsdp"),
        P(None, "fsdp", "seq"),
        P(None, "seq", "fsdp"),
        P(None, "seq", "fsdp"),
        P(None, "fsdp", "seq"),
        P(),
        P(),
        P(),
        P(),
        P(),
        P(("seq", "fsdp"), None),
    )
    return jax.shard_map(
        local,
        mesh=mesh,
        in_specs=placed,
        out_specs=(
            P(("seq", "fsdp"), None),
            P(("seq", "fsdp"), None),
            P(None, "seq", "fsdp"),
            P(None, "seq", "fsdp"),
            P(None, "seq", "fsdp"),
            P(None, "fsdp", "seq"),
            P(None, "seq", "fsdp"),
            P(None, "seq", "fsdp"),
            P(None, "fsdp", "seq"),
            P(),
            P(),
            P(),
            P(),
        ),
        check_vma=False,
    )
```

profile of v0, /device:TPU:0, one launch (start us, length us, event | category | flops | bytes accessed | tf_op | source)
XLA Modules:
  0.0 2709.3 jit_solution(14502727540435845923)
XLA Ops:
  16.4 25.6 all-gather.61.cloned.1.call-done
  42.0 41.6 %all-gather.45.cloned.1.call-done = bf16[640,2048]{1,0:T(8,128)(2,1)} async-done(((bf16[160,2048]{1,0:T(8,128)(2,1)}), bf16[640,2048]{1,0:T(8,128)(2,1)}) %all-gather.45.cloned.1.call-update) | async-done | bytes 2621456 | tf_op jit(solution)/shard_map/all_gather | solution.py:67
  88.6 26.4 all-gather.63.cloned.1.call-done
  233.3 12.7 all-gather.15
  258.4 12.7 all-gather.14
  274.0 10.1 psum.56
  296.8 33.8 %reduce-scatter.23.cloned.1.call-done = bf16[160,2048]{1,0:T(8,128)(2,1)} async-done(((bf16[640,2048]{1,0:T(8,128)(2,1)}), bf16[160,2048]{1,0:T(8,128)(2,1)}) %reduce-scatter.23.cloned.1.call-update) | async-done | bytes 655376 | tf_op jit(solution)/shard_map/reduce_scatter | solution.py:79
  338.4 54.8 %all-gather.69.cloned.1.call-done = bf16[1,2048,1408]{2,1,0:T(8,128)(2,1)} async-done(((bf16[1,256,1408]{2,1,0:T(8,128)(2,1)}), bf16[1,2048,1408]{2,1,0:T(8,128)(2,1)}) %all-gather.69.cloned.1.call-update) | async-done | bytes 5767184 | tf_op jit(solution)/shard_map/all_gather | solution.py:141
  393.2 40.8 %all-gather.47.cloned.1.call-done = bf16[640,2048]{1,0:T(8,128)(2,1)} async-done(((bf16[160,2048]{1,0:T(8,128)(2,1)}), bf16[640,2048]{1,0:T(8,128)(2,1)}) %all-gather.47.cloned.1.call-update) | async-done | bytes 2621456 | tf_op jit(solution)/shard_map/all_gather | solution.py:67
  434.0 9.4 fusion.22
  443.5 53.2 %all-gather.71.cloned.1.call-done = bf16[1,2048,1408]{2,1,0:T(8,128)(2,1)} async-done(((bf16[1,256,1408]{2,1,0:T(8,128)(2,1)}), bf16[1,2048,1408]{2,1,0:T(8,128)(2,1)}) %all-gather.71.cloned.1.call-update) | async-done | bytes 5767184 | tf_op jit(solution)/shard_map/all_gather | solution.py:140
  496.7 11.1 multiply_convert_fusion.5
  507.8 50.5 %all-gather.73.cloned.1.call-done = bf16[1,1408,2048]{2,1,0:T(8,128)(2,1)} async-done(((bf16[1,1408,256]{2,1,0:T(8,128)(2,1)}), bf16[1,1408,2048]{2,1,0:T(8,128)(2,1)}) %all-gather.73.cloned.1.call-update) | async-done | bytes 5767184 | tf_op jit(solution)/shard_map/all_gather | solution.py:142
  558.3 8.9 fusion.30
  567.8 37.3 %reduce-scatter.25.cloned.1.call-done = bf16[160,2048]{1,0:T(8,128)(2,1)} async-done(((bf16[640,2048]{1,0:T(8,128)(2,1)}), bf16[160,2048]{1,0:T(8,128)(2,1)}) %reduce-scatter.25.cloned.1.call-update) | async-done | bytes 655376 | tf_op jit(solution)/shard_map/reduce_scatter | solution.py:79
  607.7 9.7 all-gather.77.cloned.1.call-start
  618.6 17.1 all-gather.75.cloned.1.call-done
  635.7 41.6 %all-gather.49.cloned.1.call-done = bf16[640,2048]{1,0:T(8,128)(2,1)} async-done(((bf16[160,2048]{1,0:T(8,128)(2,1)}), bf16[640,2048]{1,0:T(8,128)(2,1)}) %all-gather.49.cloned.1.call-update) | async-done | bytes 2621456 | tf_op jit(solution)/shard_map/all_gather | solution.py:67
  682.3 25.6 all-gather.77.cloned.1.call-done
  844.4 12.7 all-gather.17
  863.8 12.7 all-gather.16
  879.8 9.9 psum.57
  901.7 34.5 %reduce-scatter.27.cloned.1.call-done = bf16[160,2048]{1,0:T(8,128)(2,1)} async-done(((bf16[640,2048]{1,0:T(8,128)(2,1)}), bf16[160,2048]{1,0:T(8,128)(2,1)}) %reduce-scatter.27.cloned.1.call-update) | async-done | bytes 655376 | tf_op jit(solution)/shard_map/reduce_scatter | solution.py:79
  939.9 37.7 %all-gather.53.cloned.1.call-done = bf16[640,2048]{1,0:T(8,128)(2,1)} async-done(((bf16[160,2048]{1,0:T(8,128)(2,1)}), bf16[640,2048]{1,0:T(8,128)(2,1)}) %all-gather.53.cloned.1.call-update) | async-done | bytes 2621456 | tf_op jit(solution)/shard_map/all_gather | solution.py:71
  977.5 62.5 %all-gather.87.cloned.1.call-done = bf16[1,1408,2048]{2,1,0:T(8,128)(2,1)} async-done(((bf16[1,1408,256]{2,1,0:T(8,128)(2,1)}), bf16[1,1408,2048]{2,1,0:T(8,128)(2,1)}) %all-gather.87.cloned.1.call-update) | async-done | bytes 5767184 | tf_op jit(solution)/shard_map/all_gather | solution.py:142
  1040.0 9.4 fusion
  1049.4 51.3 %all-gather.85.cloned.1.call-done = bf16[1,2048,1408]{2,1,0:T(8,128)(2,1)} async-done(((bf16[1,256,1408]{2,1,0:T(8,128)(2,1)}), bf16[1,2048,1408]{2,1,0:T(8,128)(2,1)}) %all-gather.85.cloned.1.call-update) | async-done | bytes 5767184 | tf_op jit(solution)/shard_map/all_gather | solution.py:140
  1100.7 40.8 %all-gather.51.cloned.1.call-done = bf16[640,2048]{1,0:T(8,128)(2,1)} async-done(((bf16[160,2048]{1,0:T(8,128)(2,1)}), bf16[640,2048]{1,0:T(8,128)(2,1)}) %all-gather.51.cloned.1.call-update) | async-done | bytes 2621456 | tf_op jit(solution)/shard_map/all_gather | solution.py:67
  1141.5 9.4 fusion.6
  1150.9 53.2 %all-gather.83.cloned.1.call-done = bf16[1,2048,1408]{2,1,0:T(8,128)(2,1)} async-done(((bf16[1,256,1408]{2,1,0:T(8,128)(2,1)}), bf16[1,2048,1408]{2,1,0:T(8,128)(2,1)}) %all-gather.83.cloned.1.call-update) | async-done | bytes 5767184 | tf_op jit(solution)/shard_map/all_gather | solution.py:141
  1204.2 12.4 multiply_convert_fusion.2
  1226.7 38.4 %reduce-scatter.31.cloned.1.call-done = bf16[160,2048]{1,0:T(8,128)(2,1)} async-done(((bf16[640,2048]{1,0:T(8,128)(2,1)}), bf16[160,2048]{1,0:T(8,128)(2,1)}) %reduce-scatter.31.cloned.1.call-update) | async-done | bytes 655376 | tf_op jit(solution)/shard_map/reduce_scatter | solution.py:95
  1315.3 8.9 psum.58
  1548.1 12.7 all-gather.19
  1560.8 12.7 all-gather.18
  1574.2 10.7 rev.17
  1585.0 10.7 rev.16
  1608.6 8.9 fusion.33
  1617.6 28.3 %reduce-scatter.33.cloned.1.call-done = bf16[160,2048]{1,0:T(8,128)(2,1)} async-done(((bf16[640,2048]{1,0:T(8,128)(2,1)}), bf16[160,2048]{1,0:T(8,128)(2,1)}) %reduce-scatter.33.cloned.1.call-update) | async-done | bytes 655376 | tf_op jit(solution)/shard_map/reduce_scatter | solution.py:95
  1648.1 40.8 %reduce-scatter.29.cloned.1.call-done = bf16[160,2048]{1,0:T(8,128)(2,1)} async-done(((bf16[640,2048]{1,0:T(8,128)(2,1)}), bf16[160,2048]{1,0:T(8,128)(2,1)}) %reduce-scatter.29.cloned.1.call-update) | async-done | bytes 655376 | tf_op jit(solution)/shard_map/reduce_scatter | solution.py:79
  1693.1 39.3 %all-gather.57.cloned.1.call-done = bf16[640,2048]{1,0:T(8,128)(2,1)} async-done(((bf16[160,2048]{1,0:T(8,128)(2,1)}), bf16[640,2048]{1,0:T(8,128)(2,1)}) %all-gather.57.cloned.1.call-update) | async-done | bytes 2621456 | tf_op jit(solution)/shard_map/all_gather | solution.py:71
  1732.4 10.7 multiply_convert_fusion
  1759.1 39.7 %reduce-scatter.35.cloned.1.call-done = bf16[160,2048]{1,0:T(8,128)(2,1)} async-done(((bf16[640,2048]{1,0:T(8,128)(2,1)}), bf16[160,2048]{1,0:T(8,128)(2,1)}) %reduce-scatter.35.cloned.1.call-update) | async-done | bytes 655376 | tf_op jit(solution)/shard_map/reduce_scatter | solution.py:95
  1802.9 9.5 convolution_convert_fusion
  1812.5 9.5 convolution_convert_fusion.1
  1822.0 8.7 convolution_convert_fusion.2
  1831.0 8.7 convolution_convert_fusion.3
  1839.7 8.8 convolution_convert_fusion.4
  1848.6 8.7 convolution_convert_fusion.5
  1928.0 9.1 psum.59
  2158.8 13.4 all-gather.21
  2172.2 12.7 all-gather.20
  2184.9 10.7 rev.19
  2195.6 10.7 rev.18
  2249.0 24.6 reduce-scatter.53.cloned.1.call-done
  2273.5 36.5 %reduce-scatter.51.cloned.1.call-done = bf16[512,256]{1,0:T(8,128)(2,1)} async-done(((bf16[512,2048]{1,0:T(8,128)(2,1)}), bf16[512,256]{1,0:T(8,128)(2,1)}) %reduce-scatter.51.cloned.1.call-update) | async-done | bytes 262160 | tf_op jit(solution)/shard_map/reduce_scatter | solution.py:316
  2312.1 34.6 %reduce-scatter.49.cloned.1.call-done = bf16[256,512]{1,0:T(8,128)(2,1)} async-done(((bf16[2048,512]{1,0:T(8,128)(2,1)}), bf16[256,512]{1,0:T(8,128)(2,1)}) %reduce-scatter.49.cloned.1.call-update) | async-done | bytes 262160 | tf_op jit(solution)/shard_map/reduce_scatter | solution.py:313
  2346.7 36.7 %reduce-scatter.47.cloned.1.call-done = bf16[256,512]{1,0:T(8,128)(2,1)} async-done(((bf16[2048,512]{1,0:T(8,128)(2,1)}), bf16[256,512]{1,0:T(8,128)(2,1)}) %reduce-scatter.47.cloned.1.call-update) | async-done | bytes 262160 | tf_op jit(solution)/shard_map/reduce_scatter | solution.py:313
  2385.5 34.7 %reduce-scatter.45.cloned.1.call-done = bf16[256,512]{1,0:T(8,128)(2,1)} async-done(((bf16[2048,512]{1,0:T(8,128)(2,1)}), bf16[256,512]{1,0:T(8,128)(2,1)}) %reduce-scatter.45.cloned.1.call-update) | async-done | bytes 262160 | tf_op jit(solution)/shard_map/reduce_scatter | solution.py:310
  2420.2 36.9 %reduce-scatter.43.cloned.1.call-done = bf16[256,512]{1,0:T(8,128)(2,1)} async-done(((bf16[2048,512]{1,0:T(8,128)(2,1)}), bf16[256,512]{1,0:T(8,128)(2,1)}) %reduce-scatter.43.cloned.1.call-update) | async-done | bytes 262160 | tf_op jit(solution)/shard_map/reduce_scatter | solution.py:310
  2459.1 34.6 %reduce-scatter.41.cloned.1.call-done = bf16[256,512]{1,0:T(8,128)(2,1)} async-done(((bf16[2048,512]{1,0:T(8,128)(2,1)}), bf16[256,512]{1,0:T(8,128)(2,1)}) %reduce-scatter.41.cloned.1.call-update) | async-done | bytes 262160 | tf_op jit(solution)/shard_map/reduce_scatter | solution.py:307
  2493.7 36.6 %reduce-scatter.39.cloned.1.call-done = bf16[256,512]{1,0:T(8,128)(2,1)} async-done(((bf16[2048,512]{1,0:T(8,128)(2,1)}), bf16[256,512]{1,0:T(8,128)(2,1)}) %reduce-scatter.39.cloned.1.call-update) | async-done | bytes 262160 | tf_op jit(solution)/shard_map/reduce_scatter | solution.py:307
  2532.5 39.1 %reduce-scatter.37.cloned.1.call-done = bf16[160,2048]{1,0:T(8,128)(2,1)} async-done(((bf16[640,2048]{1,0:T(8,128)(2,1)}), bf16[160,2048]{1,0:T(8,128)(2,1)}) %reduce-scatter.37.cloned.1.call-update) | async-done | bytes 655376 | tf_op jit(solution)/shard_map/reduce_scatter | solution.py:95
  2577.0 120.3 %all-reduce.151.cloned.1.call-done = (f32[2,2048]{1,0:T(2,128)}, f32[2,2048]{1,0:T(2,128)}, f32[2,2048]{1,0:T(2,128)}, f32[2,2048]{1,0:T(2,128)}) async-done(((f32[2,2048]{1,0:T(2,128)}, f32[2,2048]{1,0:T(2,128)}, f32[2,2048]{1,0:T(2,128)}, f32[2,2048]{1,0:T(2,128)}), (f32[2,2048]{1,0:T(2,128)}, f32[2,2048]{1,0:T(2,128)}, f32[2,2048]{1,0:T(2,128)}, f32[2,2048]{1,0:T(2,128)})) %all-reduce.151.cloned.1.call-update) | async-done | bytes 65552 | tf_op jit(solution)/shard_map/psum | solution.py:334
  (1307 shorter events, 1016.4 us)
Async XLA Ops:
  7.2 34.8 %all-gather.61.cloned.1.call-start = ((), (), s32[]{:S(2)}) async-start(), calls=%async_computation.52 | async-start | bytes 2359296 | tf_op jit(solution)/shard_map/all_gather | solution.py:136
  9.2 74.4 %all-gather.45.cloned.1.call-start = ((), (), s32[]{:S(2)}) async-start(), calls=%async_computation.22 | async-start | bytes 3276800 | tf_op jit(solution)/shard_map/all_gather | solution.py:67
  11.8 103.2 %all-gather.63.cloned.1.call-start = ((), (), s32[]{:S(2)}) async-start(), calls=%async_computation.53 | async-start | bytes 2359296 | tf_op jit(solution)/shard_map/all_gather | solution.py:137
  12.7 271.5 %all-gather.65.cloned.1.call-start = ((), (), s32[]{:S(2)}) async-start(), calls=%async_computation.54 | async-start | bytes 2359296 | tf_op jit(solution)/shard_map/all_gather | solution.py:138
  13.6 275.6 %all-gather.67.cloned.1.call-start = ((), (), s32[]{:S(2)}) async-start(), calls=%async_computation.55 | async-start | bytes 2359296 | tf_op jit(solution)/shard_map/all_gather | solution.py:139
  14.6 316.0 %reduce-scatter.23.cloned.1.call-start = ((), (), s32[]{:S(2)}) async-start(), calls=%async_computation.23 | async-start | bytes 3276800 | tf_op jit(solution)/shard_map/reduce_scatter | solution.py:79
  15.0 100.0 %copy-start.104 = (f32[640]{0:T(1024)}, f32[640]{0:T(1024)S(1)}, u32[]{:S(2)}) copy-start(f32[640]{0:T(1024)S(1)} %convert_subtract_fusion) | copy-start | bytes 7684
  16.4 98.5 %copy-start.116 = (f32[1,512]{1,0:T(1,128)}, f32[1,512]{1,0:T(1,128)S(1)}, u32[]{:S(2)}) copy-start(f32[1,512]{1,0:T(1,128)S(1)} %get-tuple-element.757) | copy-start | bytes 6148
  16.4 98.5 %copy-start.171 = (f32[1,512]{1,0:T(1,128)}, f32[1,512]{1,0:T(1,128)S(1)}, u32[]{:S(2)}) copy-start(f32[1,512]{1,0:T(1,128)S(1)} %get-tuple-element.758) | copy-start | bytes 6148
  120.7 92.4 %copy-start.9 = (f32[640,512]{1,0:T(8,128)}, f32[640,512]{1,0:T(8,128)S(1)}, u32[]{:S(2)}) copy-start(f32[640,512]{1,0:T(8,128)S(1)} %get-tuple-element.640) | copy-start | bytes 3932164
  294.2 99.1 %all-gather.69.cloned.1.call-start = ((), (), s32[]{:S(2)}) async-start(), calls=%async_computation.56 | async-start | bytes 6488064 | tf_op jit(solution)/shard_map/all_gather | solution.py:141
  296.7 137.3 %all-gather.47.cloned.1.call-start = ((), (), s32[]{:S(2)}) async-start(), calls=%async_computation.24 | async-start | bytes 3276800 | tf_op jit(solution)/shard_map/all_gather | solution.py:67
  333.2 163.5 %all-gather.71.cloned.1.call-start = ((), (), s32[]{:S(2)}) async-start(), calls=%async_computation.57 | async-start | bytes 6488064 | tf_op jit(solution)/shard_map/all_gather | solution.py:140
  335.8 222.5 %all-gather.73.cloned.1.call-start = ((), (), s32[]{:S(2)}) async-start(), calls=%async_computation.58 | async-start | bytes 6488064 | tf_op jit(solution)/shard_map/all_gather | solution.py:142
  338.4 266.7 %reduce-scatter.25.cloned.1.call-start = ((), (), s32[]{:S(2)}) async-start(), calls=%async_computation.25 | async-start | bytes 3276800 | tf_op jit(solution)/shard_map/reduce_scatter | solution.py:79
  567.2 68.5 %all-gather.75.cloned.1.call-start = ((), (), s32[]{:S(2)}) async-start(), calls=%async_computation.59 | async-start | bytes 2359296 | tf_op jit(solution)/shard_map/all_gather | solution.py:136
  567.8 109.5 %all-gather.49.cloned.1.call-start = ((), (), s32[]{:S(2)}) async-start(), calls=%async_computation.26 | async-start | bytes 3276800 | tf_op jit(solution)/shard_map/all_gather | solution.py:67
  607.7 100.2 %all-gather.77.cloned.1.call-start = ((), (), s32[]{:S(2)}) async-start(), calls=%async_computation.60 | async-start | bytes 2359296 | tf_op jit(solution)/shard_map/all_gather | solution.py:137
  617.4 272.3 %all-gather.79.cloned.1.call-start = ((), (), s32[]{:S(2)}) async-start(), calls=%async_computation.61 | async-start | bytes 2359296 | tf_op jit(solution)/shard_map/all_gather | solution.py:138
  618.0 276.9 %all-gather.81.cloned.1.call-start = ((), (), s32[]{:S(2)}) async-start(), calls=%async_computation.62 | async-start | bytes 2359296 | tf_op jit(solution)/shard_map/all_gather | solution.py:139
  618.5 317.6 %reduce-scatter.27.cloned.1.call-start = ((), (), s32[]{:S(2)}) async-start(), calls=%async_computation.27 | async-start | bytes 3276800 | tf_op jit(solution)/shard_map/reduce_scatter | solution.py:79
  618.6 89.3 %copy-start.105 = (f32[640]{0:T(1024)S(1)}, f32[640]{0:T(1024)}, u32[]{:S(2)}) copy-start(f32[640]{0:T(1024)} %copy-done.104) | copy-start | bytes 7684
  618.6 89.3 %copy-start.118 = (f32[1,512]{1,0:T(1,128)S(1)}, f32[1,512]{1,0:T(1,128)}, u32[]{:S(2)}) copy-start(f32[1,512]{1,0:T(1,128)} %get-tuple-element.605) | copy-start | bytes 6148
  618.6 89.3 %copy-start.175 = (f32[1,512]{1,0:T(1,128)S(1)}, f32[1,512]{1,0:T(1,128)}, u32[]{:S(2)}) copy-start(f32[1,512]{1,0:T(1,128)} %get-tuple-element.606) | copy-start | bytes 6148
  714.1 107.3 %copy-start.10 = (f32[640,512]{1,0:T(8,128)}, f32[640,512]{1,0:T(8,128)S(1)}, u32[]{:S(2)}) copy-start(f32[640,512]{1,0:T(8,128)S(1)} %get-tuple-element.638) | copy-start | bytes 3932164
  899.8 77.8 %all-gather.53.cloned.1.call-start = ((), (), s32[]{:S(2)}) async-start(), calls=%async_computation.30 | async-start | bytes 3276800 | tf_op jit(solution)/shard_map/all_gather | solution.py:71
  900.3 139.7 %all-gather.87.cloned.1.call-start = ((), (), s32[]{:S(2)}) async-start(), calls=%async_computation.65 | async-start | bytes 6488064 | tf_op jit(solution)/shard_map/all_gather | solution.py:142
  901.1 199.6 %all-gather.85.cloned.1.call-start = ((), (), s32[]{:S(2)}) async-start(), calls=%async_computation.64 | async-start | bytes 6488064 | tf_op jit(solution)/shard_map/all_gather | solution.py:140
  901.7 239.8 %all-gather.51.cloned.1.call-start = ((), (), s32[]{:S(2)}) async-start(), calls=%async_computation.28 | async-start | bytes 3276800 | tf_op jit(solution)/shard_map/all_gather | solution.py:67
  938.7 265.5 %all-gather.83.cloned.1.call-start = ((), (), s32[]{:S(2)}) async-start(), calls=%async_computation.63 | async-start | bytes 6488064 | tf_op jit(solution)/shard_map/all_gather | solution.py:141
  939.4 325.6 %reduce-scatter.31.cloned.1.call-start = ((), (), s32[]{:S(2)}) async-start(), calls=%async_computation.31 | async-start | bytes 3276800 | tf_op jit(solution)/shard_map/reduce_scatter | solution.py:95
  1226.6 82.1 %all-gather.55.cloned.1.call-start = ((), (), s32[]{:S(2)}) async-start(), calls=%async_computation.32 | async-start | bytes 3276800 | tf_op jit(solution)/shard_map/all_gather | solution.py:71
  1268.9 377.0 %reduce-scatter.33.cloned.1.call-start = ((), (), s32[]{:S(2)}) async-start(), calls=%async_computation.33 | async-start | bytes 3276800 | tf_op jit(solution)/shard_map/reduce_scatter | solution.py:95
  1608.5 80.3 %reduce-scatter.29.cloned.1.call-start = ((), (), s32[]{:S(2)}) async-start(), calls=%async_computation.29 | async-start | bytes 3276800 | tf_op jit(solution)/shard_map/reduce_scatter | solution.py:79
  1617.5 71.4 %copy-start.147 = (f32[160]{0:T(256)S(1)}, f32[160]{0:T(256)}, u32[]{:S(2)}) copy-start(f32[160]{0:T(256)} %copy-done.146) | copy-start | bytes 1924
  1617.5 114.9 %all-gather.57.cloned.1.call-start = ((), (), s32[]{:S(2)}) async-start(), calls=%async_computation.34 | async-start | bytes 3276800 | tf_op jit(solution)/shard_map/all_gather | solution.py:71
  1692.6 108.7 %copy-start.7 = (f32[160,2048]{1,0:T(8,128)}, f32[160,2048]{1,0:T(8,128)S(1)}, u32[]{:S(2)}) copy-start(f32[160,2048]{1,0:T(8,128)S(1)} %get-tuple-element.602) | copy-start | bytes 3932164
  1692.6 106.2 %reduce-scatter.35.cloned.1.call-start = ((), (), s32[]{:S(2)}) async-start(), calls=%async_computation.35 | async-start | bytes 3276800 | tf_op jit(solution)/shard_map/reduce_scatter | solution.py:95
  1759.0 39.8 %copy-start.1 = (bf16[160,2048]{1,0:T(8,128)(2,1)S(1)}, bf16[160,2048]{1,0:T(8,128)(2,1)}, u32[]{:S(2)}) copy-start(bf16[160,2048]{1,0:T(8,128)(2,1)} %param.22) | copy-start | bytes 1966084
  1759.0 39.8 %copy-start.3 = (bf16[160,2048]{1,0:T(8,128)(2,1)S(1)}, bf16[160,2048]{1,0:T(8,128)(2,1)}, u32[]{:S(2)}) copy-start(bf16[160,2048]{1,0:T(8,128)(2,1)} %reduce-scatter.23.cloned.1.call-done) | copy-start | bytes 1966084
  1759.0 39.8 %copy-start.87 = (f32[1,2048]{1,0:T(1,128)S(1)}, f32[1,2048]{1,0:T(1,128)}, u32[]{:S(2)}) copy-start(f32[1,2048]{1,0:T(1,128)} %copy-done.86) | copy-start | bytes 24580
  1759.0 39.8 %copy-start.115 = (f32[160]{0:T(256)S(1)}, f32[160]{0:T(256)}, u32[]{:S(2)}) copy-start(f32[160]{0:T(256)} %copy-done.114) | copy-start | bytes 1924
  1759.1 104.3 %all-gather.59.cloned.1.call-start = ((), (), s32[]{:S(2)}) async-start(), calls=%async_computation.36 | async-start | bytes 3276800 | tf_op jit(solution)/shard_map/all_gather | solution.py:71
  1802.7 436.9 %reduce-scatter.65.cloned.1.call-start = ((), (), s32[]{:S(2)}) async-start(), calls=%async_computation.51 | async-start | bytes 6488064 | tf_op jit(solution)/shard_map/reduce_scatter | solution.py:325
  1812.4 427.1 %reduce-scatter.63.cloned.1.call-start = ((), (), s32[]{:S(2)}) async-start(), calls=%async_computation.50 | async-start | bytes 6488064 | tf_op jit(solution)/shard_map/reduce_scatter | solution.py:325
  1822.0 420.7 %reduce-scatter.61.cloned.1.call-start = ((), (), s32[]{:S(2)}) async-start(), calls=%async_computation.49 | async-start | bytes 6488064 | tf_op jit(solution)/shard_map/reduce_scatter | solution.py:322
  1830.7 411.9 %reduce-scatter.59.cloned.1.call-start = ((), (), s32[]{:S(2)}) async-start(), calls=%async_computation.48 | async-start | bytes 6488064 | tf_op jit(solution)/shard_map/reduce_scatter | solution.py:322
  1839.7 406.2 %reduce-scatter.57.cloned.1.call-start = ((), (), s32[]{:S(2)}) async-start(), calls=%async_computation.47 | async-start | bytes 6488064 | tf_op jit(solution)/shard_map/reduce_scatter | solution.py:319
  1848.5 397.3 %reduce-scatter.55.cloned.1.call-start = ((), (), s32[]{:S(2)}) async-start(), calls=%async_computation.46 | async-start | bytes 6488064 | tf_op jit(solution)/shard_map/reduce_scatter | solution.py:319
  1857.3 416.3 %reduce-scatter.53.cloned.1.call-start = ((), (), s32[]{:S(2)}) async-start(), calls=%async_computation.45 | async-start | bytes 2359296 | tf_op jit(solution)/shard_map/reduce_scatter | solution.py:316
  1863.4 446.7 %reduce-scatter.51.cloned.1.call-start = ((), (), s32[]{:S(2)}) async-start(), calls=%async_computation.44 | async-start | bytes 2359296 | tf_op jit(solution)/shard_map/reduce_scatter | solution.py:316
  1869.4 477.3 %reduce-scatter.49.cloned.1.call-start = ((), (), s32[]{:S(2)}) async-start(), calls=%async_computation.43 | async-start | bytes 2359296 | tf_op jit(solution)/shard_map/reduce_scatter | solution.py:313
  1875.4 508.0 %reduce-scatter.47.cloned.1.call-start = ((), (), s32[]{:S(2)}) async-start(), calls=%async_computation.42 | async-start | bytes 2359296 | tf_op jit(solution)/shard_map/reduce_scatter | solution.py:313
  1887.4 532.8 %reduce-scatter.45.cloned.1.call-start = ((), (), s32[]{:S(2)}) async-start(), calls=%async_computation.41 | async-start | bytes 2359296 | tf_op jit(solution)/shard_map/reduce_scatter | solution.py:310
  1928.0 529.0 %reduce-scatter.43.cloned.1.call-start = ((), (), s32[]{:S(2)}) async-start(), calls=%async_computation.40 | async-start | bytes 2359296 | tf_op jit(solution)/shard_map/reduce_scatter | solution.py:310
  2216.5 277.2 %reduce-scatter.41.cloned.1.call-start = ((), (), s32[]{:S(2)}) async-start(), calls=%async_computation.39 | async-start | bytes 2359296 | tf_op jit(solution)/shard_map/reduce_scatter | solution.py:307
  2222.6 307.7 %reduce-scatter.39.cloned.1.call-start = ((), (), s32[]{:S(2)}) async-start(), calls=%async_computation.38 | async-start | bytes 2359296 | tf_op jit(solution)/shard_map/reduce_scatter | solution.py:307
  2228.6 343.0 %reduce-scatter.37.cloned.1.call-start = ((), (), s32[]{:S(2)}) async-start(), calls=%async_computation.37 | async-start | bytes 3276800 | tf_op jit(solution)/shard_map/reduce_scatter | solution.py:95
  2236.9 460.4 %all-reduce.151.cloned.1.call-start = ((), (), s32[]{:S(2)}) async-start(), calls=%async_computation.66 | async-start | bytes 131072 | tf_op jit(solution)/shard_map/psum | solution.py:334
  2457.0 114.5 %copy-start.100 = (f32[1,2048]{1,0:T(1,128)S(1)}, f32[1,2048]{1,0:T(1,128)}, u32[]{:S(2)}) copy-start(f32[1,2048]{1,0:T(1,128)} %copy-done.99) | copy-start | bytes 24580
  2457.1 114.5 %copy-start.143 = (f32[160]{0:T(256)S(1)}, f32[160]{0:T(256)}, u32[]{:S(2)}) copy-start(f32[160]{0:T(256)} %copy-done.142) | copy-start | bytes 1924
  2530.3 43.0 %copy-start.108 = (f32[2048]{0:T(1024)S(1)}, f32[2048]{0:T(1024)}, u32[]{:S(2)}) copy-start(f32[2048]{0:T(1024)} %get-tuple-element.549) | copy-start | bytes 24580
  2530.3 43.6 %copy-start.8 = (f32[160,2048]{1,0:T(8,128)S(1)}, f32[160,2048]{1,0:T(8,128)}, u32[]{:S(2)}) copy-start(f32[160,2048]{1,0:T(8,128)} %copy-done.7) | copy-start | bytes 3932164
  2530.3 43.6 %copy-start.145 = (f32[160]{0:T(256)S(1)}, f32[160]{0:T(256)}, u32[]{:S(2)}) copy-start(f32[160]{0:T(256)} %copy-done.144) | copy-start | bytes 1924
  (195 other events, 1185.3 us)
Sparse Core Ops, SparseCore 0:
  10.2 31.7 all-gather.60
  44.5 39.1 all-gather.44
  85.8 29.0 all-gather.62
  116.4 28.5 all-gather.64
  146.5 30.3 all-gather.66
  294.3 36.2 reduce-scatter.22
  332.8 60.4 all-gather.68
  395.7 38.3 all-gather.46
  436.2 60.4 all-gather.70
  498.7 59.5 all-gather.72
  567.3 37.7 reduce-scatter.24
  606.6 29.0 all-gather.74
  638.1 39.1 all-gather.48
  678.8 29.0 all-gather.76
  709.3 28.5 all-gather.78
  739.4 30.3 all-gather.80
  899.9 36.2 reduce-scatter.26
  937.9 39.6 all-gather.52
  979.1 60.8 all-gather.86
  1042.1 58.5 all-gather.84
  1103.1 38.3 all-gather.50
  1143.7 60.4 all-gather.82
  1226.8 38.2 reduce-scatter.30
  1269.0 39.6 all-gather.54
  1608.7 37.1 reduce-scatter.32
  1649.3 39.5 reduce-scatter.28
  1692.7 39.6 all-gather.56
  1759.2 39.5 reduce-scatter.34
  1802.8 39.6 all-gather.58
  1844.6 64.8 reduce-scatter.64
  1911.8 63.2 reduce-scatter.62
  1977.4 63.2 reduce-scatter.60
  2042.8 63.2 reduce-scatter.58
  2108.3 63.3 reduce-scatter.56
  2174.0 63.2 reduce-scatter.54
  2239.4 34.0 reduce-scatter.52
  2275.7 34.3 reduce-scatter.50
  2312.3 34.3 reduce-scatter.48
  2348.9 34.4 reduce-scatter.46
  2385.7 34.4 reduce-scatter.44
  2422.5 34.5 reduce-scatter.42
  2459.3 34.3 reduce-scatter.40
  2495.9 34.3 reduce-scatter.38
  2533.3 38.2 reduce-scatter.36
  2578.2 119.0 all-reduce.150
where the time goes:
time: 2750 us; the launch traced here: 2710 us
  waiting for transfers between devices  1360 us (49%)
  local copies, waits for them, and re-layouts  683 us (25%)
  matrix products  266 us (10%)
  other arithmetic  230 us (8%)
  blocking collectives  140 us (5%)
    slice x138, local copies, waits for them, and re-layouts, local(): lax.associative_scan(combine, (next_decay, grad_state), axis=0, reverse=T...  292 us
    slice x128, local copies, waits for them, and re-layouts, local(): lax.associative_scan(combine, (decay_all, source), axis=0)  176 us
    all_gather x4, waiting for transfers between devices, gather_rows(): return lax.all_gather(values, 'fsdp', axis=0, tiled=True)  165 us
    reduce_scatter x4, waiting for transfers between devices, spread(): lax.psum_scatter(term(jnp.int32(0), lax.axis_size('fsdp') * row_count).as...  146 us
    reduce_scatter x4, waiting for transfers between devices, spread_back(): lax.psum_scatter(term(jnp.int32(0), lax.axis_size('fsdp') * row_count).as...  145 us
    psum x1, waiting for transfers between devices, local(): lax.psum((jnp.stack(grad_mix_list[::-1]), jnp.stack(grad_ffn_list[::-1]),...  120 us
    all_gather x2, waiting for transfers between devices, local(): lax.all_gather(w_down[layer_index], 'seq', axis=1, tiled=True)  113 us
    all_gather x2, waiting for transfers between devices, local(): lax.all_gather(w_glu[layer_index], 'seq', axis=0, tiled=True)  108 us
  transfers between devices with their start and end apart: 45, of which 34 were waited for; matrix products, arithmetic and copies ran while one was open for 30% of the time, Pallas kernels for 0%

commit v1 on v0

v1 whole, which is shorter than its diff:
```python
import functools

import jax
import jax.numpy as jnp
from jax import lax
from jax.experimental import pallas as pl
from jax.experimental.pallas import tpu as pltpu
from jax.sharding import PartitionSpec as P

LAYERS = 2
epsilon = 1e-06
STEP = 32
LANES = 256
f32 = jnp.float32
bf16 = jnp.bfloat16


def partners(step):
    return [(i, i ^ step) for i in range(lax.axis_size("fsdp"))]


def exchange(values, step):
    return lax.ppermute(values, "fsdp", partners(step))


def gather_rows(own):
    size = lax.axis_size("fsdp")
    return jnp.concatenate([own] + [exchange(own, step) for step in range(1, size)], axis=0)


def scatter_rows(part):
    size = lax.axis_size("fsdp")
    rows = part.shape[0] // size
    arrived = [exchange(part[step * rows : (step + 1) * rows], step) for step in range(1, size)]
    total = part[:rows].astype(f32)
    for piece in arrived:
        total = total + piece.astype(f32)
    return total


def total_rows(part):
    size = lax.axis_size("fsdp")
    pieces = part.reshape(size, -1)
    total = pieces
    for step in range(1, size):
        other = exchange(pieces, step)
        total = total + jnp.stack([other[k ^ step] for k in range(size)])
    return total.reshape(-1)


def dot(operand, matrix):
    return jnp.dot(operand, matrix, preferred_element_type=f32)


def trans_dot(operand, matrix):
    return lax.dot_general(operand, matrix, (((1,), (1,)), ((), ())), preferred_element_type=f32)


def outer_dot(operand, other):
    return lax.dot_general(operand, other, (((0,), (0,)), ((), ())), preferred_element_type=f32)


def rms_parts(values):
    factor = lax.rsqrt(jnp.mean(values * values, axis=-1, keepdims=True) + epsilon)
    return (values * factor, factor)


def norm_back(grad_unit, unit_rows, factor):
    return factor * (
        grad_unit - unit_rows * jnp.mean(grad_unit * unit_rows, axis=-1, keepdims=True)
    )


def dsilu(values, sigma):
    return sigma * (1.0 + values * (1.0 - sigma))


def sigmoid(values):
    return 1.0 / (1.0 + jnp.exp(-values))


def tile_base(place, index, size, per_piece):
    piece = lax.bitwise_xor(index // per_piece, place)
    return pl.multiple_of((piece * per_piece + lax.rem(index, per_piece)) * STEP, STEP)


def scan_kernel(size, place_ref, pi_ref, pf_ref, keep_ref, bound_ref, state_ref, decay_ref):
    rows, lanes = pi_ref.shape
    per_piece = rows // size // STEP
    place = place_ref[0]
    bound = bound_ref[...]
    row = lax.broadcasted_iota(jnp.int32, (8, lanes), 0)

    def step(index, carry):
        carry_decay, carry_state = carry
        base = tile_base(place, index, size, per_piece)
        here = pl.ds(base, STEP)
        forget = bound + (1.0 - bound) * sigmoid(pf_ref[here, :])
        inp = pi_ref[here, :]
        source = inp * sigmoid(inp) * (1.0 - forget)
        decay = forget * keep_ref[here, :]
        for part in range(STEP // 8):
            a = decay[part * 8 : part * 8 + 8]
            b = source[part * 8 : part * 8 + 8]
            for shift in (1, 2, 4):
                a_before = jnp.where(row >= shift, pltpu.roll(a, shift, 0), 1.0)
                b_before = jnp.where(row >= shift, pltpu.roll(b, shift, 0), 0.0)
                b = a * b_before + b
                a = a * a_before
            b = a * carry_state + b
            a = a * carry_decay
            state_ref[pl.ds(base + part * 8, 8), :] = b
            decay_ref[pl.ds(base + part * 8, 8), :] = a
            carry_decay, carry_state = a[7:8], b[7:8]
        return carry_decay, carry_state

    lax.fori_loop(
        0, rows // STEP, step, (jnp.ones((1, lanes), f32), jnp.zeros((1, lanes), f32))
    )


def back_kernel(
    size, width, place_ref, mixed_ref, state_ref, gate_ref, pf_ref, inverse_ref, inner_ref,
    keep_ref, bound_ref, gain_ref, adjoint_ref, reach_ref, grad_gate_ref, mix_ref, gain_out_ref,
):
    rows, lanes = mixed_ref.shape
    per_piece = rows // size // STEP
    place = place_ref[0]
    bound = bound_ref[...]
    gain = gain_ref[...]
    row = lax.broadcasted_iota(jnp.int32, (8, lanes), 0)
    tiles = rows // STEP

    def step(count, carry):
        carry_reach, carry_adjoint, later, gain_sum = carry
        base = tile_base(place, tiles - 1 - count, size, per_piece)
        here = pl.ds(base, STEP)
        grad_mixed = mixed_ref[here, :]
        inverse = inverse_ref[here, :]
        scaled = state_ref[here, :] * inverse
        gate = gate_ref[here, :]
        sigma = sigmoid(gate)
        silu_gate = gate * sigma
        piece = grad_mixed * scaled
        contribution = piece * silu_gate
        grad_gate_ref[here, :] = (piece * gain * dsilu(gate, sigma)).astype(bf16)
        mix_ref[here, :] = (scaled * gain * silu_gate).astype(bf16)
        grad_state = inverse * (
            grad_mixed * gain * silu_gate - scaled * (inner_ref[here, :] * (1.0 / width))
        )
        decay = (bound + (1.0 - bound) * sigmoid(pf_ref[here, :])) * keep_ref[here, :]
        for part in reversed(range(STEP // 8)):
            now = decay[part * 8 : part * 8 + 8]
            gain_sum = gain_sum + contribution[part * 8 : part * 8 + 8]
            a = jnp.where(row == 7, later, pltpu.roll(now, 7, 0))
            b = grad_state[part * 8 : part * 8 + 8]
            for shift in (1, 2, 4):
                a_after = jnp.where(row < 8 - shift, pltpu.roll(a, 8 - shift, 0), 1.0)
                b_after = jnp.where(row < 8 - shift, pltpu.roll(b, 8 - shift, 0), 0.0)
                b = a * b_after + b
                a = a * a_after
            b = a * carry_adjoint + b
            a = a * carry_reach
            adjoint_ref[pl.ds(base + part * 8, 8), :] = b
            reach_ref[pl.ds(base + part * 8, 8), :] = a
            carry_reach, carry_adjoint, later = a[0:1], b[0:1], now[0:1]
        return carry_reach, carry_adjoint, later, gain_sum

    one, zero = jnp.ones((1, lanes), f32), jnp.zeros((1, lanes), f32)
    last = lax.fori_loop(0, tiles, step, (one, zero, one, jnp.zeros((8, lanes), f32)))
    gain_out_ref[...] = jnp.sum(last[3], axis=0, keepdims=True)


def gates_kernel(
    size, place_ref, adjoint_ref, reach_ref, state_ref, pi_ref, pf_ref, keep_ref, bound_ref,
    coming_ref, entering_ref, grad_input_ref, grad_forget_ref, bound_out_ref,
):
    rows, lanes = adjoint_ref.shape
    per_piece = rows // size // STEP
    place = place_ref[0]
    bound = bound_ref[...]
    coming = coming_ref[...]
    row = lax.broadcasted_iota(jnp.int32, (STEP, lanes), 0)

    def step(index, carry):
        before, bound_sum = carry
        base = tile_base(place, index, size, per_piece)
        here = pl.ds(base, STEP)
        adjoint = adjoint_ref[here, :] + reach_ref[here, :] * coming
        state = state_ref[here, :]
        previous = jnp.where(row == 0, before, pltpu.roll(state, 1, 0))
        inp = pi_ref[here, :]
        sigma_input = sigmoid(inp)
        sigma_forget = sigmoid(pf_ref[here, :])
        forget = bound + (1.0 - bound) * sigma_forget
        grad_forget = adjoint * (keep_ref[here, :] * previous - inp * sigma_input)
        piece = grad_forget * (1.0 - sigma_forget)
        grad_input_ref[here, :] = (adjoint * (1.0 - forget) * dsilu(inp, sigma_input)).astype(bf16)
        grad_forget_ref[here, :] = (piece * (1.0 - bound) * sigma_forget).astype(bf16)
        for part in range(STEP // 8):
            bound_sum = bound_sum + piece[part * 8 : part * 8 + 8]
        return state[STEP - 1 : STEP], bound_sum

    last = lax.fori_loop(
        0, rows // STEP, step, (entering_ref[...], jnp.zeros((8, lanes), f32))
    )
    bound_out_ref[...] = jnp.sum(last[1], axis=0, keepdims=True)


def over_channels(kernel, place, operands, outs, cost):
    channels = operands[0].shape[1]
    lanes = min(LANES, channels)

    def spec(rows, whole):
        if whole:
            return pl.BlockSpec((rows, 1), lambda c, p: (0, 0))
        return pl.BlockSpec((rows, lanes), lambda c, p: (0, c))

    return pl.pallas_call(
        kernel,
        grid_spec=pltpu.PrefetchScalarGridSpec(
            num_scalar_prefetch=1,
            grid=(channels // lanes,),
            in_specs=[spec(o.shape[0], o.shape[1] == 1) for o in operands],
            out_specs=[spec(rows, False) for rows, _ in outs],
        ),
        out_shape=[jax.ShapeDtypeStruct((rows, channels), kind) for rows, kind in outs],
        compiler_params=pltpu.CompilerParams(vmem_limit_bytes=48 * 1024 * 1024),
        cost_estimate=pl.CostEstimate(
            flops=cost * operands[0].size, bytes_accessed=4 * (len(operands) + len(outs)) * operands[0].size,
            transcendentals=2 * operands[0].size,
        ),
    )(place, *operands)


def entering_of(decay, state, reverse):
    length, here = lax.axis_size("seq"), lax.axis_index("seq")
    everything = lax.all_gather(jnp.concatenate([decay, state], axis=0), "seq")
    total = jnp.zeros_like(state)
    for k in range(length):
        at = length - 1 - k if reverse else k
        reached = at > here if reverse else at < here
        new = everything[at, 0:1] * total + everything[at, 1:2]
        total = jnp.where(reached, new, total)
    return total


def total_small(rows_of_width, rows_of_channels, first_channel, channels):
    size = lax.axis_size("fsdp")
    place = lax.axis_index("fsdp")

    def columns(step):
        return lax.dynamic_slice_in_dim(
            rows_of_width, lax.bitwise_xor(place, step) * channels, channels, 1
        )

    mine = columns(0)
    for step in range(1, size):
        mine = mine + exchange(columns(step), step)
    mine = jnp.sum(lax.all_gather(jnp.concatenate([mine, rows_of_channels], axis=0), "seq"), axis=0)
    whole = jnp.zeros((mine.shape[0], channels * size), f32)
    whole = lax.dynamic_update_slice_in_dim(whole, mine, first_channel, 1)
    for step in range(1, size):
        whole = lax.dynamic_update_slice_in_dim(
            whole, exchange(mine, step), lax.bitwise_xor(place, step) * channels, 1
        )
    return whole


def local(
    hidden_in, w_input, w_forget, w_gate, w_out, w_up, w_glu, w_down,
    lower_bound, norm_mix, norm_ffn, out_gain, lengths, cotangent,
):
    row_count, model_width = hidden_in.shape
    channels = w_input.shape[2]
    hidden_units = w_up.shape[2]
    size = lax.axis_size("fsdp")
    place = lax.axis_index("fsdp")
    block_rows = row_count * size
    first_channel = place * channels
    place_array = jnp.reshape(place, (1,)).astype(jnp.int32)

    starts = jnp.cumsum(lengths) - lengths
    owners = lax.bitwise_xor(jnp.arange(size, dtype=jnp.int32), place.astype(jnp.int32))
    positions = (
        lax.axis_index("seq") * block_rows
        + (owners[:, None] * row_count + jnp.arange(row_count, dtype=jnp.int32)[None, :])
    ).reshape(-1)
    keep = (1.0 - jnp.any(positions[:, None] == starts[None, :], axis=1).astype(f32))[:, None]
    bounds = lax.dynamic_slice_in_dim(lower_bound, first_channel, channels, 1)
    gains = lax.dynamic_slice_in_dim(out_gain, first_channel, channels, 1)

    matrices = []
    for layer in range(LAYERS):
        mix_matrix = lax.all_gather(
            jnp.concatenate([w_input[layer], w_forget[layer], w_gate[layer]], axis=1),
            "seq", axis=0, tiled=True,
        )
        out_matrix = lax.all_gather(w_out[layer], "seq", axis=1, tiled=True)
        up_matrix = lax.all_gather(
            jnp.concatenate([w_up[layer], w_glu[layer]], axis=1), "seq", axis=0, tiled=True
        )
        down_matrix = lax.all_gather(w_down[layer], "seq", axis=1, tiled=True)
        matrices.append((mix_matrix, out_matrix, up_matrix, down_matrix))

    stream = hidden_in.astype(f32)
    saved = []
    for layer in range(LAYERS):
        mix_matrix, out_matrix, up_matrix, down_matrix = matrices[layer]
        bound, gain = bounds[layer][None, :], gains[layer][None, :]
        unit, _ = rms_parts(stream)
        normed = gather_rows((unit * norm_mix[layer]).astype(bf16))
        projected = dot(normed, mix_matrix)
        proj_input = projected[:, :channels]
        proj_forget = projected[:, channels : 2 * channels]
        proj_gate = projected[:, 2 * channels :]
        local_state, local_decay = over_channels(
            functools.partial(scan_kernel, size),
            place_array,
            (proj_input, proj_forget, keep, bound),
            ((block_rows, f32), (block_rows, f32)),
            40,
        )
        last_row = lax.bitwise_xor(size - 1, place) * row_count + row_count - 1
        entering = entering_of(
            lax.dynamic_slice_in_dim(local_decay, last_row, 1, 0),
            lax.dynamic_slice_in_dim(local_state, last_row, 1, 0),
            False,
        )
        state = local_state + local_decay * entering
        squares = total_rows(jnp.sum(state * state, axis=1))
        inverse = lax.rsqrt(squares / model_width + epsilon)[:, None]
        loose = (state * gain * jax.nn.silu(proj_gate)).astype(bf16)
        branch = scatter_rows(dot(loose, out_matrix).astype(bf16)) * inverse[:row_count]
        middle = stream + branch
        unit_two, _ = rms_parts(middle)
        normed_two = gather_rows((unit_two * norm_ffn[layer]).astype(bf16))
        both = dot(normed_two, up_matrix)
        upward, gating = both[:, :hidden_units], both[:, hidden_units:]
        hidden = (jax.nn.silu(gating) * upward).astype(bf16)
        saved.append(
            (stream, normed, proj_input, proj_forget, proj_gate, entering, state, inverse,
             branch, middle, normed_two, upward, gating, hidden)
        )
        stream = middle + scatter_rows(dot(hidden, down_matrix).astype(bf16))
    hidden_out = stream.astype(bf16)

    grad_x = cotangent.astype(f32)
    shards = [None] * LAYERS
    smalls = [None] * LAYERS
    for layer in reversed(range(LAYERS)):
        mix_matrix, out_matrix, up_matrix, down_matrix = matrices[layer]
        bound, gain = bounds[layer][None, :], gains[layer][None, :]
        (stream, normed, proj_input, proj_forget, proj_gate, entering, state, inverse,
         branch, middle, normed_two, upward, gating, hidden) = saved[layer]
        unit, factor = rms_parts(stream)
        unit_two, factor_two = rms_parts(middle)

        grad_y = gather_rows(grad_x.astype(bf16))
        grad_hidden = trans_dot(grad_y, down_matrix)
        down_part = outer_dot(hidden, grad_y).astype(bf16)
        sigma = jax.nn.sigmoid(gating)
        grad_both = jnp.concatenate(
            [
                (grad_hidden * gating * sigma).astype(bf16),
                (grad_hidden * upward * dsilu(gating, sigma)).astype(bf16),
            ],
            axis=1,
        )
        grad_normed_two = scatter_rows(trans_dot(grad_both, up_matrix).astype(bf16))
        up_part = outer_dot(normed_two, grad_both).astype(bf16)
        ffn_piece = jnp.sum(grad_normed_two * unit_two, axis=0)
        grad_middle = grad_x + norm_back(grad_normed_two * norm_ffn[layer], unit_two, factor_two)

        grad_m_own = grad_middle.astype(bf16)
        grad_m = gather_rows(grad_m_own)
        inner = gather_rows(jnp.sum(grad_m_own.astype(f32) * branch, axis=1))[:, None]
        grad_mixed = trans_dot(grad_m, out_matrix)
        adjoint, reach, grad_gate, mixed, gain_piece = over_channels(
            functools.partial(back_kernel, size, model_width),
            place_array,
            (grad_mixed, state, proj_gate, proj_forget, inverse, inner, keep, bound, gain),
            ((block_rows, f32), (block_rows, f32), (block_rows, bf16), (block_rows, bf16), (1, f32)),
            60,
        )
        out_part = outer_dot(mixed, grad_m).astype(bf16)
        first_row = place * row_count
        first_decay = (
            bound
            + (1.0 - bound)
            * jax.nn.sigmoid(lax.dynamic_slice_in_dim(proj_forget, first_row, 1, 0))
        ) * lax.dynamic_slice_in_dim(keep, first_row, 1, 0)
        coming = entering_of(
            first_decay * lax.dynamic_slice_in_dim(reach, first_row, 1, 0),
            first_decay * lax.dynamic_slice_in_dim(adjoint, first_row, 1, 0),
            True,
        )
        grad_input, grad_forget, bound_piece = over_channels(
            functools.partial(gates_kernel, size),
            place_array,
            (adjoint, reach, state, proj_input, proj_forget, keep, bound, coming, entering),
            ((block_rows, bf16), (block_rows, bf16), (1, f32)),
            40,
        )
        grad_three = jnp.concatenate([grad_input, grad_forget, grad_gate], axis=1)
        grad_normed = scatter_rows(trans_dot(grad_three, mix_matrix).astype(bf16))
        mix_part = outer_dot(normed, grad_three).astype(bf16)
        mix_piece = jnp.sum(grad_normed * unit, axis=0)
        grad_x = grad_middle + norm_back(grad_normed * norm_mix[layer], unit, factor)

        down_shard = lax.psum_scatter(down_part, "seq", scatter_dimension=1, tiled=True)
        up_shard = lax.psum_scatter(up_part, "seq", scatter_dimension=0, tiled=True)
        out_shard = lax.psum_scatter(out_part, "seq", scatter_dimension=1, tiled=True)
        mix_shard = lax.psum_scatter(mix_part, "seq", scatter_dimension=0, tiled=True)
        shards[layer] = (
            mix_shard[:, :channels],
            mix_shard[:, channels : 2 * channels],
            mix_shard[:, 2 * channels :],
            out_shard,
            up_shard[:, :hidden_units],
            up_shard[:, hidden_units:],
            down_shard,
        )
        smalls[layer] = total_small(
            jnp.stack([mix_piece, ffn_piece]),
            jnp.concatenate([bound_piece, gain_piece], axis=0),
            first_channel,
            channels,
        )
    stacked = tuple(
        jnp.stack([shards[layer][member].astype(f32) for layer in range(LAYERS)])
        for member in range(7)
    )
    small = jnp.stack(smalls)
    return (hidden_out, grad_x, *stacked, small[:, 2], small[:, 0], small[:, 1], small[:, 3])


def solution(mesh):
    rows = P(("seq", "fsdp"), None)
    wide = P(None, "seq", "fsdp")
    tall = P(None, "fsdp", "seq")
    weights = (wide, wide, wide, tall, wide, wide, tall)
    return jax.shard_map(
        local,
        mesh=mesh,
        in_specs=(rows, *weights, P(), P(), P(), P(), P(), rows),
        out_specs=(rows, rows, *weights, P(), P(), P(), P()),
        check_vma=False,
    )
```

time: 2750 us -> 1450 us (0.53); the launches traced: 2710 us -> 1440 us
  local copies, waits for them, and re-layouts: 683 us -> 56.6 us
  waiting for transfers between devices: 1360 us -> 913 us
  other arithmetic: 230 us -> 49.5 us
  starting transfers between devices: 13.3 us -> 84.7 us
  matrix products: 266 us -> 201 us
  blocking collectives: 140 us -> 84.9 us
  Pallas kernels: 0 us -> 35 us
    all_gather x22 -> x8, waiting for transfers between devices: 666 us -> 178 us  [the longest x2 92 us: local(): down_matrix = lax.all_gather(w_down[layer], 'seq', axis=1, tiled=True)]
    slice x277 -> x25, local copies, waits for them, and re-layouts: 482 us -> 13.2 us  [the longest x8 4.99 us: scatter_rows(): part[step * rows:(step + 1) * rows]]
    ppermute x0 -> x72, waiting for transfers between devices: none -> 385 us  [exchange(): return lax.ppermute(values, 'fsdp', partners(step))]
    reduce_scatter x22 -> x8, waiting for transfers between devices: 567 us -> 350 us  [the longest x2 234 us: local(): up_shard = lax.psum_scatter(up_part, 'seq', scatter_dimension=0, tiled=True)]
    pad x128 -> x0, local copies, waits for them, and re-layouts: 129 us -> none  [the longest x64 101 us: local(): lax.associative_scan(combine, (next_decay, grad_state), axis=0, reverse=T...]
    psum x1 -> x0, waiting for transfers between devices: 120 us -> none  [local(): lax.psum((jnp.stack(grad_mix_list[::-1]), jnp.stack(grad_ffn_list[::-1]),...]
    ppermute x0 -> x72, starting transfers between devices: none -> 83.8 us  [exchange(): return lax.ppermute(values, 'fsdp', partners(step))]
    add x94 -> x6, other arithmetic: 82.9 us -> 2.02 us  [the longest x1 1.78 us: local(): grad_middle + norm_back(grad_normed * norm_mix[layer], unit, factor)]
  transfers between devices with their start and end apart: 45 -> 88, of which waited for: 34 -> 46; matrix products, arithmetic and copies ran while one was open for 30% -> 16% of each run, Pallas kernels for 0% -> 2%
where the time goes in v1:
time: 1450 us; the launch traced here: 1440 us
  waiting for transfers between devices  913 us (63%)
  matrix products  201 us (14%)
  blocking collectives  84.9 us (6%)
  starting transfers between devices  84.7 us (6%)
  local copies, waits for them, and re-layouts  56.6 us (4%)
  other arithmetic  49.5 us (3%)
  Pallas kernels  35 us (2%)
  between operations  15.8 us (1%)
    ppermute x72, waiting for transfers between devices, exchange(): return lax.ppermute(values, 'fsdp', partners(step))  385 us
    reduce_scatter x2, waiting for transfers between devices, local(): up_shard = lax.psum_scatter(up_part, 'seq', scatter_dimension=0, tiled=True)  234 us
    all_gather x2, waiting for transfers between devices, local(): down_matrix = lax.all_gather(w_down[layer], 'seq', axis=1, tiled=True)  92 us
    ppermute x72, starting transfers between devices, exchange(): return lax.ppermute(values, 'fsdp', partners(step))  83.8 us
    dot_general x8, matrix products, outer_dot(): lax.dot_general(operand, other, (((0,), (0,)), ((), ())), preferred_eleme...  73 us
    reduce_scatter x2, waiting for transfers between devices, local(): lax.psum_scatter(mix_part, 'seq', scatter_dimension=0, tiled=True)  67.3 us
    dot_general x8, matrix products, trans_dot(): lax.dot_general(operand, matrix, (((1,), (1,)), ((), ())), preferred_elem...  66.5 us
    dot_general x8, matrix products, dot(): return jnp.dot(operand, matrix, preferred_element_type=f32)  61.9 us
  transfers between devices with their start and end apart: 88, of which 46 were waited for; matrix products, arithmetic and copies ran while one was open for 16% of the time, Pallas kernels for 2%

profile of v1, /device:TPU:0, one launch (start us, length us, event | category | flops | bytes accessed | tf_op | source)
XLA Modules:
  0.0 1441.0 jit_solution(5108218595754412740)
XLA Ops:
  27.0 12.5 collective-permute-done
  39.4 14.7 %collective-permute-done.1 = bf16[160,2048]{1,0:T(8,128)(2,1)S(1)} collective-permute-done((bf16[160,2048]{1,0:T(8,128)(2,1)S(1)}, bf16[160,2048]{1,0:T(8,128)(2,1)S(1)}, u32[]{:S(2)}, u32[]{:S(2)}) %collective-permute-start.1) | collective-permute-done | bytes 655392 | tf_op jit(solution)/shard_map/ppermute | solution.py:23
  54.1 24.1 %all-gather.25.cloned.1.call-done = bf16[2048,1536]{1,0:T(8,128)(2,1)} async-done(((bf16[256,1536]{1,0:T(8,128)(2,1)}), bf16[2048,1536]{1,0:T(8,128)(2,1)}) %all-gather.25.cloned.1.call-update) | async-done | bytes 6291472 | tf_op jit(solution)/shard_map/all_gather | solution.py:295
  78.2 7.2 fusion.38
  87.8 4.8 shard_map.237
  92.7 14.7 %all-gather.10 = f32[8,2,512]{2,1,0:T(2,128)S(1)} all-gather(f32[1,2,512]{2,1,0:T(2,128)S(1)} %maximum_bitcast_fusion.2), channel_id=2, replica_groups=mesh['seq'=8,'fsdp'=4] {'seq'}, dimensions={0}, use_global_device_ids=true | all-gather | bytes 36864 | tf_op jit(solution)/shard_map/all_gather | solution.py:238
  120.7 14.0 collective-permute-done.3
  134.7 13.6 collective-permute-done.4
  155.0 24.7 %collective-permute-done.10 = bf16[160,2048]{1,0:T(8,128)(2,1)S(1)} collective-permute-done((bf16[160,2048]{1,0:T(8,128)(2,1)S(1)}, bf16[160,2048]{1,0:T(8,128)(2,1)S(1)}, u32[]{:S(2)}, u32[]{:S(2)}) %collective-permute-start.10) | collective-permute-done | bytes 655392 | tf_op jit(solution)/shard_map/ppermute | solution.py:23
  181.1 38.4 %all-gather.27.cloned.1.call-done = bf16[2048,2816]{1,0:T(8,128)(2,1)} async-done(((bf16[256,2816]{1,0:T(8,128)(2,1)}), bf16[2048,2816]{1,0:T(8,128)(2,1)}) %all-gather.27.cloned.1.call-update) | async-done | bytes 11534352 | tf_op jit(solution)/shard_map/all_gather | solution.py:300
  219.5 11.4 fusion.37
  236.1 44.5 %all-gather.35.cloned.1.call-done = bf16[1,1408,2048]{2,1,0:T(8,128)(2,1)} async-done(((bf16[1,1408,256]{2,1,0:T(8,128)(2,1)}), bf16[1,1408,2048]{2,1,0:T(8,128)(2,1)}) %all-gather.35.cloned.1.call-update) | async-done | bytes 5767184 | tf_op jit(solution)/shard_map/all_gather | solution.py:303
  280.7 7.4 fusion.8
  294.6 14.0 collective-permute-done.12
  308.6 14.6 %collective-permute-done.13 = bf16[160,2048]{1,0:T(8,128)(2,1)S(1)} collective-permute-done((bf16[160,2048]{1,0:T(8,128)(2,1)}, bf16[160,2048]{1,0:T(8,128)(2,1)S(1)}, u32[]{:S(2)}, u32[]{:S(2)}) %collective-permute-start.13) | collective-permute-done | bytes 655392 | tf_op jit(solution)/shard_map/ppermute | solution.py:23
  332.6 13.1 all-gather.29.cloned.1.call-done
  345.7 8.0 collective-permute-done.16
  353.7 5.7 collective-permute-done.17
  359.4 7.5 fusion.36
  374.1 14.0 all-gather.11
  402.4 13.4 collective-permute-done.18
  416.1 28.3 %collective-permute-done.19 = bf16[160,2048]{1,0:T(8,128)(2,1)S(1)} collective-permute-done((bf16[160,2048]{1,0:T(8,128)(2,1)}, bf16[160,2048]{1,0:T(8,128)(2,1)S(1)}, u32[]{:S(2)}, u32[]{:S(2)}) %collective-permute-start.19) | collective-permute-done | bytes 655392 | tf_op jit(solution)/shard_map/ppermute | solution.py:23
  454.1 18.5 %collective-permute-done.31 = bf16[160,2048]{1,0:T(8,128)(2,1)} collective-permute-done((bf16[160,2048]{1,0:T(8,128)(2,1)}, bf16[160,2048]{1,0:T(8,128)(2,1)}, u32[]{:S(2)}, u32[]{:S(2)}) %collective-permute-start.31) | collective-permute-done | bytes 655392 | tf_op jit(solution)/shard_map/ppermute | solution.py:23
  475.5 10.1 all-gather.31.cloned.1.call-done
  485.6 13.9 fusion.35
  499.4 47.4 %all-gather.39.cloned.1.call-done = bf16[1,1408,2048]{2,1,0:T(8,128)(2,1)} async-done(((bf16[1,1408,256]{2,1,0:T(8,128)(2,1)}), bf16[1,1408,2048]{2,1,0:T(8,128)(2,1)}) %all-gather.39.cloned.1.call-update) | async-done | bytes 5767184 | tf_op jit(solution)/shard_map/all_gather | solution.py:303
  546.9 13.4 multiply_convert_fusion.3
  560.3 9.6 convolution_convert_fusion.9
  573.6 14.1 collective-permute-done.33
  587.7 14.6 %collective-permute-done.34 = bf16[160,2048]{1,0:T(8,128)(2,1)S(1)} collective-permute-done((bf16[160,2048]{1,0:T(8,128)(2,1)S(1)}, bf16[160,2048]{1,0:T(8,128)(2,1)S(1)}, u32[]{:S(2)}, u32[]{:S(2)}) %collective-permute-start.34) | collective-permute-done | bytes 655392 | tf_op jit(solution)/shard_map/ppermute | solution.py:23
  615.6 21.8 %collective-permute-done.39 = f32[160]{0:T(256)S(1)} collective-permute-done((f32[160]{0:T(256)S(1)}, f32[160]{0:T(256)S(1)}, u32[]{:S(2)}, u32[]{:S(2)}) %collective-permute-start.39) | collective-permute-done | bytes 672 | tf_op jit(solution)/shard_map/ppermute | solution.py:23
  642.1 5.0 fusion.14.mixed_ref
  647.1 7.4 shard_map.239
  655.9 14.0 all-gather.12
  669.9 5.6 shard_map.240
  684.1 7.2 fusion.11
  699.6 14.0 collective-permute-done.43
  714.3 12.0 collective-permute-done.27
  726.3 14.5 %collective-permute-done.28 = bf16[160,2048]{1,0:T(8,128)(2,1)S(1)} collective-permute-done((bf16[160,2048]{1,0:T(8,128)(2,1)S(1)}, bf16[160,2048]{1,0:T(8,128)(2,1)S(1)}, u32[]{:S(2)}, u32[]{:S(2)}) %collective-permute-start.28) | collective-permute-done | bytes 655392 | tf_op jit(solution)/shard_map/ppermute | solution.py:23
  748.1 4.8 convolution_convert_fusion.12
  753.0 9.5 collective-permute-done.45
  762.5 12.6 collective-permute-done.46
  775.1 11.3 multiply_convert_fusion.1
  787.7 10.5 convolution_convert_fusion.7
  802.1 14.2 collective-permute-done.48
  816.3 12.2 collective-permute-done.49
  839.0 21.1 %collective-permute-done.54 = f32[160]{0:T(256)S(1)} collective-permute-done((f32[160]{0:T(256)S(1)}, f32[160]{0:T(256)S(1)}, u32[]{:S(2)}, u32[]{:S(2)}) %collective-permute-start.54) | collective-permute-done | bytes 672 | tf_op jit(solution)/shard_map/ppermute | solution.py:23
  869.5 7.2 shard_map.241
  884.4 9.1 convolution_convert_fusion.4
  895.0 8.6 convolution_convert_fusion.2
  905.1 8.5 convolution_convert_fusion.3
  915.1 14.1 all-gather.13
  930.6 5.2 shard_map.242
  937.5 8.2 convolution_convert_fusion.5
  945.8 14.9 %convolution_convert_fusion = bf16[2048,2816]{1,0:T(8,128)(2,1)} fusion(bf16[640,1408]{1,0:T(8,128)(2,1)} %get-tuple-element.90, bf16[640,1408]{1,0:T(8,128)(2,1)} %get-tuple-element.89, bf16[160,2048]{1,0:T(8,128)(2,1)} %collective-permute-done.26, bf16[160,2048]{1,0:T(8,128)(2,1)} %collective-permute-done.25, bf16[160,2048]{1,0:T(8,128)(2,1)} %collective-permute-done.24, ...), kind=kOutput, calls=%fused_computation | convolution fusion | flops 7405436928 | bytes 17760256 | tf_op jit(solution)/shard_map/dot_general | solution.py:60
  961.8 14.4 convolution_convert_fusion.1
  983.8 14.0 all-gather.15
  999.8 7.6 convolution_convert_fusion.6
  1012.8 25.6 %collective-permute-done.71 = f32[4,512]{1,0:T(4,128)S(1)} collective-permute-done((f32[4,512]{1,0:T(4,128)S(1)}, f32[4,512]{1,0:T(4,128)S(1)}, u32[]{:S(2)}, u32[]{:S(2)}) %collective-permute-start.71) | collective-permute-done | bytes 8224 | tf_op jit(solution)/shard_map/ppermute | solution.py:23
  1046.1 14.1 all-gather.14
  1070.9 48.3 %reduce-scatter.21.cloned.1.call-done = bf16[1408,256]{1,0:T(8,128)(2,1)} async-done(((bf16[1408,2048]{1,0:T(8,128)(2,1)}), bf16[1408,256]{1,0:T(8,128)(2,1)}) %reduce-scatter.21.cloned.1.call-update) | async-done | bytes 720912 | tf_op jit(solution)/shard_map/reduce_scatter | solution.py:411
  1122.3 67.3 %reduce-scatter.9.cloned.1.call-done = bf16[256,1536]{1,0:T(8,128)(2,1)} async-done(((bf16[2048,1536]{1,0:T(8,128)(2,1)}), bf16[256,1536]{1,0:T(8,128)(2,1)}) %reduce-scatter.9.cloned.1.call-update) | async-done | bytes 786448 | tf_op jit(solution)/shard_map/reduce_scatter | solution.py:414
  1193.9 115.6 %reduce-scatter.19.cloned.1.call-done = bf16[256,2816]{1,0:T(8,128)(2,1)} async-done(((bf16[2048,2816]{1,0:T(8,128)(2,1)}), bf16[256,2816]{1,0:T(8,128)(2,1)}) %reduce-scatter.19.cloned.1.call-update) | async-done | bytes 1441808 | tf_op jit(solution)/shard_map/reduce_scatter | solution.py:412
  1310.9 118.4 %reduce-scatter.17.cloned.1.call-done = bf16[256,2816]{1,0:T(8,128)(2,1)} async-done(((bf16[2048,2816]{1,0:T(8,128)(2,1)}), bf16[256,2816]{1,0:T(8,128)(2,1)}) %reduce-scatter.17.cloned.1.call-update) | async-done | bytes 1441808 | tf_op jit(solution)/shard_map/reduce_scatter | solution.py:412
  (497 shorter events, 234.3 us)
Async XLA Ops:
  7.2 71.0 %all-gather.25.cloned.1.call-start = ((), (), s32[]{:S(2)}) async-start(), calls=%async_computation.8 | async-start | bytes 7077888 | tf_op jit(solution)/shard_map/all_gather | solution.py:295
  10.6 100.7 %all-gather.33.cloned.1.call-start = ((), (), s32[]{:S(2)}) async-start(), calls=%async_computation.20 | async-start | bytes 2359296 | tf_op jit(solution)/shard_map/all_gather | solution.py:299
  11.5 208.0 %all-gather.27.cloned.1.call-start = ((), (), s32[]{:S(2)}) async-start(), calls=%async_computation.9 | async-start | bytes 12976128 | tf_op jit(solution)/shard_map/all_gather | solution.py:300
  14.7 265.9 %all-gather.35.cloned.1.call-start = ((), (), s32[]{:S(2)}) async-start(), calls=%async_computation.21 | async-start | bytes 6488064 | tf_op jit(solution)/shard_map/all_gather | solution.py:303
  17.3 328.4 %all-gather.29.cloned.1.call-start = ((), (), s32[]{:S(2)}) async-start(), calls=%async_computation.10 | async-start | bytes 7077888 | tf_op jit(solution)/shard_map/all_gather | solution.py:295
  18.3 373.8 %all-gather.37.cloned.1.call-start = ((), (), s32[]{:S(2)}) async-start(), calls=%async_computation.22 | async-start | bytes 2359296 | tf_op jit(solution)/shard_map/all_gather | solution.py:299
  18.9 466.6 %all-gather.31.cloned.1.call-start = ((), (), s32[]{:S(2)}) async-start(), calls=%async_computation.11 | async-start | bytes 12976128 | tf_op jit(solution)/shard_map/all_gather | solution.py:300
  20.3 526.6 %all-gather.39.cloned.1.call-start = ((), (), s32[]{:S(2)}) async-start(), calls=%async_computation.23 | async-start | bytes 6488064 | tf_op jit(solution)/shard_map/all_gather | solution.py:303
  20.8 18.6 %collective-permute-start = (bf16[160,2048]{1,0:T(8,128)(2,1)S(1)}, bf16[160,2048]{1,0:T(8,128)(2,1)S(1)}, u32[]{:S(2)}, u32[]{:S(2)}) collective-permute-start(bf16[160,2048]{1,0:T(8,128)(2,1)S(1)} %fusion.24), channel_id=1, source_target_pairs={{0,1},{1,0},{2,3},{3,2},{4,5},{5,4},{6,7},{7,6},{8,9},{9,8},{10,11... | collective-permute-start | bytes 1966088 | tf_op jit(solution)/shard_map/ppermute | solution.py:23
  23.9 30.2 %collective-permute-start.1 = (bf16[160,2048]{1,0:T(8,128)(2,1)S(1)}, bf16[160,2048]{1,0:T(8,128)(2,1)S(1)}, u32[]{:S(2)}, u32[]{:S(2)}) collective-permute-start(bf16[160,2048]{1,0:T(8,128)(2,1)S(1)} %fusion.24), channel_id=1, source_target_pairs={{0,2},{1,3},{2,0},{3,1},{4,6},{5,7},{6,4},{7,5},{8,10},{9,11},{10,... | collective-permute-start | bytes 1966088 | tf_op jit(solution)/shard_map/ppermute | solution.py:23
  25.4 28.7 %collective-permute-start.2 = (bf16[160,2048]{1,0:T(8,128)(2,1)S(1)}, bf16[160,2048]{1,0:T(8,128)(2,1)}, u32[]{:S(2)}, u32[]{:S(2)}) collective-permute-start(bf16[160,2048]{1,0:T(8,128)(2,1)S(1)} %fusion.24), channel_id=1, source_target_pairs={{0,3},{1,2},{2,1},{3,0},{4,7},{5,6},{6,5},{7,4},{8,11},{9,10},{10,... | collective-permute-start | bytes 1966088 | tf_op jit(solution)/shard_map/ppermute | solution.py:23
  116.8 17.9 %collective-permute-start.3 = (bf16[160,2048]{1,0:T(8,128)(2,1)}, bf16[160,2048]{1,0:T(8,128)(2,1)S(1)}, u32[]{:S(2)}, u32[]{:S(2)}) collective-permute-start(bf16[160,2048]{1,0:T(8,128)(2,1)} %get-tuple-element.119), channel_id=1, source_target_pairs={{0,1},{1,0},{2,3},{3,2},{4,5},{5,4},{6,7},{7,6},{8,9},{9,8},{10,11... | collective-permute-start | bytes 1966088 | tf_op jit(solution)/shard_map/ppermute | solution.py:23
  118.2 30.1 %collective-permute-start.4 = (bf16[160,2048]{1,0:T(8,128)(2,1)}, bf16[160,2048]{1,0:T(8,128)(2,1)S(1)}, u32[]{:S(2)}, u32[]{:S(2)}) collective-permute-start(bf16[160,2048]{1,0:T(8,128)(2,1)} %get-tuple-element.121), channel_id=1, source_target_pairs={{0,2},{1,3},{2,0},{3,1},{4,6},{5,7},{6,4},{7,5},{8,10},{9,11},{10,... | collective-permute-start | bytes 1966088 | tf_op jit(solution)/shard_map/ppermute | solution.py:23
  119.7 29.4 %collective-permute-start.5 = (bf16[160,2048]{1,0:T(8,128)(2,1)S(1)}, bf16[160,2048]{1,0:T(8,128)(2,1)}, u32[]{:S(2)}, u32[]{:S(2)}) collective-permute-start(bf16[160,2048]{1,0:T(8,128)(2,1)S(1)} %get-tuple-element.120), channel_id=1, source_target_pairs={{0,3},{1,2},{2,1},{3,0},{4,7},{5,6},{6,5},{7,4},{8,11},{9,10},{10,... | collective-permute-start | bytes 1966088 | tf_op jit(solution)/shard_map/ppermute | solution.py:23
  151.5 28.3 %collective-permute-start.10 = (bf16[160,2048]{1,0:T(8,128)(2,1)S(1)}, bf16[160,2048]{1,0:T(8,128)(2,1)S(1)}, u32[]{:S(2)}, u32[]{:S(2)}) collective-permute-start(bf16[160,2048]{1,0:T(8,128)(2,1)S(1)} %multiply_convert_fusion.9), channel_id=1, source_target_pairs={{0,2},{1,3},{2,0},{3,1},{4,6},{5,7},{6,4},{7,5},{8,10},{9,11},{10,... | collective-permute-start | bytes 1966088 | tf_op jit(solution)/shard_map/ppermute | solution.py:23
  153.0 26.8 %collective-permute-start.11 = (bf16[160,2048]{1,0:T(8,128)(2,1)S(1)}, bf16[160,2048]{1,0:T(8,128)(2,1)S(1)}, u32[]{:S(2)}, u32[]{:S(2)}) collective-permute-start(bf16[160,2048]{1,0:T(8,128)(2,1)S(1)} %multiply_convert_fusion.9), channel_id=1, source_target_pairs={{0,3},{1,2},{2,1},{3,0},{4,7},{5,6},{6,5},{7,4},{8,11},{9,10},{10,... | collective-permute-start | bytes 1966088 | tf_op jit(solution)/shard_map/ppermute | solution.py:23
  153.5 27.6 %collective-permute-start.9 = (bf16[160,2048]{1,0:T(8,128)(2,1)S(1)}, bf16[160,2048]{1,0:T(8,128)(2,1)}, u32[]{:S(2)}, u32[]{:S(2)}) collective-permute-start(bf16[160,2048]{1,0:T(8,128)(2,1)S(1)} %multiply_convert_fusion.9), channel_id=1, source_target_pairs={{0,1},{1,0},{2,3},{3,2},{4,5},{5,4},{6,7},{7,6},{8,9},{9,8},{10,11... | collective-permute-start | bytes 1966088 | tf_op jit(solution)/shard_map/ppermute | solution.py:23
  292.3 30.9 %collective-permute-start.13 = (bf16[160,2048]{1,0:T(8,128)(2,1)}, bf16[160,2048]{1,0:T(8,128)(2,1)S(1)}, u32[]{:S(2)}, u32[]{:S(2)}) collective-permute-start(bf16[160,2048]{1,0:T(8,128)(2,1)} %get-tuple-element.118), channel_id=1, source_target_pairs={{0,2},{1,3},{2,0},{3,1},{4,6},{5,7},{6,4},{7,5},{8,10},{9,11},{10,... | collective-permute-start | bytes 1966088 | tf_op jit(solution)/shard_map/ppermute | solution.py:23
  293.8 30.2 %collective-permute-start.14 = (bf16[160,2048]{1,0:T(8,128)(2,1)}, bf16[160,2048]{1,0:T(8,128)(2,1)}, u32[]{:S(2)}, u32[]{:S(2)}) collective-permute-start(bf16[160,2048]{1,0:T(8,128)(2,1)} %get-tuple-element.117), channel_id=1, source_target_pairs={{0,3},{1,2},{2,1},{3,0},{4,7},{5,6},{6,5},{7,4},{8,11},{9,10},{10,... | collective-permute-start | bytes 1966088 | tf_op jit(solution)/shard_map/ppermute | solution.py:23
  294.4 773.2 %reduce-scatter.15.cloned.1.call-start = ((), (), s32[]{:S(2)}) async-start(), calls=%async_computation.15 | async-start | bytes 2359296 | tf_op jit(solution)/shard_map/reduce_scatter | solution.py:413
  326.6 19.1 %collective-permute-start.15 = (bf16[160,2048]{1,0:T(8,128)(2,1)S(1)}, bf16[160,2048]{1,0:T(8,128)(2,1)S(1)}, u32[]{:S(2)}, u32[]{:S(2)}) collective-permute-start(bf16[160,2048]{1,0:T(8,128)(2,1)S(1)} %multiply_convert_fusion.8), channel_id=1, source_target_pairs={{0,1},{1,0},{2,3},{3,2},{4,5},{5,4},{6,7},{7,6},{8,9},{9,8},{10,11... | collective-permute-start | bytes 1966088 | tf_op jit(solution)/shard_map/ppermute | solution.py:23
  327.1 26.6 %collective-permute-start.16 = (bf16[160,2048]{1,0:T(8,128)(2,1)S(1)}, bf16[160,2048]{1,0:T(8,128)(2,1)}, u32[]{:S(2)}, u32[]{:S(2)}) collective-permute-start(bf16[160,2048]{1,0:T(8,128)(2,1)S(1)} %multiply_convert_fusion.8), channel_id=1, source_target_pairs={{0,2},{1,3},{2,0},{3,1},{4,6},{5,7},{6,4},{7,5},{8,10},{9,11},{10,... | collective-permute-start | bytes 1966088 | tf_op jit(solution)/shard_map/ppermute | solution.py:23
  328.6 30.7 %collective-permute-start.17 = (bf16[160,2048]{1,0:T(8,128)(2,1)S(1)}, bf16[160,2048]{1,0:T(8,128)(2,1)}, u32[]{:S(2)}, u32[]{:S(2)}) collective-permute-start(bf16[160,2048]{1,0:T(8,128)(2,1)S(1)} %multiply_convert_fusion.8), channel_id=1, source_target_pairs={{0,3},{1,2},{2,1},{3,0},{4,7},{5,6},{6,5},{7,4},{8,11},{9,10},{10,... | collective-permute-start | bytes 1966088 | tf_op jit(solution)/shard_map/ppermute | solution.py:23
  330.1 120.5 %collective-permute-start.30 = (bf16[160,2048]{1,0:T(8,128)(2,1)}, bf16[160,2048]{1,0:T(8,128)(2,1)}, u32[]{:S(2)}, u32[]{:S(2)}) collective-permute-start(bf16[160,2048]{1,0:T(8,128)(2,1)} %param.27), channel_id=1, source_target_pairs={{0,1},{1,0},{2,3},{3,2},{4,5},{5,4},{6,7},{7,6},{8,9},{9,8},{10,11... | collective-permute-start | bytes 1966088 | tf_op jit(solution)/shard_map/ppermute | solution.py:23
  397.9 17.9 %collective-permute-start.18 = (bf16[160,2048]{1,0:T(8,128)(2,1)}, bf16[160,2048]{1,0:T(8,128)(2,1)S(1)}, u32[]{:S(2)}, u32[]{:S(2)}) collective-permute-start(bf16[160,2048]{1,0:T(8,128)(2,1)} %get-tuple-element.113), channel_id=1, source_target_pairs={{0,1},{1,0},{2,3},{3,2},{4,5},{5,4},{6,7},{7,6},{8,9},{9,8},{10,11... | collective-permute-start | bytes 1966088 | tf_op jit(solution)/shard_map/ppermute | solution.py:23
  398.4 46.0 %collective-permute-start.19 = (bf16[160,2048]{1,0:T(8,128)(2,1)}, bf16[160,2048]{1,0:T(8,128)(2,1)S(1)}, u32[]{:S(2)}, u32[]{:S(2)}) collective-permute-start(bf16[160,2048]{1,0:T(8,128)(2,1)} %get-tuple-element.115), channel_id=1, source_target_pairs={{0,2},{1,3},{2,0},{3,1},{4,6},{5,7},{6,4},{7,5},{8,10},{9,11},{10,... | collective-permute-start | bytes 1966088 | tf_op jit(solution)/shard_map/ppermute | solution.py:23
  398.8 46.4 %collective-permute-start.20 = (bf16[160,2048]{1,0:T(8,128)(2,1)}, bf16[160,2048]{1,0:T(8,128)(2,1)}, u32[]{:S(2)}, u32[]{:S(2)}) collective-permute-start(bf16[160,2048]{1,0:T(8,128)(2,1)} %get-tuple-element.114), channel_id=1, source_target_pairs={{0,3},{1,2},{2,1},{3,0},{4,7},{5,6},{6,5},{7,4},{8,11},{9,10},{10,... | collective-permute-start | bytes 1966088 | tf_op jit(solution)/shard_map/ppermute | solution.py:23
  401.6 71.0 %collective-permute-start.31 = (bf16[160,2048]{1,0:T(8,128)(2,1)}, bf16[160,2048]{1,0:T(8,128)(2,1)}, u32[]{:S(2)}, u32[]{:S(2)}) collective-permute-start(bf16[160,2048]{1,0:T(8,128)(2,1)} %param.27), channel_id=1, source_target_pairs={{0,2},{1,3},{2,0},{3,1},{4,6},{5,7},{6,4},{7,5},{8,10},{9,11},{10,... | collective-permute-start | bytes 1966088 | tf_op jit(solution)/shard_map/ppermute | solution.py:23
  415.7 58.8 %collective-permute-start.32 = (bf16[160,2048]{1,0:T(8,128)(2,1)}, bf16[160,2048]{1,0:T(8,128)(2,1)S(1)}, u32[]{:S(2)}, u32[]{:S(2)}) collective-permute-start(bf16[160,2048]{1,0:T(8,128)(2,1)} %param.27), channel_id=1, source_target_pairs={{0,3},{1,2},{2,1},{3,0},{4,7},{5,6},{6,5},{7,4},{8,11},{9,10},{10,... | collective-permute-start | bytes 1966088 | tf_op jit(solution)/shard_map/ppermute | solution.py:23
  448.6 36.9 %collective-permute-start.24 = (bf16[160,2048]{1,0:T(8,128)(2,1)}, bf16[160,2048]{1,0:T(8,128)(2,1)}, u32[]{:S(2)}, u32[]{:S(2)}) collective-permute-start(bf16[160,2048]{1,0:T(8,128)(2,1)} %multiply_convert_fusion.6), channel_id=1, source_target_pairs={{0,1},{1,0},{2,3},{3,2},{4,5},{5,4},{6,7},{7,6},{8,9},{9,8},{10,11... | collective-permute-start | bytes 1966088 | tf_op jit(solution)/shard_map/ppermute | solution.py:23
  450.1 35.5 %collective-permute-start.25 = (bf16[160,2048]{1,0:T(8,128)(2,1)}, bf16[160,2048]{1,0:T(8,128)(2,1)}, u32[]{:S(2)}, u32[]{:S(2)}) collective-permute-start(bf16[160,2048]{1,0:T(8,128)(2,1)} %multiply_convert_fusion.6), channel_id=1, source_target_pairs={{0,2},{1,3},{2,0},{3,1},{4,6},{5,7},{6,4},{7,5},{8,10},{9,11},{10,... | collective-permute-start | bytes 1966088 | tf_op jit(solution)/shard_map/ppermute | solution.py:23
  450.6 35.0 %collective-permute-start.26 = (bf16[160,2048]{1,0:T(8,128)(2,1)}, bf16[160,2048]{1,0:T(8,128)(2,1)}, u32[]{:S(2)}, u32[]{:S(2)}) collective-permute-start(bf16[160,2048]{1,0:T(8,128)(2,1)} %multiply_convert_fusion.6), channel_id=1, source_target_pairs={{0,3},{1,2},{2,1},{3,0},{4,7},{5,6},{6,5},{7,4},{8,11},{9,10},{10,... | collective-permute-start | bytes 1966088 | tf_op jit(solution)/shard_map/ppermute | solution.py:23
  571.6 30.7 %collective-permute-start.34 = (bf16[160,2048]{1,0:T(8,128)(2,1)S(1)}, bf16[160,2048]{1,0:T(8,128)(2,1)S(1)}, u32[]{:S(2)}, u32[]{:S(2)}) collective-permute-start(bf16[160,2048]{1,0:T(8,128)(2,1)S(1)} %get-tuple-element.109), channel_id=1, source_target_pairs={{0,2},{1,3},{2,0},{3,1},{4,6},{5,7},{6,4},{7,5},{8,10},{9,11},{10,... | collective-permute-start | bytes 1966088 | tf_op jit(solution)/shard_map/ppermute | solution.py:23
  573.1 29.2 %collective-permute-start.35 = (bf16[160,2048]{1,0:T(8,128)(2,1)S(1)}, bf16[160,2048]{1,0:T(8,128)(2,1)S(1)}, u32[]{:S(2)}, u32[]{:S(2)}) collective-permute-start(bf16[160,2048]{1,0:T(8,128)(2,1)S(1)} %get-tuple-element.108), channel_id=1, source_target_pairs={{0,3},{1,2},{2,1},{3,0},{4,7},{5,6},{6,5},{7,4},{8,11},{9,10},{10,... | collective-permute-start | bytes 1966088 | tf_op jit(solution)/shard_map/ppermute | solution.py:23
  607.2 34.9 %collective-permute-start.36 = (bf16[160,2048]{1,0:T(8,128)(2,1)}, bf16[160,2048]{1,0:T(8,128)(2,1)}, u32[]{:S(2)}, u32[]{:S(2)}) collective-permute-start(bf16[160,2048]{1,0:T(8,128)(2,1)} %get-tuple-element.75), channel_id=1, source_target_pairs={{0,1},{1,0},{2,3},{3,2},{4,5},{5,4},{6,7},{7,6},{8,9},{9,8},{10,11... | collective-permute-start | bytes 1966088 | tf_op jit(solution)/shard_map/ppermute | solution.py:23
  608.4 33.7 %collective-permute-start.37 = (bf16[160,2048]{1,0:T(8,128)(2,1)}, bf16[160,2048]{1,0:T(8,128)(2,1)}, u32[]{:S(2)}, u32[]{:S(2)}) collective-permute-start(bf16[160,2048]{1,0:T(8,128)(2,1)} %get-tuple-element.75), channel_id=1, source_target_pairs={{0,2},{1,3},{2,0},{3,1},{4,6},{5,7},{6,4},{7,5},{8,10},{9,11},{10,... | collective-permute-start | bytes 1966088 | tf_op jit(solution)/shard_map/ppermute | solution.py:23
  609.3 32.8 %collective-permute-start.38 = (bf16[160,2048]{1,0:T(8,128)(2,1)}, bf16[160,2048]{1,0:T(8,128)(2,1)}, u32[]{:S(2)}, u32[]{:S(2)}) collective-permute-start(bf16[160,2048]{1,0:T(8,128)(2,1)} %get-tuple-element.75), channel_id=1, source_target_pairs={{0,3},{1,2},{2,1},{3,0},{4,7},{5,6},{6,5},{7,4},{8,11},{9,10},{10,... | collective-permute-start | bytes 1966088 | tf_op jit(solution)/shard_map/ppermute | solution.py:23
  611.4 26.0 %collective-permute-start.39 = (f32[160]{0:T(256)S(1)}, f32[160]{0:T(256)S(1)}, u32[]{:S(2)}, u32[]{:S(2)}) collective-permute-start(f32[160]{0:T(256)S(1)} %get-tuple-element.74), channel_id=1, source_target_pairs={{0,1},{1,0},{2,3},{3,2},{4,5},{5,4},{6,7},{7,6},{8,9},{9,8},{10,11... | collective-permute-start | bytes 1928 | tf_op jit(solution)/shard_map/ppermute | solution.py:23
  614.7 25.3 %collective-permute-start.40 = (f32[160]{0:T(256)S(1)}, f32[160]{0:T(256)S(1)}, u32[]{:S(2)}, u32[]{:S(2)}) collective-permute-start(f32[160]{0:T(256)S(1)} %get-tuple-element.74), channel_id=1, source_target_pairs={{0,2},{1,3},{2,0},{3,1},{4,6},{5,7},{6,4},{7,5},{8,10},{9,11},{10,... | collective-permute-start | bytes 1928 | tf_op jit(solution)/shard_map/ppermute | solution.py:23
  682.0 31.6 %collective-permute-start.43 = (bf16[160,2048]{1,0:T(8,128)(2,1)S(1)}, bf16[160,2048]{1,0:T(8,128)(2,1)S(1)}, u32[]{:S(2)}, u32[]{:S(2)}) collective-permute-start(bf16[160,2048]{1,0:T(8,128)(2,1)S(1)} %get-tuple-element.106), channel_id=1, source_target_pairs={{0,2},{1,3},{2,0},{3,1},{4,6},{5,7},{6,4},{7,5},{8,10},{9,11},{10,... | collective-permute-start | bytes 1966088 | tf_op jit(solution)/shard_map/ppermute | solution.py:23
  682.6 31.0 %collective-permute-start.44 = (bf16[160,2048]{1,0:T(8,128)(2,1)S(1)}, bf16[160,2048]{1,0:T(8,128)(2,1)S(1)}, u32[]{:S(2)}, u32[]{:S(2)}) collective-permute-start(bf16[160,2048]{1,0:T(8,128)(2,1)S(1)} %get-tuple-element.105), channel_id=1, source_target_pairs={{0,3},{1,2},{2,1},{3,0},{4,7},{5,6},{6,5},{7,4},{8,11},{9,10},{10,... | collective-permute-start | bytes 1966088 | tf_op jit(solution)/shard_map/ppermute | solution.py:23
  691.5 34.7 %collective-permute-start.27 = (bf16[160,2048]{1,0:T(8,128)(2,1)S(1)}, bf16[160,2048]{1,0:T(8,128)(2,1)S(1)}, u32[]{:S(2)}, u32[]{:S(2)}) collective-permute-start(bf16[160,2048]{1,0:T(8,128)(2,1)S(1)} %get-tuple-element.110), channel_id=1, source_target_pairs={{0,1},{1,0},{2,3},{3,2},{4,5},{5,4},{6,7},{7,6},{8,9},{9,8},{10,11... | collective-permute-start | bytes 1966088 | tf_op jit(solution)/shard_map/ppermute | solution.py:23
  693.0 47.8 %collective-permute-start.28 = (bf16[160,2048]{1,0:T(8,128)(2,1)S(1)}, bf16[160,2048]{1,0:T(8,128)(2,1)S(1)}, u32[]{:S(2)}, u32[]{:S(2)}) collective-permute-start(bf16[160,2048]{1,0:T(8,128)(2,1)S(1)} %get-tuple-element.112), channel_id=1, source_target_pairs={{0,2},{1,3},{2,0},{3,1},{4,6},{5,7},{6,4},{7,5},{8,10},{9,11},{10,... | collective-permute-start | bytes 1966088 | tf_op jit(solution)/shard_map/ppermute | solution.py:23
  698.1 42.7 %collective-permute-start.29 = (bf16[160,2048]{1,0:T(8,128)(2,1)S(1)}, bf16[160,2048]{1,0:T(8,128)(2,1)S(1)}, u32[]{:S(2)}, u32[]{:S(2)}) collective-permute-start(bf16[160,2048]{1,0:T(8,128)(2,1)S(1)} %get-tuple-element.111), channel_id=1, source_target_pairs={{0,3},{1,2},{2,1},{3,0},{4,7},{5,6},{6,5},{7,4},{8,11},{9,10},{10,... | collective-permute-start | bytes 1966088 | tf_op jit(solution)/shard_map/ppermute | solution.py:23
  745.2 29.9 %collective-permute-start.46 = (bf16[160,2048]{1,0:T(8,128)(2,1)}, bf16[160,2048]{1,0:T(8,128)(2,1)S(1)}, u32[]{:S(2)}, u32[]{:S(2)}) collective-permute-start(bf16[160,2048]{1,0:T(8,128)(2,1)} %get-tuple-element.68), channel_id=1, source_target_pairs={{0,2},{1,3},{2,0},{3,1},{4,6},{5,7},{6,4},{7,5},{8,10},{9,11},{10,... | collective-permute-start | bytes 1966088 | tf_op jit(solution)/shard_map/ppermute | solution.py:23
  746.6 28.5 %collective-permute-start.47 = (bf16[160,2048]{1,0:T(8,128)(2,1)}, bf16[160,2048]{1,0:T(8,128)(2,1)S(1)}, u32[]{:S(2)}, u32[]{:S(2)}) collective-permute-start(bf16[160,2048]{1,0:T(8,128)(2,1)} %get-tuple-element.68), channel_id=1, source_target_pairs={{0,3},{1,2},{2,1},{3,0},{4,7},{5,6},{6,5},{7,4},{8,11},{9,10},{10,... | collective-permute-start | bytes 1966088 | tf_op jit(solution)/shard_map/ppermute | solution.py:23
  753.0 314.7 %reduce-scatter.13.cloned.1.call-start = ((), (), s32[]{:S(2)}) async-start(), calls=%async_computation.14 | async-start | bytes 2359296 | tf_op jit(solution)/shard_map/reduce_scatter | solution.py:413
  800.0 28.5 %collective-permute-start.49 = (bf16[160,2048]{1,0:T(8,128)(2,1)S(1)}, bf16[160,2048]{1,0:T(8,128)(2,1)S(1)}, u32[]{:S(2)}, u32[]{:S(2)}) collective-permute-start(bf16[160,2048]{1,0:T(8,128)(2,1)S(1)} %get-tuple-element.103), channel_id=1, source_target_pairs={{0,2},{1,3},{2,0},{3,1},{4,6},{5,7},{6,4},{7,5},{8,10},{9,11},{10,... | collective-permute-start | bytes 1966088 | tf_op jit(solution)/shard_map/ppermute | solution.py:23
  800.6 27.8 %collective-permute-start.50 = (bf16[160,2048]{1,0:T(8,128)(2,1)S(1)}, bf16[160,2048]{1,0:T(8,128)(2,1)S(1)}, u32[]{:S(2)}, u32[]{:S(2)}) collective-permute-start(bf16[160,2048]{1,0:T(8,128)(2,1)S(1)} %get-tuple-element.102), channel_id=1, source_target_pairs={{0,3},{1,2},{2,1},{3,0},{4,7},{5,6},{6,5},{7,4},{8,11},{9,10},{10,... | collective-permute-start | bytes 1966088 | tf_op jit(solution)/shard_map/ppermute | solution.py:23
  832.7 32.2 %collective-permute-start.51 = (bf16[160,2048]{1,0:T(8,128)(2,1)S(1)}, bf16[160,2048]{1,0:T(8,128)(2,1)S(1)}, u32[]{:S(2)}, u32[]{:S(2)}) collective-permute-start(bf16[160,2048]{1,0:T(8,128)(2,1)S(1)} %get-tuple-element.66), channel_id=1, source_target_pairs={{0,1},{1,0},{2,3},{3,2},{4,5},{5,4},{6,7},{7,6},{8,9},{9,8},{10,11... | collective-permute-start | bytes 1966088 | tf_op jit(solution)/shard_map/ppermute | solution.py:23
  833.3 31.6 %collective-permute-start.52 = (bf16[160,2048]{1,0:T(8,128)(2,1)S(1)}, bf16[160,2048]{1,0:T(8,128)(2,1)}, u32[]{:S(2)}, u32[]{:S(2)}) collective-permute-start(bf16[160,2048]{1,0:T(8,128)(2,1)S(1)} %get-tuple-element.66), channel_id=1, source_target_pairs={{0,2},{1,3},{2,0},{3,1},{4,6},{5,7},{6,4},{7,5},{8,10},{9,11},{10,... | collective-permute-start | bytes 1966088 | tf_op jit(solution)/shard_map/ppermute | solution.py:23
  834.7 30.2 %collective-permute-start.53 = (bf16[160,2048]{1,0:T(8,128)(2,1)S(1)}, bf16[160,2048]{1,0:T(8,128)(2,1)}, u32[]{:S(2)}, u32[]{:S(2)}) collective-permute-start(bf16[160,2048]{1,0:T(8,128)(2,1)S(1)} %get-tuple-element.66), channel_id=1, source_target_pairs={{0,3},{1,2},{2,1},{3,0},{4,7},{5,6},{6,5},{7,4},{8,11},{9,10},{10,... | collective-permute-start | bytes 1966088 | tf_op jit(solution)/shard_map/ppermute | solution.py:23
  836.3 23.9 %collective-permute-start.54 = (f32[160]{0:T(256)S(1)}, f32[160]{0:T(256)S(1)}, u32[]{:S(2)}, u32[]{:S(2)}) collective-permute-start(f32[160]{0:T(256)S(1)} %get-tuple-element.65), channel_id=1, source_target_pairs={{0,1},{1,0},{2,3},{3,2},{4,5},{5,4},{6,7},{7,6},{8,9},{9,8},{10,11... | collective-permute-start | bytes 1928 | tf_op jit(solution)/shard_map/ppermute | solution.py:23
  837.6 24.3 %collective-permute-start.55 = (f32[160]{0:T(256)S(1)}, f32[160]{0:T(256)S(1)}, u32[]{:S(2)}, u32[]{:S(2)}) collective-permute-start(f32[160]{0:T(256)S(1)} %get-tuple-element.65), channel_id=1, source_target_pairs={{0,2},{1,3},{2,0},{3,1},{4,6},{5,7},{6,4},{7,5},{8,10},{9,11},{10,... | collective-permute-start | bytes 1928 | tf_op jit(solution)/shard_map/ppermute | solution.py:23
  883.1 186.6 %reduce-scatter.11.cloned.1.call-start = ((), (), s32[]{:S(2)}) async-start(), calls=%async_computation.13 | async-start | bytes 7077888 | tf_op jit(solution)/shard_map/reduce_scatter | solution.py:414
  893.5 177.4 %reduce-scatter.23.cloned.1.call-start = ((), (), s32[]{:S(2)}) async-start(), calls=%async_computation.19 | async-start | bytes 6488064 | tf_op jit(solution)/shard_map/reduce_scatter | solution.py:411
  903.6 215.6 %reduce-scatter.21.cloned.1.call-start = ((), (), s32[]{:S(2)}) async-start(), calls=%async_computation.18 | async-start | bytes 6488064 | tf_op jit(solution)/shard_map/reduce_scatter | solution.py:411
  913.6 276.0 %reduce-scatter.9.cloned.1.call-start = ((), (), s32[]{:S(2)}) async-start(), calls=%async_computation.12 | async-start | bytes 7077888 | tf_op jit(solution)/shard_map/reduce_scatter | solution.py:414
  945.7 363.7 %reduce-scatter.19.cloned.1.call-start = ((), (), s32[]{:S(2)}) async-start(), calls=%async_computation.17 | async-start | bytes 12976128 | tf_op jit(solution)/shard_map/reduce_scatter | solution.py:412
  960.7 468.6 %reduce-scatter.17.cloned.1.call-start = ((), (), s32[]{:S(2)}) async-start(), calls=%async_computation.16 | async-start | bytes 12976128 | tf_op jit(solution)/shard_map/reduce_scatter | solution.py:412
  1007.6 30.9 %collective-permute-start.57 = (bf16[160,2048]{1,0:T(8,128)(2,1)S(1)}, bf16[160,2048]{1,0:T(8,128)(2,1)S(1)}, u32[]{:S(2)}, u32[]{:S(2)}) collective-permute-start(bf16[160,2048]{1,0:T(8,128)(2,1)S(1)} %get-tuple-element.98), channel_id=1, source_target_pairs={{0,1},{1,0},{2,3},{3,2},{4,5},{5,4},{6,7},{7,6},{8,9},{9,8},{10,11... | collective-permute-start | bytes 1966088 | tf_op jit(solution)/shard_map/ppermute | solution.py:23
  1008.3 30.4 %collective-permute-start.58 = (bf16[160,2048]{1,0:T(8,128)(2,1)S(1)}, bf16[160,2048]{1,0:T(8,128)(2,1)S(1)}, u32[]{:S(2)}, u32[]{:S(2)}) collective-permute-start(bf16[160,2048]{1,0:T(8,128)(2,1)S(1)} %get-tuple-element.100), channel_id=1, source_target_pairs={{0,2},{1,3},{2,0},{3,1},{4,6},{5,7},{6,4},{7,5},{8,10},{9,11},{10,... | collective-permute-start | bytes 1966088 | tf_op jit(solution)/shard_map/ppermute | solution.py:23
  1009.7 28.9 %collective-permute-start.59 = (bf16[160,2048]{1,0:T(8,128)(2,1)S(1)}, bf16[160,2048]{1,0:T(8,128)(2,1)S(1)}, u32[]{:S(2)}, u32[]{:S(2)}) collective-permute-start(bf16[160,2048]{1,0:T(8,128)(2,1)S(1)} %get-tuple-element.99), channel_id=1, source_target_pairs={{0,3},{1,2},{2,1},{3,0},{4,7},{5,6},{6,5},{7,4},{8,11},{9,10},{10,... | collective-permute-start | bytes 1966088 | tf_op jit(solution)/shard_map/ppermute | solution.py:23
  1011.2 27.2 %collective-permute-start.71 = (f32[4,512]{1,0:T(4,128)S(1)}, f32[4,512]{1,0:T(4,128)S(1)}, u32[]{:S(2)}, u32[]{:S(2)}) collective-permute-start(f32[4,512]{1,0:T(4,128)S(1)} %reduce_sum.201), channel_id=1, source_target_pairs={{0,3},{1,2},{2,1},{3,0},{4,7},{5,6},{6,5},{7,4},{8,11},{9,10},{10,... | collective-permute-start | bytes 24584 | tf_op jit(solution)/shard_map/ppermute | solution.py:23
  (111 other events, 2072.8 us)
Sparse Core Ops, SparseCore 0:
  10.7 67.4 all-gather.24
  80.4 29.6 all-gather.32
  112.3 107.1 all-gather.26
  221.5 59.1 all-gather.34
  282.7 62.9 all-gather.28
  347.1 29.4 all-gather.36
  378.3 107.1 all-gather.30
  487.7 59.1 all-gather.38
  753.1 32.8 reduce-scatter.14
  883.3 33.8 reduce-scatter.12
  919.5 68.4 reduce-scatter.10
  990.1 63.3 reduce-scatter.22
  1055.8 63.3 reduce-scatter.20
  1121.4 68.1 reduce-scatter.8
  1191.7 117.6 reduce-scatter.18
  1311.6 117.6 reduce-scatter.16

commit v2 on v1

v2 whole, which is shorter than its diff:
```python
import functools

import jax
import jax.numpy as jnp
from jax import lax
from jax.experimental import pallas as pl
from jax.experimental.pallas import tpu as pltpu
from jax.sharding import Mesh
from jax.sharding import PartitionSpec as P

LAYERS = 2
epsilon = 1e-06
STEP = 32
LANES = 256
VMEM = 52 * 1024 * 1024
f32 = jnp.float32
bf16 = jnp.bfloat16
SEQ = ("chip", "core")
NT = (((1,), (1,)), ((), ()))


def exchange(values, step):
    size = lax.axis_size("fsdp")
    return lax.ppermute(values, "fsdp", [(i, i ^ step) for i in range(size)])


def swap(values, axis):
    return lax.ppermute(values, axis, [(0, 1), (1, 0)])


def seq_length():
    return lax.axis_size("chip") * lax.axis_size("core")


def after(value, *others):
    return lax.optimization_barrier((value, *others))[0]


def all_after(values, *others):
    return list(lax.optimization_barrier((*values, *others)))[: len(values)]


def gather_rows(own, *meanwhile):
    arrived = [exchange(own, step) for step in range(1, lax.axis_size("fsdp"))]
    return [own] + all_after(arrived, *meanwhile)


def scatter_rows(pieces, between=None, *meanwhile):
    arrived = [exchange(pieces[step], step) for step in range(1, len(pieces))]
    made = None
    if between is not None:
        made, result = between()
        arrived = all_after(arrived, *made, *meanwhile)
    total = pieces[0].astype(f32)
    for piece in arrived:
        total = total + piece.astype(f32)
    return total if made is None else (total, result)


def total_rows(part):
    size = lax.axis_size("fsdp")
    pieces = part.reshape(size, -1)
    total = pieces
    for step in range(1, size):
        other = exchange(pieces, step)
        total = total + jnp.stack([other[k ^ step] for k in range(size)])
    return total.reshape(-1)


def rms_parts(values):
    factor = lax.rsqrt(jnp.mean(values * values, axis=-1, keepdims=True) + epsilon)
    return (values * factor, factor)


def norm_back(grad_unit, unit_rows, factor):
    return factor * (
        grad_unit - unit_rows * jnp.mean(grad_unit * unit_rows, axis=-1, keepdims=True)
    )


def dsilu(values, sigma):
    return sigma * (1.0 + values * (1.0 - sigma))


def sigmoid(values):
    return 1.0 / (1.0 + jnp.exp(-values))


def dot(left, right):
    return jnp.dot(left, right, preferred_element_type=f32)


def trans_dot(left, right):
    return lax.dot_general(left, right, NT, preferred_element_type=f32)


def whole(array):
    return pl.BlockSpec(array.shape, lambda j, *_: (0, 0))


def call(kernel, grid, in_specs, out_specs, out_shape, scratch, operands, cost, prefetch=()):
    return pl.pallas_call(
        kernel,
        grid_spec=pltpu.PrefetchScalarGridSpec(
            num_scalar_prefetch=len(prefetch),
            grid=grid,
            in_specs=in_specs,
            out_specs=out_specs,
            scratch_shapes=scratch,
        ),
        out_shape=out_shape,
        compiler_params=pltpu.CompilerParams(vmem_limit_bytes=VMEM),
        cost_estimate=pl.CostEstimate(flops=cost, bytes_accessed=cost // 512, transcendentals=0),
    )(*prefetch, *operands)


def assemble(pieces, rows_ref):
    rows = pieces[0].shape[0]

    @pl.when(pl.program_id(0) == 0)
    def _():
        for k, piece in enumerate(pieces):
            rows_ref[k * rows : (k + 1) * rows, :] = piece[...]


def outer(terms):
    lefts = [left for left, _ in terms]
    groups, which = [], []
    for _, pieces in terms:
        found = [k for k, group in enumerate(groups) if group is pieces]
        which.append(found[0] if found else len(groups))
        if not found:
            groups.append(pieces)
    rows, width = lefts[0].shape[0], groups[0][0].shape[1] // seq_length()
    heights = [left.shape[1] for left in lefts]
    total, count, chips = sum(heights), len(groups[0]), lax.axis_size("chip")

    def kernel(core_ref, *refs):
        left_refs, refs = refs[: len(lefts)], refs[len(lefts) :]
        piece_refs, (own, other, turned) = refs[: 2 * count * len(groups)], refs[2 * count * len(groups) :]

        @pl.when(pl.program_id(0) == 0)
        def _():
            top = 0
            for left, height in zip(left_refs, heights, strict=True):
                turned[top : top + height, :] = left[...].T
                top += height

        rights = []
        for g in range(len(groups)):
            halves = [
                jnp.concatenate([ref[...] for ref in piece_refs[k * count : (k + 1) * count]], axis=0)
                for k in (2 * g, 2 * g + 1)
            ]
            rights.append(jnp.concatenate(halves, axis=1))
        top = 0
        for height, group in zip(heights, which, strict=True):
            both = dot(turned[top : top + height, :], rights[group]).astype(bf16)
            own[top : top + height, :] = both[:, :width]
            other[top : top + height, :] = both[:, width:]
            top += height

    def columns(pieces, flip):
        return [
            pl.BlockSpec((p.shape[0], width), lambda j, core: (0, 2 * j + (1 - core[0] if flip else core[0])))
            for p in pieces
        ]

    out = jax.ShapeDtypeStruct((total, width * chips), bf16)
    return call(
        kernel,
        (chips,),
        [whole(left) for left in lefts]
        + [spec for group in groups for flip in (False, True) for spec in columns(group, flip)],
        [pl.BlockSpec((total, width), lambda j, core: (0, j))] * 2,
        [out, out],
        [pltpu.VMEM((total, rows), bf16)],
        [*lefts, *(piece for group in groups for _ in range(2) for piece in group)],
        6 * rows * total * width * 2 * chips,
        prefetch=(jnp.reshape(lax.axis_index("core"), (1,)).astype(jnp.int32),),
    )


def scatter_columns(halves):
    own, other = halves
    half = (own.astype(f32) + swap(other, "core").astype(f32)).astype(bf16)
    return lax.psum_scatter(half, "chip", scatter_dimension=1, tiled=True)


def cut(values, count):
    rows = values.shape[0] // count
    return [values[k * rows : (k + 1) * rows] for k in range(count)]


def rows_at(matrix, at, rows, tile):
    return (matrix, at // tile) if at % tile == 0 else (matrix[at : at + rows], 0)


def tile_of(units):
    return (128, units // 128) if units % 128 == 0 else (units, 1)


def up_and_gate(pieces, both, units):
    rows, depth = sum(p.shape[0] for p in pieces), pieces[0].shape[1]
    tile, steps = tile_of(units)
    chunk = rows if steps > 1 else rows // 4

    def kernel(*refs):
        piece_refs, (up_ref, gate_ref, upward_ref, gating_ref, hidden_ref, x_ref) = (
            refs[: len(pieces)], refs[len(pieces) :],
        )
        assemble(piece_refs, x_ref)
        for start in range(0, rows, chunk):
            here = slice(start, start + chunk)
            x = x_ref[here, :]
            if steps > 1:
                joined = trans_dot(x, jnp.concatenate([up_ref[...], gate_ref[...]], axis=0))
                upward, gating = joined[:, :tile], joined[:, tile:]
            else:
                upward, gating = trans_dot(x, up_ref[...]), trans_dot(x, gate_ref[...])
            upward_ref[here, :] = upward.astype(bf16)
            gating_ref[here, :] = gating.astype(bf16)
            hidden_ref[here, :] = (gating * sigmoid(gating) * upward).astype(bf16)

    out = jax.ShapeDtypeStruct((rows, units), bf16)
    return call(
        kernel,
        (steps,),
        [whole(p) for p in pieces]
        + [
            pl.BlockSpec((tile, depth), lambda j: (j, 0)),
            pl.BlockSpec((tile, depth), lambda j: (steps + j, 0)),
        ],
        [pl.BlockSpec((rows, tile), lambda j: (0, j))] * 3,
        [out] * 3,
        [pltpu.VMEM((rows, depth), bf16)],
        [*pieces, both, both],
        4 * rows * depth * units,
    )


def up_and_gate_back(pieces, down, at, upward, gating):
    rows, depth = sum(p.shape[0] for p in pieces), pieces[0].shape[1]
    units = upward.shape[1]
    tile, steps = (256, -(-units // 256)) if units % 128 == 0 else (units, 1)
    down, first = rows_at(down, at, units, tile)
    chunk = rows if steps > 1 else rows // 4

    def kernel(*refs):
        piece_refs, (down_ref, upward_ref, gating_ref, grad_up_ref, grad_gate_ref, x_ref) = (
            refs[: len(pieces)], refs[len(pieces) :],
        )
        assemble(piece_refs, x_ref)
        for start in range(0, rows, chunk):
            here = slice(start, start + chunk)
            grad = trans_dot(x_ref[here, :], down_ref[...])
            gating = gating_ref[here, :].astype(f32)
            sigma = sigmoid(gating)
            grad_up_ref[here, :] = (grad * gating * sigma).astype(bf16)
            grad_gate_ref[here, :] = (
                grad * upward_ref[here, :].astype(f32) * dsilu(gating, sigma)
            ).astype(bf16)

    block = pl.BlockSpec((rows, tile), lambda j: (0, j))
    out = jax.ShapeDtypeStruct((rows, units), bf16)
    return call(
        kernel,
        (steps,),
        [whole(p) for p in pieces]
        + [pl.BlockSpec((tile, depth), lambda j: (first + j, 0)), block, block],
        [block] * 2,
        [out] * 2,
        [pltpu.VMEM((rows, depth), bf16)],
        [*pieces, down, upward, gating],
        2 * rows * depth * units,
    )


def tile_base(place, index, size, per_piece):
    piece = lax.bitwise_xor(index // per_piece, place)
    return pl.multiple_of((piece * per_piece + lax.rem(index, per_piece)) * STEP, STEP)


def scan_kernel(count, product, place_ref, *refs):
    piece_refs, refs = refs[:count], refs[count:]
    (input_ref, forget_ref, gate_ref, keep_ref, bound_ref,
     pi_ref, pf_ref, pg_ref, state_ref, decay_ref, x_ref) = refs
    assemble(piece_refs, x_ref)
    x = x_ref[...]
    pi_ref[...] = product(x, input_ref[...])
    pf_ref[...] = product(x, forget_ref[...])
    pg_ref[...] = product(x, gate_ref[...])
    rows, lanes = pi_ref.shape
    per_piece = rows // count // STEP
    place = place_ref[0]
    bound = bound_ref[...]
    row = lax.broadcasted_iota(jnp.int32, (8, lanes), 0)

    def step(index, carry):
        carry_decay, carry_state = carry
        base = tile_base(place, index, count, per_piece)
        here = pl.ds(base, STEP)
        forget = bound + (1.0 - bound) * sigmoid(pf_ref[here, :])
        inp = pi_ref[here, :]
        source = inp * sigmoid(inp) * (1.0 - forget)
        decay = forget * keep_ref[here, :]
        for part in range(STEP // 8):
            a = decay[part * 8 : part * 8 + 8]
            b = source[part * 8 : part * 8 + 8]
            for shift in (1, 2, 4):
                a_before = jnp.where(row >= shift, pltpu.roll(a, shift, 0), 1.0)
                b_before = jnp.where(row >= shift, pltpu.roll(b, shift, 0), 0.0)
                b = a * b_before + b
                a = a * a_before
            b = a * carry_state + b
            a = a * carry_decay
            state_ref[pl.ds(base + part * 8, 8), :] = b
            decay_ref[pl.ds(base + part * 8, 8), :] = a
            carry_decay, carry_state = a[7:8], b[7:8]
        return carry_decay, carry_state

    lax.fori_loop(
        0, rows // STEP, step, (jnp.ones((1, lanes), f32), jnp.zeros((1, lanes), f32))
    )


def back_kernel(count, width, product, place_ref, *refs):
    piece_refs, refs = refs[:count], refs[count:]
    (out_ref, state_ref, gate_ref, pf_ref, inverse_ref, inner_ref, keep_ref, bound_ref, gain_ref,
     adjoint_ref, reach_ref, grad_gate_ref, mix_ref, gain_out_ref, x_ref, mixed_ref) = refs
    assemble(piece_refs, x_ref)
    mixed_ref[...] = product(x_ref[...], out_ref[...])
    rows, lanes = mixed_ref.shape
    per_piece = rows // count // STEP
    place = place_ref[0]
    bound = bound_ref[...]
    gain = gain_ref[...]
    row = lax.broadcasted_iota(jnp.int32, (8, lanes), 0)
    tiles = rows // STEP

    def step(number, carry):
        carry_reach, carry_adjoint, later, gain_sum = carry
        base = tile_base(place, tiles - 1 - number, count, per_piece)
        here = pl.ds(base, STEP)
        grad_mixed = mixed_ref[here, :]
        inverse = inverse_ref[here, :]
        scaled = state_ref[here, :] * inverse
        gate = gate_ref[here, :]
        sigma = sigmoid(gate)
        silu_gate = gate * sigma
        piece = grad_mixed * scaled
        contribution = piece * silu_gate
        grad_gate_ref[here, :] = (piece * gain * dsilu(gate, sigma)).astype(bf16)
        mix_ref[here, :] = (scaled * gain * silu_gate).astype(bf16)
        grad_state = inverse * (
            grad_mixed * gain * silu_gate - scaled * (inner_ref[here, :] * (1.0 / width))
        )
        decay = (bound + (1.0 - bound) * sigmoid(pf_ref[here, :])) * keep_ref[here, :]
        for part in reversed(range(STEP // 8)):
            now = decay[part * 8 : part * 8 + 8]
            gain_sum = gain_sum + contribution[part * 8 : part * 8 + 8]
            a = jnp.where(row == 7, later, pltpu.roll(now, 7, 0))
            b = grad_state[part * 8 : part * 8 + 8]
            for shift in (1, 2, 4):
                a_after = jnp.where(row < 8 - shift, pltpu.roll(a, 8 - shift, 0), 1.0)
                b_after = jnp.where(row < 8 - shift, pltpu.roll(b, 8 - shift, 0), 0.0)
                b = a * b_after + b
                a = a * a_after
            b = a * carry_adjoint + b
            a = a * carry_reach
            adjoint_ref[pl.ds(base + part * 8, 8), :] = b
            reach_ref[pl.ds(base + part * 8, 8), :] = a
            carry_reach, carry_adjoint, later = a[0:1], b[0:1], now[0:1]
        return carry_reach, carry_adjoint, later, gain_sum

    one, zero = jnp.ones((1, lanes), f32), jnp.zeros((1, lanes), f32)
    last = lax.fori_loop(0, tiles, step, (one, zero, one, jnp.zeros((8, lanes), f32)))
    gain_out_ref[...] = jnp.sum(last[3], axis=0, keepdims=True)


def gates_kernel(
    count, place_ref, adjoint_ref, reach_ref, state_ref, pi_ref, pf_ref, keep_ref, bound_ref,
    coming_ref, entering_ref, grad_input_ref, grad_forget_ref, bound_out_ref,
):
    rows, lanes = adjoint_ref.shape
    per_piece = rows // count // STEP
    place = place_ref[0]
    bound = bound_ref[...]
    coming = coming_ref[...]
    row = lax.broadcasted_iota(jnp.int32, (STEP, lanes), 0)

    def step(index, carry):
        before, bound_sum = carry
        base = tile_base(place, index, count, per_piece)
        here = pl.ds(base, STEP)
        adjoint = adjoint_ref[here, :] + reach_ref[here, :] * coming
        state = state_ref[here, :]
        previous = jnp.where(row == 0, before, pltpu.roll(state, 1, 0))
        inp = pi_ref[here, :]
        sigma_input = sigmoid(inp)
        sigma_forget = sigmoid(pf_ref[here, :])
        forget = bound + (1.0 - bound) * sigma_forget
        grad_forget = adjoint * (keep_ref[here, :] * previous - inp * sigma_input)
        piece = grad_forget * (1.0 - sigma_forget)
        grad_input_ref[here, :] = (adjoint * (1.0 - forget) * dsilu(inp, sigma_input)).astype(bf16)
        grad_forget_ref[here, :] = (piece * (1.0 - bound) * sigma_forget).astype(bf16)
        for part in range(STEP // 8):
            bound_sum = bound_sum + piece[part * 8 : part * 8 + 8]
        return state[STEP - 1 : STEP], bound_sum

    last = lax.fori_loop(
        0, rows // STEP, step, (entering_ref[...], jnp.zeros((8, lanes), f32))
    )
    bound_out_ref[...] = jnp.sum(last[1], axis=0, keepdims=True)


def over_channels(kernel, place, pieces, matrices, operands, outs, scratch, channels, cost):
    lanes = min(LANES, channels)

    def part(matrix, at, columns):
        if columns:
            return pl.BlockSpec((matrix.shape[0], lanes), lambda c, p: (0, at // lanes + c))
        return pl.BlockSpec((lanes, matrix.shape[1]), lambda c, p: (at // lanes + c, 0))

    def spec(rows, narrow):
        if narrow:
            return pl.BlockSpec((rows, 1), lambda c, p: (0, 0))
        return pl.BlockSpec((rows, lanes), lambda c, p: (0, c))

    return call(
        kernel,
        (channels // lanes,),
        [whole(p) for p in pieces]
        + [part(*m) for m in matrices]
        + [spec(o.shape[0], o.shape[1] == 1) for o in operands],
        [spec(rows, False) for rows, _ in outs],
        [jax.ShapeDtypeStruct((rows, channels), kind) for rows, kind in outs],
        scratch,
        [*pieces, *(m[0] for m in matrices), *operands],
        cost,
        prefetch=(place,),
    )


def entering_of(decay, state, reverse):
    length = seq_length()
    chips, core = length // 2, lax.axis_index("core")
    own = jnp.concatenate([decay, state], axis=0)
    other = swap(own, "core")
    is_first = core == (1 if reverse else 0)
    first, second = jnp.where(is_first, own, other), jnp.where(is_first, other, own)
    pair = jnp.concatenate(
        [first[0:1] * second[0:1], second[0:1] * first[1:2] + second[1:2]], axis=0
    )
    sign = -1 if reverse else 1
    arrived = [
        lax.ppermute(
            pair,
            SEQ,
            [(i, i + sign * 2 * hop) for i in range(length) if 0 <= i + sign * 2 * hop < length],
        )
        for hop in range(1, chips)
    ]
    total = jnp.zeros_like(state)
    for hop in range(chips - 1, 0, -1):
        total = arrived[hop - 1][0:1] * total + arrived[hop - 1][1:2]
    return jnp.where(is_first, total, other[0:1] * total + other[1:2])


def total_small(rows_of_width, rows_of_channels, first_channel, channels):
    size = lax.axis_size("fsdp")
    place = lax.axis_index("fsdp")

    def columns(step):
        return lax.dynamic_slice_in_dim(
            rows_of_width, lax.bitwise_xor(place, step) * channels, channels, 1
        )

    mine = columns(0)
    for step in range(1, size):
        mine = mine + exchange(columns(step), step)
    mine = jnp.sum(lax.all_gather(jnp.concatenate([mine, rows_of_channels], axis=0), SEQ), axis=0)
    total = jnp.zeros((mine.shape[0], channels * size), f32)
    total = lax.dynamic_update_slice_in_dim(total, mine, first_channel, 1)
    for step in range(1, size):
        total = lax.dynamic_update_slice_in_dim(
            total, exchange(mine, step), lax.bitwise_xor(place, step) * channels, 1
        )
    return total


def local(
    hidden_in, w_input, w_forget, w_gate, w_out, w_up, w_glu, w_down,
    lower_bound, norm_mix, norm_ffn, out_gain, lengths, cotangent,
):
    row_count, model_width = hidden_in.shape
    channels = w_input.shape[2]
    hidden_units = w_up.shape[2]
    size = lax.axis_size("fsdp")
    place = lax.axis_index("fsdp")
    block_rows = row_count * size
    first_channel = place * channels
    place_array = jnp.reshape(place, (1,)).astype(jnp.int32)
    last_layer = LAYERS - 1

    starts = jnp.cumsum(lengths) - lengths
    owners = lax.bitwise_xor(jnp.arange(size, dtype=jnp.int32), place.astype(jnp.int32))
    positions = (
        lax.axis_index(SEQ) * block_rows
        + (owners[:, None] * row_count + jnp.arange(row_count, dtype=jnp.int32)[None, :])
    ).reshape(-1)
    keep = (1.0 - jnp.any(positions[:, None] == starts[None, :], axis=1).astype(f32))[:, None]
    bounds = lax.dynamic_slice_in_dim(lower_bound, first_channel, channels, 1)
    gains = lax.dynamic_slice_in_dim(out_gain, first_channel, channels, 1)

    def side(*shards):
        return lax.all_gather(jnp.concatenate(shards, axis=1), SEQ, axis=0, tiled=True)

    def tall(*shards):
        return lax.all_gather(jnp.concatenate(shards, axis=0), SEQ, axis=1, tiled=True)

    mix_rows = [0] + [3 * channels] * last_layer
    mixes = [side(w_input[0], w_forget[0], w_gate[0])]
    lows, boths = [tall(w_out[0], w_down[0])], []
    for layer in range(LAYERS):
        if layer > 0:
            turned = (w_input[layer].T, w_forget[layer].T, w_gate[layer].T)
            lows.append(tall(*turned, w_out[layer], w_down[layer]))
            mixes.append(lows[layer])
        boths.append(tall(w_up[layer].T, w_glu[layer].T))

    stream = hidden_in.astype(f32)
    saved = []
    for layer in range(LAYERS):
        mix, low, at_out = mixes[layer], lows[layer], mix_rows[layer]
        at_down, first_layer = at_out + channels, layer == 0
        bound, gain = bounds[layer][None, :], gains[layer][None, :]
        unit, factor = rms_parts(stream)
        normed = gather_rows((unit * norm_mix[layer]).astype(bf16))
        if layer == 0:
            grad_y = gather_rows(after(cotangent, *normed))
            normed = all_after(normed, *grad_y)
        proj_input, proj_forget, proj_gate, local_state, local_decay = over_channels(
            functools.partial(scan_kernel, size, dot if first_layer else trans_dot),
            place_array,
            normed,
            [(mix, k * channels, first_layer) for k in range(3)],
            (keep, bound),
            ((block_rows, f32),) * 5,
            [pltpu.VMEM((block_rows, model_width), bf16)],
            channels,
            6 * block_rows * model_width * channels,
        )
        last_row = lax.bitwise_xor(size - 1, place) * row_count + row_count - 1
        entering = entering_of(
            lax.dynamic_slice_in_dim(local_decay, last_row, 1, 0),
            lax.dynamic_slice_in_dim(local_state, last_row, 1, 0),
            False,
        )
        state = local_state + local_decay * entering
        squares = total_rows(jnp.sum(state * state, axis=1))
        inverse = lax.rsqrt(squares / model_width + epsilon)[:, None]
        loose = (state * gain * jax.nn.silu(proj_gate)).astype(bf16)
        parts = cut(dot(loose, low[at_out:at_down]).astype(bf16), size)
        branch = scatter_rows(parts) * inverse[:row_count]
        middle = stream + branch
        unit_two, _ = rms_parts(middle)
        normed_two = (unit_two * norm_ffn[layer]).astype(bf16)
        normed_two = gather_rows(normed_two)
        upward, gating, hidden = up_and_gate(normed_two, boths[layer], hidden_units)
        if layer < last_layer:
            stream = middle + scatter_rows(cut(dot(hidden, low[at_down:]).astype(bf16), size))
        saved.append(
            (factor, normed, proj_input, proj_forget, proj_gate, entering,
             state, inverse, branch, middle, normed_two, upward, gating, hidden, unit)
        )

    grad_x = cotangent.astype(f32)
    shards = [None] * LAYERS
    smalls = [None] * LAYERS
    scattered = {}

    def arrived(*names):
        return tuple(scattered[name] for name in names if name in scattered)

    for layer in reversed(range(LAYERS)):
        mix, low, at_out, both = mixes[layer], lows[layer], mix_rows[layer], boths[layer]
        at_down, first_layer = at_out + channels, layer == 0
        bound, gain = bounds[layer][None, :], gains[layer][None, :]
        (factor, normed, proj_input, proj_forget, proj_gate, entering, state, inverse,
         branch, middle, normed_two, upward, gating, hidden, unit) = saved[layer]
        unit_two, factor_two = rms_parts(middle)

        if layer < last_layer:
            grad_y = gather_rows(grad_x.astype(bf16), *arrived(("ffn", layer + 1)))
        down_part = outer([(hidden, grad_y)])
        down_shard = scatter_columns(down_part)
        grad_up, grad_glu = up_and_gate_back(
            all_after(grad_y, *down_part), low, at_down, upward, gating
        )
        part = dot(jnp.concatenate([grad_up, grad_glu], axis=1), both).astype(bf16)

        def ffn_gradients():
            made = outer([(after(grad_up, part), normed_two), (grad_glu, normed_two)])
            return made, scatter_columns(made)

        grad_normed_two, ffn_shard = scatter_rows(
            cut(part, size), ffn_gradients, *arrived(("low", layer + 1))
        )
        ffn_piece = jnp.sum(grad_normed_two * unit_two, axis=0)
        grad_middle = grad_x + norm_back(grad_normed_two * norm_ffn[layer], unit_two, factor_two)

        grad_m_own = grad_middle.astype(bf16)
        grad_m = gather_rows(grad_m_own, down_shard)
        inner = jnp.concatenate(
            gather_rows(jnp.sum(grad_m_own.astype(f32) * branch, axis=1)), axis=0
        )[:, None]
        adjoint, reach, grad_gate, mixed, gain_piece = over_channels(
            functools.partial(back_kernel, size, model_width, trans_dot),
            place_array,
            grad_m,
            [(low, at_out, False)],
            (state, proj_gate, proj_forget, inverse, inner, keep, bound, gain),
            ((block_rows, f32), (block_rows, f32), (block_rows, bf16), (block_rows, bf16), (1, f32)),
            [pltpu.VMEM((block_rows, model_width), bf16), pltpu.VMEM((block_rows, min(LANES, channels)), f32)],
            channels,
            100 * block_rows * channels,
        )
        first_row = place * row_count
        first_decay = (
            bound
            + (1.0 - bound)
            * jax.nn.sigmoid(lax.dynamic_slice_in_dim(proj_forget, first_row, 1, 0))
        ) * lax.dynamic_slice_in_dim(keep, first_row, 1, 0)
        coming = entering_of(
            first_decay * lax.dynamic_slice_in_dim(reach, first_row, 1, 0),
            first_decay * lax.dynamic_slice_in_dim(adjoint, first_row, 1, 0),
            True,
        )
        grad_input, grad_forget, bound_piece = over_channels(
            functools.partial(gates_kernel, size),
            place_array,
            [],
            [],
            (adjoint, reach, state, proj_input, proj_forget, keep, bound, coming, entering),
            ((block_rows, bf16), (block_rows, bf16), (1, f32)),
            [],
            channels,
            100 * block_rows * channels,
        )
        grad_three = (grad_input, grad_forget, grad_gate)
        joined = jnp.concatenate([grad_input, grad_forget, grad_gate], axis=1)
        part = trans_dot(joined, mix) if first_layer else dot(joined, mix[: 3 * channels])
        part = part.astype(bf16)

        def low_gradients():
            made = outer([(after(joined, part), normed), (mixed, grad_m)])
            return made, scatter_columns(made)

        grad_normed, low_shard = scatter_rows(
            cut(part, size), low_gradients, *((ffn_shard,) if first_layer else ())
        )
        scattered.update({("ffn", layer): ffn_shard, ("low", layer): low_shard})
        mix_piece = jnp.sum(grad_normed * unit, axis=0)
        grad_x = grad_middle + norm_back(grad_normed * norm_mix[layer], unit, factor)

        scattered[layer] = (ffn_shard, down_shard, low_shard)
        smalls[layer] = (mix_piece, ffn_piece, bound_piece, gain_piece)
    middle, hidden = saved[last_layer][9], saved[last_layer][13]
    part = dot(after(hidden, grad_x), lows[-1][mix_rows[-1] + channels :]).astype(bf16)
    hidden_out = (middle + scatter_rows(cut(part, size))).astype(bf16)
    wide_rows = jnp.stack([row for pieces in smalls for row in pieces[:2]])
    own_rows = jnp.concatenate([row for pieces in smalls for row in pieces[2:]], axis=0)
    small = total_small(after(wide_rows, grad_x), own_rows, first_channel, channels)
    for layer in range(LAYERS):
        ffn_shard, down_shard, low_shard = scattered[layer]
        if layer == 0:
            low_shard = after(low_shard, hidden_out)
        shards[layer] = (
            *(low_shard[k * channels : (k + 1) * channels].T for k in range(3)),
            low_shard[3 * channels :],
            ffn_shard[:hidden_units].T,
            ffn_shard[hidden_units:].T,
            down_shard,
        )
    stacked = tuple(
        jnp.stack([shards[layer][member].astype(f32) for layer in range(LAYERS)])
        for member in range(7)
    )
    wide_rows, own_rows = small[: 2 * LAYERS], small[2 * LAYERS :]
    return (
        hidden_out, grad_x, *stacked, own_rows[0::2], wide_rows[0::2], wide_rows[1::2], own_rows[1::2]
    )


def solution(mesh):
    length, size = mesh.devices.shape
    split = Mesh(mesh.devices.reshape(length // 2, 2, size), (*SEQ, "fsdp"))
    rows = P((*SEQ, "fsdp"), None)
    wide = P(None, SEQ, "fsdp")
    tall = P(None, "fsdp", SEQ)
    weights = (wide, wide, wide, tall, wide, wide, tall)
    return jax.shard_map(
        local,
        mesh=split,
        in_specs=(rows, *weights, P(), P(), P(), P(), P(), rows),
        out_specs=(rows, rows, *weights, P(), P(), P(), P()),
        check_vma=False,
    )
```

time: 1450 us -> 1110 us (0.77)
  waiting for transfers between devices: 913 us -> 560 us
  Pallas kernels: 35 us -> 184 us
  matrix products: 201 us -> 63.6 us
  blocking collectives: 84.9 us -> 15.7 us
  other arithmetic: 49.5 us -> 94.4 us
  starting transfers between devices: 84.7 us -> 107 us
    reduce_scatter x8 -> x6, waiting for transfers between devices: 350 us -> 0.05 us  [scatter_columns(): return lax.psum_scatter(half, 'chip', scatter_dimension=1, tiled=True)]
    pallas_call x6 -> x16, Pallas kernels: 35 us -> 184 us  [call(): pl.pallas_call(kernel, grid_spec=pltpu.PrefetchScalarGridSpec(num_scalar_...]
    dot_general x24 -> x8, matrix products: 201 us -> 63.6 us  [the longest x7 54.5 us: dot(): return jnp.dot(left, right, preferred_element_type=f32)]
    all_gather x6 -> x1, blocking collectives: 84.9 us -> 15.7 us  [total_small(): lax.all_gather(jnp.concatenate([mine, rows_of_channels], axis=0), SEQ)]
    all_gather x8 -> x5, waiting for transfers between devices: 178 us -> 115 us  [the longest x4 115 us: tall(): lax.all_gather(jnp.concatenate(shards, axis=0), SEQ, axis=1, tiled=True)]
    ppermute x72 -> x88, waiting for transfers between devices: 385 us -> 445 us  [the longest x66 407 us: exchange(): return lax.ppermute(values, 'fsdp', [(i, i ^ step) for i in range(size)])]
    convert_element_type x4 -> x10, other arithmetic: 7.35 us -> 43.7 us  [the longest x6 36.8 us: scatter_columns(): half = (own.astype(f32) + swap(other, 'core').astype(f32)).astype(bf16)]
    ppermute x72 -> x88, starting transfers between devices: 83.8 us -> 106 us  [the longest x66 79.6 us: exchange(): return lax.ppermute(values, 'fsdp', [(i, i ^ step) for i in range(size)])]
  transfers between devices with their start and end apart: 88 -> 99, of which waited for: 46 -> 56; matrix products, arithmetic and copies ran while one was open for 16% -> 18% of each run, Pallas kernels for 2% -> 14%
where the time goes in v2:
time: 1110 us
  waiting for transfers between devices  560 us (50%)
  Pallas kernels  184 us (17%)
  starting transfers between devices  107 us (10%)
  other arithmetic  94.4 us (9%)
  local copies, waits for them, and re-layouts  64 us (6%)
  matrix products  63.6 us (6%)
  between operations  15.8 us (1%)
  blocking collectives  15.7 us (1%)
    ppermute x66, waiting for transfers between devices, exchange(): return lax.ppermute(values, 'fsdp', [(i, i ^ step) for i in range(size)])  407 us
    pallas_call x16, Pallas kernels, call(): pl.pallas_call(kernel, grid_spec=pltpu.PrefetchScalarGridSpec(num_scalar_...  184 us
    all_gather x4, waiting for transfers between devices, tall(): lax.all_gather(jnp.concatenate(shards, axis=0), SEQ, axis=1, tiled=True)  115 us
    ppermute x66, starting transfers between devices, exchange(): return lax.ppermute(values, 'fsdp', [(i, i ^ step) for i in range(size)])  79.6 us
    dot_general x7, matrix products, dot(): return jnp.dot(left, right, preferred_element_type=f32)  54.5 us
    convert_element_type x6, other arithmetic, scatter_columns(): half = (own.astype(f32) + swap(other, 'core').astype(f32)).astype(bf16)  36.8 us
    unnamed x214, local copies, waits for them, and re-layouts  33.8 us
    ppermute x12, starting transfers between devices, entering_of(): lax.ppermute(pair, SEQ, [(i, i + sign * 2 * hop) for i in range(length) i...  24.8 us
  transfers between devices with their start and end apart: 99, of which 56 were waited for; matrix products, arithmetic and copies ran while one was open for 18% of the time, Pallas kernels for 14%

profile of v2, /device:TPU:0, one launch (start us, length us, event | category | flops | bytes accessed | tf_op | source)
XLA Modules:
  0.0 1105.3 jit_solution(7969416699955522181)
XLA Ops:
  33.8 13.7 %collective-permute-done.refs_1_.refs_3_.refs_7_ = bf16[160,2048]{1,0:T(8,128)(2,1)S(1)} collective-permute-done((bf16[160,2048]{1,0:T(8,128)(2,1)S(1)}, bf16[160,2048]{1,0:T(8,128)(2,1)S(1)}, u32[]{:S(2)}, u32[]{:S(2)}) %collective-permute-start) | collective-permute-done | bytes 655392 | tf_op jit(solution)/shard_map/ppermute | solution.py:24
  47.5 14.7 %collective-permute-done.1.refs_2_.refs_4_.refs_8_ = bf16[160,2048]{1,0:T(8,128)(2,1)S(1)} collective-permute-done((bf16[160,2048]{1,0:T(8,128)(2,1)S(1)}, bf16[160,2048]{1,0:T(8,128)(2,1)S(1)}, u32[]{:S(2)}, u32[]{:S(2)}) %collective-permute-start.1) | collective-permute-done | bytes 655392 | tf_op jit(solution)/shard_map/ppermute | solution.py:24
  67.6 13.1 %collective-permute-done.3.refs_2_.refs_6_.refs_1_ = bf16[160,2048]{1,0:T(8,128)(2,1)S(1)} collective-permute-done((bf16[160,2048]{1,0:T(8,128)(2,1)S(1)}, bf16[160,2048]{1,0:T(8,128)(2,1)S(1)}, u32[]{:S(2)}, u32[]{:S(2)}) %collective-permute-start.3) | collective-permute-done | bytes 655392 | tf_op jit(solution)/shard_map/ppermute | solution.py:24
  80.7 12.3 %collective-permute-done.4.refs_3_.refs_7_.refs_2_ = bf16[160,2048]{1,0:T(8,128)(2,1)} collective-permute-done((bf16[160,2048]{1,0:T(8,128)(2,1)S(1)}, bf16[160,2048]{1,0:T(8,128)(2,1)}, u32[]{:S(2)}, u32[]{:S(2)}) %collective-permute-start.4) | collective-permute-done | bytes 655392 | tf_op jit(solution)/shard_map/ppermute | solution.py:24
  93.0 13.3 %shard_map.237 = (f32[640,512]{1,0:T(8,128)}, f32[640,512]{1,0:T(8,128)}, f32[640,512]{1,0:T(8,128)}, f32[640,512]{1,0:T(8,128)}, f32[640,512]{1,0:T(8,128)}) custom-call(s32[1]{0:T(128)} %bitcast.place_ref, bf16[160,2048]{1,0:T(8,128)(2,1)S(1)} %fusion.35.refs_0_.refs_2_.refs_6_, bf16[160,2048]{1,0:T(8,128)(2,1)S(1)} %collective-permute-done.refs_1_.refs_3_.refs_7_, ...), custom_call_target="tpu_custom_call" | custom-call | flops 4026531840 | bytes 7864320 | tf_op jit(solution)/shard_map/pallas_call | solution.py:102
  112.6 4.5 collective-permute-start.8
  128.1 28.9 %all-gather.9.cloned.1.call-done.refs_4_ = bf16[1920,2048]{1,0:T(8,128)(2,1)} async-done(((bf16[1920,256]{1,0:T(8,128)(2,1)}), bf16[1920,2048]{1,0:T(8,128)(2,1)}) %all-gather.9.cloned.1.call-update) | async-done | bytes 7864336 | tf_op jit(solution)/shard_map/all_gather | solution.py:520
  166.9 14.9 %collective-permute-done.12 = bf16[160,2048]{1,0:T(8,128)(2,1)S(1)} collective-permute-done((bf16[160,2048]{1,0:T(8,128)(2,1)}, bf16[160,2048]{1,0:T(8,128)(2,1)S(1)}, u32[]{:S(2)}, u32[]{:S(2)}) %collective-permute-start.12) | collective-permute-done | bytes 655392 | tf_op jit(solution)/shard_map/ppermute | solution.py:24
  181.8 13.4 %collective-permute-done.11 = bf16[160,2048]{1,0:T(8,128)(2,1)} collective-permute-done((bf16[160,2048]{1,0:T(8,128)(2,1)}, bf16[160,2048]{1,0:T(8,128)(2,1)}, u32[]{:S(2)}, u32[]{:S(2)}) %collective-permute-start.11) | collective-permute-done | bytes 655392 | tf_op jit(solution)/shard_map/ppermute | solution.py:24
  201.2 14.1 %collective-permute-done.16.refs_1_.refs_3_.refs_7_ = bf16[160,2048]{1,0:T(8,128)(2,1)S(1)} collective-permute-done((bf16[160,2048]{1,0:T(8,128)(2,1)S(1)}, bf16[160,2048]{1,0:T(8,128)(2,1)S(1)}, u32[]{:S(2)}, u32[]{:S(2)}) %collective-permute-start.16) | collective-permute-done | bytes 655392 | tf_op jit(solution)/shard_map/ppermute | solution.py:24
  215.3 14.2 %collective-permute-done.17.refs_2_.refs_4_.refs_8_ = bf16[160,2048]{1,0:T(8,128)(2,1)S(1)} collective-permute-done((bf16[160,2048]{1,0:T(8,128)(2,1)S(1)}, bf16[160,2048]{1,0:T(8,128)(2,1)S(1)}, u32[]{:S(2)}, u32[]{:S(2)}) %collective-permute-start.17) | collective-permute-done | bytes 655392 | tf_op jit(solution)/shard_map/ppermute | solution.py:24
  230.4 37.4 %all-gather.11.cloned.1.call-done.refs_4_.refs_5_ = bf16[2816,2048]{1,0:T(8,128)(2,1)} async-done(((bf16[2816,256]{1,0:T(8,128)(2,1)}), bf16[2816,2048]{1,0:T(8,128)(2,1)}) %all-gather.11.cloned.1.call-update) | async-done | bytes 11534352 | tf_op jit(solution)/shard_map/all_gather | solution.py:520
  268.9 15.6 %shard_map.238 = (bf16[640,1408]{1,0:T(8,128)(2,1)}, bf16[640,1408]{1,0:T(8,128)(2,1)}, bf16[640,1408]{1,0:T(8,128)(2,1)}) custom-call(bf16[160,2048]{1,0:T(8,128)(2,1)S(1)} %multiply_convert_fusion.3.refs_0_.refs_2_.refs_6_, bf16[160,2048]{1,0:T(8,128)(2,1)S(1)} %collective-permute-done.16.refs_1_.refs_3_.refs_7_, bf16[160,2048]{1,0:T(8,128)(2,1)S(1)} %copy-done.16, ...), custom_call_target="tpu_custom_call" | custom-call | flops 7381975040 | bytes 14417920 | tf_op jit(solution)/shard_map/pallas_call | solution.py:102
  284.6 6.0 fusion.20
  294.3 15.0 %collective-permute-done.21 = bf16[160,2048]{1,0:T(8,128)(2,1)S(1)} collective-permute-done((bf16[160,2048]{1,0:T(8,128)(2,1)S(1)}, bf16[160,2048]{1,0:T(8,128)(2,1)S(1)}, u32[]{:S(2)}, u32[]{:S(2)}) %collective-permute-start.21) | collective-permute-done | bytes 655392 | tf_op jit(solution)/shard_map/ppermute | solution.py:24
  309.3 13.3 %collective-permute-done.20 = bf16[160,2048]{1,0:T(8,128)(2,1)S(1)} collective-permute-done((bf16[160,2048]{1,0:T(8,128)(2,1)S(1)}, bf16[160,2048]{1,0:T(8,128)(2,1)S(1)}, u32[]{:S(2)}, u32[]{:S(2)}) %collective-permute-start.20) | collective-permute-done | bytes 655392 | tf_op jit(solution)/shard_map/ppermute | solution.py:24
  327.1 14.1 %collective-permute-done.22.refs_1_.refs_3_.refs_7_ = bf16[160,2048]{1,0:T(8,128)(2,1)S(1)} collective-permute-done((bf16[160,2048]{1,0:T(8,128)(2,1)S(1)}, bf16[160,2048]{1,0:T(8,128)(2,1)S(1)}, u32[]{:S(2)}, u32[]{:S(2)}) %collective-permute-start.22) | collective-permute-done | bytes 655392 | tf_op jit(solution)/shard_map/ppermute | solution.py:24
  341.2 14.3 %collective-permute-done.23.refs_2_.refs_4_.refs_8_ = bf16[160,2048]{1,0:T(8,128)(2,1)S(1)} collective-permute-done((bf16[160,2048]{1,0:T(8,128)(2,1)S(1)}, bf16[160,2048]{1,0:T(8,128)(2,1)S(1)}, u32[]{:S(2)}, u32[]{:S(2)}) %collective-permute-start.23) | collective-permute-done | bytes 655392 | tf_op jit(solution)/shard_map/ppermute | solution.py:24
  356.4 41.8 %all-gather.13.cloned.1.call-done.refs_4_.refs_5_.refs_6_ = bf16[3456,2048]{1,0:T(8,128)(2,1)} async-done(((bf16[3456,256]{1,0:T(8,128)(2,1)}), bf16[3456,2048]{1,0:T(8,128)(2,1)}) %all-gather.13.cloned.1.call-update) | async-done | bytes 14155792 | tf_op jit(solution)/shard_map/all_gather | solution.py:520
  398.2 13.0 %shard_map.239 = (f32[640,512]{1,0:T(8,128)}, f32[640,512]{1,0:T(8,128)}, f32[640,512]{1,0:T(8,128)}, f32[640,512]{1,0:T(8,128)}, f32[640,512]{1,0:T(8,128)}) custom-call(s32[1]{0:T(128)} %bitcast.place_ref, bf16[160,2048]{1,0:T(8,128)(2,1)S(1)} %multiply_convert_fusion.2.refs_0_.refs_2_.refs_6_, ...), custom_call_target="tpu_custom_call" | custom-call | flops 4026531840 | bytes 7864320 | tf_op jit(solution)/shard_map/pallas_call | solution.py:102
  415.2 4.8 collective-permute-start.27
  439.2 14.9 %collective-permute-done.31 = bf16[160,2048]{1,0:T(8,128)(2,1)S(1)} collective-permute-done((bf16[160,2048]{1,0:T(8,128)(2,1)}, bf16[160,2048]{1,0:T(8,128)(2,1)S(1)}, u32[]{:S(2)}, u32[]{:S(2)}) %collective-permute-start.31) | collective-permute-done | bytes 655392 | tf_op jit(solution)/shard_map/ppermute | solution.py:24
  454.1 11.4 %collective-permute-done.30 = bf16[160,2048]{1,0:T(8,128)(2,1)} collective-permute-done((bf16[160,2048]{1,0:T(8,128)(2,1)}, bf16[160,2048]{1,0:T(8,128)(2,1)}, u32[]{:S(2)}, u32[]{:S(2)}) %collective-permute-start.30) | collective-permute-done | bytes 655392 | tf_op jit(solution)/shard_map/ppermute | solution.py:24
  471.7 14.1 %collective-permute-done.35.refs_1_.refs_3_.refs_7_ = bf16[160,2048]{1,0:T(8,128)(2,1)S(1)} collective-permute-done((bf16[160,2048]{1,0:T(8,128)(2,1)S(1)}, bf16[160,2048]{1,0:T(8,128)(2,1)S(1)}, u32[]{:S(2)}, u32[]{:S(2)}) %collective-permute-start.35) | collective-permute-done | bytes 655392 | tf_op jit(solution)/shard_map/ppermute | solution.py:24
  486.7 12.3 %collective-permute-done.36.refs_2_.refs_4_.refs_8_ = bf16[160,2048]{1,0:T(8,128)(2,1)S(1)} collective-permute-done((bf16[160,2048]{1,0:T(8,128)(2,1)S(1)}, bf16[160,2048]{1,0:T(8,128)(2,1)S(1)}, u32[]{:S(2)}, u32[]{:S(2)}) %collective-permute-start.36) | collective-permute-done | bytes 655392 | tf_op jit(solution)/shard_map/ppermute | solution.py:24
  499.9 6.6 all-gather.15.cloned.1.call-done.refs_4_.refs_5_
  508.6 15.3 %shard_map.240 = (bf16[640,1408]{1,0:T(8,128)(2,1)}, bf16[640,1408]{1,0:T(8,128)(2,1)}, bf16[640,1408]{1,0:T(8,128)(2,1)}) custom-call(bf16[160,2048]{1,0:T(8,128)(2,1)S(1)} %multiply_convert_fusion.refs_0_.refs_2_.refs_6_, bf16[160,2048]{1,0:T(8,128)(2,1)S(1)} %copy-done.21, bf16[160,2048]{1,0:T(8,128)(2,1)S(1)} %copy-done.23, ...), custom_call_target="tpu_custom_call" | custom-call | flops 7381975040 | bytes 14417920 | tf_op jit(solution)/shard_map/pallas_call | solution.py:102
  523.9 9.0 shard_map.241
  533.1 10.2 shard_map.242
  543.3 12.6 %fusion.17 = bf16[640,2048]{1,0:T(8,128)(2,1)} fusion(bf16[2816,2048]{1,0:T(8,128)(2,1)} %all-gather.15.cloned.1.call-done.refs_4_.refs_5_, bf16[640,1408]{1,0:T(8,128)(2,1)} %get-tuple-element.160.refs_1_, bf16[640,1408]{1,0:T(8,128)(2,1)} %get-tuple-element.161.refs_0_), kind=kOutput, calls=%fused_computation.21 | convolution fusion | flops 7390494720 | bytes 17760256 | tf_op jit(solution)/shard_map/dot_general | solution.py:90
  556.0 15.2 %shard_map.243 = (bf16[2816,1024]{1,0:T(8,128)(2,1)}, bf16[2816,1024]{1,0:T(8,128)(2,1)}) custom-call(s32[1]{0:T(128)} %bitcast.32.core_ref, bf16[640,1408]{1,0:T(8,128)(2,1)} %get-tuple-element.161.refs_0_, bf16[640,1408]{1,0:T(8,128)(2,1)} %get-tuple-element.160.refs_1_, bf16[160,2048]{1,0:T(8,128)(2,1)S(1)} %multiply_convert_fusion.refs_0_.refs_2_.refs_6_, ...), custom_call_target="tpu_custom_call" | custom-call | flops 22145925120 | bytes 43253760 | tf_op jit(solution)/shard_map/pallas_call | solution.py:102
  574.7 6.2 collective-permute-done.58
  580.9 9.8 add_convert_fusion.1
  596.0 14.1 %collective-permute-done.38 = bf16[160,2048]{1,0:T(8,128)(2,1)S(1)} collective-permute-done((bf16[160,2048]{1,0:T(8,128)(2,1)S(1)}, bf16[160,2048]{1,0:T(8,128)(2,1)S(1)}, u32[]{:S(2)}, u32[]{:S(2)}) %collective-permute-start.38) | collective-permute-done | bytes 655392 | tf_op jit(solution)/shard_map/ppermute | solution.py:24
  610.1 14.5 %collective-permute-done.39 = bf16[160,2048]{1,0:T(8,128)(2,1)S(1)} collective-permute-done((bf16[160,2048]{1,0:T(8,128)(2,1)S(1)}, bf16[160,2048]{1,0:T(8,128)(2,1)S(1)}, u32[]{:S(2)}, u32[]{:S(2)}) %collective-permute-start.39) | collective-permute-done | bytes 655392 | tf_op jit(solution)/shard_map/ppermute | solution.py:24
  638.4 21.6 %collective-permute-done.45 = f32[160]{0:T(256)S(1)} collective-permute-done((f32[160]{0:T(256)S(1)}, f32[160]{0:T(256)S(1)}, u32[]{:S(2)}, u32[]{:S(2)}) %collective-permute-start.45) | collective-permute-done | bytes 672 | tf_op jit(solution)/shard_map/ppermute | solution.py:24
  664.8 11.0 shard_map.244
  690.7 5.6 shard_map.245
  696.5 8.2 fusion.26
  704.7 13.1 %shard_map.246 = (bf16[2048,1024]{1,0:T(8,128)(2,1)}, bf16[2048,1024]{1,0:T(8,128)(2,1)}) custom-call(s32[1]{0:T(128)} %bitcast.32.core_ref, bf16[640,1536]{1,0:T(8,128)(2,1)} %copy-done.72, bf16[640,512]{1,0:T(8,128)(2,1)S(1)} %copy-done.19, bf16[160,2048]{1,0:T(8,128)(2,1)S(1)} %multiply_convert_fusion.2.refs_0_.refs_2_.refs_6_, ...), custom_call_target="tpu_custom_call" | custom-call | flops 16106127360 | bytes 31457280 | tf_op jit(solution)/shard_map/pallas_call | solution.py:102
  725.2 5.7 add_convert_fusion.3
  731.2 5.7 collective-permute-done.52
  736.9 14.9 %collective-permute-done.53 = bf16[160,2048]{1,0:T(8,128)(2,1)} collective-permute-done((bf16[160,2048]{1,0:T(8,128)(2,1)}, bf16[160,2048]{1,0:T(8,128)(2,1)}, u32[]{:S(2)}, u32[]{:S(2)}) %collective-permute-start.53) | collective-permute-done | bytes 655392 | tf_op jit(solution)/shard_map/ppermute | solution.py:24
  761.7 14.2 %collective-permute-done.55.refs_2_.refs_6_.refs_1_ = bf16[160,2048]{1,0:T(8,128)(2,1)S(1)} collective-permute-done((bf16[160,2048]{1,0:T(8,128)(2,1)S(1)}, bf16[160,2048]{1,0:T(8,128)(2,1)S(1)}, u32[]{:S(2)}, u32[]{:S(2)}) %collective-permute-start.55) | collective-permute-done | bytes 655392 | tf_op jit(solution)/shard_map/ppermute | solution.py:24
  775.9 12.9 %collective-permute-done.56.refs_3_.refs_7_.refs_2_ = bf16[160,2048]{1,0:T(8,128)(2,1)S(1)} collective-permute-done((bf16[160,2048]{1,0:T(8,128)(2,1)S(1)}, bf16[160,2048]{1,0:T(8,128)(2,1)S(1)}, u32[]{:S(2)}, u32[]{:S(2)}) %collective-permute-start.56) | collective-permute-done | bytes 655392 | tf_op jit(solution)/shard_map/ppermute | solution.py:24
  789.6 8.9 shard_map.247
  798.5 10.1 shard_map.248
  808.6 12.7 %fusion.14 = bf16[640,2048]{1,0:T(8,128)(2,1)} fusion(bf16[2816,2048]{1,0:T(8,128)(2,1)} %all-gather.11.cloned.1.call-done.refs_4_.refs_5_, bf16[640,1408]{1,0:T(8,128)(2,1)} %get-tuple-element.199.refs_1_, bf16[640,1408]{1,0:T(8,128)(2,1)} %get-tuple-element.200.refs_0_), kind=kOutput, calls=%fused_computation.20 | convolution fusion | flops 7390494720 | bytes 17760256 | tf_op jit(solution)/shard_map/dot_general | solution.py:90
  821.4 15.2 %shard_map.249 = (bf16[2816,1024]{1,0:T(8,128)(2,1)}, bf16[2816,1024]{1,0:T(8,128)(2,1)}) custom-call(s32[1]{0:T(128)} %bitcast.32.core_ref, bf16[640,1408]{1,0:T(8,128)(2,1)} %get-tuple-element.200.refs_0_, bf16[640,1408]{1,0:T(8,128)(2,1)} %get-tuple-element.199.refs_1_, bf16[160,2048]{1,0:T(8,128)(2,1)S(1)} %copy-done.6, ...), custom_call_target="tpu_custom_call" | custom-call | flops 22145925120 | bytes 43253760 | tf_op jit(solution)/shard_map/pallas_call | solution.py:102
  846.8 9.8 add_convert_fusion
  861.1 14.2 %collective-permute-done.60 = bf16[160,2048]{1,0:T(8,128)(2,1)S(1)} collective-permute-done((bf16[160,2048]{1,0:T(8,128)(2,1)}, bf16[160,2048]{1,0:T(8,128)(2,1)S(1)}, u32[]{:S(2)}, u32[]{:S(2)}) %collective-permute-start.60) | collective-permute-done | bytes 655392 | tf_op jit(solution)/shard_map/ppermute | solution.py:24
  877.6 4.6 multiply_reduce_fusion.3
  888.7 23.3 %collective-permute-done.67 = f32[160]{0:T(256)S(1)} collective-permute-done((f32[160]{0:T(256)S(1)}, f32[160]{0:T(256)S(1)}, u32[]{:S(2)}, u32[]{:S(2)}) %collective-permute-start.67) | collective-permute-done | bytes 672 | tf_op jit(solution)/shard_map/ppermute | solution.py:24
  916.8 11.0 shard_map.250
  942.5 5.6 shard_map.251
  948.3 9.1 convolution_convert_fusion
  957.4 12.4 %shard_map.252 = (bf16[2048,1024]{1,0:T(8,128)(2,1)}, bf16[2048,1024]{1,0:T(8,128)(2,1)}) custom-call(s32[1]{0:T(128)} %bitcast.32.core_ref, bf16[640,1536]{1,0:T(8,128)(2,1)} %copy-done.73, bf16[640,512]{1,0:T(8,128)(2,1)S(1)} %copy-done.18, bf16[160,2048]{1,0:T(8,128)(2,1)S(1)} %copy-done.2, bf16[160,2048]{1,0:T(8,128)(2,1)S(1)} %copy-done.4, ...), custom_call_target="tpu_custom_call" | custom-call | flops 16106127360 | bytes 31457280 | tf_op jit(solution)/shard_map/pallas_call | solution.py:102
  969.9 7.4 collective-permute-done.81
  977.3 5.5 add_convert_fusion.2
  992.4 9.9 collective-permute-done.74
  1002.3 13.7 %collective-permute-done.75 = bf16[160,2048]{1,0:T(8,128)(2,1)} collective-permute-done((bf16[160,2048]{1,0:T(8,128)(2,1)S(1)}, bf16[160,2048]{1,0:T(8,128)(2,1)}, u32[]{:S(2)}, u32[]{:S(2)}) %collective-permute-start.75) | collective-permute-done | bytes 655392 | tf_op jit(solution)/shard_map/ppermute | solution.py:24
  1022.0 7.1 fusion.23
  1049.8 12.7 %collective-permute-done.83 = f32[4,512]{1,0:T(4,128)S(1)} collective-permute-done((f32[4,512]{1,0:T(4,128)S(1)}, f32[4,512]{1,0:T(4,128)S(1)}, u32[]{:S(2)}, u32[]{:S(2)}) %collective-permute-start.83) | collective-permute-done | bytes 8224 | tf_op jit(solution)/shard_map/ppermute | solution.py:24
  1062.6 15.7 %all-gather = f32[64,512]{1,0:T(8,128)S(1)} all-gather(f32[8,512]{1,0:T(8,128)S(1)} %concatenate.79), channel_id=2, replica_groups=mesh['chip'=4,'core'=2,'fsdp'=4] {'chip','core'}, dimensions={0}, use_global_device_ids=true | all-gather | bytes 147456 | tf_op jit(solution)/shard_map/all_gather | solution.py:482
  (544 shorter events, 268.9 us)
Async XLA Ops:
  7.2 85.8 %all-gather.7.cloned.1.call-start = ((), (), s32[]{:S(2)}) async-start(), calls=%async_computation.6 | async-start | bytes 7077888 | tf_op jit(solution)/shard_map/all_gather | solution.py:517
  10.4 146.6 %all-gather.9.cloned.1.call-start = ((), (), s32[]{:S(2)}) async-start(), calls=%async_computation.7 | async-start | bytes 8847360 | tf_op jit(solution)/shard_map/all_gather | solution.py:520
  12.5 255.3 %all-gather.11.cloned.1.call-start = ((), (), s32[]{:S(2)}) async-start(), calls=%async_computation.8 | async-start | bytes 12976128 | tf_op jit(solution)/shard_map/all_gather | solution.py:520
  18.5 379.7 %all-gather.13.cloned.1.call-start = ((), (), s32[]{:S(2)}) async-start(), calls=%async_computation.9 | async-start | bytes 15925248 | tf_op jit(solution)/shard_map/all_gather | solution.py:520
  25.5 480.9 %all-gather.15.cloned.1.call-start = ((), (), s32[]{:S(2)}) async-start(), calls=%async_computation.10 | async-start | bytes 12976128 | tf_op jit(solution)/shard_map/all_gather | solution.py:520
  27.4 637.4 %reduce-scatter.7.cloned.1.call-start = ((), (), s32[]{:S(2)}) async-start(), calls=%async_computation.11 | async-start | bytes 3604480 | tf_op jit(solution)/shard_map/reduce_scatter | solution.py:187
  28.9 18.6 %collective-permute-start = (bf16[160,2048]{1,0:T(8,128)(2,1)S(1)}, bf16[160,2048]{1,0:T(8,128)(2,1)S(1)}, u32[]{:S(2)}, u32[]{:S(2)}) collective-permute-start(bf16[160,2048]{1,0:T(8,128)(2,1)S(1)} %fusion.35.refs_0_.refs_2_.refs_6_), channel_id=1, source_target_pairs={{0,1},{1,0},{2,3},{3,2},{4,5},{5,4},{6,7},{7,6},{8,9},{9,8},{10,11... | collective-permute-start | bytes 1966088 | tf_op jit(solution)/shard_map/ppermute | solution.py:24
  31.9 30.2 %collective-permute-start.1 = (bf16[160,2048]{1,0:T(8,128)(2,1)S(1)}, bf16[160,2048]{1,0:T(8,128)(2,1)S(1)}, u32[]{:S(2)}, u32[]{:S(2)}) collective-permute-start(bf16[160,2048]{1,0:T(8,128)(2,1)S(1)} %fusion.35.refs_0_.refs_2_.refs_6_), channel_id=1, source_target_pairs={{0,2},{1,3},{2,0},{3,1},{4,6},{5,7},{6,4},{7,5},{8,10},{9,11},{10,... | collective-permute-start | bytes 1966088 | tf_op jit(solution)/shard_map/ppermute | solution.py:24
  33.5 29.6 %collective-permute-start.2 = (bf16[160,2048]{1,0:T(8,128)(2,1)S(1)}, bf16[160,2048]{1,0:T(8,128)(2,1)}, u32[]{:S(2)}, u32[]{:S(2)}) collective-permute-start(bf16[160,2048]{1,0:T(8,128)(2,1)S(1)} %fusion.35.refs_0_.refs_2_.refs_6_), channel_id=1, source_target_pairs={{0,3},{1,2},{2,1},{3,0},{4,7},{5,6},{6,5},{7,4},{8,11},{9,10},{10,... | collective-permute-start | bytes 1966088 | tf_op jit(solution)/shard_map/ppermute | solution.py:24
  63.0 17.7 %collective-permute-start.3 = (bf16[160,2048]{1,0:T(8,128)(2,1)S(1)}, bf16[160,2048]{1,0:T(8,128)(2,1)S(1)}, u32[]{:S(2)}, u32[]{:S(2)}) collective-permute-start(bf16[160,2048]{1,0:T(8,128)(2,1)S(1)} %copy-done), channel_id=1, source_target_pairs={{0,1},{1,0},{2,3},{3,2},{4,5},{5,4},{6,7},{7,6},{8,9},{9,8},{10,11... | collective-permute-start | bytes 1966088 | tf_op jit(solution)/shard_map/ppermute | solution.py:24
  63.5 29.5 %collective-permute-start.4 = (bf16[160,2048]{1,0:T(8,128)(2,1)S(1)}, bf16[160,2048]{1,0:T(8,128)(2,1)}, u32[]{:S(2)}, u32[]{:S(2)}) collective-permute-start(bf16[160,2048]{1,0:T(8,128)(2,1)S(1)} %copy-done), channel_id=1, source_target_pairs={{0,2},{1,3},{2,0},{3,1},{4,6},{5,7},{6,4},{7,5},{8,10},{9,11},{10,... | collective-permute-start | bytes 1966088 | tf_op jit(solution)/shard_map/ppermute | solution.py:24
  65.1 27.9 %collective-permute-start.5 = (bf16[160,2048]{1,0:T(8,128)(2,1)S(1)}, bf16[160,2048]{1,0:T(8,128)(2,1)}, u32[]{:S(2)}, u32[]{:S(2)}) collective-permute-start(bf16[160,2048]{1,0:T(8,128)(2,1)S(1)} %copy-done), channel_id=1, source_target_pairs={{0,3},{1,2},{2,1},{3,0},{4,7},{5,6},{6,5},{7,4},{8,11},{9,10},{10,... | collective-permute-start | bytes 1966088 | tf_op jit(solution)/shard_map/ppermute | solution.py:24
  125.0 41.7 %collective-permute-start.13 = (f32[4,160]{1,0:T(4,128)S(1)}, f32[4,160]{1,0:T(4,128)S(1)}, u32[]{:S(2)}, u32[]{:S(2)}) collective-permute-start(f32[4,160]{1,0:T(4,128)S(1)} %reshape.259), channel_id=1, source_target_pairs={{0,1},{1,0},{2,3},{3,2},{4,5},{5,4},{6,7},{7,6},{8,9},{9,8},{10,11... | collective-permute-start | bytes 7688 | tf_op jit(solution)/shard_map/ppermute | solution.py:24
  163.1 18.7 %collective-permute-start.12 = (bf16[160,2048]{1,0:T(8,128)(2,1)}, bf16[160,2048]{1,0:T(8,128)(2,1)S(1)}, u32[]{:S(2)}, u32[]{:S(2)}) collective-permute-start(bf16[160,2048]{1,0:T(8,128)(2,1)} %get-tuple-element.337), channel_id=1, source_target_pairs={{0,3},{1,2},{2,1},{3,0},{4,7},{5,6},{6,5},{7,4},{8,11},{9,10},{10,... | collective-permute-start | bytes 1966088 | tf_op jit(solution)/shard_map/ppermute | solution.py:24
  165.4 29.8 %collective-permute-start.11 = (bf16[160,2048]{1,0:T(8,128)(2,1)}, bf16[160,2048]{1,0:T(8,128)(2,1)}, u32[]{:S(2)}, u32[]{:S(2)}) collective-permute-start(bf16[160,2048]{1,0:T(8,128)(2,1)} %get-tuple-element.338), channel_id=1, source_target_pairs={{0,2},{1,3},{2,0},{3,1},{4,6},{5,7},{6,4},{7,5},{8,10},{9,11},{10,... | collective-permute-start | bytes 1966088 | tf_op jit(solution)/shard_map/ppermute | solution.py:24
  166.0 29.3 %collective-permute-start.10 = (bf16[160,2048]{1,0:T(8,128)(2,1)}, bf16[160,2048]{1,0:T(8,128)(2,1)}, u32[]{:S(2)}, u32[]{:S(2)}) collective-permute-start(bf16[160,2048]{1,0:T(8,128)(2,1)} %get-tuple-element.336), channel_id=1, source_target_pairs={{0,1},{1,0},{2,3},{3,2},{4,5},{5,4},{6,7},{7,6},{8,9},{9,8},{10,11... | collective-permute-start | bytes 1966088 | tf_op jit(solution)/shard_map/ppermute | solution.py:24
  197.7 17.7 %collective-permute-start.16 = (bf16[160,2048]{1,0:T(8,128)(2,1)S(1)}, bf16[160,2048]{1,0:T(8,128)(2,1)S(1)}, u32[]{:S(2)}, u32[]{:S(2)}) collective-permute-start(bf16[160,2048]{1,0:T(8,128)(2,1)S(1)} %multiply_convert_fusion.3.refs_0_.refs_2_.refs_6_), channel_id=1, source_target_pairs={{0,1},{1,0},{2,3},{3,2},{4,5},{5,4},{6,7},{7,6},{8,9},{9,8},{10,11... | collective-permute-start | bytes 1966088 | tf_op jit(solution)/shard_map/ppermute | solution.py:24
  199.2 30.4 %collective-permute-start.17 = (bf16[160,2048]{1,0:T(8,128)(2,1)S(1)}, bf16[160,2048]{1,0:T(8,128)(2,1)S(1)}, u32[]{:S(2)}, u32[]{:S(2)}) collective-permute-start(bf16[160,2048]{1,0:T(8,128)(2,1)S(1)} %multiply_convert_fusion.3.refs_0_.refs_2_.refs_6_), channel_id=1, source_target_pairs={{0,2},{1,3},{2,0},{3,1},{4,6},{5,7},{6,4},{7,5},{8,10},{9,11},{10,... | collective-permute-start | bytes 1966088 | tf_op jit(solution)/shard_map/ppermute | solution.py:24
  200.0 30.4 %collective-permute-start.18 = (bf16[160,2048]{1,0:T(8,128)(2,1)S(1)}, bf16[160,2048]{1,0:T(8,128)(2,1)}, u32[]{:S(2)}, u32[]{:S(2)}) collective-permute-start(bf16[160,2048]{1,0:T(8,128)(2,1)S(1)} %multiply_convert_fusion.3.refs_0_.refs_2_.refs_6_), channel_id=1, source_target_pairs={{0,3},{1,2},{2,1},{3,0},{4,7},{5,6},{6,5},{7,4},{8,11},{9,10},{10,... | collective-permute-start | bytes 1966088 | tf_op jit(solution)/shard_map/ppermute | solution.py:24
  290.8 18.6 %collective-permute-start.21 = (bf16[160,2048]{1,0:T(8,128)(2,1)S(1)}, bf16[160,2048]{1,0:T(8,128)(2,1)S(1)}, u32[]{:S(2)}, u32[]{:S(2)}) collective-permute-start(bf16[160,2048]{1,0:T(8,128)(2,1)S(1)} %get-tuple-element.334), channel_id=1, source_target_pairs={{0,3},{1,2},{2,1},{3,0},{4,7},{5,6},{6,5},{7,4},{8,11},{9,10},{10,... | collective-permute-start | bytes 1966088 | tf_op jit(solution)/shard_map/ppermute | solution.py:24
  293.3 29.4 %collective-permute-start.20 = (bf16[160,2048]{1,0:T(8,128)(2,1)S(1)}, bf16[160,2048]{1,0:T(8,128)(2,1)S(1)}, u32[]{:S(2)}, u32[]{:S(2)}) collective-permute-start(bf16[160,2048]{1,0:T(8,128)(2,1)S(1)} %get-tuple-element.335), channel_id=1, source_target_pairs={{0,2},{1,3},{2,0},{3,1},{4,6},{5,7},{6,4},{7,5},{8,10},{9,11},{10,... | collective-permute-start | bytes 1966088 | tf_op jit(solution)/shard_map/ppermute | solution.py:24
  293.8 28.9 %collective-permute-start.19 = (bf16[160,2048]{1,0:T(8,128)(2,1)S(1)}, bf16[160,2048]{1,0:T(8,128)(2,1)S(1)}, u32[]{:S(2)}, u32[]{:S(2)}) collective-permute-start(bf16[160,2048]{1,0:T(8,128)(2,1)S(1)} %get-tuple-element.333), channel_id=1, source_target_pairs={{0,1},{1,0},{2,3},{3,2},{4,5},{5,4},{6,7},{7,6},{8,9},{9,8},{10,11... | collective-permute-start | bytes 1966088 | tf_op jit(solution)/shard_map/ppermute | solution.py:24
  325.1 30.5 %collective-permute-start.23 = (bf16[160,2048]{1,0:T(8,128)(2,1)S(1)}, bf16[160,2048]{1,0:T(8,128)(2,1)S(1)}, u32[]{:S(2)}, u32[]{:S(2)}) collective-permute-start(bf16[160,2048]{1,0:T(8,128)(2,1)S(1)} %multiply_convert_fusion.2.refs_0_.refs_2_.refs_6_), channel_id=1, source_target_pairs={{0,2},{1,3},{2,0},{3,1},{4,6},{5,7},{6,4},{7,5},{8,10},{9,11},{10,... | collective-permute-start | bytes 1966088 | tf_op jit(solution)/shard_map/ppermute | solution.py:24
  325.9 30.6 %collective-permute-start.24 = (bf16[160,2048]{1,0:T(8,128)(2,1)S(1)}, bf16[160,2048]{1,0:T(8,128)(2,1)}, u32[]{:S(2)}, u32[]{:S(2)}) collective-permute-start(bf16[160,2048]{1,0:T(8,128)(2,1)S(1)} %multiply_convert_fusion.2.refs_0_.refs_2_.refs_6_), channel_id=1, source_target_pairs={{0,3},{1,2},{2,1},{3,0},{4,7},{5,6},{6,5},{7,4},{8,11},{9,10},{10,... | collective-permute-start | bytes 1966088 | tf_op jit(solution)/shard_map/ppermute | solution.py:24
  435.3 18.8 %collective-permute-start.31 = (bf16[160,2048]{1,0:T(8,128)(2,1)}, bf16[160,2048]{1,0:T(8,128)(2,1)S(1)}, u32[]{:S(2)}, u32[]{:S(2)}) collective-permute-start(bf16[160,2048]{1,0:T(8,128)(2,1)} %get-tuple-element.331), channel_id=1, source_target_pairs={{0,3},{1,2},{2,1},{3,0},{4,7},{5,6},{6,5},{7,4},{8,11},{9,10},{10,... | collective-permute-start | bytes 1966088 | tf_op jit(solution)/shard_map/ppermute | solution.py:24
  436.5 29.0 %collective-permute-start.30 = (bf16[160,2048]{1,0:T(8,128)(2,1)}, bf16[160,2048]{1,0:T(8,128)(2,1)}, u32[]{:S(2)}, u32[]{:S(2)}) collective-permute-start(bf16[160,2048]{1,0:T(8,128)(2,1)} %get-tuple-element.332), channel_id=1, source_target_pairs={{0,2},{1,3},{2,0},{3,1},{4,6},{5,7},{6,4},{7,5},{8,10},{9,11},{10,... | collective-permute-start | bytes 1966088 | tf_op jit(solution)/shard_map/ppermute | solution.py:24
  437.1 28.5 %collective-permute-start.29 = (bf16[160,2048]{1,0:T(8,128)(2,1)}, bf16[160,2048]{1,0:T(8,128)(2,1)}, u32[]{:S(2)}, u32[]{:S(2)}) collective-permute-start(bf16[160,2048]{1,0:T(8,128)(2,1)} %get-tuple-element.330), channel_id=1, source_target_pairs={{0,1},{1,0},{2,3},{3,2},{4,5},{5,4},{6,7},{7,6},{8,9},{9,8},{10,11... | collective-permute-start | bytes 1966088 | tf_op jit(solution)/shard_map/ppermute | solution.py:24
  468.6 30.5 %collective-permute-start.36 = (bf16[160,2048]{1,0:T(8,128)(2,1)S(1)}, bf16[160,2048]{1,0:T(8,128)(2,1)S(1)}, u32[]{:S(2)}, u32[]{:S(2)}) collective-permute-start(bf16[160,2048]{1,0:T(8,128)(2,1)S(1)} %multiply_convert_fusion.refs_0_.refs_2_.refs_6_), channel_id=1, source_target_pairs={{0,2},{1,3},{2,0},{3,1},{4,6},{5,7},{6,4},{7,5},{8,10},{9,11},{10,... | collective-permute-start | bytes 1966088 | tf_op jit(solution)/shard_map/ppermute | solution.py:24
  470.0 29.9 %collective-permute-start.37 = (bf16[160,2048]{1,0:T(8,128)(2,1)S(1)}, bf16[160,2048]{1,0:T(8,128)(2,1)}, u32[]{:S(2)}, u32[]{:S(2)}) collective-permute-start(bf16[160,2048]{1,0:T(8,128)(2,1)S(1)} %multiply_convert_fusion.refs_0_.refs_2_.refs_6_), channel_id=1, source_target_pairs={{0,3},{1,2},{2,1},{3,0},{4,7},{5,6},{6,5},{7,4},{8,11},{9,10},{10,... | collective-permute-start | bytes 1966088 | tf_op jit(solution)/shard_map/ppermute | solution.py:24
  532.9 38.5 %collective-permute-start.44 = (bf16[1408,1024]{1,0:T(8,128)(2,1)}, bf16[1408,1024]{1,0:T(8,128)(2,1)S(1)}, u32[]{:S(2)}, u32[]{:S(2)}) collective-permute-start(bf16[1408,1024]{1,0:T(8,128)(2,1)} %get-tuple-element.152), channel_id=1, source_target_pairs={{0,4},{4,0},{1,5},{5,1},{2,6},{6,2},{3,7},{7,3},{8,12},{12,8},{9,1... | collective-permute-start | bytes 8650760 | tf_op jit(solution)/shard_map/ppermute | solution.py:28
  574.5 214.3 %reduce-scatter.9.cloned.1.call-start = ((), (), s32[]{:S(2)}) async-start(), calls=%async_computation.12 | async-start | bytes 7208960 | tf_op jit(solution)/shard_map/reduce_scatter | solution.py:187
  590.7 284.6 %reduce-scatter.11.cloned.1.call-start = ((), (), s32[]{:S(2)}) async-start(), calls=%async_computation.13 | async-start | bytes 5242880 | tf_op jit(solution)/shard_map/reduce_scatter | solution.py:187
  594.0 30.7 %collective-permute-start.39 = (bf16[160,2048]{1,0:T(8,128)(2,1)S(1)}, bf16[160,2048]{1,0:T(8,128)(2,1)S(1)}, u32[]{:S(2)}, u32[]{:S(2)}) collective-permute-start(bf16[160,2048]{1,0:T(8,128)(2,1)S(1)} %get-tuple-element.328), channel_id=1, source_target_pairs={{0,2},{1,3},{2,0},{3,1},{4,6},{5,7},{6,4},{7,5},{8,10},{9,11},{10,... | collective-permute-start | bytes 1966088 | tf_op jit(solution)/shard_map/ppermute | solution.py:24
  595.5 29.2 %collective-permute-start.40 = (bf16[160,2048]{1,0:T(8,128)(2,1)S(1)}, bf16[160,2048]{1,0:T(8,128)(2,1)S(1)}, u32[]{:S(2)}, u32[]{:S(2)}) collective-permute-start(bf16[160,2048]{1,0:T(8,128)(2,1)S(1)} %get-tuple-element.327), channel_id=1, source_target_pairs={{0,3},{1,2},{2,1},{3,0},{4,7},{5,6},{6,5},{7,4},{8,11},{9,10},{10,... | collective-permute-start | bytes 1966088 | tf_op jit(solution)/shard_map/ppermute | solution.py:24
  630.0 34.8 %collective-permute-start.41 = (bf16[160,2048]{1,0:T(8,128)(2,1)S(1)}, bf16[160,2048]{1,0:T(8,128)(2,1)}, u32[]{:S(2)}, u32[]{:S(2)}) collective-permute-start(bf16[160,2048]{1,0:T(8,128)(2,1)S(1)} %get-tuple-element.303.refs_0_.refs_10_.refs_14_), channel_id=1, source_target_pairs={{0,1},{1,0},{2,3},{3,2},{4,5},{5,4},{6,7},{7,6},{8,9},{9,8},{10,11... | collective-permute-start | bytes 1966088 | tf_op jit(solution)/shard_map/ppermute | solution.py:24
  631.2 33.6 %collective-permute-start.42 = (bf16[160,2048]{1,0:T(8,128)(2,1)S(1)}, bf16[160,2048]{1,0:T(8,128)(2,1)}, u32[]{:S(2)}, u32[]{:S(2)}) collective-permute-start(bf16[160,2048]{1,0:T(8,128)(2,1)S(1)} %get-tuple-element.303.refs_0_.refs_10_.refs_14_), channel_id=1, source_target_pairs={{0,2},{1,3},{2,0},{3,1},{4,6},{5,7},{6,4},{7,5},{8,10},{9,11},{10,... | collective-permute-start | bytes 1966088 | tf_op jit(solution)/shard_map/ppermute | solution.py:24
  632.0 32.7 %collective-permute-start.43 = (bf16[160,2048]{1,0:T(8,128)(2,1)S(1)}, bf16[160,2048]{1,0:T(8,128)(2,1)}, u32[]{:S(2)}, u32[]{:S(2)}) collective-permute-start(bf16[160,2048]{1,0:T(8,128)(2,1)S(1)} %get-tuple-element.303.refs_0_.refs_10_.refs_14_), channel_id=1, source_target_pairs={{0,3},{1,2},{2,1},{3,0},{4,7},{5,6},{6,5},{7,4},{8,11},{9,10},{10,... | collective-permute-start | bytes 1966088 | tf_op jit(solution)/shard_map/ppermute | solution.py:24
  634.2 25.8 %collective-permute-start.45 = (f32[160]{0:T(256)S(1)}, f32[160]{0:T(256)S(1)}, u32[]{:S(2)}, u32[]{:S(2)}) collective-permute-start(f32[160]{0:T(256)S(1)} %get-tuple-element.302), channel_id=1, source_target_pairs={{0,1},{1,0},{2,3},{3,2},{4,5},{5,4},{6,7},{7,6},{8,9},{9,8},{10,11... | collective-permute-start | bytes 1928 | tf_op jit(solution)/shard_map/ppermute | solution.py:24
  637.5 25.1 %collective-permute-start.46 = (f32[160]{0:T(256)S(1)}, f32[160]{0:T(256)S(1)}, u32[]{:S(2)}, u32[]{:S(2)}) collective-permute-start(f32[160]{0:T(256)S(1)} %get-tuple-element.302), channel_id=1, source_target_pairs={{0,2},{1,3},{2,0},{3,1},{4,6},{5,7},{6,4},{7,5},{8,10},{9,11},{10,... | collective-permute-start | bytes 1928 | tf_op jit(solution)/shard_map/ppermute | solution.py:24
  719.2 17.7 %collective-permute-start.52 = (bf16[160,2048]{1,0:T(8,128)(2,1)}, bf16[160,2048]{1,0:T(8,128)(2,1)S(1)}, u32[]{:S(2)}, u32[]{:S(2)}) collective-permute-start(bf16[160,2048]{1,0:T(8,128)(2,1)} %get-tuple-element.326), channel_id=1, source_target_pairs={{0,1},{1,0},{2,3},{3,2},{4,5},{5,4},{6,7},{7,6},{8,9},{9,8},{10,11... | collective-permute-start | bytes 1966088 | tf_op jit(solution)/shard_map/ppermute | solution.py:24
  720.6 31.2 %collective-permute-start.53 = (bf16[160,2048]{1,0:T(8,128)(2,1)}, bf16[160,2048]{1,0:T(8,128)(2,1)}, u32[]{:S(2)}, u32[]{:S(2)}) collective-permute-start(bf16[160,2048]{1,0:T(8,128)(2,1)} %get-tuple-element.325), channel_id=1, source_target_pairs={{0,2},{1,3},{2,0},{3,1},{4,6},{5,7},{6,4},{7,5},{8,10},{9,11},{10,... | collective-permute-start | bytes 1966088 | tf_op jit(solution)/shard_map/ppermute | solution.py:24
  721.3 30.6 %collective-permute-start.54 = (bf16[160,2048]{1,0:T(8,128)(2,1)}, bf16[160,2048]{1,0:T(8,128)(2,1)}, u32[]{:S(2)}, u32[]{:S(2)}) collective-permute-start(bf16[160,2048]{1,0:T(8,128)(2,1)} %get-tuple-element.324), channel_id=1, source_target_pairs={{0,3},{1,2},{2,1},{3,0},{4,7},{5,6},{6,5},{7,4},{8,11},{9,10},{10,... | collective-permute-start | bytes 1966088 | tf_op jit(solution)/shard_map/ppermute | solution.py:24
  730.9 185.8 %reduce-scatter.13.cloned.1.call-start = ((), (), s32[]{:S(2)}) async-start(), calls=%async_computation.14 | async-start | bytes 3604480 | tf_op jit(solution)/shard_map/reduce_scatter | solution.py:187
  758.9 29.9 %collective-permute-start.56 = (bf16[160,2048]{1,0:T(8,128)(2,1)S(1)}, bf16[160,2048]{1,0:T(8,128)(2,1)S(1)}, u32[]{:S(2)}, u32[]{:S(2)}) collective-permute-start(bf16[160,2048]{1,0:T(8,128)(2,1)S(1)} %get-tuple-element.192.refs_1_.refs_5_.refs_0_), channel_id=1, source_target_pairs={{0,2},{1,3},{2,0},{3,1},{4,6},{5,7},{6,4},{7,5},{8,10},{9,11},{10,... | collective-permute-start | bytes 1966088 | tf_op jit(solution)/shard_map/ppermute | solution.py:24
  760.3 28.5 %collective-permute-start.57 = (bf16[160,2048]{1,0:T(8,128)(2,1)S(1)}, bf16[160,2048]{1,0:T(8,128)(2,1)S(1)}, u32[]{:S(2)}, u32[]{:S(2)}) collective-permute-start(bf16[160,2048]{1,0:T(8,128)(2,1)S(1)} %get-tuple-element.192.refs_1_.refs_5_.refs_0_), channel_id=1, source_target_pairs={{0,3},{1,2},{2,1},{3,0},{4,7},{5,6},{6,5},{7,4},{8,11},{9,10},{10,... | collective-permute-start | bytes 1966088 | tf_op jit(solution)/shard_map/ppermute | solution.py:24
  798.5 38.4 %collective-permute-start.66 = (bf16[1408,1024]{1,0:T(8,128)(2,1)}, bf16[1408,1024]{1,0:T(8,128)(2,1)S(1)}, u32[]{:S(2)}, u32[]{:S(2)}) collective-permute-start(bf16[1408,1024]{1,0:T(8,128)(2,1)} %get-tuple-element.191), channel_id=1, source_target_pairs={{0,4},{4,0},{1,5},{5,1},{2,6},{6,2},{3,7},{7,3},{8,12},{12,8},{9,1... | collective-permute-start | bytes 8650760 | tf_op jit(solution)/shard_map/ppermute | solution.py:28
  840.0 176.0 %reduce-scatter.15.cloned.1.call-start = ((), (), s32[]{:S(2)}) async-start(), calls=%async_computation.15 | async-start | bytes 7208960 | tf_op jit(solution)/shard_map/reduce_scatter | solution.py:187
  843.3 17.8 %collective-permute-start.59 = (bf16[160,2048]{1,0:T(8,128)(2,1)}, bf16[160,2048]{1,0:T(8,128)(2,1)S(1)}, u32[]{:S(2)}, u32[]{:S(2)}) collective-permute-start(bf16[160,2048]{1,0:T(8,128)(2,1)} %get-tuple-element.323), channel_id=1, source_target_pairs={{0,1},{1,0},{2,3},{3,2},{4,5},{5,4},{6,7},{7,6},{8,9},{9,8},{10,11... | collective-permute-start | bytes 1966088 | tf_op jit(solution)/shard_map/ppermute | solution.py:24
  844.6 30.7 %collective-permute-start.60 = (bf16[160,2048]{1,0:T(8,128)(2,1)}, bf16[160,2048]{1,0:T(8,128)(2,1)S(1)}, u32[]{:S(2)}, u32[]{:S(2)}) collective-permute-start(bf16[160,2048]{1,0:T(8,128)(2,1)} %get-tuple-element.322), channel_id=1, source_target_pairs={{0,2},{1,3},{2,0},{3,1},{4,6},{5,7},{6,4},{7,5},{8,10},{9,11},{10,... | collective-permute-start | bytes 1966088 | tf_op jit(solution)/shard_map/ppermute | solution.py:24
  845.3 29.9 %collective-permute-start.61 = (bf16[160,2048]{1,0:T(8,128)(2,1)}, bf16[160,2048]{1,0:T(8,128)(2,1)}, u32[]{:S(2)}, u32[]{:S(2)}) collective-permute-start(bf16[160,2048]{1,0:T(8,128)(2,1)} %get-tuple-element.321), channel_id=1, source_target_pairs={{0,3},{1,2},{2,1},{3,0},{4,7},{5,6},{6,5},{7,4},{8,11},{9,10},{10,... | collective-permute-start | bytes 1966088 | tf_op jit(solution)/shard_map/ppermute | solution.py:24
  856.6 235.4 %reduce-scatter.17.cloned.1.call-start = ((), (), s32[]{:S(2)}) async-start(), calls=%async_computation.16 | async-start | bytes 5242880 | tf_op jit(solution)/shard_map/reduce_scatter | solution.py:187
  882.2 34.5 %collective-permute-start.63 = (bf16[160,2048]{1,0:T(8,128)(2,1)S(1)}, bf16[160,2048]{1,0:T(8,128)(2,1)}, u32[]{:S(2)}, u32[]{:S(2)}) collective-permute-start(bf16[160,2048]{1,0:T(8,128)(2,1)S(1)} %get-tuple-element.296.refs_0_.refs_10_.refs_14_), channel_id=1, source_target_pairs={{0,1},{1,0},{2,3},{3,2},{4,5},{5,4},{6,7},{7,6},{8,9},{9,8},{10,11... | collective-permute-start | bytes 1966088 | tf_op jit(solution)/shard_map/ppermute | solution.py:24
  883.0 33.7 %collective-permute-start.64 = (bf16[160,2048]{1,0:T(8,128)(2,1)S(1)}, bf16[160,2048]{1,0:T(8,128)(2,1)}, u32[]{:S(2)}, u32[]{:S(2)}) collective-permute-start(bf16[160,2048]{1,0:T(8,128)(2,1)S(1)} %get-tuple-element.296.refs_0_.refs_10_.refs_14_), channel_id=1, source_target_pairs={{0,2},{1,3},{2,0},{3,1},{4,6},{5,7},{6,4},{7,5},{8,10},{9,11},{10,... | collective-permute-start | bytes 1966088 | tf_op jit(solution)/shard_map/ppermute | solution.py:24
  884.3 32.4 %collective-permute-start.65 = (bf16[160,2048]{1,0:T(8,128)(2,1)S(1)}, bf16[160,2048]{1,0:T(8,128)(2,1)}, u32[]{:S(2)}, u32[]{:S(2)}) collective-permute-start(bf16[160,2048]{1,0:T(8,128)(2,1)S(1)} %get-tuple-element.296.refs_0_.refs_10_.refs_14_), channel_id=1, source_target_pairs={{0,3},{1,2},{2,1},{3,0},{4,7},{5,6},{6,5},{7,4},{8,11},{9,10},{10,... | collective-permute-start | bytes 1966088 | tf_op jit(solution)/shard_map/ppermute | solution.py:24
  885.8 26.2 %collective-permute-start.67 = (f32[160]{0:T(256)S(1)}, f32[160]{0:T(256)S(1)}, u32[]{:S(2)}, u32[]{:S(2)}) collective-permute-start(f32[160]{0:T(256)S(1)} %get-tuple-element.295), channel_id=1, source_target_pairs={{0,1},{1,0},{2,3},{3,2},{4,5},{5,4},{6,7},{7,6},{8,9},{9,8},{10,11... | collective-permute-start | bytes 1928 | tf_op jit(solution)/shard_map/ppermute | solution.py:24
  887.3 26.1 %collective-permute-start.68 = (f32[160]{0:T(256)S(1)}, f32[160]{0:T(256)S(1)}, u32[]{:S(2)}, u32[]{:S(2)}) collective-permute-start(f32[160]{0:T(256)S(1)} %get-tuple-element.295), channel_id=1, source_target_pairs={{0,2},{1,3},{2,0},{3,1},{4,6},{5,7},{6,4},{7,5},{8,10},{9,11},{10,... | collective-permute-start | bytes 1928 | tf_op jit(solution)/shard_map/ppermute | solution.py:24
  984.6 17.7 %collective-permute-start.74 = (bf16[160,2048]{1,0:T(8,128)(2,1)S(1)}, bf16[160,2048]{1,0:T(8,128)(2,1)}, u32[]{:S(2)}, u32[]{:S(2)}) collective-permute-start(bf16[160,2048]{1,0:T(8,128)(2,1)S(1)} %get-tuple-element.320), channel_id=1, source_target_pairs={{0,1},{1,0},{2,3},{3,2},{4,5},{5,4},{6,7},{7,6},{8,9},{9,8},{10,11... | collective-permute-start | bytes 1966088 | tf_op jit(solution)/shard_map/ppermute | solution.py:24
  985.4 30.6 %collective-permute-start.75 = (bf16[160,2048]{1,0:T(8,128)(2,1)S(1)}, bf16[160,2048]{1,0:T(8,128)(2,1)}, u32[]{:S(2)}, u32[]{:S(2)}) collective-permute-start(bf16[160,2048]{1,0:T(8,128)(2,1)S(1)} %get-tuple-element.319), channel_id=1, source_target_pairs={{0,2},{1,3},{2,0},{3,1},{4,6},{5,7},{6,4},{7,5},{8,10},{9,11},{10,... | collective-permute-start | bytes 1966088 | tf_op jit(solution)/shard_map/ppermute | solution.py:24
  986.9 29.2 %collective-permute-start.76 = (bf16[160,2048]{1,0:T(8,128)(2,1)S(1)}, bf16[160,2048]{1,0:T(8,128)(2,1)}, u32[]{:S(2)}, u32[]{:S(2)}) collective-permute-start(bf16[160,2048]{1,0:T(8,128)(2,1)S(1)} %get-tuple-element.318), channel_id=1, source_target_pairs={{0,3},{1,2},{2,1},{3,0},{4,7},{5,6},{6,5},{7,4},{8,11},{9,10},{10,... | collective-permute-start | bytes 1966088 | tf_op jit(solution)/shard_map/ppermute | solution.py:24
  1031.2 58.1 %collective-permute-start.80 = (bf16[160,2048]{1,0:T(8,128)(2,1)}, bf16[160,2048]{1,0:T(8,128)(2,1)S(1)}, u32[]{:S(2)}, u32[]{:S(2)}) collective-permute-start(bf16[160,2048]{1,0:T(8,128)(2,1)} %get-tuple-element.316), channel_id=1, source_target_pairs={{0,3},{1,2},{2,1},{3,0},{4,7},{5,6},{6,5},{7,4},{8,11},{9,10},{10,... | collective-permute-start | bytes 1966088 | tf_op jit(solution)/shard_map/ppermute | solution.py:24
  1032.9 56.5 %collective-permute-start.79 = (bf16[160,2048]{1,0:T(8,128)(2,1)}, bf16[160,2048]{1,0:T(8,128)(2,1)}, u32[]{:S(2)}, u32[]{:S(2)}) collective-permute-start(bf16[160,2048]{1,0:T(8,128)(2,1)} %get-tuple-element.317), channel_id=1, source_target_pairs={{0,2},{1,3},{2,0},{3,1},{4,6},{5,7},{6,4},{7,5},{8,10},{9,11},{10,... | collective-permute-start | bytes 1966088 | tf_op jit(solution)/shard_map/ppermute | solution.py:24
  1035.7 26.8 %collective-permute-start.83 = (f32[4,512]{1,0:T(4,128)S(1)}, f32[4,512]{1,0:T(4,128)S(1)}, u32[]{:S(2)}, u32[]{:S(2)}) collective-permute-start(f32[4,512]{1,0:T(4,128)S(1)} %get-tuple-element.365), channel_id=1, source_target_pairs={{0,2},{1,3},{2,0},{3,1},{4,6},{5,7},{6,4},{7,5},{8,10},{9,11},{10,... | collective-permute-start | bytes 24584 | tf_op jit(solution)/shard_map/ppermute | solution.py:24
  1036.3 26.2 %collective-permute-start.82 = (f32[4,512]{1,0:T(4,128)S(1)}, f32[4,512]{1,0:T(4,128)S(1)}, u32[]{:S(2)}, u32[]{:S(2)}) collective-permute-start(f32[4,512]{1,0:T(4,128)S(1)} %get-tuple-element.363), channel_id=1, source_target_pairs={{0,1},{1,0},{2,3},{3,2},{4,5},{5,4},{6,7},{7,6},{8,9},{9,8},{10,11... | collective-permute-start | bytes 24584 | tf_op jit(solution)/shard_map/ppermute | solution.py:24
  1048.5 40.9 %collective-permute-start.78 = (bf16[160,2048]{1,0:T(8,128)(2,1)}, bf16[160,2048]{1,0:T(8,128)(2,1)}, u32[]{:S(2)}, u32[]{:S(2)}) collective-permute-start(bf16[160,2048]{1,0:T(8,128)(2,1)} %get-tuple-element.315), channel_id=1, source_target_pairs={{0,1},{1,0},{2,3},{3,2},{4,5},{5,4},{6,7},{7,6},{8,9},{9,8},{10,11... | collective-permute-start | bytes 1966088 | tf_op jit(solution)/shard_map/ppermute | solution.py:24
  (132 other events, 2133.5 us)
Sparse Core Ops, SparseCore 0:
  10.5 67.4 all-gather.6
  80.1 76.8 all-gather.8
  159.1 108.6 all-gather.10
  269.8 128.3 all-gather.12
  399.7 106.7 all-gather.14
  574.6 54.6 reduce-scatter.6
  631.5 102.3 reduce-scatter.8
  736.2 77.2 reduce-scatter.10
  840.2 53.4 reduce-scatter.12
  895.9 102.3 reduce-scatter.14
  1000.7 78.3 reduce-scatter.16

commit v3 on v2

--- a/solution.py
+++ b/solution.py
@@ -13,6 +13,12 @@
 STEP = 32
 LANES = 256
 VMEM = 52 * 1024 * 1024
+OUTER = 4
+SCALE = 5.5
+DUE = {
+    ("down", 1): (1, "sum"), ("ffn", 1): (0, "gather"), ("low", 1): (0, "part"),
+    ("down", 0): (0, "middle"), ("ffn", 0): (0, "last"),
+}
 f32 = jnp.float32
 bf16 = jnp.bfloat16
 SEQ = ("chip", "core")
@@ -45,16 +51,14 @@
     return [own] + all_after(arrived, *meanwhile)
 
 
-def scatter_rows(pieces, between=None, *meanwhile):
+def scatter_rows(pieces, *meanwhile):
     arrived = [exchange(pieces[step], step) for step in range(1, len(pieces))]
-    made = None
-    if between is not None:
-        made, result = between()
-        arrived = all_after(arrived, *made, *meanwhile)
+    if meanwhile:
+        arrived = all_after(arrived, *meanwhile)
     total = pieces[0].astype(f32)
     for piece in arrived:
         total = total + piece.astype(f32)
-    return total if made is None else (total, result)
+    return total
 
 
 def total_rows(part):
@@ -110,7 +114,7 @@
         ),
         out_shape=out_shape,
         compiler_params=pltpu.CompilerParams(vmem_limit_bytes=VMEM),
-        cost_estimate=pl.CostEstimate(flops=cost, bytes_accessed=cost // 512, transcendentals=0),
+        cost_estimate=pl.CostEstimate(flops=int(SCALE * cost), bytes_accessed=cost // 512, transcendentals=0),
     )(*prefetch, *operands)
 
 
@@ -121,6 +125,10 @@
     def _():
         for k, piece in enumerate(pieces):
             rows_ref[k * rows : (k + 1) * rows, :] = piece[...]
+
+
+def twins(values):
+    return [swap(v, "core") for v in values]
 
 
 def outer(terms):
@@ -131,60 +139,54 @@
         which.append(found[0] if found else len(groups))
         if not found:
             groups.append(pieces)
-    rows, width = lefts[0].shape[0], groups[0][0].shape[1] // seq_length()
-    heights = [left.shape[1] for left in lefts]
+    rows, width = sum(p.shape[0] for p in groups[0]), groups[0][0].shape[1] // seq_length()
+    heights = [left[0].shape[1] for left in lefts]
+    flat = [piece for left in lefts for piece in left]
     total, count, chips = sum(heights), len(groups[0]), lax.axis_size("chip")
 
     def kernel(core_ref, *refs):
-        left_refs, refs = refs[: len(lefts)], refs[len(lefts) :]
-        piece_refs, (own, other, turned) = refs[: 2 * count * len(groups)], refs[2 * count * len(groups) :]
+        left_refs, refs = refs[: len(flat)], refs[len(flat) :]
+        piece_refs, (out, turned) = refs[: count * len(groups)], refs[count * len(groups) :]
 
         @pl.when(pl.program_id(0) == 0)
         def _():
-            top = 0
-            for left, height in zip(left_refs, heights, strict=True):
-                turned[top : top + height, :] = left[...].T
-                top += height
-
-        rights = []
-        for g in range(len(groups)):
-            halves = [
-                jnp.concatenate([ref[...] for ref in piece_refs[k * count : (k + 1) * count]], axis=0)
-                for k in (2 * g, 2 * g + 1)
-            ]
-            rights.append(jnp.concatenate(halves, axis=1))
+            top, at = 0, 0
+            for left, height in zip(lefts, heights, strict=True):
+                start = 0
+                for k, piece in enumerate(left):
+                    turned[top : top + height, start : start + piece.shape[0]] = left_refs[at + k][...].T
+                    start += piece.shape[0]
+                top, at = top + height, at + len(left)
+
+        rights = [
+            jnp.concatenate([ref[...] for ref in piece_refs[g * count : (g + 1) * count]], axis=0)
+            for g in range(len(groups))
+        ]
         top = 0
         for height, group in zip(heights, which, strict=True):
-            both = dot(turned[top : top + height, :], rights[group]).astype(bf16)
-            own[top : top + height, :] = both[:, :width]
-            other[top : top + height, :] = both[:, width:]
+            out[top : top + height, :] = dot(turned[top : top + height, :], rights[group]).astype(bf16)
             top += height
 
-    def columns(pieces, flip):
-        return [
-            pl.BlockSpec((p.shape[0], width), lambda j, core: (0, 2 * j + (1 - core[0] if flip else core[0])))
-            for p in pieces
-        ]
-
-    out = jax.ShapeDtypeStruct((total, width * chips), bf16)
     return call(
         kernel,
         (chips,),
-        [whole(left) for left in lefts]
-        + [spec for group in groups for flip in (False, True) for spec in columns(group, flip)],
-        [pl.BlockSpec((total, width), lambda j, core: (0, j))] * 2,
-        [out, out],
+        [whole(left) for left in flat]
+        + [
+            pl.BlockSpec((p.shape[0], width), lambda j, core: (0, 2 * j + core[0]))
+            for group in groups
+            for p in group
+        ],
+        pl.BlockSpec((total, width), lambda j, core: (0, j)),
+        jax.ShapeDtypeStruct((total, width * chips), bf16),
         [pltpu.VMEM((total, rows), bf16)],
-        [*lefts, *(piece for group in groups for _ in range(2) for piece in group)],
-        6 * rows * total * width * 2 * chips,
+        [*flat, *(piece for group in groups for piece in group)],
+        OUTER * rows * total * width * chips,
         prefetch=(jnp.reshape(lax.axis_index("core"), (1,)).astype(jnp.int32),),
     )
 
 
-def scatter_columns(halves):
-    own, other = halves
-    half = (own.astype(f32) + swap(other, "core").astype(f32)).astype(bf16)
-    return lax.psum_scatter(half, "chip", scatter_dimension=1, tiled=True)
+def scatter_columns(part):
+    return lax.psum_scatter(part, "chip", scatter_dimension=1, tiled=True)
 
 
 def cut(values, count):
@@ -519,27 +521,31 @@
     def tall(*shards):
         return lax.all_gather(jnp.concatenate(shards, axis=0), SEQ, axis=1, tiled=True)
 
-    mix_rows = [0] + [3 * channels] * last_layer
-    mixes = [side(w_input[0], w_forget[0], w_gate[0])]
-    lows, boths = [tall(w_out[0], w_down[0])], []
+    first_mix = side(w_input[0], w_forget[0], w_gate[0])
+    joined = tall(w_out[0], w_down[0])
+    mixes, outs, boths, downs = [first_mix], [(joined, 0)], [], [(joined, channels)]
     for layer in range(LAYERS):
         if layer > 0:
-            turned = (w_input[layer].T, w_forget[layer].T, w_gate[layer].T)
-            lows.append(tall(*turned, w_out[layer], w_down[layer]))
-            mixes.append(lows[layer])
+            joined = tall(w_input[layer].T, w_forget[layer].T, w_gate[layer].T, w_out[layer])
+            mixes.append(joined)
+            outs.append((joined, 3 * channels))
         boths.append(tall(w_up[layer].T, w_glu[layer].T))
+        if layer > 0:
+            downs.append((tall(w_down[layer]), 0))
+
+    def rows_of(matrix_at, rows):
+        matrix, at = matrix_at
+        return matrix[at : at + rows]
 
     stream = hidden_in.astype(f32)
     saved = []
     for layer in range(LAYERS):
-        mix, low, at_out = mixes[layer], lows[layer], mix_rows[layer]
-        at_down, first_layer = at_out + channels, layer == 0
+        mix, first_layer = mixes[layer], layer == 0
         bound, gain = bounds[layer][None, :], gains[layer][None, :]
         unit, factor = rms_parts(stream)
         normed = gather_rows((unit * norm_mix[layer]).astype(bf16))
         if layer == 0:
             grad_y = gather_rows(after(cotangent, *normed))
-            normed = all_after(normed, *grad_y)
         proj_input, proj_forget, proj_gate, local_state, local_decay = over_channels(
             functools.partial(scan_kernel, size, dot if first_layer else trans_dot),
             place_array,
@@ -551,6 +557,8 @@
             channels,
             6 * block_rows * model_width * channels,
         )
+        if layer == 0:
+            local_state, local_decay = all_after((local_state, local_decay), *grad_y)
         last_row = lax.bitwise_xor(size - 1, place) * row_count + row_count - 1
         entering = entering_of(
             lax.dynamic_slice_in_dim(local_decay, last_row, 1, 0),
@@ -561,7 +569,7 @@
         squares = total_rows(jnp.sum(state * state, axis=1))
         inverse = lax.rsqrt(squares / model_width + epsilon)[:, None]
         loose = (state * gain * jax.nn.silu(proj_gate)).astype(bf16)
-        parts = cut(dot(loose, low[at_out:at_down]).astype(bf16), size)
+        parts = cut(dot(loose, rows_of(outs[layer], channels)).astype(bf16), size)
         branch = scatter_rows(parts) * inverse[:row_count]
         middle = stream + branch
         unit_two, _ = rms_parts(middle)
@@ -569,9 +577,10 @@
         normed_two = gather_rows(normed_two)
         upward, gating, hidden = up_and_gate(normed_two, boths[layer], hidden_units)
         if layer < last_layer:
-            stream = middle + scatter_rows(cut(dot(hidden, low[at_down:]).astype(bf16), size))
+            stream = middle + scatter_rows(cut(dot(hidden, rows_of(downs[layer], hidden_units)).astype(bf16), size))
+        twin_rows = (twins(normed), twins(normed_two), twins([hidden]))
         saved.append(
-            (factor, normed, proj_input, proj_forget, proj_gate, entering,
+            (factor, twin_rows, normed, proj_input, proj_forget, proj_gate, entering,
              state, inverse, branch, middle, normed_two, upward, gating, hidden, unit)
         )
 
@@ -580,38 +589,39 @@
     smalls = [None] * LAYERS
     scattered = {}
 
-    def arrived(*names):
+    def due(layer, place):
+        names = [name for name, when in DUE.items() if when == (layer, place)]
         return tuple(scattered[name] for name in names if name in scattered)
 
+    final_middle, final_hidden = saved[last_layer][10], saved[last_layer][14]
     for layer in reversed(range(LAYERS)):
-        mix, low, at_out, both = mixes[layer], lows[layer], mix_rows[layer], boths[layer]
-        at_down, first_layer = at_out + channels, layer == 0
+        mix, both, first_layer = mixes[layer], boths[layer], layer == 0
         bound, gain = bounds[layer][None, :], gains[layer][None, :]
-        (factor, normed, proj_input, proj_forget, proj_gate, entering, state, inverse,
+        (factor, twin_rows, normed, proj_input, proj_forget, proj_gate, entering, state, inverse,
          branch, middle, normed_two, upward, gating, hidden, unit) = saved[layer]
         unit_two, factor_two = rms_parts(middle)
+        all_normed, all_two = normed + twin_rows[0], normed_two + twin_rows[1]
 
         if layer < last_layer:
-            grad_y = gather_rows(grad_x.astype(bf16), *arrived(("ffn", layer + 1)))
-        down_part = outer([(hidden, grad_y)])
-        down_shard = scatter_columns(down_part)
+            grad_y = gather_rows(grad_x.astype(bf16), *due(layer, "gather"))
+        down_part = outer([([hidden, *twin_rows[2]], grad_y + twins(grad_y))])
+        down_shard = scattered["down", layer] = scatter_columns(down_part)
         grad_up, grad_glu = up_and_gate_back(
-            all_after(grad_y, *down_part), low, at_down, upward, gating
-        )
+            all_after(grad_y, down_part), *downs[layer], upward, gating
+        )
+        twin_up, twin_glu = twins((grad_up, grad_glu))
+        grad_up, grad_glu = all_after((grad_up, grad_glu), *due(layer, "part"))
         part = dot(jnp.concatenate([grad_up, grad_glu], axis=1), both).astype(bf16)
-
-        def ffn_gradients():
-            made = outer([(after(grad_up, part), normed_two), (grad_glu, normed_two)])
-            return made, scatter_columns(made)
-
-        grad_normed_two, ffn_shard = scatter_rows(
-            cut(part, size), ffn_gradients, *arrived(("low", layer + 1))
-        )
+        *parts, ready = all_after((*cut(part, size), grad_up))
+        ffn_part = outer([([ready, twin_up], all_two), ([grad_glu, twin_glu], all_two)])
+        ffn_shard = scattered["ffn", layer] = scatter_columns(ffn_part)
+        grad_normed_two = scatter_rows(parts, ffn_part, *due(layer, "sum"))
         ffn_piece = jnp.sum(grad_normed_two * unit_two, axis=0)
         grad_middle = grad_x + norm_back(grad_normed_two * norm_ffn[layer], unit_two, factor_two)
 
         grad_m_own = grad_middle.astype(bf16)
-        grad_m = gather_rows(grad_m_own, down_shard)
+        grad_m_own = after(grad_m_own, *due(layer, "norm"))
+        grad_m = gather_rows(grad_m_own, *due(layer, "middle"))
         inner = jnp.concatenate(
             gather_rows(jnp.sum(grad_m_own.astype(f32) * branch, axis=1)), axis=0
         )[:, None]
@@ -619,13 +629,14 @@
             functools.partial(back_kernel, size, model_width, trans_dot),
             place_array,
             grad_m,
-            [(low, at_out, False)],
+            [(*outs[layer], False)],
             (state, proj_gate, proj_forget, inverse, inner, keep, bound, gain),
             ((block_rows, f32), (block_rows, f32), (block_rows, bf16), (block_rows, bf16), (1, f32)),
             [pltpu.VMEM((block_rows, model_width), bf16), pltpu.VMEM((block_rows, min(LANES, channels)), f32)],
             channels,
             100 * block_rows * channels,
         )
+        all_m, twin_mixed = grad_m + twins(grad_m), twins([mixed])
         first_row = place * row_count
         first_decay = (
             bound
@@ -637,6 +648,12 @@
             first_decay * lax.dynamic_slice_in_dim(adjoint, first_row, 1, 0),
             True,
         )
+        ready = [*all_m, *twin_mixed, *due(layer, "coming")]
+        if first_layer:
+            output = dot(after(final_hidden, adjoint), rows_of(downs[last_layer], hidden_units)).astype(bf16)
+            hidden_out = (final_middle + scatter_rows(cut(output, size))).astype(bf16)
+            ready.append(output)
+        coming = after(coming, *ready)
         grad_input, grad_forget, bound_piece = over_channels(
             functools.partial(gates_kernel, size),
             place_array,
@@ -650,32 +667,32 @@
         )
         grad_three = (grad_input, grad_forget, grad_gate)
         joined = jnp.concatenate([grad_input, grad_forget, grad_gate], axis=1)
-        part = trans_dot(joined, mix) if first_layer else dot(joined, mix[: 3 * channels])
+        (twin_joined,) = twins((joined,))
+        if first_layer:
+            low_part = outer([([joined, twin_joined], all_normed), ([mixed, *twin_mixed], all_m)])
+            part = trans_dot(after(joined, low_part), mix)
+        else:
+            part = dot(joined, mix[: 3 * channels])
         part = part.astype(bf16)
 
-        def low_gradients():
-            made = outer([(after(joined, part), normed), (mixed, grad_m)])
-            return made, scatter_columns(made)
-
-        grad_normed, low_shard = scatter_rows(
-            cut(part, size), low_gradients, *((ffn_shard,) if first_layer else ())
-        )
-        scattered.update({("ffn", layer): ffn_shard, ("low", layer): low_shard})
+        if first_layer:
+            parts = cut(part, size)
+        else:
+            *parts, ready = all_after((*cut(part, size), joined))
+            low_part = outer([([ready, twin_joined], all_normed), ([mixed, *twin_mixed], all_m)])
+        low_shard = scattered["low", layer] = scatter_columns(low_part)
+        grad_normed = scatter_rows(parts, low_part, *due(layer, "last"))
         mix_piece = jnp.sum(grad_normed * unit, axis=0)
         grad_x = grad_middle + norm_back(grad_normed * norm_mix[layer], unit, factor)
 
-        scattered[layer] = (ffn_shard, down_shard, low_shard)
         smalls[layer] = (mix_piece, ffn_piece, bound_piece, gain_piece)
-    middle, hidden = saved[last_layer][9], saved[last_layer][13]
-    part = dot(after(hidden, grad_x), lows[-1][mix_rows[-1] + channels :]).astype(bf16)
-    hidden_out = (middle + scatter_rows(cut(part, size))).astype(bf16)
     wide_rows = jnp.stack([row for pieces in smalls for row in pieces[:2]])
     own_rows = jnp.concatenate([row for pieces in smalls for row in pieces[2:]], axis=0)
-    small = total_small(after(wide_rows, grad_x), own_rows, first_channel, channels)
+    small = total_small(after(wide_rows, grad_x, *due(0, "after")), own_rows, first_channel, channels)
     for layer in range(LAYERS):
-        ffn_shard, down_shard, low_shard = scattered[layer]
+        ffn_shard, down_shard, low_shard = (scattered[name, layer] for name in ("ffn", "down", "low"))
         if layer == 0:
-            low_shard = after(low_shard, hidden_out)
+            low_shard = after(low_shard, small)
         shards[layer] = (
             *(low_shard[k * channels : (k + 1) * channels].T for k in range(3)),
             low_shard[3 * channels :],

time: 1110 us -> 1040 us (0.937)
  waiting for transfers between devices: 560 us -> 518 us
  other arithmetic: 94.4 us -> 54.2 us
    convert_element_type x8 -> x4, other arithmetic: 43.3 us -> 10.2 us  [the longest x1 3.9 us: local(): grad_y = gather_rows(grad_x.astype(bf16), *due(layer, 'gather'))]
    ppermute x66, waiting for transfers between devices: 407 us -> 376 us  [exchange(): return lax.ppermute(values, 'fsdp', [(i, i ^ step) for i in range(size)])]
    all_gather x4 -> x5, waiting for transfers between devices: 115 us -> 105 us  [tall(): lax.all_gather(jnp.concatenate(shards, axis=0), SEQ, axis=1, tiled=True)]
    unnamed x214 -> x340, local copies, waits for them, and re-layouts: 33.8 us -> 40 us
  transfers between devices with their start and end apart: 99 -> 136, of which waited for: 56 -> 64; matrix products, arithmetic and copies ran while one was open for 18% -> 14% of each run, Pallas kernels for 14% -> 18%
where the time goes in v3:
time: 1040 us; the launch traced here: 1030 us
  waiting for transfers between devices  518 us (50%)
  Pallas kernels  185 us (18%)
  starting transfers between devices  114 us (11%)
  local copies, waits for them, and re-layouts  69.8 us (7%)
  matrix products  59.2 us (6%)
  other arithmetic  54.2 us (5%)
  between operations  16.8 us (2%)
  blocking collectives  14.8 us (1%)
    ppermute x66, waiting for transfers between devices, exchange(): return lax.ppermute(values, 'fsdp', [(i, i ^ step) for i in range(size)])  376 us
    pallas_call x16, Pallas kernels, call(): pl.pallas_call(kernel, grid_spec=pltpu.PrefetchScalarGridSpec(num_scalar_...  185 us
    all_gather x5, waiting for transfers between devices, tall(): lax.all_gather(jnp.concatenate(shards, axis=0), SEQ, axis=1, tiled=True)  105 us
    ppermute x66, starting transfers between devices, exchange(): return lax.ppermute(values, 'fsdp', [(i, i ^ step) for i in range(size)])  80.6 us
    dot_general x7, matrix products, dot(): return jnp.dot(left, right, preferred_element_type=f32)  52 us
    unnamed x340, local copies, waits for them, and re-layouts  40 us
    ppermute x12, starting transfers between devices, entering_of(): lax.ppermute(pair, SEQ, [(i, i + sign * 2 * hop) for i in range(length) i...  23.2 us
  transfers between devices with their start and end apart: 136, of which 64 were waited for; matrix products, arithmetic and copies ran while one was open for 14% of the time, Pallas kernels for 18%

profile of v3, /device:TPU:0, one launch (start us, length us, event | category | flops | bytes accessed | tf_op | source)
XLA Modules:
  0.0 1032.7 jit_solution(1086728926791618483)
XLA Ops:
  30.6 13.7 %collective-permute-done.refs_1_.refs_5_ = bf16[160,2048]{1,0:T(8,128)(2,1)S(1)} collective-permute-done((bf16[160,2048]{1,0:T(8,128)(2,1)S(1)}, bf16[160,2048]{1,0:T(8,128)(2,1)S(1)}, u32[]{:S(2)}, u32[]{:S(2)}) %collective-permute-start) | collective-permute-done | bytes 655392 | tf_op jit(solution)/shard_map/ppermute | solution.py:30
  44.3 14.6 %collective-permute-done.1.refs_2_.refs_6_ = bf16[160,2048]{1,0:T(8,128)(2,1)S(1)} collective-permute-done((bf16[160,2048]{1,0:T(8,128)(2,1)S(1)}, bf16[160,2048]{1,0:T(8,128)(2,1)S(1)}, u32[]{:S(2)}, u32[]{:S(2)}) %collective-permute-start.1) | collective-permute-done | bytes 655392 | tf_op jit(solution)/shard_map/ppermute | solution.py:30
  64.8 12.6 %collective-permute-done.3.refs_3_.refs_1_ = bf16[160,2048]{1,0:T(8,128)(2,1)S(1)} collective-permute-done((bf16[160,2048]{1,0:T(8,128)(2,1)S(1)}, bf16[160,2048]{1,0:T(8,128)(2,1)S(1)}, u32[]{:S(2)}, u32[]{:S(2)}) %collective-permute-start.3) | collective-permute-done | bytes 655392 | tf_op jit(solution)/shard_map/ppermute | solution.py:30
  77.4 12.3 %collective-permute-done.4.refs_4_.refs_2_ = bf16[160,2048]{1,0:T(8,128)(2,1)} collective-permute-done((bf16[160,2048]{1,0:T(8,128)(2,1)S(1)}, bf16[160,2048]{1,0:T(8,128)(2,1)}, u32[]{:S(2)}, u32[]{:S(2)}) %collective-permute-start.4) | collective-permute-done | bytes 655392 | tf_op jit(solution)/shard_map/ppermute | solution.py:30
  89.7 13.4 %shard_map.237 = (f32[640,512]{1,0:T(8,128)}, f32[640,512]{1,0:T(8,128)}, f32[640,512]{1,0:T(8,128)}, f32[640,512]{1,0:T(8,128)}, f32[640,512]{1,0:T(8,128)}) custom-call(s32[1]{0:T(128)} %bitcast.place_ref, bf16[160,2048]{1,0:T(8,128)(2,1)S(1)} %fusion.30.refs_0_.refs_4_, bf16[160,2048]{1,0:T(8,128)(2,1)S(1)} %collective-permute-done.refs_1_.refs_5_, ...), custom_call_target="tpu_custom_call" | custom-call | flops 22145925120 | bytes 7864320 | tf_op jit(solution)/shard_map/pallas_call | solution.py:106
  105.9 3.5 collective-permute-start.7
  109.4 4.6 collective-permute-start.8
  123.8 33.2 %all-gather.11.cloned.1.call-done.refs_4_ = bf16[1920,2048]{1,0:T(8,128)(2,1)} async-done(((bf16[1920,256]{1,0:T(8,128)(2,1)}), bf16[1920,2048]{1,0:T(8,128)(2,1)}) %all-gather.11.cloned.1.call-update) | async-done | bytes 7864336 | tf_op jit(solution)/shard_map/all_gather | solution.py:522
  166.2 13.9 %collective-permute-done.10 = bf16[160,2048]{1,0:T(8,128)(2,1)S(1)} collective-permute-done((bf16[160,2048]{1,0:T(8,128)(2,1)}, bf16[160,2048]{1,0:T(8,128)(2,1)S(1)}, u32[]{:S(2)}, u32[]{:S(2)}) %collective-permute-start.10) | collective-permute-done | bytes 655392 | tf_op jit(solution)/shard_map/ppermute | solution.py:30
  180.1 14.6 %collective-permute-done.11 = bf16[160,2048]{1,0:T(8,128)(2,1)S(1)} collective-permute-done((bf16[160,2048]{1,0:T(8,128)(2,1)}, bf16[160,2048]{1,0:T(8,128)(2,1)S(1)}, u32[]{:S(2)}, u32[]{:S(2)}) %collective-permute-start.11) | collective-permute-done | bytes 655392 | tf_op jit(solution)/shard_map/ppermute | solution.py:30
  201.6 14.2 %collective-permute-done.16.refs_1_.refs_5_ = bf16[160,2048]{1,0:T(8,128)(2,1)S(1)} collective-permute-done((bf16[160,2048]{1,0:T(8,128)(2,1)S(1)}, bf16[160,2048]{1,0:T(8,128)(2,1)S(1)}, u32[]{:S(2)}, u32[]{:S(2)}) %collective-permute-start.16) | collective-permute-done | bytes 655392 | tf_op jit(solution)/shard_map/ppermute | solution.py:30
  215.8 11.4 %collective-permute-done.17.refs_2_.refs_6_ = bf16[160,2048]{1,0:T(8,128)(2,1)S(1)} collective-permute-done((bf16[160,2048]{1,0:T(8,128)(2,1)S(1)}, bf16[160,2048]{1,0:T(8,128)(2,1)S(1)}, u32[]{:S(2)}, u32[]{:S(2)}) %collective-permute-start.17) | collective-permute-done | bytes 655392 | tf_op jit(solution)/shard_map/ppermute | solution.py:30
  229.1 38.8 %all-gather.13.cloned.1.call-done.refs_4_.refs_5_ = bf16[2816,2048]{1,0:T(8,128)(2,1)} async-done(((bf16[2816,256]{1,0:T(8,128)(2,1)}), bf16[2816,2048]{1,0:T(8,128)(2,1)}) %all-gather.13.cloned.1.call-update) | async-done | bytes 11534352 | tf_op jit(solution)/shard_map/all_gather | solution.py:522
  267.9 15.0 %shard_map.238 = (bf16[640,1408]{1,0:T(8,128)(2,1)}, bf16[640,1408]{1,0:T(8,128)(2,1)}, bf16[640,1408]{1,0:T(8,128)(2,1)}) custom-call(bf16[160,2048]{1,0:T(8,128)(2,1)S(1)} %multiply_convert_fusion.3.refs_0_.refs_4_, bf16[160,2048]{1,0:T(8,128)(2,1)S(1)} %collective-permute-done.16.refs_1_.refs_5_, ...), custom_call_target="tpu_custom_call" | custom-call | flops 40600862720 | bytes 14417920 | tf_op jit(solution)/shard_map/pallas_call | solution.py:106
  282.9 7.4 fusion.18
  294.0 14.1 %collective-permute-done.19 = bf16[160,2048]{1,0:T(8,128)(2,1)S(1)} collective-permute-done((bf16[160,2048]{1,0:T(8,128)(2,1)S(1)}, bf16[160,2048]{1,0:T(8,128)(2,1)S(1)}, u32[]{:S(2)}, u32[]{:S(2)}) %collective-permute-start.19) | collective-permute-done | bytes 655392 | tf_op jit(solution)/shard_map/ppermute | solution.py:30
  308.1 14.6 %collective-permute-done.20 = bf16[160,2048]{1,0:T(8,128)(2,1)S(1)} collective-permute-done((bf16[160,2048]{1,0:T(8,128)(2,1)S(1)}, bf16[160,2048]{1,0:T(8,128)(2,1)S(1)}, u32[]{:S(2)}, u32[]{:S(2)}) %collective-permute-start.20) | collective-permute-done | bytes 655392 | tf_op jit(solution)/shard_map/ppermute | solution.py:30
  327.1 14.2 %collective-permute-done.22.refs_1_.refs_5_ = bf16[160,2048]{1,0:T(8,128)(2,1)S(1)} collective-permute-done((bf16[160,2048]{1,0:T(8,128)(2,1)S(1)}, bf16[160,2048]{1,0:T(8,128)(2,1)S(1)}, u32[]{:S(2)}, u32[]{:S(2)}) %collective-permute-start.22) | collective-permute-done | bytes 655392 | tf_op jit(solution)/shard_map/ppermute | solution.py:30
  341.3 13.5 %collective-permute-done.23.refs_2_.refs_6_ = bf16[160,2048]{1,0:T(8,128)(2,1)S(1)} collective-permute-done((bf16[160,2048]{1,0:T(8,128)(2,1)S(1)}, bf16[160,2048]{1,0:T(8,128)(2,1)S(1)}, u32[]{:S(2)}, u32[]{:S(2)}) %collective-permute-start.23) | collective-permute-done | bytes 655392 | tf_op jit(solution)/shard_map/ppermute | solution.py:30
  355.6 13.9 %shard_map.239 = (f32[640,512]{1,0:T(8,128)}, f32[640,512]{1,0:T(8,128)}, f32[640,512]{1,0:T(8,128)}, f32[640,512]{1,0:T(8,128)}, f32[640,512]{1,0:T(8,128)}) custom-call(s32[1]{0:T(128)} %bitcast.place_ref, bf16[160,2048]{1,0:T(8,128)(2,1)S(1)} %multiply_convert_fusion.2.refs_0_.refs_4_, bf16[160,2048]{1,0:T(8,128)(2,1)S(1)} %collective-permute-done.22.refs_1_.refs_5_, ...), custom_call_target="tpu_custom_call" | custom-call | flops 22145925120 | bytes 7864320 | tf_op jit(solution)/shard_map/pallas_call | solution.py:106
  385.1 3.6 convolution_convert_fusion.2
  394.6 14.0 %collective-permute-done.29 = bf16[160,2048]{1,0:T(8,128)(2,1)S(1)} collective-permute-done((bf16[160,2048]{1,0:T(8,128)(2,1)}, bf16[160,2048]{1,0:T(8,128)(2,1)S(1)}, u32[]{:S(2)}, u32[]{:S(2)}) %collective-permute-start.29) | collective-permute-done | bytes 655392 | tf_op jit(solution)/shard_map/ppermute | solution.py:30
  408.7 11.8 %collective-permute-done.30 = bf16[160,2048]{1,0:T(8,128)(2,1)S(1)} collective-permute-done((bf16[160,2048]{1,0:T(8,128)(2,1)}, bf16[160,2048]{1,0:T(8,128)(2,1)S(1)}, u32[]{:S(2)}, u32[]{:S(2)}) %collective-permute-start.30) | collective-permute-done | bytes 655392 | tf_op jit(solution)/shard_map/ppermute | solution.py:30
  426.4 14.2 %collective-permute-done.35.refs_1_.refs_5_ = bf16[160,2048]{1,0:T(8,128)(2,1)S(1)} collective-permute-done((bf16[160,2048]{1,0:T(8,128)(2,1)S(1)}, bf16[160,2048]{1,0:T(8,128)(2,1)S(1)}, u32[]{:S(2)}, u32[]{:S(2)}) %collective-permute-start.35) | collective-permute-done | bytes 655392 | tf_op jit(solution)/shard_map/ppermute | solution.py:30
  440.6 11.0 %collective-permute-done.36.refs_2_.refs_6_ = bf16[160,2048]{1,0:T(8,128)(2,1)S(1)} collective-permute-done((bf16[160,2048]{1,0:T(8,128)(2,1)S(1)}, bf16[160,2048]{1,0:T(8,128)(2,1)S(1)}, u32[]{:S(2)}, u32[]{:S(2)}) %collective-permute-start.36) | collective-permute-done | bytes 655392 | tf_op jit(solution)/shard_map/ppermute | solution.py:30
  452.4 8.2 all-gather.17.cloned.1.call-done.refs_4_.refs_5_
  461.7 14.9 %shard_map.240 = (bf16[640,1408]{1,0:T(8,128)(2,1)}, bf16[640,1408]{1,0:T(8,128)(2,1)}, bf16[640,1408]{1,0:T(8,128)(2,1)}) custom-call(bf16[160,2048]{1,0:T(8,128)(2,1)S(1)} %multiply_convert_fusion.refs_0_.refs_4_, bf16[160,2048]{1,0:T(8,128)(2,1)S(1)} %collective-permute-done.35.refs_1_.refs_5_, bf16[160,2048]{1,0:T(8,128)(2,1)S(1)} %copy-done.31, ...), custom_call_target="tpu_custom_call" | custom-call | flops 40600862720 | bytes 14417920 | tf_op jit(solution)/shard_map/pallas_call | solution.py:106
  485.5 9.1 shard_map.241
  495.1 25.0 %all-gather.19.cloned.1.call-done = bf16[1,1408,2048]{2,1,0:T(8,128)(2,1)} async-done(((bf16[1,1408,256]{2,1,0:T(8,128)(2,1)}), bf16[1,1408,2048]{2,1,0:T(8,128)(2,1)}) %all-gather.19.cloned.1.call-update) | async-done | bytes 5767184 | tf_op jit(solution)/shard_map/all_gather | solution.py:522
  520.0 10.5 %shard_map.242 = (bf16[640,1408]{1,0:T(8,128)(2,1)}, bf16[640,1408]{1,0:T(8,128)(2,1)}) custom-call(bf16[160,2048]{1,0:T(8,128)(2,1)S(1)} %copy-done.1, bf16[160,2048]{1,0:T(8,128)(2,1)S(1)} %copy-done.27, bf16[160,2048]{1,0:T(8,128)(2,1)} %collective-permute-done.4.refs_4_.refs_2_, bf16[160,2048]{1,0:T(8,128)(2,1)} %collective-permute-done.5.refs_5_.refs_3_, ...), custom_call_target="tpu_custom_call" | custom-call | flops 20300431360 | bytes 7208960 | tf_op jit(solution)/shard_map/pallas_call | solution.py:106
  531.1 11.6 %fusion.15 = bf16[640,2048]{1,0:T(8,128)(2,1)S(1)} fusion(bf16[2816,2048]{1,0:T(8,128)(2,1)} %all-gather.17.cloned.1.call-done.refs_4_.refs_5_, bf16[640,1408]{1,0:T(8,128)(2,1)} %get-tuple-element.160.refs_2_, bf16[640,1408]{1,0:T(8,128)(2,1)} %get-tuple-element.166), kind=kOutput, calls=%fused_computation.13 | convolution fusion | flops 7390494720 | bytes 17760256 | tf_op jit(solution)/shard_map/dot_general | solution.py:94
  550.0 15.2 %shard_map.243 = bf16[2816,1024]{1,0:T(8,128)(2,1)} custom-call(s32[1]{0:T(128)} %bitcast.31.core_ref, bf16[640,1408]{1,0:T(8,128)(2,1)} %get-tuple-element.166, bf16[640,1408]{1,0:T(8,128)(2,1)} %copy-done.138, bf16[640,1408]{1,0:T(8,128)(2,1)} %get-tuple-element.160.refs_2_, bf16[640,1408]{1,0:T(8,128)(2,1)} %copy-done.139, ...), custom_call_target="tpu_custom_call" | custom-call | flops 81201725440 | bytes 28835840 | tf_op jit(solution)/shard_map/pallas_call | solution.py:106
  565.3 11.0 %collective-permute-done.44 = bf16[160,2048]{1,0:T(8,128)(2,1)} collective-permute-done((bf16[160,2048]{1,0:T(8,128)(2,1)}, bf16[160,2048]{1,0:T(8,128)(2,1)}, u32[]{:S(2)}, u32[]{:S(2)}) %collective-permute-start.44) | collective-permute-done | bytes 655392 | tf_op jit(solution)/shard_map/ppermute | solution.py:30
  590.9 20.9 %collective-permute-done.55 = f32[160]{0:T(256)S(1)} collective-permute-done((f32[160]{0:T(256)S(1)}, f32[160]{0:T(256)S(1)}, u32[]{:S(2)}, u32[]{:S(2)}) %collective-permute-start.55) | collective-permute-done | bytes 672 | tf_op jit(solution)/shard_map/ppermute | solution.py:30
  616.6 11.2 %shard_map.244 = (f32[640,512]{1,0:T(8,128)}, f32[640,512]{1,0:T(8,128)}, bf16[640,512]{1,0:T(8,128)(2,1)S(1)}, bf16[640,512]{1,0:T(8,128)(2,1)}, f32[1,512]{1,0:T(1,128)S(1)}) custom-call(s32[1]{0:T(128)} %bitcast.place_ref, bf16[160,2048]{1,0:T(8,128)(2,1)} %copy-done.56, bf16[160,2048]{1,0:T(8,128)(2,1)} %collective-permute-done.52.refs_1_.refs_13_, ...), custom_call_target="tpu_custom_call" | custom-call | flops 180224000 | bytes 64000 | tf_op jit(solution)/shard_map/pallas_call | solution.py:106
  635.8 4.4 collective-permute-done.59
  645.7 5.7 shard_map.245
  654.1 7.2 fusion.21
  666.6 12.3 %shard_map.246 = bf16[2048,1024]{1,0:T(8,128)(2,1)} custom-call(s32[1]{0:T(128)} %bitcast.31.core_ref, bf16[640,1536]{1,0:T(8,128)(2,1)} %copy-done.92, bf16[640,1536]{1,0:T(8,128)(2,1)} %collective-permute-done.70.refs_1_, bf16[640,512]{1,0:T(8,128)(2,1)S(1)} %copy-done.28, bf16[640,512]{1,0:T(8,128)(2,1)S(1)} %collective-permute-done.66.refs_3_, ...), custom_call_target="tpu_custom_call" | custom-call | flops 59055800320 | bytes 20971520 | tf_op jit(solution)/shard_map/pallas_call | solution.py:106
  680.7 14.5 %collective-permute-done.68 = bf16[160,2048]{1,0:T(8,128)(2,1)} collective-permute-done((bf16[160,2048]{1,0:T(8,128)(2,1)}, bf16[160,2048]{1,0:T(8,128)(2,1)}, u32[]{:S(2)}, u32[]{:S(2)}) %collective-permute-start.68) | collective-permute-done | bytes 655392 | tf_op jit(solution)/shard_map/ppermute | solution.py:30
  698.1 3.9 fusion.70
  705.4 14.2 %collective-permute-done.75.refs_3_.refs_1_ = bf16[160,2048]{1,0:T(8,128)(2,1)S(1)} collective-permute-done((bf16[160,2048]{1,0:T(8,128)(2,1)S(1)}, bf16[160,2048]{1,0:T(8,128)(2,1)S(1)}, u32[]{:S(2)}, u32[]{:S(2)}) %collective-permute-start.75) | collective-permute-done | bytes 655392 | tf_op jit(solution)/shard_map/ppermute | solution.py:30
  719.6 13.2 %collective-permute-done.76.refs_4_.refs_2_ = bf16[160,2048]{1,0:T(8,128)(2,1)S(1)} collective-permute-done((bf16[160,2048]{1,0:T(8,128)(2,1)S(1)}, bf16[160,2048]{1,0:T(8,128)(2,1)S(1)}, u32[]{:S(2)}, u32[]{:S(2)}) %collective-permute-start.76) | collective-permute-done | bytes 655392 | tf_op jit(solution)/shard_map/ppermute | solution.py:30
  740.0 9.0 shard_map.247
  750.1 10.0 shard_map.248
  761.6 11.6 %fusion.12 = bf16[640,2048]{1,0:T(8,128)(2,1)S(1)} fusion(bf16[2816,2048]{1,0:T(8,128)(2,1)} %all-gather.13.cloned.1.call-done.refs_4_.refs_5_, bf16[640,1408]{1,0:T(8,128)(2,1)} %get-tuple-element.206.refs_2_, bf16[640,1408]{1,0:T(8,128)(2,1)} %get-tuple-element.211.refs_0_), kind=kOutput, calls=%fused_computation.12 | convolution fusion | flops 7390494720 | bytes 17760256 | tf_op jit(solution)/shard_map/dot_general | solution.py:94
  779.3 15.2 %shard_map.249 = bf16[2816,1024]{1,0:T(8,128)(2,1)} custom-call(s32[1]{0:T(128)} %bitcast.31.core_ref, bf16[640,1408]{1,0:T(8,128)(2,1)} %get-tuple-element.211.refs_0_, bf16[640,1408]{1,0:T(8,128)(2,1)} %collective-permute-done.86.refs_1_, bf16[640,1408]{1,0:T(8,128)(2,1)} %get-tuple-element.206.refs_2_, bf16[640,1408]{1,0:T(8,128)(2,1)} %copy-done.140, ...), custom_call_target="tpu_custom_call" | custom-call | flops 81201725440 | bytes 28835840 | tf_op jit(solution)/shard_map/pallas_call | solution.py:106
  794.6 12.7 %collective-permute-done.84 = bf16[160,2048]{1,0:T(8,128)(2,1)} collective-permute-done((bf16[160,2048]{1,0:T(8,128)(2,1)}, bf16[160,2048]{1,0:T(8,128)(2,1)}, u32[]{:S(2)}, u32[]{:S(2)}) %collective-permute-start.84) | collective-permute-done | bytes 655392 | tf_op jit(solution)/shard_map/ppermute | solution.py:30
  809.5 3.5 fusion.69
  821.1 22.1 %collective-permute-done.95 = f32[160]{0:T(256)S(1)} collective-permute-done((f32[160]{0:T(256)S(1)}, f32[160]{0:T(256)S(1)}, u32[]{:S(2)}, u32[]{:S(2)}) %collective-permute-start.95) | collective-permute-done | bytes 672 | tf_op jit(solution)/shard_map/ppermute | solution.py:30
  848.8 11.1 %shard_map.250 = (f32[640,512]{1,0:T(8,128)}, f32[640,512]{1,0:T(8,128)}, bf16[640,512]{1,0:T(8,128)(2,1)S(1)}, bf16[640,512]{1,0:T(8,128)(2,1)}, f32[1,512]{1,0:T(1,128)S(1)}) custom-call(s32[1]{0:T(128)} %bitcast.place_ref, bf16[160,2048]{1,0:T(8,128)(2,1)} %copy-done.54, bf16[160,2048]{1,0:T(8,128)(2,1)} %copy-done.88, ...), custom_call_target="tpu_custom_call" | custom-call | flops 180224000 | bytes 64000 | tf_op jit(solution)/shard_map/pallas_call | solution.py:106
  871.3 3.5 collective-permute-done.104
  874.8 7.5 convolution_convert_fusion.1
  883.2 6.5 shard_map.251
  892.7 3.3 collective-permute-done.111.refs_8_
  900.9 12.4 %shard_map.252 = bf16[2048,1024]{1,0:T(8,128)(2,1)} custom-call(s32[1]{0:T(128)} %bitcast.31.core_ref, bf16[640,1536]{1,0:T(8,128)(2,1)} %copy-done.93, bf16[640,1536]{1,0:T(8,128)(2,1)} %copy-done.136, bf16[640,512]{1,0:T(8,128)(2,1)S(1)} %copy-done.29, bf16[640,512]{1,0:T(8,128)(2,1)S(1)} %collective-permute-done.109.refs_3_, ...), custom_call_target="tpu_custom_call" | custom-call | flops 59055800320 | bytes 20971520 | tf_op jit(solution)/shard_map/pallas_call | solution.py:106
  920.6 7.3 convolution_convert_fusion
  931.4 4.2 collective-permute-done.100
  938.8 10.7 %collective-permute-done.98 = bf16[160,2048]{1,0:T(8,128)(2,1)S(1)} collective-permute-done((bf16[160,2048]{1,0:T(8,128)(2,1)S(1)}, bf16[160,2048]{1,0:T(8,128)(2,1)S(1)}, u32[]{:S(2)}, u32[]{:S(2)}) %collective-permute-start.98) | collective-permute-done | bytes 655392 | tf_op jit(solution)/shard_map/ppermute | solution.py:30
  952.1 11.6 %collective-permute-done.115 = bf16[160,2048]{1,0:T(8,128)(2,1)S(1)} collective-permute-done((bf16[160,2048]{1,0:T(8,128)(2,1)S(1)}, bf16[160,2048]{1,0:T(8,128)(2,1)S(1)}, u32[]{:S(2)}, u32[]{:S(2)}) %collective-permute-start.115) | collective-permute-done | bytes 655392 | tf_op jit(solution)/shard_map/ppermute | solution.py:30
  963.7 13.6 %collective-permute-done.117 = bf16[160,2048]{1,0:T(8,128)(2,1)} collective-permute-done((bf16[160,2048]{1,0:T(8,128)(2,1)S(1)}, bf16[160,2048]{1,0:T(8,128)(2,1)}, u32[]{:S(2)}, u32[]{:S(2)}) %collective-permute-start.117) | collective-permute-done | bytes 655392 | tf_op jit(solution)/shard_map/ppermute | solution.py:30
  979.5 3.4 fusion.34
  991.6 3.4 copy.119
  995.1 14.8 %all-gather.1 = f32[64,512]{1,0:T(8,128)S(1)} all-gather(f32[8,512]{1,0:T(8,128)S(1)} %concatenate.79), channel_id=3, replica_groups=mesh['chip'=4,'core'=2,'fsdp'=4] {'chip','core'}, dimensions={0}, use_global_device_ids=true | all-gather | bytes 147456 | tf_op jit(solution)/shard_map/all_gather | solution.py:484
  (742 shorter events, 258.0 us)
Async XLA Ops:
  7.2 82.5 %all-gather.9.cloned.1.call-start = ((), (), s32[]{:S(2)}) async-start(), calls=%async_computation.6 | async-start | bytes 7077888 | tf_op jit(solution)/shard_map/all_gather | solution.py:519
  10.4 146.6 %all-gather.11.cloned.1.call-start = ((), (), s32[]{:S(2)}) async-start(), calls=%async_computation.7 | async-start | bytes 8847360 | tf_op jit(solution)/shard_map/all_gather | solution.py:522
  13.8 254.1 %all-gather.13.cloned.1.call-start = ((), (), s32[]{:S(2)}) async-start(), calls=%async_computation.8 | async-start | bytes 12976128 | tf_op jit(solution)/shard_map/all_gather | solution.py:522
  19.8 335.8 %all-gather.15.cloned.1.call-start = ((), (), s32[]{:S(2)}) async-start(), calls=%async_computation.9 | async-start | bytes 9437184 | tf_op jit(solution)/shard_map/all_gather | solution.py:522
  22.3 438.4 %all-gather.17.cloned.1.call-start = ((), (), s32[]{:S(2)}) async-start(), calls=%async_computation.10 | async-start | bytes 12976128 | tf_op jit(solution)/shard_map/all_gather | solution.py:522
  24.2 495.9 %all-gather.19.cloned.1.call-start = ((), (), s32[]{:S(2)}) async-start(), calls=%async_computation.17 | async-start | bytes 6488064 | tf_op jit(solution)/shard_map/all_gather | solution.py:522
  28.7 30.2 %collective-permute-start.1 = (bf16[160,2048]{1,0:T(8,128)(2,1)S(1)}, bf16[160,2048]{1,0:T(8,128)(2,1)S(1)}, u32[]{:S(2)}, u32[]{:S(2)}) collective-permute-start(bf16[160,2048]{1,0:T(8,128)(2,1)S(1)} %fusion.30.refs_0_.refs_4_), channel_id=1, source_target_pairs={{0,2},{1,3},{2,0},{3,1},{4,6},{5,7},{6,4},{7,5},{8,10},{9,11},{10,... | collective-permute-start | bytes 1966088 | tf_op jit(solution)/shard_map/ppermute | solution.py:30
  30.3 29.5 %collective-permute-start.2 = (bf16[160,2048]{1,0:T(8,128)(2,1)S(1)}, bf16[160,2048]{1,0:T(8,128)(2,1)}, u32[]{:S(2)}, u32[]{:S(2)}) collective-permute-start(bf16[160,2048]{1,0:T(8,128)(2,1)S(1)} %fusion.30.refs_0_.refs_4_), channel_id=1, source_target_pairs={{0,3},{1,2},{2,1},{3,0},{4,7},{5,6},{6,5},{7,4},{8,11},{9,10},{10,... | collective-permute-start | bytes 1966088 | tf_op jit(solution)/shard_map/ppermute | solution.py:30
  60.3 29.4 %collective-permute-start.4 = (bf16[160,2048]{1,0:T(8,128)(2,1)S(1)}, bf16[160,2048]{1,0:T(8,128)(2,1)}, u32[]{:S(2)}, u32[]{:S(2)}) collective-permute-start(bf16[160,2048]{1,0:T(8,128)(2,1)S(1)} %copy-done), channel_id=1, source_target_pairs={{0,2},{1,3},{2,0},{3,1},{4,6},{5,7},{6,4},{7,5},{8,10},{9,11},{10,... | collective-permute-start | bytes 1966088 | tf_op jit(solution)/shard_map/ppermute | solution.py:30
  61.8 27.9 %collective-permute-start.5 = (bf16[160,2048]{1,0:T(8,128)(2,1)S(1)}, bf16[160,2048]{1,0:T(8,128)(2,1)}, u32[]{:S(2)}, u32[]{:S(2)}) collective-permute-start(bf16[160,2048]{1,0:T(8,128)(2,1)S(1)} %copy-done), channel_id=1, source_target_pairs={{0,3},{1,2},{2,1},{3,0},{4,7},{5,6},{6,5},{7,4},{8,11},{9,10},{10,... | collective-permute-start | bytes 1966088 | tf_op jit(solution)/shard_map/ppermute | solution.py:30
  121.4 44.6 %collective-permute-start.15 = (f32[4,160]{1,0:T(4,128)S(1)}, f32[4,160]{1,0:T(4,128)S(1)}, u32[]{:S(2)}, u32[]{:S(2)}) collective-permute-start(f32[4,160]{1,0:T(4,128)S(1)} %reshape.259), channel_id=1, source_target_pairs={{0,3},{1,2},{2,1},{3,0},{4,7},{5,6},{6,5},{7,4},{8,11},{9,10},{10,... | collective-permute-start | bytes 7688 | tf_op jit(solution)/shard_map/ppermute | solution.py:30
  163.8 30.9 %collective-permute-start.11 = (bf16[160,2048]{1,0:T(8,128)(2,1)}, bf16[160,2048]{1,0:T(8,128)(2,1)S(1)}, u32[]{:S(2)}, u32[]{:S(2)}) collective-permute-start(bf16[160,2048]{1,0:T(8,128)(2,1)} %get-tuple-element.346), channel_id=1, source_target_pairs={{0,2},{1,3},{2,0},{3,1},{4,6},{5,7},{6,4},{7,5},{8,10},{9,11},{10,... | collective-permute-start | bytes 1966088 | tf_op jit(solution)/shard_map/ppermute | solution.py:30
  165.3 29.4 %collective-permute-start.12 = (bf16[160,2048]{1,0:T(8,128)(2,1)}, bf16[160,2048]{1,0:T(8,128)(2,1)S(1)}, u32[]{:S(2)}, u32[]{:S(2)}) collective-permute-start(bf16[160,2048]{1,0:T(8,128)(2,1)} %get-tuple-element.345), channel_id=1, source_target_pairs={{0,3},{1,2},{2,1},{3,0},{4,7},{5,6},{6,5},{7,4},{8,11},{9,10},{10,... | collective-permute-start | bytes 1966088 | tf_op jit(solution)/shard_map/ppermute | solution.py:30
  199.1 28.1 %collective-permute-start.17 = (bf16[160,2048]{1,0:T(8,128)(2,1)S(1)}, bf16[160,2048]{1,0:T(8,128)(2,1)S(1)}, u32[]{:S(2)}, u32[]{:S(2)}) collective-permute-start(bf16[160,2048]{1,0:T(8,128)(2,1)S(1)} %multiply_convert_fusion.3.refs_0_.refs_4_), channel_id=1, source_target_pairs={{0,2},{1,3},{2,0},{3,1},{4,6},{5,7},{6,4},{7,5},{8,10},{9,11},{10,... | collective-permute-start | bytes 1966088 | tf_op jit(solution)/shard_map/ppermute | solution.py:30
  200.2 28.9 %collective-permute-start.18 = (bf16[160,2048]{1,0:T(8,128)(2,1)S(1)}, bf16[160,2048]{1,0:T(8,128)(2,1)S(1)}, u32[]{:S(2)}, u32[]{:S(2)}) collective-permute-start(bf16[160,2048]{1,0:T(8,128)(2,1)S(1)} %multiply_convert_fusion.3.refs_0_.refs_4_), channel_id=1, source_target_pairs={{0,3},{1,2},{2,1},{3,0},{4,7},{5,6},{6,5},{7,4},{8,11},{9,10},{10,... | collective-permute-start | bytes 1966088 | tf_op jit(solution)/shard_map/ppermute | solution.py:30
  292.1 30.7 %collective-permute-start.20 = (bf16[160,2048]{1,0:T(8,128)(2,1)S(1)}, bf16[160,2048]{1,0:T(8,128)(2,1)S(1)}, u32[]{:S(2)}, u32[]{:S(2)}) collective-permute-start(bf16[160,2048]{1,0:T(8,128)(2,1)S(1)} %get-tuple-element.343), channel_id=1, source_target_pairs={{0,2},{1,3},{2,0},{3,1},{4,6},{5,7},{6,4},{7,5},{8,10},{9,11},{10,... | collective-permute-start | bytes 1966088 | tf_op jit(solution)/shard_map/ppermute | solution.py:30
  293.5 29.2 %collective-permute-start.21 = (bf16[160,2048]{1,0:T(8,128)(2,1)S(1)}, bf16[160,2048]{1,0:T(8,128)(2,1)S(1)}, u32[]{:S(2)}, u32[]{:S(2)}) collective-permute-start(bf16[160,2048]{1,0:T(8,128)(2,1)S(1)} %get-tuple-element.342), channel_id=1, source_target_pairs={{0,3},{1,2},{2,1},{3,0},{4,7},{5,6},{6,5},{7,4},{8,11},{9,10},{10,... | collective-permute-start | bytes 1966088 | tf_op jit(solution)/shard_map/ppermute | solution.py:30
  324.8 30.0 %collective-permute-start.23 = (bf16[160,2048]{1,0:T(8,128)(2,1)S(1)}, bf16[160,2048]{1,0:T(8,128)(2,1)S(1)}, u32[]{:S(2)}, u32[]{:S(2)}) collective-permute-start(bf16[160,2048]{1,0:T(8,128)(2,1)S(1)} %multiply_convert_fusion.2.refs_0_.refs_4_), channel_id=1, source_target_pairs={{0,2},{1,3},{2,0},{3,1},{4,6},{5,7},{6,4},{7,5},{8,10},{9,11},{10,... | collective-permute-start | bytes 1966088 | tf_op jit(solution)/shard_map/ppermute | solution.py:30
  325.6 30.0 %collective-permute-start.24 = (bf16[160,2048]{1,0:T(8,128)(2,1)S(1)}, bf16[160,2048]{1,0:T(8,128)(2,1)}, u32[]{:S(2)}, u32[]{:S(2)}) collective-permute-start(bf16[160,2048]{1,0:T(8,128)(2,1)S(1)} %multiply_convert_fusion.2.refs_0_.refs_4_), channel_id=1, source_target_pairs={{0,3},{1,2},{2,1},{3,0},{4,7},{5,6},{6,5},{7,4},{8,11},{9,10},{10,... | collective-permute-start | bytes 1966088 | tf_op jit(solution)/shard_map/ppermute | solution.py:30
  378.1 199.2 %reduce-scatter.7.cloned.1.call-start = ((), (), s32[]{:S(2)}) async-start(), calls=%async_computation.11 | async-start | bytes 3604480 | tf_op jit(solution)/shard_map/reduce_scatter | solution.py:189
  391.4 29.0 %collective-permute-start.30 = (bf16[160,2048]{1,0:T(8,128)(2,1)}, bf16[160,2048]{1,0:T(8,128)(2,1)S(1)}, u32[]{:S(2)}, u32[]{:S(2)}) collective-permute-start(bf16[160,2048]{1,0:T(8,128)(2,1)} %get-tuple-element.340), channel_id=1, source_target_pairs={{0,2},{1,3},{2,0},{3,1},{4,6},{5,7},{6,4},{7,5},{8,10},{9,11},{10,... | collective-permute-start | bytes 1966088 | tf_op jit(solution)/shard_map/ppermute | solution.py:30
  392.8 27.7 %collective-permute-start.31 = (bf16[160,2048]{1,0:T(8,128)(2,1)}, bf16[160,2048]{1,0:T(8,128)(2,1)}, u32[]{:S(2)}, u32[]{:S(2)}) collective-permute-start(bf16[160,2048]{1,0:T(8,128)(2,1)} %get-tuple-element.339), channel_id=1, source_target_pairs={{0,3},{1,2},{2,1},{3,0},{4,7},{5,6},{6,5},{7,4},{8,11},{9,10},{10,... | collective-permute-start | bytes 1966088 | tf_op jit(solution)/shard_map/ppermute | solution.py:30
  424.1 27.5 %collective-permute-start.36 = (bf16[160,2048]{1,0:T(8,128)(2,1)S(1)}, bf16[160,2048]{1,0:T(8,128)(2,1)S(1)}, u32[]{:S(2)}, u32[]{:S(2)}) collective-permute-start(bf16[160,2048]{1,0:T(8,128)(2,1)S(1)} %multiply_convert_fusion.refs_0_.refs_4_), channel_id=1, source_target_pairs={{0,2},{1,3},{2,0},{3,1},{4,6},{5,7},{6,4},{7,5},{8,10},{9,11},{10,... | collective-permute-start | bytes 1966088 | tf_op jit(solution)/shard_map/ppermute | solution.py:30
  424.9 27.5 %collective-permute-start.37 = (bf16[160,2048]{1,0:T(8,128)(2,1)S(1)}, bf16[160,2048]{1,0:T(8,128)(2,1)}, u32[]{:S(2)}, u32[]{:S(2)}) collective-permute-start(bf16[160,2048]{1,0:T(8,128)(2,1)S(1)} %multiply_convert_fusion.refs_0_.refs_4_), channel_id=1, source_target_pairs={{0,3},{1,2},{2,1},{3,0},{4,7},{5,6},{6,5},{7,4},{8,11},{9,10},{10,... | collective-permute-start | bytes 1966088 | tf_op jit(solution)/shard_map/ppermute | solution.py:30
  483.0 47.8 %collective-permute-start.48 = (bf16[160,2048]{1,0:T(8,128)(2,1)S(1)}, bf16[160,2048]{1,0:T(8,128)(2,1)}, u32[]{:S(2)}, u32[]{:S(2)}) collective-permute-start(bf16[160,2048]{1,0:T(8,128)(2,1)S(1)} %multiply_convert_fusion.refs_0_.refs_4_), channel_id=1, source_target_pairs={{0,4},{4,0},{1,5},{5,1},{2,6},{6,2},{3,7},{7,3},{8,12},{12,8},{9,1... | collective-permute-start | bytes 1966088 | tf_op jit(solution)/shard_map/ppermute | solution.py:34
  484.8 59.2 %collective-permute-start.49 = (bf16[160,2048]{1,0:T(8,128)(2,1)S(1)}, bf16[160,2048]{1,0:T(8,128)(2,1)}, u32[]{:S(2)}, u32[]{:S(2)}) collective-permute-start(bf16[160,2048]{1,0:T(8,128)(2,1)S(1)} %collective-permute-done.35.refs_1_.refs_5_), channel_id=1, source_target_pairs={{0,4},{4,0},{1,5},{5,1},{2,6},{6,2},{3,7},{7,3},{8,12},{12,8},{9,1... | collective-permute-start | bytes 1966088 | tf_op jit(solution)/shard_map/ppermute | solution.py:34
  485.0 60.3 %collective-permute-start.50 = (bf16[160,2048]{1,0:T(8,128)(2,1)}, bf16[160,2048]{1,0:T(8,128)(2,1)}, u32[]{:S(2)}, u32[]{:S(2)}) collective-permute-start(bf16[160,2048]{1,0:T(8,128)(2,1)} %copy-done.30), channel_id=1, source_target_pairs={{0,4},{4,0},{1,5},{5,1},{2,6},{6,2},{3,7},{7,3},{8,12},{12,8},{9,1... | collective-permute-start | bytes 1966088 | tf_op jit(solution)/shard_map/ppermute | solution.py:34
  485.4 61.5 %collective-permute-start.51 = (bf16[160,2048]{1,0:T(8,128)(2,1)}, bf16[160,2048]{1,0:T(8,128)(2,1)}, u32[]{:S(2)}, u32[]{:S(2)}) collective-permute-start(bf16[160,2048]{1,0:T(8,128)(2,1)} %collective-permute-done.37.refs_3_.refs_7_), channel_id=1, source_target_pairs={{0,4},{4,0},{1,5},{5,1},{2,6},{6,2},{3,7},{7,3},{8,12},{12,8},{9,1... | collective-permute-start | bytes 1966088 | tf_op jit(solution)/shard_map/ppermute | solution.py:34
  494.6 239.1 %reduce-scatter.9.cloned.1.call-start = ((), (), s32[]{:S(2)}) async-start(), calls=%async_computation.12 | async-start | bytes 7208960 | tf_op jit(solution)/shard_map/reduce_scatter | solution.py:189
  544.0 21.3 %collective-permute-start.43 = (bf16[160,2048]{1,0:T(8,128)(2,1)}, bf16[160,2048]{1,0:T(8,128)(2,1)}, u32[]{:S(2)}, u32[]{:S(2)}) collective-permute-start(bf16[160,2048]{1,0:T(8,128)(2,1)} %get-tuple-element.162), channel_id=1, source_target_pairs={{0,1},{1,0},{2,3},{3,2},{4,5},{5,4},{6,7},{7,6},{8,9},{9,8},{10,11... | collective-permute-start | bytes 1966088 | tf_op jit(solution)/shard_map/ppermute | solution.py:30
  545.3 31.0 %collective-permute-start.44 = (bf16[160,2048]{1,0:T(8,128)(2,1)}, bf16[160,2048]{1,0:T(8,128)(2,1)}, u32[]{:S(2)}, u32[]{:S(2)}) collective-permute-start(bf16[160,2048]{1,0:T(8,128)(2,1)} %get-tuple-element.163), channel_id=1, source_target_pairs={{0,2},{1,3},{2,0},{3,1},{4,6},{5,7},{6,4},{7,5},{8,10},{9,11},{10,... | collective-permute-start | bytes 1966088 | tf_op jit(solution)/shard_map/ppermute | solution.py:30
  546.8 29.5 %collective-permute-start.45 = (bf16[160,2048]{1,0:T(8,128)(2,1)}, bf16[160,2048]{1,0:T(8,128)(2,1)}, u32[]{:S(2)}, u32[]{:S(2)}) collective-permute-start(bf16[160,2048]{1,0:T(8,128)(2,1)} %get-tuple-element.164), channel_id=1, source_target_pairs={{0,3},{1,2},{2,1},{3,0},{4,7},{5,6},{6,5},{7,4},{8,11},{9,10},{10,... | collective-permute-start | bytes 1966088 | tf_op jit(solution)/shard_map/ppermute | solution.py:30
  565.2 196.4 %reduce-scatter.11.cloned.1.call-start = ((), (), s32[]{:S(2)}) async-start(), calls=%async_computation.13 | async-start | bytes 5242880 | tf_op jit(solution)/shard_map/reduce_scatter | solution.py:189
  581.3 35.2 %collective-permute-start.52 = (bf16[160,2048]{1,0:T(8,128)(2,1)S(1)}, bf16[160,2048]{1,0:T(8,128)(2,1)}, u32[]{:S(2)}, u32[]{:S(2)}) collective-permute-start(bf16[160,2048]{1,0:T(8,128)(2,1)S(1)} %fusion.67.refs_0_.refs_12_), channel_id=1, source_target_pairs={{0,1},{1,0},{2,3},{3,2},{4,5},{5,4},{6,7},{7,6},{8,9},{9,8},{10,11... | collective-permute-start | bytes 1966088 | tf_op jit(solution)/shard_map/ppermute | solution.py:30
  582.9 33.7 %collective-permute-start.53 = (bf16[160,2048]{1,0:T(8,128)(2,1)S(1)}, bf16[160,2048]{1,0:T(8,128)(2,1)}, u32[]{:S(2)}, u32[]{:S(2)}) collective-permute-start(bf16[160,2048]{1,0:T(8,128)(2,1)S(1)} %fusion.67.refs_0_.refs_12_), channel_id=1, source_target_pairs={{0,2},{1,3},{2,0},{3,1},{4,6},{5,7},{6,4},{7,5},{8,10},{9,11},{10,... | collective-permute-start | bytes 1966088 | tf_op jit(solution)/shard_map/ppermute | solution.py:30
  584.4 32.2 %collective-permute-start.54 = (bf16[160,2048]{1,0:T(8,128)(2,1)S(1)}, bf16[160,2048]{1,0:T(8,128)(2,1)}, u32[]{:S(2)}, u32[]{:S(2)}) collective-permute-start(bf16[160,2048]{1,0:T(8,128)(2,1)S(1)} %fusion.67.refs_0_.refs_12_), channel_id=1, source_target_pairs={{0,3},{1,2},{2,1},{3,0},{4,7},{5,6},{6,5},{7,4},{8,11},{9,10},{10,... | collective-permute-start | bytes 1966088 | tf_op jit(solution)/shard_map/ppermute | solution.py:30
  587.1 24.7 %collective-permute-start.55 = (f32[160]{0:T(256)S(1)}, f32[160]{0:T(256)S(1)}, u32[]{:S(2)}, u32[]{:S(2)}) collective-permute-start(f32[160]{0:T(256)S(1)} %multiply_reduce_fusion.6), channel_id=1, source_target_pairs={{0,1},{1,0},{2,3},{3,2},{4,5},{5,4},{6,7},{7,6},{8,9},{9,8},{10,11... | collective-permute-start | bytes 1928 | tf_op jit(solution)/shard_map/ppermute | solution.py:30
  589.3 24.9 %collective-permute-start.56 = (f32[160]{0:T(256)S(1)}, f32[160]{0:T(256)S(1)}, u32[]{:S(2)}, u32[]{:S(2)}) collective-permute-start(f32[160]{0:T(256)S(1)} %multiply_reduce_fusion.6), channel_id=1, source_target_pairs={{0,2},{1,3},{2,0},{3,1},{4,6},{5,7},{6,4},{7,5},{8,10},{9,11},{10,... | collective-permute-start | bytes 1928 | tf_op jit(solution)/shard_map/ppermute | solution.py:30
  664.3 30.9 %collective-permute-start.68 = (bf16[160,2048]{1,0:T(8,128)(2,1)}, bf16[160,2048]{1,0:T(8,128)(2,1)}, u32[]{:S(2)}, u32[]{:S(2)}) collective-permute-start(bf16[160,2048]{1,0:T(8,128)(2,1)} %get-tuple-element.188), channel_id=1, source_target_pairs={{0,2},{1,3},{2,0},{3,1},{4,6},{5,7},{6,4},{7,5},{8,10},{9,11},{10,... | collective-permute-start | bytes 1966088 | tf_op jit(solution)/shard_map/ppermute | solution.py:30
  665.7 29.5 %collective-permute-start.69 = (bf16[160,2048]{1,0:T(8,128)(2,1)}, bf16[160,2048]{1,0:T(8,128)(2,1)}, u32[]{:S(2)}, u32[]{:S(2)}) collective-permute-start(bf16[160,2048]{1,0:T(8,128)(2,1)} %get-tuple-element.189), channel_id=1, source_target_pairs={{0,3},{1,2},{2,1},{3,0},{4,7},{5,6},{6,5},{7,4},{8,11},{9,10},{10,... | collective-permute-start | bytes 1966088 | tf_op jit(solution)/shard_map/ppermute | solution.py:30
  678.9 169.1 %reduce-scatter.13.cloned.1.call-start = ((), (), s32[]{:S(2)}) async-start(), calls=%async_computation.14 | async-start | bytes 3604480 | tf_op jit(solution)/shard_map/reduce_scatter | solution.py:189
  679.0 55.9 %collective-permute-start.78 = (bf16[640,1408]{1,0:T(8,128)(2,1)}, bf16[640,1408]{1,0:T(8,128)(2,1)}, u32[]{:S(2)}, u32[]{:S(2)}) collective-permute-start(bf16[640,1408]{1,0:T(8,128)(2,1)} %get-tuple-element.142.refs_0_), channel_id=1, source_target_pairs={{0,4},{4,0},{1,5},{5,1},{2,6},{6,2},{3,7},{7,3},{8,12},{12,8},{9,1... | collective-permute-start | bytes 5406728 | tf_op jit(solution)/shard_map/ppermute | solution.py:34
  703.1 29.8 %collective-permute-start.76 = (bf16[160,2048]{1,0:T(8,128)(2,1)S(1)}, bf16[160,2048]{1,0:T(8,128)(2,1)S(1)}, u32[]{:S(2)}, u32[]{:S(2)}) collective-permute-start(bf16[160,2048]{1,0:T(8,128)(2,1)S(1)} %get-tuple-element.197.refs_2_.refs_0_), channel_id=1, source_target_pairs={{0,2},{1,3},{2,0},{3,1},{4,6},{5,7},{6,4},{7,5},{8,10},{9,11},{10,... | collective-permute-start | bytes 1966088 | tf_op jit(solution)/shard_map/ppermute | solution.py:30
  704.0 29.7 %collective-permute-start.77 = (bf16[160,2048]{1,0:T(8,128)(2,1)S(1)}, bf16[160,2048]{1,0:T(8,128)(2,1)}, u32[]{:S(2)}, u32[]{:S(2)}) collective-permute-start(bf16[160,2048]{1,0:T(8,128)(2,1)S(1)} %get-tuple-element.197.refs_2_.refs_0_), channel_id=1, source_target_pairs={{0,3},{1,2},{2,1},{3,0},{4,7},{5,6},{6,5},{7,4},{8,11},{9,10},{10,... | collective-permute-start | bytes 1966088 | tf_op jit(solution)/shard_map/ppermute | solution.py:30
  705.4 29.9 %collective-permute-start.79 = (bf16[160,2048]{1,0:T(8,128)(2,1)S(1)}, bf16[160,2048]{1,0:T(8,128)(2,1)}, u32[]{:S(2)}, u32[]{:S(2)}) collective-permute-start(bf16[160,2048]{1,0:T(8,128)(2,1)S(1)} %get-tuple-element.197.refs_2_.refs_0_), channel_id=1, source_target_pairs={{0,4},{4,0},{1,5},{5,1},{2,6},{6,2},{3,7},{7,3},{8,12},{12,8},{9,1... | collective-permute-start | bytes 1966088 | tf_op jit(solution)/shard_map/ppermute | solution.py:34
  734.9 26.7 %collective-permute-start.88 = (bf16[160,2048]{1,0:T(8,128)(2,1)S(1)}, bf16[160,2048]{1,0:T(8,128)(2,1)}, u32[]{:S(2)}, u32[]{:S(2)}) collective-permute-start(bf16[160,2048]{1,0:T(8,128)(2,1)S(1)} %copy-done.3), channel_id=1, source_target_pairs={{0,4},{4,0},{1,5},{5,1},{2,6},{6,2},{3,7},{7,3},{8,12},{12,8},{9,1... | collective-permute-start | bytes 1966088 | tf_op jit(solution)/shard_map/ppermute | solution.py:34
  735.4 39.2 %collective-permute-start.89 = (bf16[160,2048]{1,0:T(8,128)(2,1)S(1)}, bf16[160,2048]{1,0:T(8,128)(2,1)}, u32[]{:S(2)}, u32[]{:S(2)}) collective-permute-start(bf16[160,2048]{1,0:T(8,128)(2,1)S(1)} %copy-done.21), channel_id=1, source_target_pairs={{0,4},{4,0},{1,5},{5,1},{2,6},{6,2},{3,7},{7,3},{8,12},{12,8},{9,1... | collective-permute-start | bytes 1966088 | tf_op jit(solution)/shard_map/ppermute | solution.py:34
  736.1 39.9 %collective-permute-start.90 = (bf16[160,2048]{1,0:T(8,128)(2,1)}, bf16[160,2048]{1,0:T(8,128)(2,1)}, u32[]{:S(2)}, u32[]{:S(2)}) collective-permute-start(bf16[160,2048]{1,0:T(8,128)(2,1)} %copy-done.22), channel_id=1, source_target_pairs={{0,4},{4,0},{1,5},{5,1},{2,6},{6,2},{3,7},{7,3},{8,12},{12,8},{9,1... | collective-permute-start | bytes 1966088 | tf_op jit(solution)/shard_map/ppermute | solution.py:34
  737.1 40.5 %collective-permute-start.91 = (bf16[160,2048]{1,0:T(8,128)(2,1)}, bf16[160,2048]{1,0:T(8,128)(2,1)}, u32[]{:S(2)}, u32[]{:S(2)}) collective-permute-start(bf16[160,2048]{1,0:T(8,128)(2,1)} %copy-done.143), channel_id=1, source_target_pairs={{0,4},{4,0},{1,5},{5,1},{2,6},{6,2},{3,7},{7,3},{8,12},{12,8},{9,1... | collective-permute-start | bytes 1966088 | tf_op jit(solution)/shard_map/ppermute | solution.py:34
  760.3 217.0 %reduce-scatter.15.cloned.1.call-start = ((), (), s32[]{:S(2)}) async-start(), calls=%async_computation.15 | async-start | bytes 7208960 | tf_op jit(solution)/shard_map/reduce_scatter | solution.py:189
  774.6 20.0 %collective-permute-start.83 = (bf16[160,2048]{1,0:T(8,128)(2,1)}, bf16[160,2048]{1,0:T(8,128)(2,1)}, u32[]{:S(2)}, u32[]{:S(2)}) collective-permute-start(bf16[160,2048]{1,0:T(8,128)(2,1)} %get-tuple-element.208), channel_id=1, source_target_pairs={{0,1},{1,0},{2,3},{3,2},{4,5},{5,4},{6,7},{7,6},{8,9},{9,8},{10,11... | collective-permute-start | bytes 1966088 | tf_op jit(solution)/shard_map/ppermute | solution.py:30
  776.0 31.2 %collective-permute-start.84 = (bf16[160,2048]{1,0:T(8,128)(2,1)}, bf16[160,2048]{1,0:T(8,128)(2,1)}, u32[]{:S(2)}, u32[]{:S(2)}) collective-permute-start(bf16[160,2048]{1,0:T(8,128)(2,1)} %get-tuple-element.209), channel_id=1, source_target_pairs={{0,2},{1,3},{2,0},{3,1},{4,6},{5,7},{6,4},{7,5},{8,10},{9,11},{10,... | collective-permute-start | bytes 1966088 | tf_op jit(solution)/shard_map/ppermute | solution.py:30
  777.5 29.7 %collective-permute-start.85 = (bf16[160,2048]{1,0:T(8,128)(2,1)}, bf16[160,2048]{1,0:T(8,128)(2,1)}, u32[]{:S(2)}, u32[]{:S(2)}) collective-permute-start(bf16[160,2048]{1,0:T(8,128)(2,1)} %get-tuple-element.210), channel_id=1, source_target_pairs={{0,3},{1,2},{2,1},{3,0},{4,7},{5,6},{6,5},{7,4},{8,11},{9,10},{10,... | collective-permute-start | bytes 1966088 | tf_op jit(solution)/shard_map/ppermute | solution.py:30
  794.5 224.7 %reduce-scatter.17.cloned.1.call-start = ((), (), s32[]{:S(2)}) async-start(), calls=%async_computation.16 | async-start | bytes 5242880 | tf_op jit(solution)/shard_map/reduce_scatter | solution.py:189
  812.9 35.0 %collective-permute-start.92 = (bf16[160,2048]{1,0:T(8,128)(2,1)S(1)}, bf16[160,2048]{1,0:T(8,128)(2,1)S(1)}, u32[]{:S(2)}, u32[]{:S(2)}) collective-permute-start(bf16[160,2048]{1,0:T(8,128)(2,1)S(1)} %get-tuple-element.303.refs_0_.refs_12_), channel_id=1, source_target_pairs={{0,1},{1,0},{2,3},{3,2},{4,5},{5,4},{6,7},{7,6},{8,9},{9,8},{10,11... | collective-permute-start | bytes 1966088 | tf_op jit(solution)/shard_map/ppermute | solution.py:30
  814.2 33.8 %collective-permute-start.93 = (bf16[160,2048]{1,0:T(8,128)(2,1)S(1)}, bf16[160,2048]{1,0:T(8,128)(2,1)}, u32[]{:S(2)}, u32[]{:S(2)}) collective-permute-start(bf16[160,2048]{1,0:T(8,128)(2,1)S(1)} %get-tuple-element.303.refs_0_.refs_12_), channel_id=1, source_target_pairs={{0,2},{1,3},{2,0},{3,1},{4,6},{5,7},{6,4},{7,5},{8,10},{9,11},{10,... | collective-permute-start | bytes 1966088 | tf_op jit(solution)/shard_map/ppermute | solution.py:30
  815.1 32.9 %collective-permute-start.94 = (bf16[160,2048]{1,0:T(8,128)(2,1)S(1)}, bf16[160,2048]{1,0:T(8,128)(2,1)}, u32[]{:S(2)}, u32[]{:S(2)}) collective-permute-start(bf16[160,2048]{1,0:T(8,128)(2,1)S(1)} %get-tuple-element.303.refs_0_.refs_12_), channel_id=1, source_target_pairs={{0,3},{1,2},{2,1},{3,0},{4,7},{5,6},{6,5},{7,4},{8,11},{9,10},{10,... | collective-permute-start | bytes 1966088 | tf_op jit(solution)/shard_map/ppermute | solution.py:30
  818.2 25.0 %collective-permute-start.95 = (f32[160]{0:T(256)S(1)}, f32[160]{0:T(256)S(1)}, u32[]{:S(2)}, u32[]{:S(2)}) collective-permute-start(f32[160]{0:T(256)S(1)} %multiply_reduce_fusion.3), channel_id=1, source_target_pairs={{0,1},{1,0},{2,3},{3,2},{4,5},{5,4},{6,7},{7,6},{8,9},{9,8},{10,11... | collective-permute-start | bytes 1928 | tf_op jit(solution)/shard_map/ppermute | solution.py:30
  820.2 24.7 %collective-permute-start.96 = (f32[160]{0:T(256)S(1)}, f32[160]{0:T(256)S(1)}, u32[]{:S(2)}, u32[]{:S(2)}) collective-permute-start(f32[160]{0:T(256)S(1)} %multiply_reduce_fusion.3), channel_id=1, source_target_pairs={{0,2},{1,3},{2,0},{3,1},{4,6},{5,7},{6,4},{7,5},{8,10},{9,11},{10,... | collective-permute-start | bytes 1928 | tf_op jit(solution)/shard_map/ppermute | solution.py:30
  918.6 31.0 %collective-permute-start.98 = (bf16[160,2048]{1,0:T(8,128)(2,1)S(1)}, bf16[160,2048]{1,0:T(8,128)(2,1)S(1)}, u32[]{:S(2)}, u32[]{:S(2)}) collective-permute-start(bf16[160,2048]{1,0:T(8,128)(2,1)S(1)} %get-tuple-element.323), channel_id=1, source_target_pairs={{0,1},{1,0},{2,3},{3,2},{4,5},{5,4},{6,7},{7,6},{8,9},{9,8},{10,11... | collective-permute-start | bytes 1966088 | tf_op jit(solution)/shard_map/ppermute | solution.py:30
  920.0 29.6 %collective-permute-start.99 = (bf16[160,2048]{1,0:T(8,128)(2,1)S(1)}, bf16[160,2048]{1,0:T(8,128)(2,1)S(1)}, u32[]{:S(2)}, u32[]{:S(2)}) collective-permute-start(bf16[160,2048]{1,0:T(8,128)(2,1)S(1)} %get-tuple-element.325), channel_id=1, source_target_pairs={{0,2},{1,3},{2,0},{3,1},{4,6},{5,7},{6,4},{7,5},{8,10},{9,11},{10,... | collective-permute-start | bytes 1966088 | tf_op jit(solution)/shard_map/ppermute | solution.py:30
  929.4 34.3 %collective-permute-start.115 = (bf16[160,2048]{1,0:T(8,128)(2,1)S(1)}, bf16[160,2048]{1,0:T(8,128)(2,1)S(1)}, u32[]{:S(2)}, u32[]{:S(2)}) collective-permute-start(bf16[160,2048]{1,0:T(8,128)(2,1)S(1)} %get-tuple-element.322), channel_id=1, source_target_pairs={{0,1},{1,0},{2,3},{3,2},{4,5},{5,4},{6,7},{7,6},{8,9},{9,8},{10,11... | collective-permute-start | bytes 1966088 | tf_op jit(solution)/shard_map/ppermute | solution.py:30
  930.8 32.9 %collective-permute-start.116 = (bf16[160,2048]{1,0:T(8,128)(2,1)S(1)}, bf16[160,2048]{1,0:T(8,128)(2,1)}, u32[]{:S(2)}, u32[]{:S(2)}) collective-permute-start(bf16[160,2048]{1,0:T(8,128)(2,1)S(1)} %get-tuple-element.321), channel_id=1, source_target_pairs={{0,2},{1,3},{2,0},{3,1},{4,6},{5,7},{6,4},{7,5},{8,10},{9,11},{10,... | collective-permute-start | bytes 1966088 | tf_op jit(solution)/shard_map/ppermute | solution.py:30
  935.6 41.7 %collective-permute-start.117 = (bf16[160,2048]{1,0:T(8,128)(2,1)S(1)}, bf16[160,2048]{1,0:T(8,128)(2,1)}, u32[]{:S(2)}, u32[]{:S(2)}) collective-permute-start(bf16[160,2048]{1,0:T(8,128)(2,1)S(1)} %get-tuple-element.320), channel_id=1, source_target_pairs={{0,3},{1,2},{2,1},{3,0},{4,7},{5,6},{6,5},{7,4},{8,11},{9,10},{10,... | collective-permute-start | bytes 1966088 | tf_op jit(solution)/shard_map/ppermute | solution.py:30
  (234 other events, 4240.8 us)
Sparse Core Ops, SparseCore 0:
  10.5 67.4 all-gather.8
  80.1 76.8 all-gather.10
  159.2 108.6 all-gather.12
  269.9 80.6 all-gather.14
  352.1 108.5 all-gather.16
  462.7 57.3 all-gather.18
  522.9 54.3 reduce-scatter.6
  579.6 102.3 reduce-scatter.8
  684.3 77.2 reduce-scatter.10
  764.5 56.6 reduce-scatter.12
  823.6 102.3 reduce-scatter.14
  928.3 77.9 reduce-scatter.16

commit v4 on v3

--- a/solution.py
+++ b/solution.py
@@ -521,16 +521,16 @@
     def tall(*shards):
         return lax.all_gather(jnp.concatenate(shards, axis=0), SEQ, axis=1, tiled=True)
 
-    first_mix = side(w_input[0], w_forget[0], w_gate[0])
-    joined = tall(w_out[0], w_down[0])
-    mixes, outs, boths, downs = [first_mix], [(joined, 0)], [], [(joined, channels)]
+    mixes, boths, downs = [side(w_input[0], w_forget[0], w_gate[0], w_out[0].T)], [], []
     for layer in range(LAYERS):
         if layer > 0:
-            joined = tall(w_input[layer].T, w_forget[layer].T, w_gate[layer].T, w_out[layer])
-            mixes.append(joined)
-            outs.append((joined, 3 * channels))
-        boths.append(tall(w_up[layer].T, w_glu[layer].T))
-        if layer > 0:
+            mixes.append(tall(w_input[layer].T, w_forget[layer].T, w_gate[layer].T, w_out[layer]))
+        if layer < last_layer:
+            joined = tall(w_up[layer].T, w_glu[layer].T, w_down[layer])
+            boths.append((joined, 0))
+            downs.append((joined, 2 * hidden_units))
+        else:
+            boths.append((tall(w_up[layer].T, w_glu[layer].T), 0))
             downs.append((tall(w_down[layer]), 0))
 
     def rows_of(matrix_at, rows):
@@ -569,13 +569,17 @@
         squares = total_rows(jnp.sum(state * state, axis=1))
         inverse = lax.rsqrt(squares / model_width + epsilon)[:, None]
         loose = (state * gain * jax.nn.silu(proj_gate)).astype(bf16)
-        parts = cut(dot(loose, rows_of(outs[layer], channels)).astype(bf16), size)
+        if first_layer:
+            part = trans_dot(loose, mix[:, 3 * channels :])
+        else:
+            part = dot(loose, mix[3 * channels :])
+        parts = cut(part.astype(bf16), size)
         branch = scatter_rows(parts) * inverse[:row_count]
         middle = stream + branch
         unit_two, _ = rms_parts(middle)
         normed_two = (unit_two * norm_ffn[layer]).astype(bf16)
         normed_two = gather_rows(normed_two)
-        upward, gating, hidden = up_and_gate(normed_two, boths[layer], hidden_units)
+        upward, gating, hidden = up_and_gate(normed_two, boths[layer][0], hidden_units)
         if layer < last_layer:
             stream = middle + scatter_rows(cut(dot(hidden, rows_of(downs[layer], hidden_units)).astype(bf16), size))
         twin_rows = (twins(normed), twins(normed_two), twins([hidden]))
@@ -595,7 +599,7 @@
 
     final_middle, final_hidden = saved[last_layer][10], saved[last_layer][14]
     for layer in reversed(range(LAYERS)):
-        mix, both, first_layer = mixes[layer], boths[layer], layer == 0
+        mix, both, first_layer = mixes[layer], rows_of(boths[layer], 2 * hidden_units), layer == 0
         bound, gain = bounds[layer][None, :], gains[layer][None, :]
         (factor, twin_rows, normed, proj_input, proj_forget, proj_gate, entering, state, inverse,
          branch, middle, normed_two, upward, gating, hidden, unit) = saved[layer]
@@ -621,15 +625,20 @@
 
         grad_m_own = grad_middle.astype(bf16)
         grad_m_own = after(grad_m_own, *due(layer, "norm"))
-        grad_m = gather_rows(grad_m_own, *due(layer, "middle"))
+        if first_layer:
+            output = dot(after(final_hidden, grad_m_own), rows_of(downs[last_layer], hidden_units)).astype(bf16)
+            grad_m = gather_rows(grad_m_own, output, *due(layer, "middle"))
+            hidden_out = (final_middle + scatter_rows(cut(output, size))).astype(bf16)
+        else:
+            grad_m = gather_rows(grad_m_own, *due(layer, "middle"))
         inner = jnp.concatenate(
             gather_rows(jnp.sum(grad_m_own.astype(f32) * branch, axis=1)), axis=0
         )[:, None]
         adjoint, reach, grad_gate, mixed, gain_piece = over_channels(
-            functools.partial(back_kernel, size, model_width, trans_dot),
+            functools.partial(back_kernel, size, model_width, dot if first_layer else trans_dot),
             place_array,
             grad_m,
-            [(*outs[layer], False)],
+            [(mix, 3 * channels, first_layer)],
             (state, proj_gate, proj_forget, inverse, inner, keep, bound, gain),
             ((block_rows, f32), (block_rows, f32), (block_rows, bf16), (block_rows, bf16), (1, f32)),
             [pltpu.VMEM((block_rows, model_width), bf16), pltpu.VMEM((block_rows, min(LANES, channels)), f32)],
@@ -649,10 +658,6 @@
             True,
         )
         ready = [*all_m, *twin_mixed, *due(layer, "coming")]
-        if first_layer:
-            output = dot(after(final_hidden, adjoint), rows_of(downs[last_layer], hidden_units)).astype(bf16)
-            hidden_out = (final_middle + scatter_rows(cut(output, size))).astype(bf16)
-            ready.append(output)
         coming = after(coming, *ready)
         grad_input, grad_forget, bound_piece = over_channels(
             functools.partial(gates_kernel, size),
@@ -667,10 +672,12 @@
         )
         grad_three = (grad_input, grad_forget, grad_gate)
         joined = jnp.concatenate([grad_input, grad_forget, grad_gate], axis=1)
+        if first_layer:
+            joined = after(joined, hidden_out)
         (twin_joined,) = twins((joined,))
         if first_layer:
             low_part = outer([([joined, twin_joined], all_normed), ([mixed, *twin_mixed], all_m)])
-            part = trans_dot(after(joined, low_part), mix)
+            part = trans_dot(after(joined, low_part), mix[:, : 3 * channels])
         else:
             part = dot(joined, mix[: 3 * channels])
         part = part.astype(bf16)

time: 1040 us -> 1020 us (0.981)
  waiting for transfers between devices: 518 us -> 490 us
    all_gather x5 -> x4, waiting for transfers between devices: 105 us -> 91.2 us  [tall(): lax.all_gather(jnp.concatenate(shards, axis=0), SEQ, axis=1, tiled=True)]
    unnamed x340 -> x345, local copies, waits for them, and re-layouts: 40 us -> 44.3 us
    dot_general x7 -> x6, matrix products: 52 us -> 48.3 us  [dot(): return jnp.dot(left, right, preferred_element_type=f32)]
  transfers between devices with their start and end apart: 136 -> 135, of which waited for: 64 -> 55; matrix products, arithmetic and copies ran while one was open for 14% -> 15% of each run, Pallas kernels for 18% -> 18%
where the time goes in v4:
time: 1020 us; the launch traced here: 1010 us
  waiting for transfers between devices  490 us (48%)
  Pallas kernels  185 us (18%)
  starting transfers between devices  112 us (11%)
  local copies, waits for them, and re-layouts  77.4 us (8%)
  matrix products  58.8 us (6%)
  other arithmetic  53.4 us (5%)
  between operations  16.5 us (2%)
  blocking collectives  15 us (1%)
    ppermute x66, waiting for transfers between devices, exchange(): return lax.ppermute(values, 'fsdp', [(i, i ^ step) for i in range(size)])  365 us
    pallas_call x16, Pallas kernels, call(): pl.pallas_call(kernel, grid_spec=pltpu.PrefetchScalarGridSpec(num_scalar_...  185 us
    all_gather x4, waiting for transfers between devices, tall(): lax.all_gather(jnp.concatenate(shards, axis=0), SEQ, axis=1, tiled=True)  91.2 us
    ppermute x66, starting transfers between devices, exchange(): return lax.ppermute(values, 'fsdp', [(i, i ^ step) for i in range(size)])  80.4 us
    dot_general x6, matrix products, dot(): return jnp.dot(left, right, preferred_element_type=f32)  48.3 us
    unnamed x345, local copies, waits for them, and re-layouts  44.3 us
    ppermute x12, starting transfers between devices, entering_of(): lax.ppermute(pair, SEQ, [(i, i + sign * 2 * hop) for i in range(length) i...  20.9 us
  transfers between devices with their start and end apart: 135, of which 55 were waited for; matrix products, arithmetic and copies ran while one was open for 15% of the time, Pallas kernels for 18%

profile of v4, /device:TPU:0, one launch (start us, length us, event | category | flops | bytes accessed | tf_op | source)
XLA Modules:
  0.0 1009.3 jit_solution(10442494501008857434)
XLA Ops:
  30.5 13.7 %collective-permute-done.refs_1_.refs_5_ = bf16[160,2048]{1,0:T(8,128)(2,1)S(1)} collective-permute-done((bf16[160,2048]{1,0:T(8,128)(2,1)S(1)}, bf16[160,2048]{1,0:T(8,128)(2,1)S(1)}, u32[]{:S(2)}, u32[]{:S(2)}) %collective-permute-start) | collective-permute-done | bytes 655392 | tf_op jit(solution)/shard_map/ppermute | solution.py:30
  44.1 14.7 %collective-permute-done.1.refs_2_.refs_6_ = bf16[160,2048]{1,0:T(8,128)(2,1)S(1)} collective-permute-done((bf16[160,2048]{1,0:T(8,128)(2,1)S(1)}, bf16[160,2048]{1,0:T(8,128)(2,1)S(1)}, u32[]{:S(2)}, u32[]{:S(2)}) %collective-permute-start.1) | collective-permute-done | bytes 655392 | tf_op jit(solution)/shard_map/ppermute | solution.py:30
  64.7 12.6 %collective-permute-done.3.refs_3_.refs_1_ = bf16[160,2048]{1,0:T(8,128)(2,1)S(1)} collective-permute-done((bf16[160,2048]{1,0:T(8,128)(2,1)S(1)}, bf16[160,2048]{1,0:T(8,128)(2,1)S(1)}, u32[]{:S(2)}, u32[]{:S(2)}) %collective-permute-start.3) | collective-permute-done | bytes 655392 | tf_op jit(solution)/shard_map/ppermute | solution.py:30
  77.3 12.3 %collective-permute-done.4.refs_4_.refs_2_ = bf16[160,2048]{1,0:T(8,128)(2,1)} collective-permute-done((bf16[160,2048]{1,0:T(8,128)(2,1)S(1)}, bf16[160,2048]{1,0:T(8,128)(2,1)}, u32[]{:S(2)}, u32[]{:S(2)}) %collective-permute-start.4) | collective-permute-done | bytes 655392 | tf_op jit(solution)/shard_map/ppermute | solution.py:30
  89.6 6.5 all-gather.8.cloned.1.call-done.refs_4_.refs_5_.refs_6_
  96.2 13.3 %shard_map.237 = (f32[640,512]{1,0:T(8,128)}, f32[640,512]{1,0:T(8,128)}, f32[640,512]{1,0:T(8,128)}, f32[640,512]{1,0:T(8,128)}, f32[640,512]{1,0:T(8,128)}) custom-call(s32[1]{0:T(128)} %bitcast.place_ref, bf16[160,2048]{1,0:T(8,128)(2,1)S(1)} %fusion.38.refs_0_.refs_4_, bf16[160,2048]{1,0:T(8,128)(2,1)S(1)} %collective-permute-done.refs_1_.refs_5_, ...), custom_call_target="tpu_custom_call" | custom-call | flops 22145925120 | bytes 7864320 | tf_op jit(solution)/shard_map/pallas_call | solution.py:106
  113.5 3.7 collective-permute-start.8
  125.6 3.2 convolution_convert_fusion.2
  134.8 14.0 %collective-permute-done.10 = bf16[160,2048]{1,0:T(8,128)(2,1)S(1)} collective-permute-done((bf16[160,2048]{1,0:T(8,128)(2,1)}, bf16[160,2048]{1,0:T(8,128)(2,1)S(1)}, u32[]{:S(2)}, u32[]{:S(2)}) %collective-permute-start.10) | collective-permute-done | bytes 655392 | tf_op jit(solution)/shard_map/ppermute | solution.py:30
  148.8 13.0 %collective-permute-done.11 = bf16[160,2048]{1,0:T(8,128)(2,1)S(1)} collective-permute-done((bf16[160,2048]{1,0:T(8,128)(2,1)}, bf16[160,2048]{1,0:T(8,128)(2,1)S(1)}, u32[]{:S(2)}, u32[]{:S(2)}) %collective-permute-start.11) | collective-permute-done | bytes 655392 | tf_op jit(solution)/shard_map/ppermute | solution.py:30
  168.9 14.2 %collective-permute-done.16.refs_1_.refs_5_ = bf16[160,2048]{1,0:T(8,128)(2,1)S(1)} collective-permute-done((bf16[160,2048]{1,0:T(8,128)(2,1)S(1)}, bf16[160,2048]{1,0:T(8,128)(2,1)S(1)}, u32[]{:S(2)}, u32[]{:S(2)}) %collective-permute-start.16) | collective-permute-done | bytes 655392 | tf_op jit(solution)/shard_map/ppermute | solution.py:30
  183.1 11.4 %collective-permute-done.17.refs_2_.refs_6_ = bf16[160,2048]{1,0:T(8,128)(2,1)S(1)} collective-permute-done((bf16[160,2048]{1,0:T(8,128)(2,1)S(1)}, bf16[160,2048]{1,0:T(8,128)(2,1)S(1)}, u32[]{:S(2)}, u32[]{:S(2)}) %collective-permute-start.17) | collective-permute-done | bytes 655392 | tf_op jit(solution)/shard_map/ppermute | solution.py:30
  194.4 58.6 %all-gather.10.cloned.1.call-done.refs_4_.refs_5_ = bf16[4224,2048]{1,0:T(8,128)(2,1)} async-done(((bf16[4224,256]{1,0:T(8,128)(2,1)}), bf16[4224,2048]{1,0:T(8,128)(2,1)}) %all-gather.10.cloned.1.call-update) | async-done | bytes 17301520 | tf_op jit(solution)/shard_map/all_gather | solution.py:522
  253.1 15.1 %shard_map.238 = (bf16[640,1408]{1,0:T(8,128)(2,1)}, bf16[640,1408]{1,0:T(8,128)(2,1)}, bf16[640,1408]{1,0:T(8,128)(2,1)}) custom-call(bf16[160,2048]{1,0:T(8,128)(2,1)S(1)} %multiply_convert_fusion.3.refs_0_.refs_4_, bf16[160,2048]{1,0:T(8,128)(2,1)S(1)} %collective-permute-done.16.refs_1_.refs_5_, ...), custom_call_target="tpu_custom_call" | custom-call | flops 40600862720 | bytes 14417920 | tf_op jit(solution)/shard_map/pallas_call | solution.py:106
  268.1 7.4 fusion.18
  279.3 14.1 %collective-permute-done.19 = bf16[160,2048]{1,0:T(8,128)(2,1)S(1)} collective-permute-done((bf16[160,2048]{1,0:T(8,128)(2,1)S(1)}, bf16[160,2048]{1,0:T(8,128)(2,1)S(1)}, u32[]{:S(2)}, u32[]{:S(2)}) %collective-permute-start.19) | collective-permute-done | bytes 655392 | tf_op jit(solution)/shard_map/ppermute | solution.py:30
  293.4 14.6 %collective-permute-done.20 = bf16[160,2048]{1,0:T(8,128)(2,1)S(1)} collective-permute-done((bf16[160,2048]{1,0:T(8,128)(2,1)S(1)}, bf16[160,2048]{1,0:T(8,128)(2,1)S(1)}, u32[]{:S(2)}, u32[]{:S(2)}) %collective-permute-start.20) | collective-permute-done | bytes 655392 | tf_op jit(solution)/shard_map/ppermute | solution.py:30
  312.3 14.2 %collective-permute-done.22.refs_1_.refs_5_ = bf16[160,2048]{1,0:T(8,128)(2,1)S(1)} collective-permute-done((bf16[160,2048]{1,0:T(8,128)(2,1)S(1)}, bf16[160,2048]{1,0:T(8,128)(2,1)S(1)}, u32[]{:S(2)}, u32[]{:S(2)}) %collective-permute-start.22) | collective-permute-done | bytes 655392 | tf_op jit(solution)/shard_map/ppermute | solution.py:30
  326.5 13.4 %collective-permute-done.23.refs_2_.refs_6_ = bf16[160,2048]{1,0:T(8,128)(2,1)S(1)} collective-permute-done((bf16[160,2048]{1,0:T(8,128)(2,1)S(1)}, bf16[160,2048]{1,0:T(8,128)(2,1)S(1)}, u32[]{:S(2)}, u32[]{:S(2)}) %collective-permute-start.23) | collective-permute-done | bytes 655392 | tf_op jit(solution)/shard_map/ppermute | solution.py:30
  340.8 13.7 %shard_map.239 = (f32[640,512]{1,0:T(8,128)}, f32[640,512]{1,0:T(8,128)}, f32[640,512]{1,0:T(8,128)}, f32[640,512]{1,0:T(8,128)}, f32[640,512]{1,0:T(8,128)}) custom-call(s32[1]{0:T(128)} %bitcast.place_ref, bf16[160,2048]{1,0:T(8,128)(2,1)S(1)} %multiply_convert_fusion.2.refs_0_.refs_4_, bf16[160,2048]{1,0:T(8,128)(2,1)S(1)} %collective-permute-done.22.refs_1_.refs_5_, ...), custom_call_target="tpu_custom_call" | custom-call | flops 22145925120 | bytes 7864320 | tf_op jit(solution)/shard_map/pallas_call | solution.py:106
  358.6 3.8 collective-permute-start.27
  370.7 3.6 convolution_convert_fusion.1
  380.3 14.0 %collective-permute-done.29 = bf16[160,2048]{1,0:T(8,128)(2,1)S(1)} collective-permute-done((bf16[160,2048]{1,0:T(8,128)(2,1)}, bf16[160,2048]{1,0:T(8,128)(2,1)S(1)}, u32[]{:S(2)}, u32[]{:S(2)}) %collective-permute-start.29) | collective-permute-done | bytes 655392 | tf_op jit(solution)/shard_map/ppermute | solution.py:30
  394.3 11.7 %collective-permute-done.30 = bf16[160,2048]{1,0:T(8,128)(2,1)S(1)} collective-permute-done((bf16[160,2048]{1,0:T(8,128)(2,1)}, bf16[160,2048]{1,0:T(8,128)(2,1)S(1)}, u32[]{:S(2)}, u32[]{:S(2)}) %collective-permute-start.30) | collective-permute-done | bytes 655392 | tf_op jit(solution)/shard_map/ppermute | solution.py:30
  412.0 14.2 %collective-permute-done.35.refs_1_.refs_5_ = bf16[160,2048]{1,0:T(8,128)(2,1)S(1)} collective-permute-done((bf16[160,2048]{1,0:T(8,128)(2,1)S(1)}, bf16[160,2048]{1,0:T(8,128)(2,1)S(1)}, u32[]{:S(2)}, u32[]{:S(2)}) %collective-permute-start.35) | collective-permute-done | bytes 655392 | tf_op jit(solution)/shard_map/ppermute | solution.py:30
  426.2 11.4 %collective-permute-done.36.refs_2_.refs_6_ = bf16[160,2048]{1,0:T(8,128)(2,1)S(1)} collective-permute-done((bf16[160,2048]{1,0:T(8,128)(2,1)S(1)}, bf16[160,2048]{1,0:T(8,128)(2,1)S(1)}, u32[]{:S(2)}, u32[]{:S(2)}) %collective-permute-start.36) | collective-permute-done | bytes 655392 | tf_op jit(solution)/shard_map/ppermute | solution.py:30
  438.5 6.0 all-gather.14.cloned.1.call-done.refs_4_.refs_5_
  445.5 15.1 %shard_map.240 = (bf16[640,1408]{1,0:T(8,128)(2,1)}, bf16[640,1408]{1,0:T(8,128)(2,1)}, bf16[640,1408]{1,0:T(8,128)(2,1)}) custom-call(bf16[160,2048]{1,0:T(8,128)(2,1)S(1)} %multiply_convert_fusion.refs_0_.refs_4_, bf16[160,2048]{1,0:T(8,128)(2,1)S(1)} %collective-permute-done.35.refs_1_.refs_5_, bf16[160,2048]{1,0:T(8,128)(2,1)S(1)} %copy-done.31, ...), custom_call_target="tpu_custom_call" | custom-call | flops 40600862720 | bytes 14417920 | tf_op jit(solution)/shard_map/pallas_call | solution.py:106
  469.5 9.1 shard_map.241
  479.1 26.6 %all-gather.16.cloned.1.call-done = bf16[1,1408,2048]{2,1,0:T(8,128)(2,1)} async-done(((bf16[1,1408,256]{2,1,0:T(8,128)(2,1)}), bf16[1,1408,2048]{2,1,0:T(8,128)(2,1)}) %all-gather.16.cloned.1.call-update) | async-done | bytes 5767184 | tf_op jit(solution)/shard_map/all_gather | solution.py:522
  505.7 10.6 %shard_map.242 = (bf16[640,1408]{1,0:T(8,128)(2,1)}, bf16[640,1408]{1,0:T(8,128)(2,1)}) custom-call(bf16[160,2048]{1,0:T(8,128)(2,1)S(1)} %copy-done.1, bf16[160,2048]{1,0:T(8,128)(2,1)S(1)} %copy-done.27, bf16[160,2048]{1,0:T(8,128)(2,1)} %collective-permute-done.4.refs_4_.refs_2_, bf16[160,2048]{1,0:T(8,128)(2,1)} %collective-permute-done.5.refs_5_.refs_3_, ...), custom_call_target="tpu_custom_call" | custom-call | flops 20300431360 | bytes 7208960 | tf_op jit(solution)/shard_map/pallas_call | solution.py:106
  516.8 11.6 %fusion.15 = bf16[640,2048]{1,0:T(8,128)(2,1)S(1)} fusion(bf16[2816,2048]{1,0:T(8,128)(2,1)} %all-gather.14.cloned.1.call-done.refs_4_.refs_5_, bf16[640,1408]{1,0:T(8,128)(2,1)} %get-tuple-element.161.refs_2_, bf16[640,1408]{1,0:T(8,128)(2,1)} %get-tuple-element.167), kind=kOutput, calls=%fused_computation.15 | convolution fusion | flops 7390494720 | bytes 17760256 | tf_op jit(solution)/shard_map/dot_general | solution.py:94
  535.7 15.2 %shard_map.243 = bf16[2816,1024]{1,0:T(8,128)(2,1)} custom-call(s32[1]{0:T(128)} %bitcast.32.core_ref, bf16[640,1408]{1,0:T(8,128)(2,1)} %get-tuple-element.167, bf16[640,1408]{1,0:T(8,128)(2,1)} %copy-done.141, bf16[640,1408]{1,0:T(8,128)(2,1)} %get-tuple-element.161.refs_2_, bf16[640,1408]{1,0:T(8,128)(2,1)} %copy-done.142, ...), custom_call_target="tpu_custom_call" | custom-call | flops 81201725440 | bytes 28835840 | tf_op jit(solution)/shard_map/pallas_call | solution.py:106
  551.0 11.0 %collective-permute-done.44 = bf16[160,2048]{1,0:T(8,128)(2,1)} collective-permute-done((bf16[160,2048]{1,0:T(8,128)(2,1)}, bf16[160,2048]{1,0:T(8,128)(2,1)}, u32[]{:S(2)}, u32[]{:S(2)}) %collective-permute-start.44) | collective-permute-done | bytes 655392 | tf_op jit(solution)/shard_map/ppermute | solution.py:30
  576.4 20.9 %collective-permute-done.55 = f32[160]{0:T(256)S(1)} collective-permute-done((f32[160]{0:T(256)S(1)}, f32[160]{0:T(256)S(1)}, u32[]{:S(2)}, u32[]{:S(2)}) %collective-permute-start.55) | collective-permute-done | bytes 672 | tf_op jit(solution)/shard_map/ppermute | solution.py:30
  602.0 11.2 %shard_map.244 = (f32[640,512]{1,0:T(8,128)}, f32[640,512]{1,0:T(8,128)}, bf16[640,512]{1,0:T(8,128)(2,1)S(1)}, bf16[640,512]{1,0:T(8,128)(2,1)}, f32[1,512]{1,0:T(1,128)S(1)}) custom-call(s32[1]{0:T(128)} %bitcast.place_ref, bf16[160,2048]{1,0:T(8,128)(2,1)} %copy-done.58, bf16[160,2048]{1,0:T(8,128)(2,1)} %collective-permute-done.52.refs_1_.refs_13_, ...), custom_call_target="tpu_custom_call" | custom-call | flops 180224000 | bytes 64000 | tf_op jit(solution)/shard_map/pallas_call | solution.py:106
  621.4 4.1 collective-permute-done.59
  631.2 5.6 shard_map.245
  639.7 7.2 fusion.21
  649.6 12.3 %shard_map.246 = bf16[2048,1024]{1,0:T(8,128)(2,1)} custom-call(s32[1]{0:T(128)} %bitcast.32.core_ref, bf16[640,1536]{1,0:T(8,128)(2,1)} %copy-done.98, bf16[640,1536]{1,0:T(8,128)(2,1)} %collective-permute-done.70.refs_1_, bf16[640,512]{1,0:T(8,128)(2,1)S(1)} %copy-done.29, bf16[640,512]{1,0:T(8,128)(2,1)S(1)} %collective-permute-done.66.refs_3_, ...), custom_call_target="tpu_custom_call" | custom-call | flops 59055800320 | bytes 20971520 | tf_op jit(solution)/shard_map/pallas_call | solution.py:106
  665.6 14.3 %collective-permute-done.67 = bf16[160,2048]{1,0:T(8,128)(2,1)S(1)} collective-permute-done((bf16[160,2048]{1,0:T(8,128)(2,1)}, bf16[160,2048]{1,0:T(8,128)(2,1)S(1)}, u32[]{:S(2)}, u32[]{:S(2)}) %collective-permute-start.67) | collective-permute-done | bytes 655392 | tf_op jit(solution)/shard_map/ppermute | solution.py:30
  679.8 14.6 %collective-permute-done.68 = bf16[160,2048]{1,0:T(8,128)(2,1)S(1)} collective-permute-done((bf16[160,2048]{1,0:T(8,128)(2,1)}, bf16[160,2048]{1,0:T(8,128)(2,1)S(1)}, u32[]{:S(2)}, u32[]{:S(2)}) %collective-permute-start.68) | collective-permute-done | bytes 655392 | tf_op jit(solution)/shard_map/ppermute | solution.py:30
  697.1 3.2 fusion.78
  703.8 14.2 %collective-permute-done.75.refs_3_.refs_1_ = bf16[160,2048]{1,0:T(8,128)(2,1)S(1)} collective-permute-done((bf16[160,2048]{1,0:T(8,128)(2,1)S(1)}, bf16[160,2048]{1,0:T(8,128)(2,1)S(1)}, u32[]{:S(2)}, u32[]{:S(2)}) %collective-permute-start.75) | collective-permute-done | bytes 655392 | tf_op jit(solution)/shard_map/ppermute | solution.py:30
  718.0 13.4 %collective-permute-done.76.refs_4_.refs_2_ = bf16[160,2048]{1,0:T(8,128)(2,1)S(1)} collective-permute-done((bf16[160,2048]{1,0:T(8,128)(2,1)S(1)}, bf16[160,2048]{1,0:T(8,128)(2,1)S(1)}, u32[]{:S(2)}, u32[]{:S(2)}) %collective-permute-start.76) | collective-permute-done | bytes 655392 | tf_op jit(solution)/shard_map/ppermute | solution.py:30
  740.4 9.1 shard_map.247
  752.1 10.1 %shard_map.248 = (bf16[640,1408]{1,0:T(8,128)(2,1)}, bf16[640,1408]{1,0:T(8,128)(2,1)}) custom-call(bf16[160,2048]{1,0:T(8,128)(2,1)S(1)} %get-tuple-element.198.refs_2_.refs_0_, bf16[160,2048]{1,0:T(8,128)(2,1)S(1)} %copy-done.35, bf16[160,2048]{1,0:T(8,128)(2,1)S(1)} %copy-done.38, bf16[160,2048]{1,0:T(8,128)(2,1)} %collective-permute-done.77.refs_5_.refs_3_, ...), custom_call_target="tpu_custom_call" | custom-call | flops 20300431360 | bytes 7208960 | tf_op jit(solution)/shard_map/pallas_call | solution.py:106
  762.7 11.6 %fusion.27 = bf16[640,2048]{1,0:T(8,128)(2,1)S(1)} fusion(bf16[4224,2048]{1,0:T(8,128)(2,1)} %all-gather.10.cloned.1.call-done.refs_4_.refs_5_, bf16[640,1408]{1,0:T(8,128)(2,1)} %get-tuple-element.207.refs_2_, bf16[640,1408]{1,0:T(8,128)(2,1)} %get-tuple-element.212.refs_0_), kind=kOutput, calls=%fused_computation.19 | convolution fusion | flops 7390494720 | bytes 17760256 | tf_op jit(solution)/shard_map/dot_general | solution.py:94
  780.4 15.1 %shard_map.249 = bf16[2816,1024]{1,0:T(8,128)(2,1)} custom-call(s32[1]{0:T(128)} %bitcast.32.core_ref, bf16[640,1408]{1,0:T(8,128)(2,1)} %get-tuple-element.212.refs_0_, bf16[640,1408]{1,0:T(8,128)(2,1)} %collective-permute-done.86.refs_1_, bf16[640,1408]{1,0:T(8,128)(2,1)} %get-tuple-element.207.refs_2_, bf16[640,1408]{1,0:T(8,128)(2,1)} %copy-done.143, ...), custom_call_target="tpu_custom_call" | custom-call | flops 81201725440 | bytes 28835840 | tf_op jit(solution)/shard_map/pallas_call | solution.py:106
  795.6 11.8 %collective-permute-done.84 = bf16[160,2048]{1,0:T(8,128)(2,1)} collective-permute-done((bf16[160,2048]{1,0:T(8,128)(2,1)}, bf16[160,2048]{1,0:T(8,128)(2,1)}, u32[]{:S(2)}, u32[]{:S(2)}) %collective-permute-start.84) | collective-permute-done | bytes 655392 | tf_op jit(solution)/shard_map/ppermute | solution.py:30
  809.6 3.4 fusion.77
  821.4 7.0 convolution_convert_fusion
  831.8 15.9 %collective-permute-done.99 = f32[160]{0:T(256)S(1)} collective-permute-done((f32[160]{0:T(256)S(1)}, f32[160]{0:T(256)S(1)}, u32[]{:S(2)}, u32[]{:S(2)}) %collective-permute-start.99) | collective-permute-done | bytes 672 | tf_op jit(solution)/shard_map/ppermute | solution.py:30
  851.4 11.3 %shard_map.250 = (f32[640,512]{1,0:T(8,128)}, f32[640,512]{1,0:T(8,128)}, bf16[640,512]{1,0:T(8,128)(2,1)S(1)}, bf16[640,512]{1,0:T(8,128)(2,1)}, f32[1,512]{1,0:T(1,128)S(1)}) custom-call(s32[1]{0:T(128)} %bitcast.place_ref, bf16[160,2048]{1,0:T(8,128)(2,1)} %copy-done.56, bf16[160,2048]{1,0:T(8,128)(2,1)} %copy-done.91, bf16[160,2048]{1,0:T(8,128)(2,1)} %copy-done.93, ...), custom_call_target="tpu_custom_call" | custom-call | flops 180224000 | bytes 64000 | tf_op jit(solution)/shard_map/pallas_call | solution.py:106
  870.2 5.8 collective-permute-done.93
  882.1 6.3 shard_map.251
  891.1 3.4 collective-permute-done.111.refs_8_
  898.7 12.3 %shard_map.252 = bf16[2048,1024]{1,0:T(8,128)(2,1)} custom-call(s32[1]{0:T(128)} %bitcast.32.core_ref, bf16[640,1536]{1,0:T(8,128)(2,1)} %copy-done.78, bf16[640,1536]{1,0:T(8,128)(2,1)} %copy-done.139, bf16[640,512]{1,0:T(8,128)(2,1)S(1)} %copy-done.28, bf16[640,512]{1,0:T(8,128)(2,1)S(1)} %collective-permute-done.109.refs_3_, ...), custom_call_target="tpu_custom_call" | custom-call | flops 59055800320 | bytes 20971520 | tf_op jit(solution)/shard_map/pallas_call | solution.py:106
  912.7 7.3 fusion.24
  929.4 9.6 collective-permute-done.115
  939.0 12.6 %collective-permute-done.116 = bf16[160,2048]{1,0:T(8,128)(2,1)} collective-permute-done((bf16[160,2048]{1,0:T(8,128)(2,1)S(1)}, bf16[160,2048]{1,0:T(8,128)(2,1)}, u32[]{:S(2)}, u32[]{:S(2)}) %collective-permute-start.116) | collective-permute-done | bytes 655392 | tf_op jit(solution)/shard_map/ppermute | solution.py:30
  955.3 3.4 fusion.42
  967.4 3.4 copy.123
  970.8 15.0 %all-gather.1 = f32[64,512]{1,0:T(8,128)S(1)} all-gather(f32[8,512]{1,0:T(8,128)S(1)} %concatenate.75), channel_id=3, replica_groups=mesh['chip'=4,'core'=2,'fsdp'=4] {'chip','core'}, dimensions={0}, use_global_device_ids=true | all-gather | bytes 147456 | tf_op jit(solution)/shard_map/all_gather | solution.py:484
  (743 shorter events, 250.0 us)
Async XLA Ops:
  7.2 89.0 %all-gather.8.cloned.1.call-start = ((), (), s32[]{:S(2)}) async-start(), calls=%async_computation.6 | async-start | bytes 9437184 | tf_op jit(solution)/shard_map/all_gather | solution.py:519
  11.3 241.8 %all-gather.10.cloned.1.call-start = ((), (), s32[]{:S(2)}) async-start(), calls=%async_computation.7 | async-start | bytes 19464192 | tf_op jit(solution)/shard_map/all_gather | solution.py:522
  19.7 321.1 %all-gather.12.cloned.1.call-start = ((), (), s32[]{:S(2)}) async-start(), calls=%async_computation.8 | async-start | bytes 9437184 | tf_op jit(solution)/shard_map/all_gather | solution.py:522
  22.2 422.2 %all-gather.14.cloned.1.call-start = ((), (), s32[]{:S(2)}) async-start(), calls=%async_computation.9 | async-start | bytes 12976128 | tf_op jit(solution)/shard_map/all_gather | solution.py:522
  24.0 481.6 %all-gather.16.cloned.1.call-start = ((), (), s32[]{:S(2)}) async-start(), calls=%async_computation.16 | async-start | bytes 6488064 | tf_op jit(solution)/shard_map/all_gather | solution.py:522
  25.6 18.5 %collective-permute-start = (bf16[160,2048]{1,0:T(8,128)(2,1)S(1)}, bf16[160,2048]{1,0:T(8,128)(2,1)S(1)}, u32[]{:S(2)}, u32[]{:S(2)}) collective-permute-start(bf16[160,2048]{1,0:T(8,128)(2,1)S(1)} %fusion.38.refs_0_.refs_4_), channel_id=1, source_target_pairs={{0,1},{1,0},{2,3},{3,2},{4,5},{5,4},{6,7},{7,6},{8,9},{9,8},{10,11... | collective-permute-start | bytes 1966088 | tf_op jit(solution)/shard_map/ppermute | solution.py:30
  28.6 30.2 %collective-permute-start.1 = (bf16[160,2048]{1,0:T(8,128)(2,1)S(1)}, bf16[160,2048]{1,0:T(8,128)(2,1)S(1)}, u32[]{:S(2)}, u32[]{:S(2)}) collective-permute-start(bf16[160,2048]{1,0:T(8,128)(2,1)S(1)} %fusion.38.refs_0_.refs_4_), channel_id=1, source_target_pairs={{0,2},{1,3},{2,0},{3,1},{4,6},{5,7},{6,4},{7,5},{8,10},{9,11},{10,... | collective-permute-start | bytes 1966088 | tf_op jit(solution)/shard_map/ppermute | solution.py:30
  30.1 29.6 %collective-permute-start.2 = (bf16[160,2048]{1,0:T(8,128)(2,1)S(1)}, bf16[160,2048]{1,0:T(8,128)(2,1)}, u32[]{:S(2)}, u32[]{:S(2)}) collective-permute-start(bf16[160,2048]{1,0:T(8,128)(2,1)S(1)} %fusion.38.refs_0_.refs_4_), channel_id=1, source_target_pairs={{0,3},{1,2},{2,1},{3,0},{4,7},{5,6},{6,5},{7,4},{8,11},{9,10},{10,... | collective-permute-start | bytes 1966088 | tf_op jit(solution)/shard_map/ppermute | solution.py:30
  60.2 29.5 %collective-permute-start.4 = (bf16[160,2048]{1,0:T(8,128)(2,1)S(1)}, bf16[160,2048]{1,0:T(8,128)(2,1)}, u32[]{:S(2)}, u32[]{:S(2)}) collective-permute-start(bf16[160,2048]{1,0:T(8,128)(2,1)S(1)} %copy-done), channel_id=1, source_target_pairs={{0,2},{1,3},{2,0},{3,1},{4,6},{5,7},{6,4},{7,5},{8,10},{9,11},{10,... | collective-permute-start | bytes 1966088 | tf_op jit(solution)/shard_map/ppermute | solution.py:30
  61.7 27.9 %collective-permute-start.5 = (bf16[160,2048]{1,0:T(8,128)(2,1)S(1)}, bf16[160,2048]{1,0:T(8,128)(2,1)}, u32[]{:S(2)}, u32[]{:S(2)}) collective-permute-start(bf16[160,2048]{1,0:T(8,128)(2,1)S(1)} %copy-done), channel_id=1, source_target_pairs={{0,3},{1,2},{2,1},{3,0},{4,7},{5,6},{6,5},{7,4},{8,11},{9,10},{10,... | collective-permute-start | bytes 1966088 | tf_op jit(solution)/shard_map/ppermute | solution.py:30
  130.9 17.9 %collective-permute-start.10 = (bf16[160,2048]{1,0:T(8,128)(2,1)}, bf16[160,2048]{1,0:T(8,128)(2,1)S(1)}, u32[]{:S(2)}, u32[]{:S(2)}) collective-permute-start(bf16[160,2048]{1,0:T(8,128)(2,1)} %get-tuple-element.346), channel_id=1, source_target_pairs={{0,1},{1,0},{2,3},{3,2},{4,5},{5,4},{6,7},{7,6},{8,9},{9,8},{10,11... | collective-permute-start | bytes 1966088 | tf_op jit(solution)/shard_map/ppermute | solution.py:30
  132.6 29.2 %collective-permute-start.11 = (bf16[160,2048]{1,0:T(8,128)(2,1)}, bf16[160,2048]{1,0:T(8,128)(2,1)S(1)}, u32[]{:S(2)}, u32[]{:S(2)}) collective-permute-start(bf16[160,2048]{1,0:T(8,128)(2,1)} %get-tuple-element.348), channel_id=1, source_target_pairs={{0,2},{1,3},{2,0},{3,1},{4,6},{5,7},{6,4},{7,5},{8,10},{9,11},{10,... | collective-permute-start | bytes 1966088 | tf_op jit(solution)/shard_map/ppermute | solution.py:30
  134.1 27.7 %collective-permute-start.12 = (bf16[160,2048]{1,0:T(8,128)(2,1)}, bf16[160,2048]{1,0:T(8,128)(2,1)S(1)}, u32[]{:S(2)}, u32[]{:S(2)}) collective-permute-start(bf16[160,2048]{1,0:T(8,128)(2,1)} %get-tuple-element.347), channel_id=1, source_target_pairs={{0,3},{1,2},{2,1},{3,0},{4,7},{5,6},{6,5},{7,4},{8,11},{9,10},{10,... | collective-permute-start | bytes 1966088 | tf_op jit(solution)/shard_map/ppermute | solution.py:30
  166.3 28.1 %collective-permute-start.17 = (bf16[160,2048]{1,0:T(8,128)(2,1)S(1)}, bf16[160,2048]{1,0:T(8,128)(2,1)S(1)}, u32[]{:S(2)}, u32[]{:S(2)}) collective-permute-start(bf16[160,2048]{1,0:T(8,128)(2,1)S(1)} %multiply_convert_fusion.3.refs_0_.refs_4_), channel_id=1, source_target_pairs={{0,2},{1,3},{2,0},{3,1},{4,6},{5,7},{6,4},{7,5},{8,10},{9,11},{10,... | collective-permute-start | bytes 1966088 | tf_op jit(solution)/shard_map/ppermute | solution.py:30
  167.4 27.0 %collective-permute-start.18 = (bf16[160,2048]{1,0:T(8,128)(2,1)S(1)}, bf16[160,2048]{1,0:T(8,128)(2,1)S(1)}, u32[]{:S(2)}, u32[]{:S(2)}) collective-permute-start(bf16[160,2048]{1,0:T(8,128)(2,1)S(1)} %multiply_convert_fusion.3.refs_0_.refs_4_), channel_id=1, source_target_pairs={{0,3},{1,2},{2,1},{3,0},{4,7},{5,6},{6,5},{7,4},{8,11},{9,10},{10,... | collective-permute-start | bytes 1966088 | tf_op jit(solution)/shard_map/ppermute | solution.py:30
  277.3 30.6 %collective-permute-start.20 = (bf16[160,2048]{1,0:T(8,128)(2,1)S(1)}, bf16[160,2048]{1,0:T(8,128)(2,1)S(1)}, u32[]{:S(2)}, u32[]{:S(2)}) collective-permute-start(bf16[160,2048]{1,0:T(8,128)(2,1)S(1)} %get-tuple-element.345), channel_id=1, source_target_pairs={{0,2},{1,3},{2,0},{3,1},{4,6},{5,7},{6,4},{7,5},{8,10},{9,11},{10,... | collective-permute-start | bytes 1966088 | tf_op jit(solution)/shard_map/ppermute | solution.py:30
  278.8 29.2 %collective-permute-start.21 = (bf16[160,2048]{1,0:T(8,128)(2,1)S(1)}, bf16[160,2048]{1,0:T(8,128)(2,1)S(1)}, u32[]{:S(2)}, u32[]{:S(2)}) collective-permute-start(bf16[160,2048]{1,0:T(8,128)(2,1)S(1)} %get-tuple-element.344), channel_id=1, source_target_pairs={{0,3},{1,2},{2,1},{3,0},{4,7},{5,6},{6,5},{7,4},{8,11},{9,10},{10,... | collective-permute-start | bytes 1966088 | tf_op jit(solution)/shard_map/ppermute | solution.py:30
  310.0 29.9 %collective-permute-start.23 = (bf16[160,2048]{1,0:T(8,128)(2,1)S(1)}, bf16[160,2048]{1,0:T(8,128)(2,1)S(1)}, u32[]{:S(2)}, u32[]{:S(2)}) collective-permute-start(bf16[160,2048]{1,0:T(8,128)(2,1)S(1)} %multiply_convert_fusion.2.refs_0_.refs_4_), channel_id=1, source_target_pairs={{0,2},{1,3},{2,0},{3,1},{4,6},{5,7},{6,4},{7,5},{8,10},{9,11},{10,... | collective-permute-start | bytes 1966088 | tf_op jit(solution)/shard_map/ppermute | solution.py:30
  310.9 29.9 %collective-permute-start.24 = (bf16[160,2048]{1,0:T(8,128)(2,1)S(1)}, bf16[160,2048]{1,0:T(8,128)(2,1)}, u32[]{:S(2)}, u32[]{:S(2)}) collective-permute-start(bf16[160,2048]{1,0:T(8,128)(2,1)S(1)} %multiply_convert_fusion.2.refs_0_.refs_4_), channel_id=1, source_target_pairs={{0,3},{1,2},{2,1},{3,0},{4,7},{5,6},{6,5},{7,4},{8,11},{9,10},{10,... | collective-permute-start | bytes 1966088 | tf_op jit(solution)/shard_map/ppermute | solution.py:30
  363.7 199.1 %reduce-scatter.7.cloned.1.call-start = ((), (), s32[]{:S(2)}) async-start(), calls=%async_computation.10 | async-start | bytes 3604480 | tf_op jit(solution)/shard_map/reduce_scatter | solution.py:189
  376.4 17.9 %collective-permute-start.29 = (bf16[160,2048]{1,0:T(8,128)(2,1)}, bf16[160,2048]{1,0:T(8,128)(2,1)S(1)}, u32[]{:S(2)}, u32[]{:S(2)}) collective-permute-start(bf16[160,2048]{1,0:T(8,128)(2,1)} %get-tuple-element.340), channel_id=1, source_target_pairs={{0,1},{1,0},{2,3},{3,2},{4,5},{5,4},{6,7},{7,6},{8,9},{9,8},{10,11... | collective-permute-start | bytes 1966088 | tf_op jit(solution)/shard_map/ppermute | solution.py:30
  377.0 28.9 %collective-permute-start.30 = (bf16[160,2048]{1,0:T(8,128)(2,1)}, bf16[160,2048]{1,0:T(8,128)(2,1)S(1)}, u32[]{:S(2)}, u32[]{:S(2)}) collective-permute-start(bf16[160,2048]{1,0:T(8,128)(2,1)} %get-tuple-element.342), channel_id=1, source_target_pairs={{0,2},{1,3},{2,0},{3,1},{4,6},{5,7},{6,4},{7,5},{8,10},{9,11},{10,... | collective-permute-start | bytes 1966088 | tf_op jit(solution)/shard_map/ppermute | solution.py:30
  378.6 27.4 %collective-permute-start.31 = (bf16[160,2048]{1,0:T(8,128)(2,1)}, bf16[160,2048]{1,0:T(8,128)(2,1)}, u32[]{:S(2)}, u32[]{:S(2)}) collective-permute-start(bf16[160,2048]{1,0:T(8,128)(2,1)} %get-tuple-element.341), channel_id=1, source_target_pairs={{0,3},{1,2},{2,1},{3,0},{4,7},{5,6},{6,5},{7,4},{8,11},{9,10},{10,... | collective-permute-start | bytes 1966088 | tf_op jit(solution)/shard_map/ppermute | solution.py:30
  409.7 27.9 %collective-permute-start.36 = (bf16[160,2048]{1,0:T(8,128)(2,1)S(1)}, bf16[160,2048]{1,0:T(8,128)(2,1)S(1)}, u32[]{:S(2)}, u32[]{:S(2)}) collective-permute-start(bf16[160,2048]{1,0:T(8,128)(2,1)S(1)} %multiply_convert_fusion.refs_0_.refs_4_), channel_id=1, source_target_pairs={{0,2},{1,3},{2,0},{3,1},{4,6},{5,7},{6,4},{7,5},{8,10},{9,11},{10,... | collective-permute-start | bytes 1966088 | tf_op jit(solution)/shard_map/ppermute | solution.py:30
  410.6 27.9 %collective-permute-start.37 = (bf16[160,2048]{1,0:T(8,128)(2,1)S(1)}, bf16[160,2048]{1,0:T(8,128)(2,1)}, u32[]{:S(2)}, u32[]{:S(2)}) collective-permute-start(bf16[160,2048]{1,0:T(8,128)(2,1)S(1)} %multiply_convert_fusion.refs_0_.refs_4_), channel_id=1, source_target_pairs={{0,3},{1,2},{2,1},{3,0},{4,7},{5,6},{6,5},{7,4},{8,11},{9,10},{10,... | collective-permute-start | bytes 1966088 | tf_op jit(solution)/shard_map/ppermute | solution.py:30
  466.2 50.3 %collective-permute-start.48 = (bf16[160,2048]{1,0:T(8,128)(2,1)S(1)}, bf16[160,2048]{1,0:T(8,128)(2,1)}, u32[]{:S(2)}, u32[]{:S(2)}) collective-permute-start(bf16[160,2048]{1,0:T(8,128)(2,1)S(1)} %multiply_convert_fusion.refs_0_.refs_4_), channel_id=1, source_target_pairs={{0,4},{4,0},{1,5},{5,1},{2,6},{6,2},{3,7},{7,3},{8,12},{12,8},{9,1... | collective-permute-start | bytes 1966088 | tf_op jit(solution)/shard_map/ppermute | solution.py:34
  468.6 61.1 %collective-permute-start.49 = (bf16[160,2048]{1,0:T(8,128)(2,1)S(1)}, bf16[160,2048]{1,0:T(8,128)(2,1)}, u32[]{:S(2)}, u32[]{:S(2)}) collective-permute-start(bf16[160,2048]{1,0:T(8,128)(2,1)S(1)} %collective-permute-done.35.refs_1_.refs_5_), channel_id=1, source_target_pairs={{0,4},{4,0},{1,5},{5,1},{2,6},{6,2},{3,7},{7,3},{8,12},{12,8},{9,1... | collective-permute-start | bytes 1966088 | tf_op jit(solution)/shard_map/ppermute | solution.py:34
  469.0 61.9 %collective-permute-start.50 = (bf16[160,2048]{1,0:T(8,128)(2,1)}, bf16[160,2048]{1,0:T(8,128)(2,1)}, u32[]{:S(2)}, u32[]{:S(2)}) collective-permute-start(bf16[160,2048]{1,0:T(8,128)(2,1)} %copy-done.30), channel_id=1, source_target_pairs={{0,4},{4,0},{1,5},{5,1},{2,6},{6,2},{3,7},{7,3},{8,12},{12,8},{9,1... | collective-permute-start | bytes 1966088 | tf_op jit(solution)/shard_map/ppermute | solution.py:34
  469.1 63.3 %collective-permute-start.51 = (bf16[160,2048]{1,0:T(8,128)(2,1)}, bf16[160,2048]{1,0:T(8,128)(2,1)}, u32[]{:S(2)}, u32[]{:S(2)}) collective-permute-start(bf16[160,2048]{1,0:T(8,128)(2,1)} %collective-permute-done.37.refs_3_.refs_7_), channel_id=1, source_target_pairs={{0,4},{4,0},{1,5},{5,1},{2,6},{6,2},{3,7},{7,3},{8,12},{12,8},{9,1... | collective-permute-start | bytes 1966088 | tf_op jit(solution)/shard_map/ppermute | solution.py:34
  478.6 253.6 %reduce-scatter.9.cloned.1.call-start = ((), (), s32[]{:S(2)}) async-start(), calls=%async_computation.11 | async-start | bytes 7208960 | tf_op jit(solution)/shard_map/reduce_scatter | solution.py:189
  529.7 21.3 %collective-permute-start.43 = (bf16[160,2048]{1,0:T(8,128)(2,1)}, bf16[160,2048]{1,0:T(8,128)(2,1)}, u32[]{:S(2)}, u32[]{:S(2)}) collective-permute-start(bf16[160,2048]{1,0:T(8,128)(2,1)} %get-tuple-element.163), channel_id=1, source_target_pairs={{0,1},{1,0},{2,3},{3,2},{4,5},{5,4},{6,7},{7,6},{8,9},{9,8},{10,11... | collective-permute-start | bytes 1966088 | tf_op jit(solution)/shard_map/ppermute | solution.py:30
  530.9 31.1 %collective-permute-start.44 = (bf16[160,2048]{1,0:T(8,128)(2,1)}, bf16[160,2048]{1,0:T(8,128)(2,1)}, u32[]{:S(2)}, u32[]{:S(2)}) collective-permute-start(bf16[160,2048]{1,0:T(8,128)(2,1)} %get-tuple-element.164), channel_id=1, source_target_pairs={{0,2},{1,3},{2,0},{3,1},{4,6},{5,7},{6,4},{7,5},{8,10},{9,11},{10,... | collective-permute-start | bytes 1966088 | tf_op jit(solution)/shard_map/ppermute | solution.py:30
  532.4 29.6 %collective-permute-start.45 = (bf16[160,2048]{1,0:T(8,128)(2,1)}, bf16[160,2048]{1,0:T(8,128)(2,1)}, u32[]{:S(2)}, u32[]{:S(2)}) collective-permute-start(bf16[160,2048]{1,0:T(8,128)(2,1)} %get-tuple-element.165), channel_id=1, source_target_pairs={{0,3},{1,2},{2,1},{3,0},{4,7},{5,6},{6,5},{7,4},{8,11},{9,10},{10,... | collective-permute-start | bytes 1966088 | tf_op jit(solution)/shard_map/ppermute | solution.py:30
  550.9 211.6 %reduce-scatter.11.cloned.1.call-start = ((), (), s32[]{:S(2)}) async-start(), calls=%async_computation.12 | async-start | bytes 5242880 | tf_op jit(solution)/shard_map/reduce_scatter | solution.py:189
  566.8 35.1 %collective-permute-start.52 = (bf16[160,2048]{1,0:T(8,128)(2,1)S(1)}, bf16[160,2048]{1,0:T(8,128)(2,1)}, u32[]{:S(2)}, u32[]{:S(2)}) collective-permute-start(bf16[160,2048]{1,0:T(8,128)(2,1)S(1)} %fusion.75.refs_0_.refs_12_), channel_id=1, source_target_pairs={{0,1},{1,0},{2,3},{3,2},{4,5},{5,4},{6,7},{7,6},{8,9},{9,8},{10,11... | collective-permute-start | bytes 1966088 | tf_op jit(solution)/shard_map/ppermute | solution.py:30
  568.4 33.6 %collective-permute-start.53 = (bf16[160,2048]{1,0:T(8,128)(2,1)S(1)}, bf16[160,2048]{1,0:T(8,128)(2,1)}, u32[]{:S(2)}, u32[]{:S(2)}) collective-permute-start(bf16[160,2048]{1,0:T(8,128)(2,1)S(1)} %fusion.75.refs_0_.refs_12_), channel_id=1, source_target_pairs={{0,2},{1,3},{2,0},{3,1},{4,6},{5,7},{6,4},{7,5},{8,10},{9,11},{10,... | collective-permute-start | bytes 1966088 | tf_op jit(solution)/shard_map/ppermute | solution.py:30
  569.8 32.2 %collective-permute-start.54 = (bf16[160,2048]{1,0:T(8,128)(2,1)S(1)}, bf16[160,2048]{1,0:T(8,128)(2,1)}, u32[]{:S(2)}, u32[]{:S(2)}) collective-permute-start(bf16[160,2048]{1,0:T(8,128)(2,1)S(1)} %fusion.75.refs_0_.refs_12_), channel_id=1, source_target_pairs={{0,3},{1,2},{2,1},{3,0},{4,7},{5,6},{6,5},{7,4},{8,11},{9,10},{10,... | collective-permute-start | bytes 1966088 | tf_op jit(solution)/shard_map/ppermute | solution.py:30
  572.6 24.7 %collective-permute-start.55 = (f32[160]{0:T(256)S(1)}, f32[160]{0:T(256)S(1)}, u32[]{:S(2)}, u32[]{:S(2)}) collective-permute-start(f32[160]{0:T(256)S(1)} %multiply_reduce_fusion.6), channel_id=1, source_target_pairs={{0,1},{1,0},{2,3},{3,2},{4,5},{5,4},{6,7},{7,6},{8,9},{9,8},{10,11... | collective-permute-start | bytes 1928 | tf_op jit(solution)/shard_map/ppermute | solution.py:30
  574.8 24.8 %collective-permute-start.56 = (f32[160]{0:T(256)S(1)}, f32[160]{0:T(256)S(1)}, u32[]{:S(2)}, u32[]{:S(2)}) collective-permute-start(f32[160]{0:T(256)S(1)} %multiply_reduce_fusion.6), channel_id=1, source_target_pairs={{0,2},{1,3},{2,0},{3,1},{4,6},{5,7},{6,4},{7,5},{8,10},{9,11},{10,... | collective-permute-start | bytes 1928 | tf_op jit(solution)/shard_map/ppermute | solution.py:30
  661.9 189.4 %reduce-scatter.13.cloned.1.call-start = ((), (), s32[]{:S(2)}) async-start(), calls=%async_computation.13 | async-start | bytes 3604480 | tf_op jit(solution)/shard_map/reduce_scatter | solution.py:189
  663.6 30.9 %collective-permute-start.68 = (bf16[160,2048]{1,0:T(8,128)(2,1)}, bf16[160,2048]{1,0:T(8,128)(2,1)S(1)}, u32[]{:S(2)}, u32[]{:S(2)}) collective-permute-start(bf16[160,2048]{1,0:T(8,128)(2,1)} %get-tuple-element.189), channel_id=1, source_target_pairs={{0,2},{1,3},{2,0},{3,1},{4,6},{5,7},{6,4},{7,5},{8,10},{9,11},{10,... | collective-permute-start | bytes 1966088 | tf_op jit(solution)/shard_map/ppermute | solution.py:30
  664.9 29.5 %collective-permute-start.69 = (bf16[160,2048]{1,0:T(8,128)(2,1)}, bf16[160,2048]{1,0:T(8,128)(2,1)S(1)}, u32[]{:S(2)}, u32[]{:S(2)}) collective-permute-start(bf16[160,2048]{1,0:T(8,128)(2,1)} %get-tuple-element.190), channel_id=1, source_target_pairs={{0,3},{1,2},{2,1},{3,0},{4,7},{5,6},{6,5},{7,4},{8,11},{9,10},{10,... | collective-permute-start | bytes 1966088 | tf_op jit(solution)/shard_map/ppermute | solution.py:30
  665.6 71.5 %collective-permute-start.78 = (bf16[640,1408]{1,0:T(8,128)(2,1)}, bf16[640,1408]{1,0:T(8,128)(2,1)}, u32[]{:S(2)}, u32[]{:S(2)}) collective-permute-start(bf16[640,1408]{1,0:T(8,128)(2,1)} %get-tuple-element.143.refs_0_), channel_id=1, source_target_pairs={{0,4},{4,0},{1,5},{5,1},{2,6},{6,2},{3,7},{7,3},{8,12},{12,8},{9,1... | collective-permute-start | bytes 5406728 | tf_op jit(solution)/shard_map/ppermute | solution.py:34
  701.4 30.0 %collective-permute-start.76 = (bf16[160,2048]{1,0:T(8,128)(2,1)S(1)}, bf16[160,2048]{1,0:T(8,128)(2,1)S(1)}, u32[]{:S(2)}, u32[]{:S(2)}) collective-permute-start(bf16[160,2048]{1,0:T(8,128)(2,1)S(1)} %get-tuple-element.198.refs_2_.refs_0_), channel_id=1, source_target_pairs={{0,2},{1,3},{2,0},{3,1},{4,6},{5,7},{6,4},{7,5},{8,10},{9,11},{10,... | collective-permute-start | bytes 1966088 | tf_op jit(solution)/shard_map/ppermute | solution.py:30
  702.4 29.9 %collective-permute-start.77 = (bf16[160,2048]{1,0:T(8,128)(2,1)S(1)}, bf16[160,2048]{1,0:T(8,128)(2,1)}, u32[]{:S(2)}, u32[]{:S(2)}) collective-permute-start(bf16[160,2048]{1,0:T(8,128)(2,1)S(1)} %get-tuple-element.198.refs_2_.refs_0_), channel_id=1, source_target_pairs={{0,3},{1,2},{2,1},{3,0},{4,7},{5,6},{6,5},{7,4},{8,11},{9,10},{10,... | collective-permute-start | bytes 1966088 | tf_op jit(solution)/shard_map/ppermute | solution.py:30
  703.8 33.7 %collective-permute-start.79 = (bf16[160,2048]{1,0:T(8,128)(2,1)S(1)}, bf16[160,2048]{1,0:T(8,128)(2,1)}, u32[]{:S(2)}, u32[]{:S(2)}) collective-permute-start(bf16[160,2048]{1,0:T(8,128)(2,1)S(1)} %get-tuple-element.198.refs_2_.refs_0_), channel_id=1, source_target_pairs={{0,4},{4,0},{1,5},{5,1},{2,6},{6,2},{3,7},{7,3},{8,12},{12,8},{9,1... | collective-permute-start | bytes 1966088 | tf_op jit(solution)/shard_map/ppermute | solution.py:34
  737.1 25.5 %collective-permute-start.88 = (bf16[160,2048]{1,0:T(8,128)(2,1)S(1)}, bf16[160,2048]{1,0:T(8,128)(2,1)}, u32[]{:S(2)}, u32[]{:S(2)}) collective-permute-start(bf16[160,2048]{1,0:T(8,128)(2,1)S(1)} %copy-done.3), channel_id=1, source_target_pairs={{0,4},{4,0},{1,5},{5,1},{2,6},{6,2},{3,7},{7,3},{8,12},{12,8},{9,1... | collective-permute-start | bytes 1966088 | tf_op jit(solution)/shard_map/ppermute | solution.py:34
  737.6 38.1 %collective-permute-start.89 = (bf16[160,2048]{1,0:T(8,128)(2,1)S(1)}, bf16[160,2048]{1,0:T(8,128)(2,1)}, u32[]{:S(2)}, u32[]{:S(2)}) collective-permute-start(bf16[160,2048]{1,0:T(8,128)(2,1)S(1)} %copy-done.21), channel_id=1, source_target_pairs={{0,4},{4,0},{1,5},{5,1},{2,6},{6,2},{3,7},{7,3},{8,12},{12,8},{9,1... | collective-permute-start | bytes 1966088 | tf_op jit(solution)/shard_map/ppermute | solution.py:34
  737.7 38.6 %collective-permute-start.90 = (bf16[160,2048]{1,0:T(8,128)(2,1)S(1)}, bf16[160,2048]{1,0:T(8,128)(2,1)}, u32[]{:S(2)}, u32[]{:S(2)}) collective-permute-start(bf16[160,2048]{1,0:T(8,128)(2,1)S(1)} %copy-done.23), channel_id=1, source_target_pairs={{0,4},{4,0},{1,5},{5,1},{2,6},{6,2},{3,7},{7,3},{8,12},{12,8},{9,1... | collective-permute-start | bytes 1966088 | tf_op jit(solution)/shard_map/ppermute | solution.py:34
  738.1 39.5 %collective-permute-start.91 = (bf16[160,2048]{1,0:T(8,128)(2,1)}, bf16[160,2048]{1,0:T(8,128)(2,1)}, u32[]{:S(2)}, u32[]{:S(2)}) collective-permute-start(bf16[160,2048]{1,0:T(8,128)(2,1)} %copy-done.146), channel_id=1, source_target_pairs={{0,4},{4,0},{1,5},{5,1},{2,6},{6,2},{3,7},{7,3},{8,12},{12,8},{9,1... | collective-permute-start | bytes 1966088 | tf_op jit(solution)/shard_map/ppermute | solution.py:34
  749.5 203.6 %reduce-scatter.15.cloned.1.call-start = ((), (), s32[]{:S(2)}) async-start(), calls=%async_computation.14 | async-start | bytes 7208960 | tf_op jit(solution)/shard_map/reduce_scatter | solution.py:189
  775.6 20.0 %collective-permute-start.83 = (bf16[160,2048]{1,0:T(8,128)(2,1)}, bf16[160,2048]{1,0:T(8,128)(2,1)}, u32[]{:S(2)}, u32[]{:S(2)}) collective-permute-start(bf16[160,2048]{1,0:T(8,128)(2,1)} %get-tuple-element.209), channel_id=1, source_target_pairs={{0,1},{1,0},{2,3},{3,2},{4,5},{5,4},{6,7},{7,6},{8,9},{9,8},{10,11... | collective-permute-start | bytes 1966088 | tf_op jit(solution)/shard_map/ppermute | solution.py:30
  776.3 31.1 %collective-permute-start.84 = (bf16[160,2048]{1,0:T(8,128)(2,1)}, bf16[160,2048]{1,0:T(8,128)(2,1)}, u32[]{:S(2)}, u32[]{:S(2)}) collective-permute-start(bf16[160,2048]{1,0:T(8,128)(2,1)} %get-tuple-element.210), channel_id=1, source_target_pairs={{0,2},{1,3},{2,0},{3,1},{4,6},{5,7},{6,4},{7,5},{8,10},{9,11},{10,... | collective-permute-start | bytes 1966088 | tf_op jit(solution)/shard_map/ppermute | solution.py:30
  777.6 29.8 %collective-permute-start.85 = (bf16[160,2048]{1,0:T(8,128)(2,1)}, bf16[160,2048]{1,0:T(8,128)(2,1)}, u32[]{:S(2)}, u32[]{:S(2)}) collective-permute-start(bf16[160,2048]{1,0:T(8,128)(2,1)} %get-tuple-element.211), channel_id=1, source_target_pairs={{0,3},{1,2},{2,1},{3,0},{4,7},{5,6},{6,5},{7,4},{8,11},{9,10},{10,... | collective-permute-start | bytes 1966088 | tf_op jit(solution)/shard_map/ppermute | solution.py:30
  795.5 200.6 %reduce-scatter.17.cloned.1.call-start = ((), (), s32[]{:S(2)}) async-start(), calls=%async_computation.15 | async-start | bytes 5242880 | tf_op jit(solution)/shard_map/reduce_scatter | solution.py:189
  817.9 31.3 %collective-permute-start.95 = (bf16[160,2048]{1,0:T(8,128)(2,1)S(1)}, bf16[160,2048]{1,0:T(8,128)(2,1)S(1)}, u32[]{:S(2)}, u32[]{:S(2)}) collective-permute-start(bf16[160,2048]{1,0:T(8,128)(2,1)S(1)} %get-tuple-element.305.refs_0_.refs_12_), channel_id=1, source_target_pairs={{0,1},{1,0},{2,3},{3,2},{4,5},{5,4},{6,7},{7,6},{8,9},{9,8},{10,11... | collective-permute-start | bytes 1966088 | tf_op jit(solution)/shard_map/ppermute | solution.py:30
  818.6 31.9 %collective-permute-start.96 = (bf16[160,2048]{1,0:T(8,128)(2,1)S(1)}, bf16[160,2048]{1,0:T(8,128)(2,1)S(1)}, u32[]{:S(2)}, u32[]{:S(2)}) collective-permute-start(bf16[160,2048]{1,0:T(8,128)(2,1)S(1)} %get-tuple-element.305.refs_0_.refs_12_), channel_id=1, source_target_pairs={{0,2},{1,3},{2,0},{3,1},{4,6},{5,7},{6,4},{7,5},{8,10},{9,11},{10,... | collective-permute-start | bytes 1966088 | tf_op jit(solution)/shard_map/ppermute | solution.py:30
  819.9 31.4 %collective-permute-start.97 = (bf16[160,2048]{1,0:T(8,128)(2,1)S(1)}, bf16[160,2048]{1,0:T(8,128)(2,1)}, u32[]{:S(2)}, u32[]{:S(2)}) collective-permute-start(bf16[160,2048]{1,0:T(8,128)(2,1)S(1)} %get-tuple-element.305.refs_0_.refs_12_), channel_id=1, source_target_pairs={{0,3},{1,2},{2,1},{3,0},{4,7},{5,6},{6,5},{7,4},{8,11},{9,10},{10,... | collective-permute-start | bytes 1966088 | tf_op jit(solution)/shard_map/ppermute | solution.py:30
  828.5 19.3 %collective-permute-start.99 = (f32[160]{0:T(256)S(1)}, f32[160]{0:T(256)S(1)}, u32[]{:S(2)}, u32[]{:S(2)}) collective-permute-start(f32[160]{0:T(256)S(1)} %multiply_reduce_fusion.3), channel_id=1, source_target_pairs={{0,2},{1,3},{2,0},{3,1},{4,6},{5,7},{6,4},{7,5},{8,10},{9,11},{10,... | collective-permute-start | bytes 1928 | tf_op jit(solution)/shard_map/ppermute | solution.py:30
  830.6 38.1 %collective-permute-start.92 = (bf16[160,2048]{1,0:T(8,128)(2,1)}, bf16[160,2048]{1,0:T(8,128)(2,1)S(1)}, u32[]{:S(2)}, u32[]{:S(2)}) collective-permute-start(bf16[160,2048]{1,0:T(8,128)(2,1)} %get-tuple-element.325), channel_id=1, source_target_pairs={{0,1},{1,0},{2,3},{3,2},{4,5},{5,4},{6,7},{7,6},{8,9},{9,8},{10,11... | collective-permute-start | bytes 1966088 | tf_op jit(solution)/shard_map/ppermute | solution.py:30
  847.8 28.2 %collective-permute-start.93 = (bf16[160,2048]{1,0:T(8,128)(2,1)}, bf16[160,2048]{1,0:T(8,128)(2,1)S(1)}, u32[]{:S(2)}, u32[]{:S(2)}) collective-permute-start(bf16[160,2048]{1,0:T(8,128)(2,1)} %get-tuple-element.327), channel_id=1, source_target_pairs={{0,2},{1,3},{2,0},{3,1},{4,6},{5,7},{6,4},{7,5},{8,10},{9,11},{10,... | collective-permute-start | bytes 1966088 | tf_op jit(solution)/shard_map/ppermute | solution.py:30
  849.2 26.7 %collective-permute-start.94 = (bf16[160,2048]{1,0:T(8,128)(2,1)}, bf16[160,2048]{1,0:T(8,128)(2,1)}, u32[]{:S(2)}, u32[]{:S(2)}) collective-permute-start(bf16[160,2048]{1,0:T(8,128)(2,1)} %get-tuple-element.326), channel_id=1, source_target_pairs={{0,3},{1,2},{2,1},{3,0},{4,7},{5,6},{6,5},{7,4},{8,11},{9,10},{10,... | collective-permute-start | bytes 1966088 | tf_op jit(solution)/shard_map/ppermute | solution.py:30
  921.8 29.7 %collective-permute-start.116 = (bf16[160,2048]{1,0:T(8,128)(2,1)S(1)}, bf16[160,2048]{1,0:T(8,128)(2,1)}, u32[]{:S(2)}, u32[]{:S(2)}) collective-permute-start(bf16[160,2048]{1,0:T(8,128)(2,1)S(1)} %get-tuple-element.323), channel_id=1, source_target_pairs={{0,2},{1,3},{2,0},{3,1},{4,6},{5,7},{6,4},{7,5},{8,10},{9,11},{10,... | collective-permute-start | bytes 1966088 | tf_op jit(solution)/shard_map/ppermute | solution.py:30
  923.4 29.6 %collective-permute-start.117 = (bf16[160,2048]{1,0:T(8,128)(2,1)S(1)}, bf16[160,2048]{1,0:T(8,128)(2,1)}, u32[]{:S(2)}, u32[]{:S(2)}) collective-permute-start(bf16[160,2048]{1,0:T(8,128)(2,1)S(1)} %get-tuple-element.322), channel_id=1, source_target_pairs={{0,3},{1,2},{2,1},{3,0},{4,7},{5,6},{6,5},{7,4},{8,11},{9,10},{10,... | collective-permute-start | bytes 1966088 | tf_op jit(solution)/shard_map/ppermute | solution.py:30
  (236 other events, 4190.9 us)
Sparse Core Ops, SparseCore 0:
  11.4 84.7 all-gather.7
  98.3 154.6 all-gather.9
  255.2 80.9 all-gather.11
  337.7 106.6 all-gather.13
  446.4 59.2 all-gather.15
  508.4 54.3 reduce-scatter.6
  565.1 102.3 reduce-scatter.8
  669.8 77.2 reduce-scatter.10
  750.1 56.6 reduce-scatter.12
  809.1 102.3 reduce-scatter.14
  913.9 78.3 reduce-scatter.16

commit v5 on v4

--- a/solution.py
+++ b/solution.py
@@ -192,6 +192,29 @@
 def cut(values, count):
     rows = values.shape[0] // count
     return [values[k * rows : (k + 1) * rows] for k in range(count)]
+
+
+def unfold(shards):
+    height, width = shards[0].shape
+    units, layers = height // 4, len(shards)
+
+    def kernel(*refs):
+        for layer, ref in enumerate(refs[:layers]):
+            for k, out in enumerate(refs[layers:]):
+                part = ref[k * units : (k + 1) * units, :].astype(f32)
+                out[layer] = part if k == 3 else part.T
+
+    shapes = [(layers, width, units)] * 3 + [(layers, units, width)]
+    return call(
+        kernel,
+        (1,),
+        [whole(shard) for shard in shards],
+        [pl.BlockSpec(shape, lambda j: (0, 0, 0)) for shape in shapes],
+        [jax.ShapeDtypeStruct(shape, f32) for shape in shapes],
+        [],
+        shards,
+        0,
+    )
 
 
 def rows_at(matrix, at, rows, tile):
@@ -481,7 +504,12 @@
     mine = columns(0)
     for step in range(1, size):
         mine = mine + exchange(columns(step), step)
-    mine = jnp.sum(lax.all_gather(jnp.concatenate([mine, rows_of_channels], axis=0), SEQ), axis=0)
+    mine = jnp.concatenate([mine, rows_of_channels], axis=0)
+    mine = mine + swap(mine, "core")
+    chips, step = lax.axis_size("chip"), 1
+    while step < chips:
+        mine = mine + lax.ppermute(mine, "chip", [(i, i ^ step) for i in range(chips)])
+        step *= 2
     total = jnp.zeros((mine.shape[0], channels * size), f32)
     total = lax.dynamic_update_slice_in_dim(total, mine, first_channel, 1)
     for step in range(1, size):
@@ -675,18 +703,11 @@
         if first_layer:
             joined = after(joined, hidden_out)
         (twin_joined,) = twins((joined,))
-        if first_layer:
-            low_part = outer([([joined, twin_joined], all_normed), ([mixed, *twin_mixed], all_m)])
-            part = trans_dot(after(joined, low_part), mix[:, : 3 * channels])
-        else:
-            part = dot(joined, mix[: 3 * channels])
+        part = trans_dot(joined, mix[:, : 3 * channels]) if first_layer else dot(joined, mix[: 3 * channels])
         part = part.astype(bf16)
 
-        if first_layer:
-            parts = cut(part, size)
-        else:
-            *parts, ready = all_after((*cut(part, size), joined))
-            low_part = outer([([ready, twin_joined], all_normed), ([mixed, *twin_mixed], all_m)])
+        *parts, ready = all_after((*cut(part, size), joined))
+        low_part = outer([([ready, twin_joined], all_normed), ([mixed, *twin_mixed], all_m)])
         low_shard = scattered["low", layer] = scatter_columns(low_part)
         grad_normed = scatter_rows(parts, low_part, *due(layer, "last"))
         mix_piece = jnp.sum(grad_normed * unit, axis=0)
@@ -695,22 +716,14 @@
         smalls[layer] = (mix_piece, ffn_piece, bound_piece, gain_piece)
     wide_rows = jnp.stack([row for pieces in smalls for row in pieces[:2]])
     own_rows = jnp.concatenate([row for pieces in smalls for row in pieces[2:]], axis=0)
-    small = total_small(after(wide_rows, grad_x, *due(0, "after")), own_rows, first_channel, channels)
+    small = total_small(after(wide_rows, *due(0, "after")), own_rows, first_channel, channels)
     for layer in range(LAYERS):
-        ffn_shard, down_shard, low_shard = (scattered[name, layer] for name in ("ffn", "down", "low"))
-        if layer == 0:
-            low_shard = after(low_shard, small)
-        shards[layer] = (
-            *(low_shard[k * channels : (k + 1) * channels].T for k in range(3)),
-            low_shard[3 * channels :],
-            ffn_shard[:hidden_units].T,
-            ffn_shard[hidden_units:].T,
-            down_shard,
-        )
-    stacked = tuple(
-        jnp.stack([shards[layer][member].astype(f32) for layer in range(LAYERS)])
-        for member in range(7)
-    )
+        ffn_shard, down_shard = scattered["ffn", layer], scattered["down", layer]
+        shards[layer] = (ffn_shard[:hidden_units].T, ffn_shard[hidden_units:].T, down_shard)
+    low_shards = [after(scattered["low", 0], grad_x)] + [scattered["low", k] for k in range(1, LAYERS)]
+    stacked = [*unfold(low_shards)] + [
+        jnp.stack([shards[layer][member].astype(f32) for layer in range(LAYERS)]) for member in range(3)
+    ]
     wide_rows, own_rows = small[: 2 * LAYERS], small[2 * LAYERS :]
     return (
         hidden_out, grad_x, *stacked, own_rows[0::2], wide_rows[0::2], wide_rows[1::2], own_rows[1::2]

time: 1020 us -> 1010 us (level)
  blocking collectives: 15 us -> 0 us
  waiting for transfers between devices: 490 us -> 502 us
    reduce_scatter x6, waiting for transfers between devices: 0.86 us -> 18.2 us  [scatter_columns(): return lax.psum_scatter(part, 'chip', scatter_dimension=1, tiled=True)]
    all_gather x1 -> x0, blocking collectives: 15 us -> none  [total_small(): lax.all_gather(jnp.concatenate([mine, rows_of_channels], axis=0), SEQ)]
    unnamed x345 -> x328, local copies, waits for them, and re-layouts: 44.3 us -> 36.5 us
    pallas_call x16 -> x17, Pallas kernels: 185 us -> 188 us  [call(): pl.pallas_call(kernel, grid_spec=pltpu.PrefetchScalarGridSpec(num_scalar_...]
  transfers between devices with their start and end apart: 135 -> 138, of which waited for: 55 -> 55; matrix products, arithmetic and copies ran while one was open for 15% -> 15% of each run, Pallas kernels for 18% -> 18%
where the time goes in v5:
time: 1010 us; the launch traced here: 1000 us
  waiting for transfers between devices  502 us (50%)
  Pallas kernels  188 us (19%)
  starting transfers between devices  116 us (11%)
  local copies, waits for them, and re-layouts  68.8 us (7%)
  matrix products  58.7 us (6%)
  other arithmetic  53.4 us (5%)
  between operations  16.5 us (2%)
    ppermute x66, waiting for transfers between devices, exchange(): return lax.ppermute(values, 'fsdp', [(i, i ^ step) for i in range(size)])  358 us
    pallas_call x17, Pallas kernels, call(): pl.pallas_call(kernel, grid_spec=pltpu.PrefetchScalarGridSpec(num_scalar_...  188 us
    all_gather x4, waiting for transfers between devices, tall(): lax.all_gather(jnp.concatenate(shards, axis=0), SEQ, axis=1, tiled=True)  90.8 us
    ppermute x66, starting transfers between devices, exchange(): return lax.ppermute(values, 'fsdp', [(i, i ^ step) for i in range(size)])  81.3 us
    dot_general x6, matrix products, dot(): return jnp.dot(left, right, preferred_element_type=f32)  48.3 us
    unnamed x328, local copies, waits for them, and re-layouts  36.5 us
    ppermute x12, starting transfers between devices, entering_of(): lax.ppermute(pair, SEQ, [(i, i + sign * 2 * hop) for i in range(length) i...  20.6 us
  transfers between devices with their start and end apart: 138, of which 55 were waited for; matrix products, arithmetic and copies ran while one was open for 15% of the time, Pallas kernels for 18%

profile of v5, /device:TPU:0, one launch (start us, length us, event | category | flops | bytes accessed | tf_op | source)
XLA Modules:
  0.0 1003.4 jit_solution(14065290992265327029)
XLA Ops:
  30.5 13.7 %collective-permute-done.refs_1_.refs_5_ = bf16[160,2048]{1,0:T(8,128)(2,1)S(1)} collective-permute-done((bf16[160,2048]{1,0:T(8,128)(2,1)S(1)}, bf16[160,2048]{1,0:T(8,128)(2,1)S(1)}, u32[]{:S(2)}, u32[]{:S(2)}) %collective-permute-start) | collective-permute-done | bytes 655392 | tf_op jit(solution)/shard_map/ppermute | solution.py:30
  44.1 14.8 %collective-permute-done.1.refs_2_.refs_6_ = bf16[160,2048]{1,0:T(8,128)(2,1)} collective-permute-done((bf16[160,2048]{1,0:T(8,128)(2,1)S(1)}, bf16[160,2048]{1,0:T(8,128)(2,1)}, u32[]{:S(2)}, u32[]{:S(2)}) %collective-permute-start.1) | collective-permute-done | bytes 655392 | tf_op jit(solution)/shard_map/ppermute | solution.py:30
  64.0 12.7 %collective-permute-done.3.refs_3_.refs_1_ = bf16[160,2048]{1,0:T(8,128)(2,1)S(1)} collective-permute-done((bf16[160,2048]{1,0:T(8,128)(2,1)S(1)}, bf16[160,2048]{1,0:T(8,128)(2,1)S(1)}, u32[]{:S(2)}, u32[]{:S(2)}) %collective-permute-start.3) | collective-permute-done | bytes 655392 | tf_op jit(solution)/shard_map/ppermute | solution.py:30
  76.7 13.0 %collective-permute-done.4.refs_4_.refs_2_ = bf16[160,2048]{1,0:T(8,128)(2,1)} collective-permute-done((bf16[160,2048]{1,0:T(8,128)(2,1)S(1)}, bf16[160,2048]{1,0:T(8,128)(2,1)}, u32[]{:S(2)}, u32[]{:S(2)}) %collective-permute-start.4) | collective-permute-done | bytes 655392 | tf_op jit(solution)/shard_map/ppermute | solution.py:30
  89.6 6.6 all-gather.7.cloned.1.call-done.refs_4_.refs_5_.refs_6_
  96.2 13.3 %shard_map.237 = (f32[640,512]{1,0:T(8,128)}, f32[640,512]{1,0:T(8,128)}, f32[640,512]{1,0:T(8,128)}, f32[640,512]{1,0:T(8,128)}, f32[640,512]{1,0:T(8,128)}) custom-call(s32[1]{0:T(128)} %bitcast.place_ref, bf16[160,2048]{1,0:T(8,128)(2,1)S(1)} %fusion.38.refs_0_.refs_4_, bf16[160,2048]{1,0:T(8,128)(2,1)S(1)} %collective-permute-done.refs_1_.refs_5_, ...), custom_call_target="tpu_custom_call" | custom-call | flops 22145925120 | bytes 7864320 | tf_op jit(solution)/shard_map/pallas_call | solution.py:106
  113.5 3.7 collective-permute-start.8
  125.7 3.2 convolution_convert_fusion.2
  134.9 14.0 %collective-permute-done.10 = bf16[160,2048]{1,0:T(8,128)(2,1)S(1)} collective-permute-done((bf16[160,2048]{1,0:T(8,128)(2,1)}, bf16[160,2048]{1,0:T(8,128)(2,1)S(1)}, u32[]{:S(2)}, u32[]{:S(2)}) %collective-permute-start.10) | collective-permute-done | bytes 655392 | tf_op jit(solution)/shard_map/ppermute | solution.py:30
  148.9 13.3 %collective-permute-done.11 = bf16[160,2048]{1,0:T(8,128)(2,1)S(1)} collective-permute-done((bf16[160,2048]{1,0:T(8,128)(2,1)}, bf16[160,2048]{1,0:T(8,128)(2,1)S(1)}, u32[]{:S(2)}, u32[]{:S(2)}) %collective-permute-start.11) | collective-permute-done | bytes 655392 | tf_op jit(solution)/shard_map/ppermute | solution.py:30
  169.2 14.2 %collective-permute-done.16.refs_1_.refs_5_ = bf16[160,2048]{1,0:T(8,128)(2,1)S(1)} collective-permute-done((bf16[160,2048]{1,0:T(8,128)(2,1)S(1)}, bf16[160,2048]{1,0:T(8,128)(2,1)S(1)}, u32[]{:S(2)}, u32[]{:S(2)}) %collective-permute-start.16) | collective-permute-done | bytes 655392 | tf_op jit(solution)/shard_map/ppermute | solution.py:30
  183.4 11.6 %collective-permute-done.17.refs_2_.refs_6_ = bf16[160,2048]{1,0:T(8,128)(2,1)S(1)} collective-permute-done((bf16[160,2048]{1,0:T(8,128)(2,1)S(1)}, bf16[160,2048]{1,0:T(8,128)(2,1)S(1)}, u32[]{:S(2)}, u32[]{:S(2)}) %collective-permute-start.17) | collective-permute-done | bytes 655392 | tf_op jit(solution)/shard_map/ppermute | solution.py:30
  195.0 58.0 %all-gather.9.cloned.1.call-done.refs_4_.refs_5_ = bf16[4224,2048]{1,0:T(8,128)(2,1)} async-done(((bf16[4224,256]{1,0:T(8,128)(2,1)}), bf16[4224,2048]{1,0:T(8,128)(2,1)}) %all-gather.9.cloned.1.call-update) | async-done | bytes 17301520 | tf_op jit(solution)/shard_map/all_gather | solution.py:550
  253.1 15.1 %shard_map.238 = (bf16[640,1408]{1,0:T(8,128)(2,1)}, bf16[640,1408]{1,0:T(8,128)(2,1)}, bf16[640,1408]{1,0:T(8,128)(2,1)}) custom-call(bf16[160,2048]{1,0:T(8,128)(2,1)S(1)} %multiply_convert_fusion.3.refs_0_.refs_4_, bf16[160,2048]{1,0:T(8,128)(2,1)S(1)} %collective-permute-done.16.refs_1_.refs_5_, ...), custom_call_target="tpu_custom_call" | custom-call | flops 40600862720 | bytes 14417920 | tf_op jit(solution)/shard_map/pallas_call | solution.py:106
  268.2 7.4 fusion.18
  279.3 14.1 %collective-permute-done.19 = bf16[160,2048]{1,0:T(8,128)(2,1)S(1)} collective-permute-done((bf16[160,2048]{1,0:T(8,128)(2,1)S(1)}, bf16[160,2048]{1,0:T(8,128)(2,1)S(1)}, u32[]{:S(2)}, u32[]{:S(2)}) %collective-permute-start.19) | collective-permute-done | bytes 655392 | tf_op jit(solution)/shard_map/ppermute | solution.py:30
  293.4 14.6 %collective-permute-done.20 = bf16[160,2048]{1,0:T(8,128)(2,1)S(1)} collective-permute-done((bf16[160,2048]{1,0:T(8,128)(2,1)S(1)}, bf16[160,2048]{1,0:T(8,128)(2,1)S(1)}, u32[]{:S(2)}, u32[]{:S(2)}) %collective-permute-start.20) | collective-permute-done | bytes 655392 | tf_op jit(solution)/shard_map/ppermute | solution.py:30
  312.4 14.2 %collective-permute-done.22.refs_1_.refs_5_ = bf16[160,2048]{1,0:T(8,128)(2,1)S(1)} collective-permute-done((bf16[160,2048]{1,0:T(8,128)(2,1)S(1)}, bf16[160,2048]{1,0:T(8,128)(2,1)S(1)}, u32[]{:S(2)}, u32[]{:S(2)}) %collective-permute-start.22) | collective-permute-done | bytes 655392 | tf_op jit(solution)/shard_map/ppermute | solution.py:30
  326.6 13.5 %collective-permute-done.23.refs_2_.refs_6_ = bf16[160,2048]{1,0:T(8,128)(2,1)S(1)} collective-permute-done((bf16[160,2048]{1,0:T(8,128)(2,1)S(1)}, bf16[160,2048]{1,0:T(8,128)(2,1)S(1)}, u32[]{:S(2)}, u32[]{:S(2)}) %collective-permute-start.23) | collective-permute-done | bytes 655392 | tf_op jit(solution)/shard_map/ppermute | solution.py:30
  340.9 13.8 %shard_map.239 = (f32[640,512]{1,0:T(8,128)}, f32[640,512]{1,0:T(8,128)}, f32[640,512]{1,0:T(8,128)}, f32[640,512]{1,0:T(8,128)}, f32[640,512]{1,0:T(8,128)}) custom-call(s32[1]{0:T(128)} %bitcast.place_ref, bf16[160,2048]{1,0:T(8,128)(2,1)S(1)} %multiply_convert_fusion.2.refs_0_.refs_4_, bf16[160,2048]{1,0:T(8,128)(2,1)S(1)} %collective-permute-done.22.refs_1_.refs_5_, ...), custom_call_target="tpu_custom_call" | custom-call | flops 22145925120 | bytes 7864320 | tf_op jit(solution)/shard_map/pallas_call | solution.py:106
  370.0 3.6 convolution_convert_fusion.1
  379.6 14.0 %collective-permute-done.29 = bf16[160,2048]{1,0:T(8,128)(2,1)S(1)} collective-permute-done((bf16[160,2048]{1,0:T(8,128)(2,1)}, bf16[160,2048]{1,0:T(8,128)(2,1)S(1)}, u32[]{:S(2)}, u32[]{:S(2)}) %collective-permute-start.29) | collective-permute-done | bytes 655392 | tf_op jit(solution)/shard_map/ppermute | solution.py:30
  393.6 12.5 %collective-permute-done.30 = bf16[160,2048]{1,0:T(8,128)(2,1)S(1)} collective-permute-done((bf16[160,2048]{1,0:T(8,128)(2,1)}, bf16[160,2048]{1,0:T(8,128)(2,1)S(1)}, u32[]{:S(2)}, u32[]{:S(2)}) %collective-permute-start.30) | collective-permute-done | bytes 655392 | tf_op jit(solution)/shard_map/ppermute | solution.py:30
  412.1 14.2 %collective-permute-done.35.refs_1_.refs_5_ = bf16[160,2048]{1,0:T(8,128)(2,1)S(1)} collective-permute-done((bf16[160,2048]{1,0:T(8,128)(2,1)S(1)}, bf16[160,2048]{1,0:T(8,128)(2,1)S(1)}, u32[]{:S(2)}, u32[]{:S(2)}) %collective-permute-start.35) | collective-permute-done | bytes 655392 | tf_op jit(solution)/shard_map/ppermute | solution.py:30
  426.3 11.4 %collective-permute-done.36.refs_2_.refs_6_ = bf16[160,2048]{1,0:T(8,128)(2,1)S(1)} collective-permute-done((bf16[160,2048]{1,0:T(8,128)(2,1)S(1)}, bf16[160,2048]{1,0:T(8,128)(2,1)S(1)}, u32[]{:S(2)}, u32[]{:S(2)}) %collective-permute-start.36) | collective-permute-done | bytes 655392 | tf_op jit(solution)/shard_map/ppermute | solution.py:30
  438.5 6.0 all-gather.13.cloned.1.call-done.refs_4_.refs_5_
  445.5 15.0 %shard_map.240 = (bf16[640,1408]{1,0:T(8,128)(2,1)}, bf16[640,1408]{1,0:T(8,128)(2,1)}, bf16[640,1408]{1,0:T(8,128)(2,1)}) custom-call(bf16[160,2048]{1,0:T(8,128)(2,1)S(1)} %multiply_convert_fusion.refs_0_.refs_4_, bf16[160,2048]{1,0:T(8,128)(2,1)S(1)} %collective-permute-done.35.refs_1_.refs_5_, bf16[160,2048]{1,0:T(8,128)(2,1)S(1)} %copy-done.32, ...), custom_call_target="tpu_custom_call" | custom-call | flops 40600862720 | bytes 14417920 | tf_op jit(solution)/shard_map/pallas_call | solution.py:106
  469.5 9.1 shard_map.241
  478.9 26.7 %all-gather.15.cloned.1.call-done = bf16[1,1408,2048]{2,1,0:T(8,128)(2,1)} async-done(((bf16[1,1408,256]{2,1,0:T(8,128)(2,1)}), bf16[1,1408,2048]{2,1,0:T(8,128)(2,1)}) %all-gather.15.cloned.1.call-update) | async-done | bytes 5767184 | tf_op jit(solution)/shard_map/all_gather | solution.py:550
  505.7 10.5 %shard_map.242 = (bf16[640,1408]{1,0:T(8,128)(2,1)}, bf16[640,1408]{1,0:T(8,128)(2,1)}) custom-call(bf16[160,2048]{1,0:T(8,128)(2,1)S(1)} %copy-done.1, bf16[160,2048]{1,0:T(8,128)(2,1)S(1)} %copy-done.28, bf16[160,2048]{1,0:T(8,128)(2,1)} %collective-permute-done.4.refs_4_.refs_2_, bf16[160,2048]{1,0:T(8,128)(2,1)} %collective-permute-done.5.refs_5_.refs_3_, ...), custom_call_target="tpu_custom_call" | custom-call | flops 20300431360 | bytes 7208960 | tf_op jit(solution)/shard_map/pallas_call | solution.py:106
  516.7 11.5 %fusion.15 = bf16[640,2048]{1,0:T(8,128)(2,1)S(1)} fusion(bf16[2816,2048]{1,0:T(8,128)(2,1)} %all-gather.13.cloned.1.call-done.refs_4_.refs_5_, bf16[640,1408]{1,0:T(8,128)(2,1)} %get-tuple-element.168.refs_2_, bf16[640,1408]{1,0:T(8,128)(2,1)} %get-tuple-element.174), kind=kOutput, calls=%fused_computation.15 | convolution fusion | flops 7390494720 | bytes 17760256 | tf_op jit(solution)/shard_map/dot_general | solution.py:94
  535.7 15.2 %shard_map.243 = bf16[2816,1024]{1,0:T(8,128)(2,1)} custom-call(s32[1]{0:T(128)} %bitcast.32.core_ref, bf16[640,1408]{1,0:T(8,128)(2,1)} %get-tuple-element.174, bf16[640,1408]{1,0:T(8,128)(2,1)} %copy-done.137, bf16[640,1408]{1,0:T(8,128)(2,1)} %get-tuple-element.168.refs_2_, bf16[640,1408]{1,0:T(8,128)(2,1)} %copy-done.138, ...), custom_call_target="tpu_custom_call" | custom-call | flops 81201725440 | bytes 28835840 | tf_op jit(solution)/shard_map/pallas_call | solution.py:106
  551.0 10.9 %collective-permute-done.44 = bf16[160,2048]{1,0:T(8,128)(2,1)} collective-permute-done((bf16[160,2048]{1,0:T(8,128)(2,1)}, bf16[160,2048]{1,0:T(8,128)(2,1)}, u32[]{:S(2)}, u32[]{:S(2)}) %collective-permute-start.44) | collective-permute-done | bytes 655392 | tf_op jit(solution)/shard_map/ppermute | solution.py:30
  576.4 20.9 %collective-permute-done.55 = f32[160]{0:T(256)S(1)} collective-permute-done((f32[160]{0:T(256)S(1)}, f32[160]{0:T(256)S(1)}, u32[]{:S(2)}, u32[]{:S(2)}) %collective-permute-start.55) | collective-permute-done | bytes 672 | tf_op jit(solution)/shard_map/ppermute | solution.py:30
  602.1 11.2 %shard_map.244 = (f32[640,512]{1,0:T(8,128)}, f32[640,512]{1,0:T(8,128)}, bf16[640,512]{1,0:T(8,128)(2,1)S(1)}, bf16[640,512]{1,0:T(8,128)(2,1)}, f32[1,512]{1,0:T(1,128)S(1)}) custom-call(s32[1]{0:T(128)} %bitcast.place_ref, bf16[160,2048]{1,0:T(8,128)(2,1)} %copy-done.59, bf16[160,2048]{1,0:T(8,128)(2,1)} %collective-permute-done.52.refs_1_.refs_13_, ...), custom_call_target="tpu_custom_call" | custom-call | flops 180224000 | bytes 64000 | tf_op jit(solution)/shard_map/pallas_call | solution.py:106
  621.5 4.0 collective-permute-done.59
  631.2 5.6 shard_map.245
  639.6 7.2 fusion.21
  652.1 12.2 %shard_map.246 = bf16[2048,1024]{1,0:T(8,128)(2,1)} custom-call(s32[1]{0:T(128)} %bitcast.32.core_ref, bf16[640,1536]{1,0:T(8,128)(2,1)} %copy-done.94, bf16[640,1536]{1,0:T(8,128)(2,1)} %collective-permute-done.70.refs_1_, bf16[640,512]{1,0:T(8,128)(2,1)S(1)} %copy-done.30, bf16[640,512]{1,0:T(8,128)(2,1)S(1)} %collective-permute-done.66.refs_3_, ...), custom_call_target="tpu_custom_call" | custom-call | flops 59055800320 | bytes 20971520 | tf_op jit(solution)/shard_map/pallas_call | solution.py:106
  666.2 14.5 %collective-permute-done.68 = bf16[160,2048]{1,0:T(8,128)(2,1)} collective-permute-done((bf16[160,2048]{1,0:T(8,128)(2,1)}, bf16[160,2048]{1,0:T(8,128)(2,1)}, u32[]{:S(2)}, u32[]{:S(2)}) %collective-permute-start.68) | collective-permute-done | bytes 655392 | tf_op jit(solution)/shard_map/ppermute | solution.py:30
  683.9 3.8 fusion.78
  691.2 14.2 %collective-permute-done.75.refs_3_.refs_1_ = bf16[160,2048]{1,0:T(8,128)(2,1)S(1)} collective-permute-done((bf16[160,2048]{1,0:T(8,128)(2,1)S(1)}, bf16[160,2048]{1,0:T(8,128)(2,1)S(1)}, u32[]{:S(2)}, u32[]{:S(2)}) %collective-permute-start.75) | collective-permute-done | bytes 655392 | tf_op jit(solution)/shard_map/ppermute | solution.py:30
  705.4 13.2 %collective-permute-done.76.refs_4_.refs_2_ = bf16[160,2048]{1,0:T(8,128)(2,1)S(1)} collective-permute-done((bf16[160,2048]{1,0:T(8,128)(2,1)S(1)}, bf16[160,2048]{1,0:T(8,128)(2,1)S(1)}, u32[]{:S(2)}, u32[]{:S(2)}) %collective-permute-start.76) | collective-permute-done | bytes 655392 | tf_op jit(solution)/shard_map/ppermute | solution.py:30
  727.6 9.0 shard_map.247
  738.8 10.0 shard_map.248
  749.6 11.5 %fusion.27 = bf16[640,2048]{1,0:T(8,128)(2,1)S(1)} fusion(bf16[4224,2048]{1,0:T(8,128)(2,1)} %all-gather.9.cloned.1.call-done.refs_4_.refs_5_, bf16[640,1408]{1,0:T(8,128)(2,1)} %get-tuple-element.214.refs_2_, bf16[640,1408]{1,0:T(8,128)(2,1)} %get-tuple-element.219.refs_0_), kind=kOutput, calls=%fused_computation.19 | convolution fusion | flops 7390494720 | bytes 17760256 | tf_op jit(solution)/shard_map/dot_general | solution.py:94
  767.2 15.1 %shard_map.249 = bf16[2816,1024]{1,0:T(8,128)(2,1)} custom-call(s32[1]{0:T(128)} %bitcast.32.core_ref, bf16[640,1408]{1,0:T(8,128)(2,1)} %get-tuple-element.219.refs_0_, bf16[640,1408]{1,0:T(8,128)(2,1)} %collective-permute-done.86.refs_1_, bf16[640,1408]{1,0:T(8,128)(2,1)} %get-tuple-element.214.refs_2_, bf16[640,1408]{1,0:T(8,128)(2,1)} %copy-done.139, ...), custom_call_target="tpu_custom_call" | custom-call | flops 81201725440 | bytes 28835840 | tf_op jit(solution)/shard_map/pallas_call | solution.py:106
  782.6 11.6 %collective-permute-done.84 = bf16[160,2048]{1,0:T(8,128)(2,1)} collective-permute-done((bf16[160,2048]{1,0:T(8,128)(2,1)}, bf16[160,2048]{1,0:T(8,128)(2,1)}, u32[]{:S(2)}, u32[]{:S(2)}) %collective-permute-start.84) | collective-permute-done | bytes 655392 | tf_op jit(solution)/shard_map/ppermute | solution.py:30
  796.5 3.4 fusion.77
  808.3 7.0 convolution_convert_fusion
  818.8 15.6 %collective-permute-done.99 = f32[160]{0:T(256)S(1)} collective-permute-done((f32[160]{0:T(256)S(1)}, f32[160]{0:T(256)S(1)}, u32[]{:S(2)}, u32[]{:S(2)}) %collective-permute-start.99) | collective-permute-done | bytes 672 | tf_op jit(solution)/shard_map/ppermute | solution.py:30
  838.6 11.3 %shard_map.250 = (f32[640,512]{1,0:T(8,128)}, f32[640,512]{1,0:T(8,128)}, bf16[640,512]{1,0:T(8,128)(2,1)S(1)}, bf16[640,512]{1,0:T(8,128)(2,1)}, f32[1,512]{1,0:T(1,128)S(1)}) custom-call(s32[1]{0:T(128)} %bitcast.place_ref, bf16[160,2048]{1,0:T(8,128)(2,1)} %copy-done.57, bf16[160,2048]{1,0:T(8,128)(2,1)} %copy-done.87, bf16[160,2048]{1,0:T(8,128)(2,1)} %copy-done.89, ...), custom_call_target="tpu_custom_call" | custom-call | flops 180224000 | bytes 64000 | tf_op jit(solution)/shard_map/pallas_call | solution.py:106
  857.5 5.1 collective-permute-done.93
  869.8 5.9 shard_map.251
  878.1 7.3 fusion.24
  889.3 12.4 %shard_map.252 = bf16[2048,1024]{1,0:T(8,128)(2,1)} custom-call(s32[1]{0:T(128)} %bitcast.32.core_ref, bf16[640,1536]{1,0:T(8,128)(2,1)} %copy-done.78, bf16[640,1536]{1,0:T(8,128)(2,1)} %copy-done.135, bf16[640,512]{1,0:T(8,128)(2,1)S(1)} %copy-done.29, bf16[640,512]{1,0:T(8,128)(2,1)S(1)} %collective-permute-done.109.refs_3_, ...), custom_call_target="tpu_custom_call" | custom-call | flops 59055800320 | bytes 20971520 | tf_op jit(solution)/shard_map/pallas_call | solution.py:106
  908.3 11.4 %collective-permute-done.110 = bf16[160,2048]{1,0:T(8,128)(2,1)} collective-permute-done((bf16[160,2048]{1,0:T(8,128)(2,1)}, bf16[160,2048]{1,0:T(8,128)(2,1)}, u32[]{:S(2)}, u32[]{:S(2)}) %collective-permute-start.110) | collective-permute-done | bytes 655392 | tf_op jit(solution)/shard_map/ppermute | solution.py:30
  919.7 14.8 %collective-permute-done.111 = bf16[160,2048]{1,0:T(8,128)(2,1)} collective-permute-done((bf16[160,2048]{1,0:T(8,128)(2,1)}, bf16[160,2048]{1,0:T(8,128)(2,1)}, u32[]{:S(2)}, u32[]{:S(2)}) %collective-permute-start.111) | collective-permute-done | bytes 655392 | tf_op jit(solution)/shard_map/ppermute | solution.py:30
  943.3 3.4 fusion.42
  947.4 3.5 collective-permute-done.122
  952.8 4.2 collective-permute-done.123
  962.5 3.4 copy.111
  974.6 17.3 %reduce-scatter.17.cloned.1.call-done.refs_0_ = bf16[2048,256]{1,0:T(8,128)(2,1)} async-done(((bf16[2048,1024]{1,0:T(8,128)(2,1)}), bf16[2048,256]{1,0:T(8,128)(2,1)}) %reduce-scatter.17.cloned.1.call-update) | async-done | bytes 1048592 | tf_op jit(solution)/shard_map/reduce_scatter | solution.py:189
  993.1 3.6 shard_map.253
  (727 shorter events, 248.4 us)
Async XLA Ops:
  7.2 89.0 %all-gather.7.cloned.1.call-start = ((), (), s32[]{:S(2)}) async-start(), calls=%async_computation.6 | async-start | bytes 9437184 | tf_op jit(solution)/shard_map/all_gather | solution.py:547
  11.3 241.8 %all-gather.9.cloned.1.call-start = ((), (), s32[]{:S(2)}) async-start(), calls=%async_computation.7 | async-start | bytes 19464192 | tf_op jit(solution)/shard_map/all_gather | solution.py:550
  19.7 321.1 %all-gather.11.cloned.1.call-start = ((), (), s32[]{:S(2)}) async-start(), calls=%async_computation.8 | async-start | bytes 9437184 | tf_op jit(solution)/shard_map/all_gather | solution.py:550
  22.2 422.3 %all-gather.13.cloned.1.call-start = ((), (), s32[]{:S(2)}) async-start(), calls=%async_computation.9 | async-start | bytes 12976128 | tf_op jit(solution)/shard_map/all_gather | solution.py:550
  24.0 481.6 %all-gather.15.cloned.1.call-start = ((), (), s32[]{:S(2)}) async-start(), calls=%async_computation.16 | async-start | bytes 6488064 | tf_op jit(solution)/shard_map/all_gather | solution.py:550
  25.6 18.5 %collective-permute-start = (bf16[160,2048]{1,0:T(8,128)(2,1)S(1)}, bf16[160,2048]{1,0:T(8,128)(2,1)S(1)}, u32[]{:S(2)}, u32[]{:S(2)}) collective-permute-start(bf16[160,2048]{1,0:T(8,128)(2,1)S(1)} %fusion.38.refs_0_.refs_4_), channel_id=1, source_target_pairs={{0,1},{1,0},{2,3},{3,2},{4,5},{5,4},{6,7},{7,6},{8,9},{9,8},{10,11... | collective-permute-start | bytes 1966088 | tf_op jit(solution)/shard_map/ppermute | solution.py:30
  28.6 30.3 %collective-permute-start.1 = (bf16[160,2048]{1,0:T(8,128)(2,1)S(1)}, bf16[160,2048]{1,0:T(8,128)(2,1)}, u32[]{:S(2)}, u32[]{:S(2)}) collective-permute-start(bf16[160,2048]{1,0:T(8,128)(2,1)S(1)} %fusion.38.refs_0_.refs_4_), channel_id=1, source_target_pairs={{0,2},{1,3},{2,0},{3,1},{4,6},{5,7},{6,4},{7,5},{8,10},{9,11},{10,... | collective-permute-start | bytes 1966088 | tf_op jit(solution)/shard_map/ppermute | solution.py:30
  30.1 28.8 %collective-permute-start.2 = (bf16[160,2048]{1,0:T(8,128)(2,1)S(1)}, bf16[160,2048]{1,0:T(8,128)(2,1)}, u32[]{:S(2)}, u32[]{:S(2)}) collective-permute-start(bf16[160,2048]{1,0:T(8,128)(2,1)S(1)} %fusion.38.refs_0_.refs_4_), channel_id=1, source_target_pairs={{0,3},{1,2},{2,1},{3,0},{4,7},{5,6},{6,5},{7,4},{8,11},{9,10},{10,... | collective-permute-start | bytes 1966088 | tf_op jit(solution)/shard_map/ppermute | solution.py:30
  60.1 29.5 %collective-permute-start.4 = (bf16[160,2048]{1,0:T(8,128)(2,1)S(1)}, bf16[160,2048]{1,0:T(8,128)(2,1)}, u32[]{:S(2)}, u32[]{:S(2)}) collective-permute-start(bf16[160,2048]{1,0:T(8,128)(2,1)S(1)} %copy-done), channel_id=1, source_target_pairs={{0,2},{1,3},{2,0},{3,1},{4,6},{5,7},{6,4},{7,5},{8,10},{9,11},{10,... | collective-permute-start | bytes 1966088 | tf_op jit(solution)/shard_map/ppermute | solution.py:30
  61.0 28.6 %collective-permute-start.5 = (bf16[160,2048]{1,0:T(8,128)(2,1)S(1)}, bf16[160,2048]{1,0:T(8,128)(2,1)}, u32[]{:S(2)}, u32[]{:S(2)}) collective-permute-start(bf16[160,2048]{1,0:T(8,128)(2,1)S(1)} %copy-done), channel_id=1, source_target_pairs={{0,3},{1,2},{2,1},{3,0},{4,7},{5,6},{6,5},{7,4},{8,11},{9,10},{10,... | collective-permute-start | bytes 1966088 | tf_op jit(solution)/shard_map/ppermute | solution.py:30
  132.7 29.5 %collective-permute-start.11 = (bf16[160,2048]{1,0:T(8,128)(2,1)}, bf16[160,2048]{1,0:T(8,128)(2,1)S(1)}, u32[]{:S(2)}, u32[]{:S(2)}) collective-permute-start(bf16[160,2048]{1,0:T(8,128)(2,1)} %get-tuple-element.365), channel_id=1, source_target_pairs={{0,2},{1,3},{2,0},{3,1},{4,6},{5,7},{6,4},{7,5},{8,10},{9,11},{10,... | collective-permute-start | bytes 1966088 | tf_op jit(solution)/shard_map/ppermute | solution.py:30
  134.2 28.0 %collective-permute-start.12 = (bf16[160,2048]{1,0:T(8,128)(2,1)}, bf16[160,2048]{1,0:T(8,128)(2,1)S(1)}, u32[]{:S(2)}, u32[]{:S(2)}) collective-permute-start(bf16[160,2048]{1,0:T(8,128)(2,1)} %get-tuple-element.364), channel_id=1, source_target_pairs={{0,3},{1,2},{2,1},{3,0},{4,7},{5,6},{6,5},{7,4},{8,11},{9,10},{10,... | collective-permute-start | bytes 1966088 | tf_op jit(solution)/shard_map/ppermute | solution.py:30
  166.7 28.3 %collective-permute-start.17 = (bf16[160,2048]{1,0:T(8,128)(2,1)S(1)}, bf16[160,2048]{1,0:T(8,128)(2,1)S(1)}, u32[]{:S(2)}, u32[]{:S(2)}) collective-permute-start(bf16[160,2048]{1,0:T(8,128)(2,1)S(1)} %multiply_convert_fusion.3.refs_0_.refs_4_), channel_id=1, source_target_pairs={{0,2},{1,3},{2,0},{3,1},{4,6},{5,7},{6,4},{7,5},{8,10},{9,11},{10,... | collective-permute-start | bytes 1966088 | tf_op jit(solution)/shard_map/ppermute | solution.py:30
  167.8 27.2 %collective-permute-start.18 = (bf16[160,2048]{1,0:T(8,128)(2,1)S(1)}, bf16[160,2048]{1,0:T(8,128)(2,1)S(1)}, u32[]{:S(2)}, u32[]{:S(2)}) collective-permute-start(bf16[160,2048]{1,0:T(8,128)(2,1)S(1)} %multiply_convert_fusion.3.refs_0_.refs_4_), channel_id=1, source_target_pairs={{0,3},{1,2},{2,1},{3,0},{4,7},{5,6},{6,5},{7,4},{8,11},{9,10},{10,... | collective-permute-start | bytes 1966088 | tf_op jit(solution)/shard_map/ppermute | solution.py:30
  277.4 30.7 %collective-permute-start.20 = (bf16[160,2048]{1,0:T(8,128)(2,1)S(1)}, bf16[160,2048]{1,0:T(8,128)(2,1)S(1)}, u32[]{:S(2)}, u32[]{:S(2)}) collective-permute-start(bf16[160,2048]{1,0:T(8,128)(2,1)S(1)} %get-tuple-element.362), channel_id=1, source_target_pairs={{0,2},{1,3},{2,0},{3,1},{4,6},{5,7},{6,4},{7,5},{8,10},{9,11},{10,... | collective-permute-start | bytes 1966088 | tf_op jit(solution)/shard_map/ppermute | solution.py:30
  278.8 29.2 %collective-permute-start.21 = (bf16[160,2048]{1,0:T(8,128)(2,1)S(1)}, bf16[160,2048]{1,0:T(8,128)(2,1)S(1)}, u32[]{:S(2)}, u32[]{:S(2)}) collective-permute-start(bf16[160,2048]{1,0:T(8,128)(2,1)S(1)} %get-tuple-element.361), channel_id=1, source_target_pairs={{0,3},{1,2},{2,1},{3,0},{4,7},{5,6},{6,5},{7,4},{8,11},{9,10},{10,... | collective-permute-start | bytes 1966088 | tf_op jit(solution)/shard_map/ppermute | solution.py:30
  310.1 30.0 %collective-permute-start.23 = (bf16[160,2048]{1,0:T(8,128)(2,1)S(1)}, bf16[160,2048]{1,0:T(8,128)(2,1)S(1)}, u32[]{:S(2)}, u32[]{:S(2)}) collective-permute-start(bf16[160,2048]{1,0:T(8,128)(2,1)S(1)} %multiply_convert_fusion.2.refs_0_.refs_4_), channel_id=1, source_target_pairs={{0,2},{1,3},{2,0},{3,1},{4,6},{5,7},{6,4},{7,5},{8,10},{9,11},{10,... | collective-permute-start | bytes 1966088 | tf_op jit(solution)/shard_map/ppermute | solution.py:30
  310.9 29.9 %collective-permute-start.24 = (bf16[160,2048]{1,0:T(8,128)(2,1)S(1)}, bf16[160,2048]{1,0:T(8,128)(2,1)}, u32[]{:S(2)}, u32[]{:S(2)}) collective-permute-start(bf16[160,2048]{1,0:T(8,128)(2,1)S(1)} %multiply_convert_fusion.2.refs_0_.refs_4_), channel_id=1, source_target_pairs={{0,3},{1,2},{2,1},{3,0},{4,7},{5,6},{6,5},{7,4},{8,11},{9,10},{10,... | collective-permute-start | bytes 1966088 | tf_op jit(solution)/shard_map/ppermute | solution.py:30
  363.0 199.8 %reduce-scatter.7.cloned.1.call-start = ((), (), s32[]{:S(2)}) async-start(), calls=%async_computation.10 | async-start | bytes 3604480 | tf_op jit(solution)/shard_map/reduce_scatter | solution.py:189
  377.1 29.0 %collective-permute-start.30 = (bf16[160,2048]{1,0:T(8,128)(2,1)}, bf16[160,2048]{1,0:T(8,128)(2,1)S(1)}, u32[]{:S(2)}, u32[]{:S(2)}) collective-permute-start(bf16[160,2048]{1,0:T(8,128)(2,1)} %get-tuple-element.359), channel_id=1, source_target_pairs={{0,2},{1,3},{2,0},{3,1},{4,6},{5,7},{6,4},{7,5},{8,10},{9,11},{10,... | collective-permute-start | bytes 1966088 | tf_op jit(solution)/shard_map/ppermute | solution.py:30
  378.6 27.4 %collective-permute-start.31 = (bf16[160,2048]{1,0:T(8,128)(2,1)}, bf16[160,2048]{1,0:T(8,128)(2,1)}, u32[]{:S(2)}, u32[]{:S(2)}) collective-permute-start(bf16[160,2048]{1,0:T(8,128)(2,1)} %get-tuple-element.358), channel_id=1, source_target_pairs={{0,3},{1,2},{2,1},{3,0},{4,7},{5,6},{6,5},{7,4},{8,11},{9,10},{10,... | collective-permute-start | bytes 1966088 | tf_op jit(solution)/shard_map/ppermute | solution.py:30
  409.7 27.9 %collective-permute-start.36 = (bf16[160,2048]{1,0:T(8,128)(2,1)S(1)}, bf16[160,2048]{1,0:T(8,128)(2,1)S(1)}, u32[]{:S(2)}, u32[]{:S(2)}) collective-permute-start(bf16[160,2048]{1,0:T(8,128)(2,1)S(1)} %multiply_convert_fusion.refs_0_.refs_4_), channel_id=1, source_target_pairs={{0,2},{1,3},{2,0},{3,1},{4,6},{5,7},{6,4},{7,5},{8,10},{9,11},{10,... | collective-permute-start | bytes 1966088 | tf_op jit(solution)/shard_map/ppermute | solution.py:30
  410.6 27.9 %collective-permute-start.37 = (bf16[160,2048]{1,0:T(8,128)(2,1)S(1)}, bf16[160,2048]{1,0:T(8,128)(2,1)}, u32[]{:S(2)}, u32[]{:S(2)}) collective-permute-start(bf16[160,2048]{1,0:T(8,128)(2,1)S(1)} %multiply_convert_fusion.refs_0_.refs_4_), channel_id=1, source_target_pairs={{0,3},{1,2},{2,1},{3,0},{4,7},{5,6},{6,5},{7,4},{8,11},{9,10},{10,... | collective-permute-start | bytes 1966088 | tf_op jit(solution)/shard_map/ppermute | solution.py:30
  466.4 50.1 %collective-permute-start.48 = (bf16[160,2048]{1,0:T(8,128)(2,1)S(1)}, bf16[160,2048]{1,0:T(8,128)(2,1)}, u32[]{:S(2)}, u32[]{:S(2)}) collective-permute-start(bf16[160,2048]{1,0:T(8,128)(2,1)S(1)} %multiply_convert_fusion.refs_0_.refs_4_), channel_id=1, source_target_pairs={{0,4},{4,0},{1,5},{5,1},{2,6},{6,2},{3,7},{7,3},{8,12},{12,8},{9,1... | collective-permute-start | bytes 1966088 | tf_op jit(solution)/shard_map/ppermute | solution.py:34
  468.8 60.9 %collective-permute-start.49 = (bf16[160,2048]{1,0:T(8,128)(2,1)S(1)}, bf16[160,2048]{1,0:T(8,128)(2,1)}, u32[]{:S(2)}, u32[]{:S(2)}) collective-permute-start(bf16[160,2048]{1,0:T(8,128)(2,1)S(1)} %collective-permute-done.35.refs_1_.refs_5_), channel_id=1, source_target_pairs={{0,4},{4,0},{1,5},{5,1},{2,6},{6,2},{3,7},{7,3},{8,12},{12,8},{9,1... | collective-permute-start | bytes 1966088 | tf_op jit(solution)/shard_map/ppermute | solution.py:34
  469.0 61.8 %collective-permute-start.50 = (bf16[160,2048]{1,0:T(8,128)(2,1)}, bf16[160,2048]{1,0:T(8,128)(2,1)}, u32[]{:S(2)}, u32[]{:S(2)}) collective-permute-start(bf16[160,2048]{1,0:T(8,128)(2,1)} %copy-done.31), channel_id=1, source_target_pairs={{0,4},{4,0},{1,5},{5,1},{2,6},{6,2},{3,7},{7,3},{8,12},{12,8},{9,1... | collective-permute-start | bytes 1966088 | tf_op jit(solution)/shard_map/ppermute | solution.py:34
  469.3 63.1 %collective-permute-start.51 = (bf16[160,2048]{1,0:T(8,128)(2,1)}, bf16[160,2048]{1,0:T(8,128)(2,1)}, u32[]{:S(2)}, u32[]{:S(2)}) collective-permute-start(bf16[160,2048]{1,0:T(8,128)(2,1)} %collective-permute-done.37.refs_3_.refs_7_), channel_id=1, source_target_pairs={{0,4},{4,0},{1,5},{5,1},{2,6},{6,2},{3,7},{7,3},{8,12},{12,8},{9,1... | collective-permute-start | bytes 1966088 | tf_op jit(solution)/shard_map/ppermute | solution.py:34
  478.7 240.8 %reduce-scatter.9.cloned.1.call-start = ((), (), s32[]{:S(2)}) async-start(), calls=%async_computation.11 | async-start | bytes 7208960 | tf_op jit(solution)/shard_map/reduce_scatter | solution.py:189
  529.6 21.4 %collective-permute-start.43 = (bf16[160,2048]{1,0:T(8,128)(2,1)}, bf16[160,2048]{1,0:T(8,128)(2,1)}, u32[]{:S(2)}, u32[]{:S(2)}) collective-permute-start(bf16[160,2048]{1,0:T(8,128)(2,1)} %get-tuple-element.170), channel_id=1, source_target_pairs={{0,1},{1,0},{2,3},{3,2},{4,5},{5,4},{6,7},{7,6},{8,9},{9,8},{10,11... | collective-permute-start | bytes 1966088 | tf_op jit(solution)/shard_map/ppermute | solution.py:30
  530.8 31.1 %collective-permute-start.44 = (bf16[160,2048]{1,0:T(8,128)(2,1)}, bf16[160,2048]{1,0:T(8,128)(2,1)}, u32[]{:S(2)}, u32[]{:S(2)}) collective-permute-start(bf16[160,2048]{1,0:T(8,128)(2,1)} %get-tuple-element.171), channel_id=1, source_target_pairs={{0,2},{1,3},{2,0},{3,1},{4,6},{5,7},{6,4},{7,5},{8,10},{9,11},{10,... | collective-permute-start | bytes 1966088 | tf_op jit(solution)/shard_map/ppermute | solution.py:30
  532.3 29.6 %collective-permute-start.45 = (bf16[160,2048]{1,0:T(8,128)(2,1)}, bf16[160,2048]{1,0:T(8,128)(2,1)}, u32[]{:S(2)}, u32[]{:S(2)}) collective-permute-start(bf16[160,2048]{1,0:T(8,128)(2,1)} %get-tuple-element.172), channel_id=1, source_target_pairs={{0,3},{1,2},{2,1},{3,0},{4,7},{5,6},{6,5},{7,4},{8,11},{9,10},{10,... | collective-permute-start | bytes 1966088 | tf_op jit(solution)/shard_map/ppermute | solution.py:30
  551.0 198.5 %reduce-scatter.11.cloned.1.call-start = ((), (), s32[]{:S(2)}) async-start(), calls=%async_computation.12 | async-start | bytes 5242880 | tf_op jit(solution)/shard_map/reduce_scatter | solution.py:189
  566.9 35.2 %collective-permute-start.52 = (bf16[160,2048]{1,0:T(8,128)(2,1)S(1)}, bf16[160,2048]{1,0:T(8,128)(2,1)}, u32[]{:S(2)}, u32[]{:S(2)}) collective-permute-start(bf16[160,2048]{1,0:T(8,128)(2,1)S(1)} %fusion.75.refs_0_.refs_12_), channel_id=1, source_target_pairs={{0,1},{1,0},{2,3},{3,2},{4,5},{5,4},{6,7},{7,6},{8,9},{9,8},{10,11... | collective-permute-start | bytes 1966088 | tf_op jit(solution)/shard_map/ppermute | solution.py:30
  568.4 33.6 %collective-permute-start.53 = (bf16[160,2048]{1,0:T(8,128)(2,1)S(1)}, bf16[160,2048]{1,0:T(8,128)(2,1)}, u32[]{:S(2)}, u32[]{:S(2)}) collective-permute-start(bf16[160,2048]{1,0:T(8,128)(2,1)S(1)} %fusion.75.refs_0_.refs_12_), channel_id=1, source_target_pairs={{0,2},{1,3},{2,0},{3,1},{4,6},{5,7},{6,4},{7,5},{8,10},{9,11},{10,... | collective-permute-start | bytes 1966088 | tf_op jit(solution)/shard_map/ppermute | solution.py:30
  569.9 32.2 %collective-permute-start.54 = (bf16[160,2048]{1,0:T(8,128)(2,1)S(1)}, bf16[160,2048]{1,0:T(8,128)(2,1)}, u32[]{:S(2)}, u32[]{:S(2)}) collective-permute-start(bf16[160,2048]{1,0:T(8,128)(2,1)S(1)} %fusion.75.refs_0_.refs_12_), channel_id=1, source_target_pairs={{0,3},{1,2},{2,1},{3,0},{4,7},{5,6},{6,5},{7,4},{8,11},{9,10},{10,... | collective-permute-start | bytes 1966088 | tf_op jit(solution)/shard_map/ppermute | solution.py:30
  572.7 24.7 %collective-permute-start.55 = (f32[160]{0:T(256)S(1)}, f32[160]{0:T(256)S(1)}, u32[]{:S(2)}, u32[]{:S(2)}) collective-permute-start(f32[160]{0:T(256)S(1)} %multiply_reduce_fusion.6), channel_id=1, source_target_pairs={{0,1},{1,0},{2,3},{3,2},{4,5},{5,4},{6,7},{7,6},{8,9},{9,8},{10,11... | collective-permute-start | bytes 1928 | tf_op jit(solution)/shard_map/ppermute | solution.py:30
  574.9 24.9 %collective-permute-start.56 = (f32[160]{0:T(256)S(1)}, f32[160]{0:T(256)S(1)}, u32[]{:S(2)}, u32[]{:S(2)}) collective-permute-start(f32[160]{0:T(256)S(1)} %multiply_reduce_fusion.6), channel_id=1, source_target_pairs={{0,2},{1,3},{2,0},{3,1},{4,6},{5,7},{6,4},{7,5},{8,10},{9,11},{10,... | collective-permute-start | bytes 1928 | tf_op jit(solution)/shard_map/ppermute | solution.py:30
  648.2 18.0 %collective-permute-start.67 = (bf16[160,2048]{1,0:T(8,128)(2,1)}, bf16[160,2048]{1,0:T(8,128)(2,1)}, u32[]{:S(2)}, u32[]{:S(2)}) collective-permute-start(bf16[160,2048]{1,0:T(8,128)(2,1)} %get-tuple-element.195), channel_id=1, source_target_pairs={{0,1},{1,0},{2,3},{3,2},{4,5},{5,4},{6,7},{7,6},{8,9},{9,8},{10,11... | collective-permute-start | bytes 1966088 | tf_op jit(solution)/shard_map/ppermute | solution.py:30
  649.8 30.9 %collective-permute-start.68 = (bf16[160,2048]{1,0:T(8,128)(2,1)}, bf16[160,2048]{1,0:T(8,128)(2,1)}, u32[]{:S(2)}, u32[]{:S(2)}) collective-permute-start(bf16[160,2048]{1,0:T(8,128)(2,1)} %get-tuple-element.196), channel_id=1, source_target_pairs={{0,2},{1,3},{2,0},{3,1},{4,6},{5,7},{6,4},{7,5},{8,10},{9,11},{10,... | collective-permute-start | bytes 1966088 | tf_op jit(solution)/shard_map/ppermute | solution.py:30
  651.2 29.5 %collective-permute-start.69 = (bf16[160,2048]{1,0:T(8,128)(2,1)}, bf16[160,2048]{1,0:T(8,128)(2,1)}, u32[]{:S(2)}, u32[]{:S(2)}) collective-permute-start(bf16[160,2048]{1,0:T(8,128)(2,1)} %get-tuple-element.197), channel_id=1, source_target_pairs={{0,3},{1,2},{2,1},{3,0},{4,7},{5,6},{6,5},{7,4},{8,11},{9,10},{10,... | collective-permute-start | bytes 1966088 | tf_op jit(solution)/shard_map/ppermute | solution.py:30
  664.4 174.2 %reduce-scatter.13.cloned.1.call-start = ((), (), s32[]{:S(2)}) async-start(), calls=%async_computation.13 | async-start | bytes 3604480 | tf_op jit(solution)/shard_map/reduce_scatter | solution.py:189
  664.9 59.4 %collective-permute-start.78 = (bf16[640,1408]{1,0:T(8,128)(2,1)}, bf16[640,1408]{1,0:T(8,128)(2,1)}, u32[]{:S(2)}, u32[]{:S(2)}) collective-permute-start(bf16[640,1408]{1,0:T(8,128)(2,1)} %get-tuple-element.150.refs_0_), channel_id=1, source_target_pairs={{0,4},{4,0},{1,5},{5,1},{2,6},{6,2},{3,7},{7,3},{8,12},{12,8},{9,1... | collective-permute-start | bytes 5406728 | tf_op jit(solution)/shard_map/ppermute | solution.py:34
  688.9 29.8 %collective-permute-start.76 = (bf16[160,2048]{1,0:T(8,128)(2,1)S(1)}, bf16[160,2048]{1,0:T(8,128)(2,1)S(1)}, u32[]{:S(2)}, u32[]{:S(2)}) collective-permute-start(bf16[160,2048]{1,0:T(8,128)(2,1)S(1)} %get-tuple-element.205.refs_2_.refs_0_), channel_id=1, source_target_pairs={{0,2},{1,3},{2,0},{3,1},{4,6},{5,7},{6,4},{7,5},{8,10},{9,11},{10,... | collective-permute-start | bytes 1966088 | tf_op jit(solution)/shard_map/ppermute | solution.py:30
  689.8 29.7 %collective-permute-start.77 = (bf16[160,2048]{1,0:T(8,128)(2,1)S(1)}, bf16[160,2048]{1,0:T(8,128)(2,1)}, u32[]{:S(2)}, u32[]{:S(2)}) collective-permute-start(bf16[160,2048]{1,0:T(8,128)(2,1)S(1)} %get-tuple-element.205.refs_2_.refs_0_), channel_id=1, source_target_pairs={{0,3},{1,2},{2,1},{3,0},{4,7},{5,6},{6,5},{7,4},{8,11},{9,10},{10,... | collective-permute-start | bytes 1966088 | tf_op jit(solution)/shard_map/ppermute | solution.py:30
  691.2 33.6 %collective-permute-start.79 = (bf16[160,2048]{1,0:T(8,128)(2,1)S(1)}, bf16[160,2048]{1,0:T(8,128)(2,1)}, u32[]{:S(2)}, u32[]{:S(2)}) collective-permute-start(bf16[160,2048]{1,0:T(8,128)(2,1)S(1)} %get-tuple-element.205.refs_2_.refs_0_), channel_id=1, source_target_pairs={{0,4},{4,0},{1,5},{5,1},{2,6},{6,2},{3,7},{7,3},{8,12},{12,8},{9,1... | collective-permute-start | bytes 1966088 | tf_op jit(solution)/shard_map/ppermute | solution.py:34
  724.3 25.2 %collective-permute-start.88 = (bf16[160,2048]{1,0:T(8,128)(2,1)S(1)}, bf16[160,2048]{1,0:T(8,128)(2,1)}, u32[]{:S(2)}, u32[]{:S(2)}) collective-permute-start(bf16[160,2048]{1,0:T(8,128)(2,1)S(1)} %copy-done.4), channel_id=1, source_target_pairs={{0,4},{4,0},{1,5},{5,1},{2,6},{6,2},{3,7},{7,3},{8,12},{12,8},{9,1... | collective-permute-start | bytes 1966088 | tf_op jit(solution)/shard_map/ppermute | solution.py:34
  724.8 37.6 %collective-permute-start.89 = (bf16[160,2048]{1,0:T(8,128)(2,1)S(1)}, bf16[160,2048]{1,0:T(8,128)(2,1)}, u32[]{:S(2)}, u32[]{:S(2)}) collective-permute-start(bf16[160,2048]{1,0:T(8,128)(2,1)S(1)} %copy-done.22), channel_id=1, source_target_pairs={{0,4},{4,0},{1,5},{5,1},{2,6},{6,2},{3,7},{7,3},{8,12},{12,8},{9,1... | collective-permute-start | bytes 1966088 | tf_op jit(solution)/shard_map/ppermute | solution.py:34
  724.9 38.2 %collective-permute-start.90 = (bf16[160,2048]{1,0:T(8,128)(2,1)S(1)}, bf16[160,2048]{1,0:T(8,128)(2,1)}, u32[]{:S(2)}, u32[]{:S(2)}) collective-permute-start(bf16[160,2048]{1,0:T(8,128)(2,1)S(1)} %copy-done.24), channel_id=1, source_target_pairs={{0,4},{4,0},{1,5},{5,1},{2,6},{6,2},{3,7},{7,3},{8,12},{12,8},{9,1... | collective-permute-start | bytes 1966088 | tf_op jit(solution)/shard_map/ppermute | solution.py:34
  725.3 39.2 %collective-permute-start.91 = (bf16[160,2048]{1,0:T(8,128)(2,1)}, bf16[160,2048]{1,0:T(8,128)(2,1)}, u32[]{:S(2)}, u32[]{:S(2)}) collective-permute-start(bf16[160,2048]{1,0:T(8,128)(2,1)} %copy-done.140), channel_id=1, source_target_pairs={{0,4},{4,0},{1,5},{5,1},{2,6},{6,2},{3,7},{7,3},{8,12},{12,8},{9,1... | collective-permute-start | bytes 1966088 | tf_op jit(solution)/shard_map/ppermute | solution.py:34
  749.2 185.3 %reduce-scatter.15.cloned.1.call-start = ((), (), s32[]{:S(2)}) async-start(), calls=%async_computation.14 | async-start | bytes 7208960 | tf_op jit(solution)/shard_map/reduce_scatter | solution.py:189
  762.4 20.2 %collective-permute-start.83 = (bf16[160,2048]{1,0:T(8,128)(2,1)}, bf16[160,2048]{1,0:T(8,128)(2,1)}, u32[]{:S(2)}, u32[]{:S(2)}) collective-permute-start(bf16[160,2048]{1,0:T(8,128)(2,1)} %get-tuple-element.216), channel_id=1, source_target_pairs={{0,1},{1,0},{2,3},{3,2},{4,5},{5,4},{6,7},{7,6},{8,9},{9,8},{10,11... | collective-permute-start | bytes 1966088 | tf_op jit(solution)/shard_map/ppermute | solution.py:30
  763.1 31.1 %collective-permute-start.84 = (bf16[160,2048]{1,0:T(8,128)(2,1)}, bf16[160,2048]{1,0:T(8,128)(2,1)}, u32[]{:S(2)}, u32[]{:S(2)}) collective-permute-start(bf16[160,2048]{1,0:T(8,128)(2,1)} %get-tuple-element.217), channel_id=1, source_target_pairs={{0,2},{1,3},{2,0},{3,1},{4,6},{5,7},{6,4},{7,5},{8,10},{9,11},{10,... | collective-permute-start | bytes 1966088 | tf_op jit(solution)/shard_map/ppermute | solution.py:30
  764.5 29.7 %collective-permute-start.85 = (bf16[160,2048]{1,0:T(8,128)(2,1)}, bf16[160,2048]{1,0:T(8,128)(2,1)}, u32[]{:S(2)}, u32[]{:S(2)}) collective-permute-start(bf16[160,2048]{1,0:T(8,128)(2,1)} %get-tuple-element.218), channel_id=1, source_target_pairs={{0,3},{1,2},{2,1},{3,0},{4,7},{5,6},{6,5},{7,4},{8,11},{9,10},{10,... | collective-permute-start | bytes 1966088 | tf_op jit(solution)/shard_map/ppermute | solution.py:30
  782.3 209.5 %reduce-scatter.17.cloned.1.call-start = ((), (), s32[]{:S(2)}) async-start(), calls=%async_computation.15 | async-start | bytes 5242880 | tf_op jit(solution)/shard_map/reduce_scatter | solution.py:189
  804.8 31.1 %collective-permute-start.95 = (bf16[160,2048]{1,0:T(8,128)(2,1)S(1)}, bf16[160,2048]{1,0:T(8,128)(2,1)S(1)}, u32[]{:S(2)}, u32[]{:S(2)}) collective-permute-start(bf16[160,2048]{1,0:T(8,128)(2,1)S(1)} %get-tuple-element.321.refs_0_.refs_12_), channel_id=1, source_target_pairs={{0,1},{1,0},{2,3},{3,2},{4,5},{5,4},{6,7},{7,6},{8,9},{9,8},{10,11... | collective-permute-start | bytes 1966088 | tf_op jit(solution)/shard_map/ppermute | solution.py:30
  805.4 32.3 %collective-permute-start.96 = (bf16[160,2048]{1,0:T(8,128)(2,1)S(1)}, bf16[160,2048]{1,0:T(8,128)(2,1)S(1)}, u32[]{:S(2)}, u32[]{:S(2)}) collective-permute-start(bf16[160,2048]{1,0:T(8,128)(2,1)S(1)} %get-tuple-element.321.refs_0_.refs_12_), channel_id=1, source_target_pairs={{0,2},{1,3},{2,0},{3,1},{4,6},{5,7},{6,4},{7,5},{8,10},{9,11},{10,... | collective-permute-start | bytes 1966088 | tf_op jit(solution)/shard_map/ppermute | solution.py:30
  806.8 31.7 %collective-permute-start.97 = (bf16[160,2048]{1,0:T(8,128)(2,1)S(1)}, bf16[160,2048]{1,0:T(8,128)(2,1)}, u32[]{:S(2)}, u32[]{:S(2)}) collective-permute-start(bf16[160,2048]{1,0:T(8,128)(2,1)S(1)} %get-tuple-element.321.refs_0_.refs_12_), channel_id=1, source_target_pairs={{0,3},{1,2},{2,1},{3,0},{4,7},{5,6},{6,5},{7,4},{8,11},{9,10},{10,... | collective-permute-start | bytes 1966088 | tf_op jit(solution)/shard_map/ppermute | solution.py:30
  815.4 19.1 %collective-permute-start.99 = (f32[160]{0:T(256)S(1)}, f32[160]{0:T(256)S(1)}, u32[]{:S(2)}, u32[]{:S(2)}) collective-permute-start(f32[160]{0:T(256)S(1)} %multiply_reduce_fusion.3), channel_id=1, source_target_pairs={{0,2},{1,3},{2,0},{3,1},{4,6},{5,7},{6,4},{7,5},{8,10},{9,11},{10,... | collective-permute-start | bytes 1928 | tf_op jit(solution)/shard_map/ppermute | solution.py:30
  817.5 38.4 %collective-permute-start.92 = (bf16[160,2048]{1,0:T(8,128)(2,1)}, bf16[160,2048]{1,0:T(8,128)(2,1)S(1)}, u32[]{:S(2)}, u32[]{:S(2)}) collective-permute-start(bf16[160,2048]{1,0:T(8,128)(2,1)} %get-tuple-element.342), channel_id=1, source_target_pairs={{0,1},{1,0},{2,3},{3,2},{4,5},{5,4},{6,7},{7,6},{8,9},{9,8},{10,11... | collective-permute-start | bytes 1966088 | tf_op jit(solution)/shard_map/ppermute | solution.py:30
  834.5 28.2 %collective-permute-start.93 = (bf16[160,2048]{1,0:T(8,128)(2,1)}, bf16[160,2048]{1,0:T(8,128)(2,1)S(1)}, u32[]{:S(2)}, u32[]{:S(2)}) collective-permute-start(bf16[160,2048]{1,0:T(8,128)(2,1)} %get-tuple-element.344), channel_id=1, source_target_pairs={{0,2},{1,3},{2,0},{3,1},{4,6},{5,7},{6,4},{7,5},{8,10},{9,11},{10,... | collective-permute-start | bytes 1966088 | tf_op jit(solution)/shard_map/ppermute | solution.py:30
  835.9 26.7 %collective-permute-start.94 = (bf16[160,2048]{1,0:T(8,128)(2,1)}, bf16[160,2048]{1,0:T(8,128)(2,1)}, u32[]{:S(2)}, u32[]{:S(2)}) collective-permute-start(bf16[160,2048]{1,0:T(8,128)(2,1)} %get-tuple-element.343), channel_id=1, source_target_pairs={{0,3},{1,2},{2,1},{3,0},{4,7},{5,6},{6,5},{7,4},{8,11},{9,10},{10,... | collective-permute-start | bytes 1966088 | tf_op jit(solution)/shard_map/ppermute | solution.py:30
  901.8 17.9 %collective-permute-start.110 = (bf16[160,2048]{1,0:T(8,128)(2,1)}, bf16[160,2048]{1,0:T(8,128)(2,1)}, u32[]{:S(2)}, u32[]{:S(2)}) collective-permute-start(bf16[160,2048]{1,0:T(8,128)(2,1)} %get-tuple-element.241), channel_id=1, source_target_pairs={{0,1},{1,0},{2,3},{3,2},{4,5},{5,4},{6,7},{7,6},{8,9},{9,8},{10,11... | collective-permute-start | bytes 1966088 | tf_op jit(solution)/shard_map/ppermute | solution.py:30
  903.4 31.1 %collective-permute-start.111 = (bf16[160,2048]{1,0:T(8,128)(2,1)}, bf16[160,2048]{1,0:T(8,128)(2,1)}, u32[]{:S(2)}, u32[]{:S(2)}) collective-permute-start(bf16[160,2048]{1,0:T(8,128)(2,1)} %get-tuple-element.242), channel_id=1, source_target_pairs={{0,2},{1,3},{2,0},{3,1},{4,6},{5,7},{6,4},{7,5},{8,10},{9,11},{10,... | collective-permute-start | bytes 1966088 | tf_op jit(solution)/shard_map/ppermute | solution.py:30
  904.1 30.4 %collective-permute-start.112 = (bf16[160,2048]{1,0:T(8,128)(2,1)}, bf16[160,2048]{1,0:T(8,128)(2,1)}, u32[]{:S(2)}, u32[]{:S(2)}) collective-permute-start(bf16[160,2048]{1,0:T(8,128)(2,1)} %get-tuple-element.243), channel_id=1, source_target_pairs={{0,3},{1,2},{2,1},{3,0},{4,7},{5,6},{6,5},{7,4},{8,11},{9,10},{10,... | collective-permute-start | bytes 1966088 | tf_op jit(solution)/shard_map/ppermute | solution.py:30
  (232 other events, 4092.2 us)
Sparse Core Ops, SparseCore 0:
  11.4 84.7 all-gather.6
  98.3 154.6 all-gather.8
  255.2 80.9 all-gather.10
  337.7 106.7 all-gather.12
  446.5 59.1 all-gather.14
  508.4 54.3 reduce-scatter.6
  565.1 102.3 reduce-scatter.8
  669.8 77.2 reduce-scatter.10
  750.1 56.6 reduce-scatter.12
  809.1 102.3 reduce-scatter.14
  913.9 77.8 reduce-scatter.16

commit v6 on v5

--- a/solution.py
+++ b/solution.py
@@ -194,27 +194,26 @@
     return [values[k * rows : (k + 1) * rows] for k in range(count)]
 
 
-def unfold(shards):
-    height, width = shards[0].shape
-    units, layers = height // 4, len(shards)
-
-    def kernel(*refs):
-        for layer, ref in enumerate(refs[:layers]):
-            for k, out in enumerate(refs[layers:]):
-                part = ref[k * units : (k + 1) * units, :].astype(f32)
-                out[layer] = part if k == 3 else part.T
-
-    shapes = [(layers, width, units)] * 3 + [(layers, units, width)]
-    return call(
+def unfold(shard, layer, layers, before=()):
+    height, width = shard.shape
+    units = height // 4
+
+    def kernel(ref, *refs):
+        for k, out in enumerate(refs[len(before) :]):
+            part = ref[k * units : (k + 1) * units, :].astype(f32)
+            out[0] = part if k == 3 else part.T
+
+    shapes = [(width, units)] * 3 + [(units, width)]
+    return pl.pallas_call(
         kernel,
-        (1,),
-        [whole(shard) for shard in shards],
-        [pl.BlockSpec(shape, lambda j: (0, 0, 0)) for shape in shapes],
-        [jax.ShapeDtypeStruct(shape, f32) for shape in shapes],
-        [],
-        shards,
-        0,
-    )
+        grid=(1,),
+        in_specs=[whole(shard)] + [pl.BlockSpec(memory_space=pl.ANY)] * len(before),
+        out_specs=[pl.BlockSpec((1, *shape), lambda j: (layer, 0, 0)) for shape in shapes],
+        out_shape=[jax.ShapeDtypeStruct((layers, *shape), f32) for shape in shapes],
+        input_output_aliases={k + 1: k for k in range(len(before))},
+        compiler_params=pltpu.CompilerParams(vmem_limit_bytes=VMEM),
+        cost_estimate=pl.CostEstimate(flops=0, bytes_accessed=0, transcendentals=0),
+    )(shard, *before)
 
 
 def rows_at(matrix, at, rows, tile):
@@ -720,8 +719,13 @@
     for layer in range(LAYERS):
         ffn_shard, down_shard = scattered["ffn", layer], scattered["down", layer]
         shards[layer] = (ffn_shard[:hidden_units].T, ffn_shard[hidden_units:].T, down_shard)
-    low_shards = [after(scattered["low", 0], grad_x)] + [scattered["low", k] for k in range(1, LAYERS)]
-    stacked = [*unfold(low_shards)] + [
+    low_gradients = ()
+    for layer in reversed(range(LAYERS)):
+        low_shard = scattered["low", layer]
+        if layer == 0:
+            low_shard = after(low_shard, grad_x, *low_gradients)
+        low_gradients = unfold(low_shard, layer, LAYERS, low_gradients)
+    stacked = [*low_gradients] + [
         jnp.stack([shards[layer][member].astype(f32) for layer in range(LAYERS)]) for member in range(3)
     ]
     wide_rows, own_rows = small[: 2 * LAYERS], small[2 * LAYERS :]

time: 1010 us -> 1010 us (level)
    pallas_call x17 -> x16, Pallas kernels: 188 us -> 185 us  [call(): pl.pallas_call(kernel, grid_spec=pltpu.PrefetchScalarGridSpec(num_scalar_...]
    unnamed x328 -> x330, local copies, waits for them, and re-layouts: 36.5 us -> 36.5 us
  transfers between devices with their start and end apart: 138 -> 138, of which waited for: 55 -> 55; matrix products, arithmetic and copies ran while one was open for 15% -> 15% of each run, Pallas kernels for 18% -> 19%
where the time goes in v6:
time: 1010 us; the launch traced here: 1000 us
  waiting for transfers between devices  502 us (50%)
  Pallas kernels  188 us (19%)
  starting transfers between devices  115 us (11%)
  local copies, waits for them, and re-layouts  68.8 us (7%)
  matrix products  58.7 us (6%)
  other arithmetic  53.3 us (5%)
  between operations  16.5 us (2%)
    ppermute x66, waiting for transfers between devices, exchange(): return lax.ppermute(values, 'fsdp', [(i, i ^ step) for i in range(size)])  357 us
    pallas_call x16, Pallas kernels, call(): pl.pallas_call(kernel, grid_spec=pltpu.PrefetchScalarGridSpec(num_scalar_...  185 us
    all_gather x4, waiting for transfers between devices, tall(): lax.all_gather(jnp.concatenate(shards, axis=0), SEQ, axis=1, tiled=True)  90.7 us
    ppermute x66, starting transfers between devices, exchange(): return lax.ppermute(values, 'fsdp', [(i, i ^ step) for i in range(size)])  80.9 us
    dot_general x6, matrix products, dot(): return jnp.dot(left, right, preferred_element_type=f32)  48.3 us
    unnamed x330, local copies, waits for them, and re-layouts  36.5 us
    ppermute x12, starting transfers between devices, entering_of(): lax.ppermute(pair, SEQ, [(i, i + sign * 2 * hop) for i in range(length) i...  20.6 us
  transfers between devices with their start and end apart: 138, of which 55 were waited for; matrix products, arithmetic and copies ran while one was open for 15% of the time, Pallas kernels for 19%

profile of v6, /device:TPU:0, one launch (start us, length us, event | category | flops | bytes accessed | tf_op | source)
XLA Modules:
  0.0 1001.3 jit_solution(18338280403550244415)
XLA Ops:
  30.4 13.7 %collective-permute-done.refs_1_.refs_5_ = bf16[160,2048]{1,0:T(8,128)(2,1)S(1)} collective-permute-done((bf16[160,2048]{1,0:T(8,128)(2,1)S(1)}, bf16[160,2048]{1,0:T(8,128)(2,1)S(1)}, u32[]{:S(2)}, u32[]{:S(2)}) %collective-permute-start) | collective-permute-done | bytes 655392 | tf_op jit(solution)/shard_map/ppermute | solution.py:30
  44.1 14.8 %collective-permute-done.1.refs_2_.refs_6_ = bf16[160,2048]{1,0:T(8,128)(2,1)} collective-permute-done((bf16[160,2048]{1,0:T(8,128)(2,1)S(1)}, bf16[160,2048]{1,0:T(8,128)(2,1)}, u32[]{:S(2)}, u32[]{:S(2)}) %collective-permute-start.1) | collective-permute-done | bytes 655392 | tf_op jit(solution)/shard_map/ppermute | solution.py:30
  64.0 12.7 %collective-permute-done.3.refs_3_.refs_1_ = bf16[160,2048]{1,0:T(8,128)(2,1)S(1)} collective-permute-done((bf16[160,2048]{1,0:T(8,128)(2,1)S(1)}, bf16[160,2048]{1,0:T(8,128)(2,1)S(1)}, u32[]{:S(2)}, u32[]{:S(2)}) %collective-permute-start.3) | collective-permute-done | bytes 655392 | tf_op jit(solution)/shard_map/ppermute | solution.py:30
  76.6 13.0 %collective-permute-done.4.refs_4_.refs_2_ = bf16[160,2048]{1,0:T(8,128)(2,1)} collective-permute-done((bf16[160,2048]{1,0:T(8,128)(2,1)S(1)}, bf16[160,2048]{1,0:T(8,128)(2,1)}, u32[]{:S(2)}, u32[]{:S(2)}) %collective-permute-start.4) | collective-permute-done | bytes 655392 | tf_op jit(solution)/shard_map/ppermute | solution.py:30
  89.6 6.6 all-gather.7.cloned.1.call-done.refs_4_.refs_5_.refs_6_
  96.2 13.3 %shard_map.237 = (f32[640,512]{1,0:T(8,128)}, f32[640,512]{1,0:T(8,128)}, f32[640,512]{1,0:T(8,128)}, f32[640,512]{1,0:T(8,128)}, f32[640,512]{1,0:T(8,128)}) custom-call(s32[1]{0:T(128)} %bitcast.place_ref, bf16[160,2048]{1,0:T(8,128)(2,1)S(1)} %fusion.38.refs_0_.refs_4_, bf16[160,2048]{1,0:T(8,128)(2,1)S(1)} %collective-permute-done.refs_1_.refs_5_, ...), custom_call_target="tpu_custom_call" | custom-call | flops 22145925120 | bytes 7864320 | tf_op jit(solution)/shard_map/pallas_call | solution.py:106
  113.5 3.7 collective-permute-start.8
  125.7 3.2 convolution_convert_fusion.2
  134.9 14.0 %collective-permute-done.10 = bf16[160,2048]{1,0:T(8,128)(2,1)S(1)} collective-permute-done((bf16[160,2048]{1,0:T(8,128)(2,1)}, bf16[160,2048]{1,0:T(8,128)(2,1)S(1)}, u32[]{:S(2)}, u32[]{:S(2)}) %collective-permute-start.10) | collective-permute-done | bytes 655392 | tf_op jit(solution)/shard_map/ppermute | solution.py:30
  148.9 13.3 %collective-permute-done.11 = bf16[160,2048]{1,0:T(8,128)(2,1)S(1)} collective-permute-done((bf16[160,2048]{1,0:T(8,128)(2,1)}, bf16[160,2048]{1,0:T(8,128)(2,1)S(1)}, u32[]{:S(2)}, u32[]{:S(2)}) %collective-permute-start.11) | collective-permute-done | bytes 655392 | tf_op jit(solution)/shard_map/ppermute | solution.py:30
  169.2 14.2 %collective-permute-done.16.refs_1_.refs_5_ = bf16[160,2048]{1,0:T(8,128)(2,1)S(1)} collective-permute-done((bf16[160,2048]{1,0:T(8,128)(2,1)S(1)}, bf16[160,2048]{1,0:T(8,128)(2,1)S(1)}, u32[]{:S(2)}, u32[]{:S(2)}) %collective-permute-start.16) | collective-permute-done | bytes 655392 | tf_op jit(solution)/shard_map/ppermute | solution.py:30
  183.4 11.6 %collective-permute-done.17.refs_2_.refs_6_ = bf16[160,2048]{1,0:T(8,128)(2,1)S(1)} collective-permute-done((bf16[160,2048]{1,0:T(8,128)(2,1)S(1)}, bf16[160,2048]{1,0:T(8,128)(2,1)S(1)}, u32[]{:S(2)}, u32[]{:S(2)}) %collective-permute-start.17) | collective-permute-done | bytes 655392 | tf_op jit(solution)/shard_map/ppermute | solution.py:30
  195.0 58.0 %all-gather.9.cloned.1.call-done.refs_4_.refs_5_ = bf16[4224,2048]{1,0:T(8,128)(2,1)} async-done(((bf16[4224,256]{1,0:T(8,128)(2,1)}), bf16[4224,2048]{1,0:T(8,128)(2,1)}) %all-gather.9.cloned.1.call-update) | async-done | bytes 17301520 | tf_op jit(solution)/shard_map/all_gather | solution.py:549
  253.1 15.1 %shard_map.238 = (bf16[640,1408]{1,0:T(8,128)(2,1)}, bf16[640,1408]{1,0:T(8,128)(2,1)}, bf16[640,1408]{1,0:T(8,128)(2,1)}) custom-call(bf16[160,2048]{1,0:T(8,128)(2,1)S(1)} %multiply_convert_fusion.3.refs_0_.refs_4_, bf16[160,2048]{1,0:T(8,128)(2,1)S(1)} %collective-permute-done.16.refs_1_.refs_5_, ...), custom_call_target="tpu_custom_call" | custom-call | flops 40600862720 | bytes 14417920 | tf_op jit(solution)/shard_map/pallas_call | solution.py:106
  268.1 7.4 fusion.18
  279.3 14.1 %collective-permute-done.19 = bf16[160,2048]{1,0:T(8,128)(2,1)S(1)} collective-permute-done((bf16[160,2048]{1,0:T(8,128)(2,1)S(1)}, bf16[160,2048]{1,0:T(8,128)(2,1)S(1)}, u32[]{:S(2)}, u32[]{:S(2)}) %collective-permute-start.19) | collective-permute-done | bytes 655392 | tf_op jit(solution)/shard_map/ppermute | solution.py:30
  293.4 14.6 %collective-permute-done.20 = bf16[160,2048]{1,0:T(8,128)(2,1)S(1)} collective-permute-done((bf16[160,2048]{1,0:T(8,128)(2,1)S(1)}, bf16[160,2048]{1,0:T(8,128)(2,1)S(1)}, u32[]{:S(2)}, u32[]{:S(2)}) %collective-permute-start.20) | collective-permute-done | bytes 655392 | tf_op jit(solution)/shard_map/ppermute | solution.py:30
  312.4 14.2 %collective-permute-done.22.refs_1_.refs_5_ = bf16[160,2048]{1,0:T(8,128)(2,1)S(1)} collective-permute-done((bf16[160,2048]{1,0:T(8,128)(2,1)S(1)}, bf16[160,2048]{1,0:T(8,128)(2,1)S(1)}, u32[]{:S(2)}, u32[]{:S(2)}) %collective-permute-start.22) | collective-permute-done | bytes 655392 | tf_op jit(solution)/shard_map/ppermute | solution.py:30
  326.6 13.5 %collective-permute-done.23.refs_2_.refs_6_ = bf16[160,2048]{1,0:T(8,128)(2,1)S(1)} collective-permute-done((bf16[160,2048]{1,0:T(8,128)(2,1)S(1)}, bf16[160,2048]{1,0:T(8,128)(2,1)S(1)}, u32[]{:S(2)}, u32[]{:S(2)}) %collective-permute-start.23) | collective-permute-done | bytes 655392 | tf_op jit(solution)/shard_map/ppermute | solution.py:30
  340.9 13.8 %shard_map.239 = (f32[640,512]{1,0:T(8,128)}, f32[640,512]{1,0:T(8,128)}, f32[640,512]{1,0:T(8,128)}, f32[640,512]{1,0:T(8,128)}, f32[640,512]{1,0:T(8,128)}) custom-call(s32[1]{0:T(128)} %bitcast.place_ref, bf16[160,2048]{1,0:T(8,128)(2,1)S(1)} %multiply_convert_fusion.2.refs_0_.refs_4_, bf16[160,2048]{1,0:T(8,128)(2,1)S(1)} %collective-permute-done.22.refs_1_.refs_5_, ...), custom_call_target="tpu_custom_call" | custom-call | flops 22145925120 | bytes 7864320 | tf_op jit(solution)/shard_map/pallas_call | solution.py:106
  369.9 3.6 convolution_convert_fusion.1
  379.6 14.0 %collective-permute-done.29 = bf16[160,2048]{1,0:T(8,128)(2,1)S(1)} collective-permute-done((bf16[160,2048]{1,0:T(8,128)(2,1)}, bf16[160,2048]{1,0:T(8,128)(2,1)S(1)}, u32[]{:S(2)}, u32[]{:S(2)}) %collective-permute-start.29) | collective-permute-done | bytes 655392 | tf_op jit(solution)/shard_map/ppermute | solution.py:30
  393.6 12.5 %collective-permute-done.30 = bf16[160,2048]{1,0:T(8,128)(2,1)S(1)} collective-permute-done((bf16[160,2048]{1,0:T(8,128)(2,1)}, bf16[160,2048]{1,0:T(8,128)(2,1)S(1)}, u32[]{:S(2)}, u32[]{:S(2)}) %collective-permute-start.30) | collective-permute-done | bytes 655392 | tf_op jit(solution)/shard_map/ppermute | solution.py:30
  412.1 14.2 %collective-permute-done.35.refs_1_.refs_5_ = bf16[160,2048]{1,0:T(8,128)(2,1)S(1)} collective-permute-done((bf16[160,2048]{1,0:T(8,128)(2,1)S(1)}, bf16[160,2048]{1,0:T(8,128)(2,1)S(1)}, u32[]{:S(2)}, u32[]{:S(2)}) %collective-permute-start.35) | collective-permute-done | bytes 655392 | tf_op jit(solution)/shard_map/ppermute | solution.py:30
  426.2 11.4 %collective-permute-done.36.refs_2_.refs_6_ = bf16[160,2048]{1,0:T(8,128)(2,1)S(1)} collective-permute-done((bf16[160,2048]{1,0:T(8,128)(2,1)S(1)}, bf16[160,2048]{1,0:T(8,128)(2,1)S(1)}, u32[]{:S(2)}, u32[]{:S(2)}) %collective-permute-start.36) | collective-permute-done | bytes 655392 | tf_op jit(solution)/shard_map/ppermute | solution.py:30
  438.5 5.9 all-gather.13.cloned.1.call-done.refs_4_.refs_5_
  445.5 15.1 %shard_map.240 = (bf16[640,1408]{1,0:T(8,128)(2,1)}, bf16[640,1408]{1,0:T(8,128)(2,1)}, bf16[640,1408]{1,0:T(8,128)(2,1)}) custom-call(bf16[160,2048]{1,0:T(8,128)(2,1)S(1)} %multiply_convert_fusion.refs_0_.refs_4_, bf16[160,2048]{1,0:T(8,128)(2,1)S(1)} %collective-permute-done.35.refs_1_.refs_5_, bf16[160,2048]{1,0:T(8,128)(2,1)S(1)} %copy-done.33, ...), custom_call_target="tpu_custom_call" | custom-call | flops 40600862720 | bytes 14417920 | tf_op jit(solution)/shard_map/pallas_call | solution.py:106
  469.5 9.1 shard_map.241
  478.9 26.8 %all-gather.15.cloned.1.call-done = bf16[1,1408,2048]{2,1,0:T(8,128)(2,1)} async-done(((bf16[1,1408,256]{2,1,0:T(8,128)(2,1)}), bf16[1,1408,2048]{2,1,0:T(8,128)(2,1)}) %all-gather.15.cloned.1.call-update) | async-done | bytes 5767184 | tf_op jit(solution)/shard_map/all_gather | solution.py:549
  505.7 10.5 %shard_map.242 = (bf16[640,1408]{1,0:T(8,128)(2,1)}, bf16[640,1408]{1,0:T(8,128)(2,1)}) custom-call(bf16[160,2048]{1,0:T(8,128)(2,1)S(1)} %copy-done.1, bf16[160,2048]{1,0:T(8,128)(2,1)S(1)} %copy-done.29, bf16[160,2048]{1,0:T(8,128)(2,1)} %collective-permute-done.4.refs_4_.refs_2_, bf16[160,2048]{1,0:T(8,128)(2,1)} %collective-permute-done.5.refs_5_.refs_3_, ...), custom_call_target="tpu_custom_call" | custom-call | flops 20300431360 | bytes 7208960 | tf_op jit(solution)/shard_map/pallas_call | solution.py:106
  516.7 11.5 %fusion.15 = bf16[640,2048]{1,0:T(8,128)(2,1)S(1)} fusion(bf16[2816,2048]{1,0:T(8,128)(2,1)} %all-gather.13.cloned.1.call-done.refs_4_.refs_5_, bf16[640,1408]{1,0:T(8,128)(2,1)} %get-tuple-element.172.refs_2_, bf16[640,1408]{1,0:T(8,128)(2,1)} %get-tuple-element.178), kind=kOutput, calls=%fused_computation.15 | convolution fusion | flops 7390494720 | bytes 17760256 | tf_op jit(solution)/shard_map/dot_general | solution.py:94
  535.7 15.2 %shard_map.243 = bf16[2816,1024]{1,0:T(8,128)(2,1)} custom-call(s32[1]{0:T(128)} %bitcast.32.core_ref, bf16[640,1408]{1,0:T(8,128)(2,1)} %get-tuple-element.178, bf16[640,1408]{1,0:T(8,128)(2,1)} %copy-done.138, bf16[640,1408]{1,0:T(8,128)(2,1)} %get-tuple-element.172.refs_2_, bf16[640,1408]{1,0:T(8,128)(2,1)} %copy-done.139, ...), custom_call_target="tpu_custom_call" | custom-call | flops 81201725440 | bytes 28835840 | tf_op jit(solution)/shard_map/pallas_call | solution.py:106
  551.0 10.9 %collective-permute-done.44 = bf16[160,2048]{1,0:T(8,128)(2,1)} collective-permute-done((bf16[160,2048]{1,0:T(8,128)(2,1)}, bf16[160,2048]{1,0:T(8,128)(2,1)}, u32[]{:S(2)}, u32[]{:S(2)}) %collective-permute-start.44) | collective-permute-done | bytes 655392 | tf_op jit(solution)/shard_map/ppermute | solution.py:30
  576.4 20.9 %collective-permute-done.55 = f32[160]{0:T(256)S(1)} collective-permute-done((f32[160]{0:T(256)S(1)}, f32[160]{0:T(256)S(1)}, u32[]{:S(2)}, u32[]{:S(2)}) %collective-permute-start.55) | collective-permute-done | bytes 672 | tf_op jit(solution)/shard_map/ppermute | solution.py:30
  602.1 11.2 %shard_map.244 = (f32[640,512]{1,0:T(8,128)}, f32[640,512]{1,0:T(8,128)}, bf16[640,512]{1,0:T(8,128)(2,1)S(1)}, bf16[640,512]{1,0:T(8,128)(2,1)}, f32[1,512]{1,0:T(1,128)S(1)}) custom-call(s32[1]{0:T(128)} %bitcast.place_ref, bf16[160,2048]{1,0:T(8,128)(2,1)} %copy-done.60, bf16[160,2048]{1,0:T(8,128)(2,1)} %collective-permute-done.52.refs_1_.refs_13_, ...), custom_call_target="tpu_custom_call" | custom-call | flops 180224000 | bytes 64000 | tf_op jit(solution)/shard_map/pallas_call | solution.py:106
  621.4 4.0 collective-permute-done.59
  631.2 5.6 shard_map.245
  639.6 7.2 fusion.21
  652.0 12.3 %shard_map.246 = bf16[2048,1024]{1,0:T(8,128)(2,1)} custom-call(s32[1]{0:T(128)} %bitcast.32.core_ref, bf16[640,1536]{1,0:T(8,128)(2,1)} %copy-done.95, bf16[640,1536]{1,0:T(8,128)(2,1)} %collective-permute-done.70.refs_1_, bf16[640,512]{1,0:T(8,128)(2,1)S(1)} %copy-done.31, bf16[640,512]{1,0:T(8,128)(2,1)S(1)} %collective-permute-done.66.refs_3_, ...), custom_call_target="tpu_custom_call" | custom-call | flops 59055800320 | bytes 20971520 | tf_op jit(solution)/shard_map/pallas_call | solution.py:106
  666.2 14.5 %collective-permute-done.68 = bf16[160,2048]{1,0:T(8,128)(2,1)} collective-permute-done((bf16[160,2048]{1,0:T(8,128)(2,1)}, bf16[160,2048]{1,0:T(8,128)(2,1)}, u32[]{:S(2)}, u32[]{:S(2)}) %collective-permute-start.68) | collective-permute-done | bytes 655392 | tf_op jit(solution)/shard_map/ppermute | solution.py:30
  680.7 3.1 multiply_reduce_fusion.1
  683.9 3.8 fusion.78
  691.2 14.2 %collective-permute-done.75.refs_3_.refs_1_ = bf16[160,2048]{1,0:T(8,128)(2,1)S(1)} collective-permute-done((bf16[160,2048]{1,0:T(8,128)(2,1)S(1)}, bf16[160,2048]{1,0:T(8,128)(2,1)S(1)}, u32[]{:S(2)}, u32[]{:S(2)}) %collective-permute-start.75) | collective-permute-done | bytes 655392 | tf_op jit(solution)/shard_map/ppermute | solution.py:30
  705.4 13.2 %collective-permute-done.76.refs_4_.refs_2_ = bf16[160,2048]{1,0:T(8,128)(2,1)S(1)} collective-permute-done((bf16[160,2048]{1,0:T(8,128)(2,1)S(1)}, bf16[160,2048]{1,0:T(8,128)(2,1)S(1)}, u32[]{:S(2)}, u32[]{:S(2)}) %collective-permute-start.76) | collective-permute-done | bytes 655392 | tf_op jit(solution)/shard_map/ppermute | solution.py:30
  727.6 9.0 shard_map.247
  738.8 10.0 shard_map.248
  749.6 11.5 %fusion.27 = bf16[640,2048]{1,0:T(8,128)(2,1)S(1)} fusion(bf16[4224,2048]{1,0:T(8,128)(2,1)} %all-gather.9.cloned.1.call-done.refs_4_.refs_5_, bf16[640,1408]{1,0:T(8,128)(2,1)} %get-tuple-element.218.refs_2_, bf16[640,1408]{1,0:T(8,128)(2,1)} %get-tuple-element.223.refs_0_), kind=kOutput, calls=%fused_computation.19 | convolution fusion | flops 7390494720 | bytes 17760256 | tf_op jit(solution)/shard_map/dot_general | solution.py:94
  767.2 15.1 %shard_map.249 = bf16[2816,1024]{1,0:T(8,128)(2,1)} custom-call(s32[1]{0:T(128)} %bitcast.32.core_ref, bf16[640,1408]{1,0:T(8,128)(2,1)} %get-tuple-element.223.refs_0_, bf16[640,1408]{1,0:T(8,128)(2,1)} %collective-permute-done.86.refs_1_, bf16[640,1408]{1,0:T(8,128)(2,1)} %get-tuple-element.218.refs_2_, bf16[640,1408]{1,0:T(8,128)(2,1)} %copy-done.140, ...), custom_call_target="tpu_custom_call" | custom-call | flops 81201725440 | bytes 28835840 | tf_op jit(solution)/shard_map/pallas_call | solution.py:106
  782.6 11.6 %collective-permute-done.84 = bf16[160,2048]{1,0:T(8,128)(2,1)} collective-permute-done((bf16[160,2048]{1,0:T(8,128)(2,1)}, bf16[160,2048]{1,0:T(8,128)(2,1)}, u32[]{:S(2)}, u32[]{:S(2)}) %collective-permute-start.84) | collective-permute-done | bytes 655392 | tf_op jit(solution)/shard_map/ppermute | solution.py:30
  796.5 3.4 fusion.77
  808.0 7.0 convolution_convert_fusion
  818.8 15.6 %collective-permute-done.99 = f32[160]{0:T(256)S(1)} collective-permute-done((f32[160]{0:T(256)S(1)}, f32[160]{0:T(256)S(1)}, u32[]{:S(2)}, u32[]{:S(2)}) %collective-permute-start.99) | collective-permute-done | bytes 672 | tf_op jit(solution)/shard_map/ppermute | solution.py:30
  838.0 11.3 %shard_map.250 = (f32[640,512]{1,0:T(8,128)}, f32[640,512]{1,0:T(8,128)}, bf16[640,512]{1,0:T(8,128)(2,1)S(1)}, bf16[640,512]{1,0:T(8,128)(2,1)}, f32[1,512]{1,0:T(1,128)S(1)}) custom-call(s32[1]{0:T(128)} %bitcast.place_ref, bf16[160,2048]{1,0:T(8,128)(2,1)} %copy-done.58, bf16[160,2048]{1,0:T(8,128)(2,1)} %copy-done.88, bf16[160,2048]{1,0:T(8,128)(2,1)} %copy-done.90, ...), custom_call_target="tpu_custom_call" | custom-call | flops 180224000 | bytes 64000 | tf_op jit(solution)/shard_map/pallas_call | solution.py:106
  856.9 5.8 collective-permute-done.93
  869.8 5.9 shard_map.251
  878.1 7.3 fusion.24
  889.3 12.4 %shard_map.252 = bf16[2048,1024]{1,0:T(8,128)(2,1)} custom-call(s32[1]{0:T(128)} %bitcast.32.core_ref, bf16[640,1536]{1,0:T(8,128)(2,1)} %copy-done.79, bf16[640,1536]{1,0:T(8,128)(2,1)} %copy-done.136, bf16[640,512]{1,0:T(8,128)(2,1)S(1)} %copy-done.30, bf16[640,512]{1,0:T(8,128)(2,1)S(1)} %collective-permute-done.109.refs_3_, ...), custom_call_target="tpu_custom_call" | custom-call | flops 59055800320 | bytes 20971520 | tf_op jit(solution)/shard_map/pallas_call | solution.py:106
  909.9 9.9 collective-permute-done.110
  919.7 14.8 %collective-permute-done.111 = bf16[160,2048]{1,0:T(8,128)(2,1)} collective-permute-done((bf16[160,2048]{1,0:T(8,128)(2,1)}, bf16[160,2048]{1,0:T(8,128)(2,1)}, u32[]{:S(2)}, u32[]{:S(2)}) %collective-permute-start.111) | collective-permute-done | bytes 655392 | tf_op jit(solution)/shard_map/ppermute | solution.py:30
  943.5 3.4 fusion.42
  947.5 3.7 collective-permute-done.122
  952.8 4.1 collective-permute-done.123
  962.5 3.4 copy.115
  974.5 17.3 %reduce-scatter.17.cloned.1.call-done.ref = bf16[2048,256]{1,0:T(8,128)(2,1)} async-done(((bf16[2048,1024]{1,0:T(8,128)(2,1)}), bf16[2048,256]{1,0:T(8,128)(2,1)}) %reduce-scatter.17.cloned.1.call-update) | async-done | bytes 1048592 | tf_op jit(solution)/shard_map/reduce_scatter | solution.py:189
  (730 shorter events, 247.4 us)
Async XLA Ops:
  7.2 89.0 %all-gather.7.cloned.1.call-start = ((), (), s32[]{:S(2)}) async-start(), calls=%async_computation.6 | async-start | bytes 9437184 | tf_op jit(solution)/shard_map/all_gather | solution.py:546
  11.3 241.8 %all-gather.9.cloned.1.call-start = ((), (), s32[]{:S(2)}) async-start(), calls=%async_computation.7 | async-start | bytes 19464192 | tf_op jit(solution)/shard_map/all_gather | solution.py:549
  19.7 321.1 %all-gather.11.cloned.1.call-start = ((), (), s32[]{:S(2)}) async-start(), calls=%async_computation.8 | async-start | bytes 9437184 | tf_op jit(solution)/shard_map/all_gather | solution.py:549
  22.2 422.3 %all-gather.13.cloned.1.call-start = ((), (), s32[]{:S(2)}) async-start(), calls=%async_computation.9 | async-start | bytes 12976128 | tf_op jit(solution)/shard_map/all_gather | solution.py:549
  24.0 481.6 %all-gather.15.cloned.1.call-start = ((), (), s32[]{:S(2)}) async-start(), calls=%async_computation.16 | async-start | bytes 6488064 | tf_op jit(solution)/shard_map/all_gather | solution.py:549
  25.6 18.5 %collective-permute-start = (bf16[160,2048]{1,0:T(8,128)(2,1)S(1)}, bf16[160,2048]{1,0:T(8,128)(2,1)S(1)}, u32[]{:S(2)}, u32[]{:S(2)}) collective-permute-start(bf16[160,2048]{1,0:T(8,128)(2,1)S(1)} %fusion.38.refs_0_.refs_4_), channel_id=1, source_target_pairs={{0,1},{1,0},{2,3},{3,2},{4,5},{5,4},{6,7},{7,6},{8,9},{9,8},{10,11... | collective-permute-start | bytes 1966088 | tf_op jit(solution)/shard_map/ppermute | solution.py:30
  28.6 30.3 %collective-permute-start.1 = (bf16[160,2048]{1,0:T(8,128)(2,1)S(1)}, bf16[160,2048]{1,0:T(8,128)(2,1)}, u32[]{:S(2)}, u32[]{:S(2)}) collective-permute-start(bf16[160,2048]{1,0:T(8,128)(2,1)S(1)} %fusion.38.refs_0_.refs_4_), channel_id=1, source_target_pairs={{0,2},{1,3},{2,0},{3,1},{4,6},{5,7},{6,4},{7,5},{8,10},{9,11},{10,... | collective-permute-start | bytes 1966088 | tf_op jit(solution)/shard_map/ppermute | solution.py:30
  30.1 28.8 %collective-permute-start.2 = (bf16[160,2048]{1,0:T(8,128)(2,1)S(1)}, bf16[160,2048]{1,0:T(8,128)(2,1)}, u32[]{:S(2)}, u32[]{:S(2)}) collective-permute-start(bf16[160,2048]{1,0:T(8,128)(2,1)S(1)} %fusion.38.refs_0_.refs_4_), channel_id=1, source_target_pairs={{0,3},{1,2},{2,1},{3,0},{4,7},{5,6},{6,5},{7,4},{8,11},{9,10},{10,... | collective-permute-start | bytes 1966088 | tf_op jit(solution)/shard_map/ppermute | solution.py:30
  60.1 29.5 %collective-permute-start.4 = (bf16[160,2048]{1,0:T(8,128)(2,1)S(1)}, bf16[160,2048]{1,0:T(8,128)(2,1)}, u32[]{:S(2)}, u32[]{:S(2)}) collective-permute-start(bf16[160,2048]{1,0:T(8,128)(2,1)S(1)} %copy-done), channel_id=1, source_target_pairs={{0,2},{1,3},{2,0},{3,1},{4,6},{5,7},{6,4},{7,5},{8,10},{9,11},{10,... | collective-permute-start | bytes 1966088 | tf_op jit(solution)/shard_map/ppermute | solution.py:30
  61.0 28.6 %collective-permute-start.5 = (bf16[160,2048]{1,0:T(8,128)(2,1)S(1)}, bf16[160,2048]{1,0:T(8,128)(2,1)}, u32[]{:S(2)}, u32[]{:S(2)}) collective-permute-start(bf16[160,2048]{1,0:T(8,128)(2,1)S(1)} %copy-done), channel_id=1, source_target_pairs={{0,3},{1,2},{2,1},{3,0},{4,7},{5,6},{6,5},{7,4},{8,11},{9,10},{10,... | collective-permute-start | bytes 1966088 | tf_op jit(solution)/shard_map/ppermute | solution.py:30
  132.7 29.5 %collective-permute-start.11 = (bf16[160,2048]{1,0:T(8,128)(2,1)}, bf16[160,2048]{1,0:T(8,128)(2,1)S(1)}, u32[]{:S(2)}, u32[]{:S(2)}) collective-permute-start(bf16[160,2048]{1,0:T(8,128)(2,1)} %get-tuple-element.373), channel_id=1, source_target_pairs={{0,2},{1,3},{2,0},{3,1},{4,6},{5,7},{6,4},{7,5},{8,10},{9,11},{10,... | collective-permute-start | bytes 1966088 | tf_op jit(solution)/shard_map/ppermute | solution.py:30
  134.2 28.0 %collective-permute-start.12 = (bf16[160,2048]{1,0:T(8,128)(2,1)}, bf16[160,2048]{1,0:T(8,128)(2,1)S(1)}, u32[]{:S(2)}, u32[]{:S(2)}) collective-permute-start(bf16[160,2048]{1,0:T(8,128)(2,1)} %get-tuple-element.372), channel_id=1, source_target_pairs={{0,3},{1,2},{2,1},{3,0},{4,7},{5,6},{6,5},{7,4},{8,11},{9,10},{10,... | collective-permute-start | bytes 1966088 | tf_op jit(solution)/shard_map/ppermute | solution.py:30
  166.7 28.3 %collective-permute-start.17 = (bf16[160,2048]{1,0:T(8,128)(2,1)S(1)}, bf16[160,2048]{1,0:T(8,128)(2,1)S(1)}, u32[]{:S(2)}, u32[]{:S(2)}) collective-permute-start(bf16[160,2048]{1,0:T(8,128)(2,1)S(1)} %multiply_convert_fusion.3.refs_0_.refs_4_), channel_id=1, source_target_pairs={{0,2},{1,3},{2,0},{3,1},{4,6},{5,7},{6,4},{7,5},{8,10},{9,11},{10,... | collective-permute-start | bytes 1966088 | tf_op jit(solution)/shard_map/ppermute | solution.py:30
  167.8 27.2 %collective-permute-start.18 = (bf16[160,2048]{1,0:T(8,128)(2,1)S(1)}, bf16[160,2048]{1,0:T(8,128)(2,1)S(1)}, u32[]{:S(2)}, u32[]{:S(2)}) collective-permute-start(bf16[160,2048]{1,0:T(8,128)(2,1)S(1)} %multiply_convert_fusion.3.refs_0_.refs_4_), channel_id=1, source_target_pairs={{0,3},{1,2},{2,1},{3,0},{4,7},{5,6},{6,5},{7,4},{8,11},{9,10},{10,... | collective-permute-start | bytes 1966088 | tf_op jit(solution)/shard_map/ppermute | solution.py:30
  277.3 30.7 %collective-permute-start.20 = (bf16[160,2048]{1,0:T(8,128)(2,1)S(1)}, bf16[160,2048]{1,0:T(8,128)(2,1)S(1)}, u32[]{:S(2)}, u32[]{:S(2)}) collective-permute-start(bf16[160,2048]{1,0:T(8,128)(2,1)S(1)} %get-tuple-element.370), channel_id=1, source_target_pairs={{0,2},{1,3},{2,0},{3,1},{4,6},{5,7},{6,4},{7,5},{8,10},{9,11},{10,... | collective-permute-start | bytes 1966088 | tf_op jit(solution)/shard_map/ppermute | solution.py:30
  278.8 29.2 %collective-permute-start.21 = (bf16[160,2048]{1,0:T(8,128)(2,1)S(1)}, bf16[160,2048]{1,0:T(8,128)(2,1)S(1)}, u32[]{:S(2)}, u32[]{:S(2)}) collective-permute-start(bf16[160,2048]{1,0:T(8,128)(2,1)S(1)} %get-tuple-element.369), channel_id=1, source_target_pairs={{0,3},{1,2},{2,1},{3,0},{4,7},{5,6},{6,5},{7,4},{8,11},{9,10},{10,... | collective-permute-start | bytes 1966088 | tf_op jit(solution)/shard_map/ppermute | solution.py:30
  310.1 30.0 %collective-permute-start.23 = (bf16[160,2048]{1,0:T(8,128)(2,1)S(1)}, bf16[160,2048]{1,0:T(8,128)(2,1)S(1)}, u32[]{:S(2)}, u32[]{:S(2)}) collective-permute-start(bf16[160,2048]{1,0:T(8,128)(2,1)S(1)} %multiply_convert_fusion.2.refs_0_.refs_4_), channel_id=1, source_target_pairs={{0,2},{1,3},{2,0},{3,1},{4,6},{5,7},{6,4},{7,5},{8,10},{9,11},{10,... | collective-permute-start | bytes 1966088 | tf_op jit(solution)/shard_map/ppermute | solution.py:30
  310.9 29.9 %collective-permute-start.24 = (bf16[160,2048]{1,0:T(8,128)(2,1)S(1)}, bf16[160,2048]{1,0:T(8,128)(2,1)}, u32[]{:S(2)}, u32[]{:S(2)}) collective-permute-start(bf16[160,2048]{1,0:T(8,128)(2,1)S(1)} %multiply_convert_fusion.2.refs_0_.refs_4_), channel_id=1, source_target_pairs={{0,3},{1,2},{2,1},{3,0},{4,7},{5,6},{6,5},{7,4},{8,11},{9,10},{10,... | collective-permute-start | bytes 1966088 | tf_op jit(solution)/shard_map/ppermute | solution.py:30
  363.0 199.8 %reduce-scatter.7.cloned.1.call-start = ((), (), s32[]{:S(2)}) async-start(), calls=%async_computation.10 | async-start | bytes 3604480 | tf_op jit(solution)/shard_map/reduce_scatter | solution.py:189
  377.0 29.0 %collective-permute-start.30 = (bf16[160,2048]{1,0:T(8,128)(2,1)}, bf16[160,2048]{1,0:T(8,128)(2,1)S(1)}, u32[]{:S(2)}, u32[]{:S(2)}) collective-permute-start(bf16[160,2048]{1,0:T(8,128)(2,1)} %get-tuple-element.367), channel_id=1, source_target_pairs={{0,2},{1,3},{2,0},{3,1},{4,6},{5,7},{6,4},{7,5},{8,10},{9,11},{10,... | collective-permute-start | bytes 1966088 | tf_op jit(solution)/shard_map/ppermute | solution.py:30
  378.7 27.4 %collective-permute-start.31 = (bf16[160,2048]{1,0:T(8,128)(2,1)}, bf16[160,2048]{1,0:T(8,128)(2,1)}, u32[]{:S(2)}, u32[]{:S(2)}) collective-permute-start(bf16[160,2048]{1,0:T(8,128)(2,1)} %get-tuple-element.366), channel_id=1, source_target_pairs={{0,3},{1,2},{2,1},{3,0},{4,7},{5,6},{6,5},{7,4},{8,11},{9,10},{10,... | collective-permute-start | bytes 1966088 | tf_op jit(solution)/shard_map/ppermute | solution.py:30
  409.8 27.9 %collective-permute-start.36 = (bf16[160,2048]{1,0:T(8,128)(2,1)S(1)}, bf16[160,2048]{1,0:T(8,128)(2,1)S(1)}, u32[]{:S(2)}, u32[]{:S(2)}) collective-permute-start(bf16[160,2048]{1,0:T(8,128)(2,1)S(1)} %multiply_convert_fusion.refs_0_.refs_4_), channel_id=1, source_target_pairs={{0,2},{1,3},{2,0},{3,1},{4,6},{5,7},{6,4},{7,5},{8,10},{9,11},{10,... | collective-permute-start | bytes 1966088 | tf_op jit(solution)/shard_map/ppermute | solution.py:30
  410.6 27.9 %collective-permute-start.37 = (bf16[160,2048]{1,0:T(8,128)(2,1)S(1)}, bf16[160,2048]{1,0:T(8,128)(2,1)}, u32[]{:S(2)}, u32[]{:S(2)}) collective-permute-start(bf16[160,2048]{1,0:T(8,128)(2,1)S(1)} %multiply_convert_fusion.refs_0_.refs_4_), channel_id=1, source_target_pairs={{0,3},{1,2},{2,1},{3,0},{4,7},{5,6},{6,5},{7,4},{8,11},{9,10},{10,... | collective-permute-start | bytes 1966088 | tf_op jit(solution)/shard_map/ppermute | solution.py:30
  466.3 50.2 %collective-permute-start.48 = (bf16[160,2048]{1,0:T(8,128)(2,1)S(1)}, bf16[160,2048]{1,0:T(8,128)(2,1)}, u32[]{:S(2)}, u32[]{:S(2)}) collective-permute-start(bf16[160,2048]{1,0:T(8,128)(2,1)S(1)} %multiply_convert_fusion.refs_0_.refs_4_), channel_id=1, source_target_pairs={{0,4},{4,0},{1,5},{5,1},{2,6},{6,2},{3,7},{7,3},{8,12},{12,8},{9,1... | collective-permute-start | bytes 1966088 | tf_op jit(solution)/shard_map/ppermute | solution.py:34
  468.7 61.0 %collective-permute-start.49 = (bf16[160,2048]{1,0:T(8,128)(2,1)S(1)}, bf16[160,2048]{1,0:T(8,128)(2,1)}, u32[]{:S(2)}, u32[]{:S(2)}) collective-permute-start(bf16[160,2048]{1,0:T(8,128)(2,1)S(1)} %collective-permute-done.35.refs_1_.refs_5_), channel_id=1, source_target_pairs={{0,4},{4,0},{1,5},{5,1},{2,6},{6,2},{3,7},{7,3},{8,12},{12,8},{9,1... | collective-permute-start | bytes 1966088 | tf_op jit(solution)/shard_map/ppermute | solution.py:34
  469.0 61.9 %collective-permute-start.50 = (bf16[160,2048]{1,0:T(8,128)(2,1)}, bf16[160,2048]{1,0:T(8,128)(2,1)}, u32[]{:S(2)}, u32[]{:S(2)}) collective-permute-start(bf16[160,2048]{1,0:T(8,128)(2,1)} %copy-done.32), channel_id=1, source_target_pairs={{0,4},{4,0},{1,5},{5,1},{2,6},{6,2},{3,7},{7,3},{8,12},{12,8},{9,1... | collective-permute-start | bytes 1966088 | tf_op jit(solution)/shard_map/ppermute | solution.py:34
  469.2 63.1 %collective-permute-start.51 = (bf16[160,2048]{1,0:T(8,128)(2,1)}, bf16[160,2048]{1,0:T(8,128)(2,1)}, u32[]{:S(2)}, u32[]{:S(2)}) collective-permute-start(bf16[160,2048]{1,0:T(8,128)(2,1)} %collective-permute-done.37.refs_3_.refs_7_), channel_id=1, source_target_pairs={{0,4},{4,0},{1,5},{5,1},{2,6},{6,2},{3,7},{7,3},{8,12},{12,8},{9,1... | collective-permute-start | bytes 1966088 | tf_op jit(solution)/shard_map/ppermute | solution.py:34
  478.6 240.9 %reduce-scatter.9.cloned.1.call-start = ((), (), s32[]{:S(2)}) async-start(), calls=%async_computation.11 | async-start | bytes 7208960 | tf_op jit(solution)/shard_map/reduce_scatter | solution.py:189
  529.6 21.4 %collective-permute-start.43 = (bf16[160,2048]{1,0:T(8,128)(2,1)}, bf16[160,2048]{1,0:T(8,128)(2,1)}, u32[]{:S(2)}, u32[]{:S(2)}) collective-permute-start(bf16[160,2048]{1,0:T(8,128)(2,1)} %get-tuple-element.174), channel_id=1, source_target_pairs={{0,1},{1,0},{2,3},{3,2},{4,5},{5,4},{6,7},{7,6},{8,9},{9,8},{10,11... | collective-permute-start | bytes 1966088 | tf_op jit(solution)/shard_map/ppermute | solution.py:30
  530.9 31.1 %collective-permute-start.44 = (bf16[160,2048]{1,0:T(8,128)(2,1)}, bf16[160,2048]{1,0:T(8,128)(2,1)}, u32[]{:S(2)}, u32[]{:S(2)}) collective-permute-start(bf16[160,2048]{1,0:T(8,128)(2,1)} %get-tuple-element.175), channel_id=1, source_target_pairs={{0,2},{1,3},{2,0},{3,1},{4,6},{5,7},{6,4},{7,5},{8,10},{9,11},{10,... | collective-permute-start | bytes 1966088 | tf_op jit(solution)/shard_map/ppermute | solution.py:30
  532.3 29.6 %collective-permute-start.45 = (bf16[160,2048]{1,0:T(8,128)(2,1)}, bf16[160,2048]{1,0:T(8,128)(2,1)}, u32[]{:S(2)}, u32[]{:S(2)}) collective-permute-start(bf16[160,2048]{1,0:T(8,128)(2,1)} %get-tuple-element.176), channel_id=1, source_target_pairs={{0,3},{1,2},{2,1},{3,0},{4,7},{5,6},{6,5},{7,4},{8,11},{9,10},{10,... | collective-permute-start | bytes 1966088 | tf_op jit(solution)/shard_map/ppermute | solution.py:30
  551.0 198.5 %reduce-scatter.11.cloned.1.call-start = ((), (), s32[]{:S(2)}) async-start(), calls=%async_computation.12 | async-start | bytes 5242880 | tf_op jit(solution)/shard_map/reduce_scatter | solution.py:189
  566.8 35.2 %collective-permute-start.52 = (bf16[160,2048]{1,0:T(8,128)(2,1)S(1)}, bf16[160,2048]{1,0:T(8,128)(2,1)}, u32[]{:S(2)}, u32[]{:S(2)}) collective-permute-start(bf16[160,2048]{1,0:T(8,128)(2,1)S(1)} %fusion.75.refs_0_.refs_12_), channel_id=1, source_target_pairs={{0,1},{1,0},{2,3},{3,2},{4,5},{5,4},{6,7},{7,6},{8,9},{9,8},{10,11... | collective-permute-start | bytes 1966088 | tf_op jit(solution)/shard_map/ppermute | solution.py:30
  568.4 33.6 %collective-permute-start.53 = (bf16[160,2048]{1,0:T(8,128)(2,1)S(1)}, bf16[160,2048]{1,0:T(8,128)(2,1)}, u32[]{:S(2)}, u32[]{:S(2)}) collective-permute-start(bf16[160,2048]{1,0:T(8,128)(2,1)S(1)} %fusion.75.refs_0_.refs_12_), channel_id=1, source_target_pairs={{0,2},{1,3},{2,0},{3,1},{4,6},{5,7},{6,4},{7,5},{8,10},{9,11},{10,... | collective-permute-start | bytes 1966088 | tf_op jit(solution)/shard_map/ppermute | solution.py:30
  569.9 32.2 %collective-permute-start.54 = (bf16[160,2048]{1,0:T(8,128)(2,1)S(1)}, bf16[160,2048]{1,0:T(8,128)(2,1)}, u32[]{:S(2)}, u32[]{:S(2)}) collective-permute-start(bf16[160,2048]{1,0:T(8,128)(2,1)S(1)} %fusion.75.refs_0_.refs_12_), channel_id=1, source_target_pairs={{0,3},{1,2},{2,1},{3,0},{4,7},{5,6},{6,5},{7,4},{8,11},{9,10},{10,... | collective-permute-start | bytes 1966088 | tf_op jit(solution)/shard_map/ppermute | solution.py:30
  572.6 24.7 %collective-permute-start.55 = (f32[160]{0:T(256)S(1)}, f32[160]{0:T(256)S(1)}, u32[]{:S(2)}, u32[]{:S(2)}) collective-permute-start(f32[160]{0:T(256)S(1)} %multiply_reduce_fusion.6), channel_id=1, source_target_pairs={{0,1},{1,0},{2,3},{3,2},{4,5},{5,4},{6,7},{7,6},{8,9},{9,8},{10,11... | collective-permute-start | bytes 1928 | tf_op jit(solution)/shard_map/ppermute | solution.py:30
  574.9 24.9 %collective-permute-start.56 = (f32[160]{0:T(256)S(1)}, f32[160]{0:T(256)S(1)}, u32[]{:S(2)}, u32[]{:S(2)}) collective-permute-start(f32[160]{0:T(256)S(1)} %multiply_reduce_fusion.6), channel_id=1, source_target_pairs={{0,2},{1,3},{2,0},{3,1},{4,6},{5,7},{6,4},{7,5},{8,10},{9,11},{10,... | collective-permute-start | bytes 1928 | tf_op jit(solution)/shard_map/ppermute | solution.py:30
  648.2 17.9 %collective-permute-start.67 = (bf16[160,2048]{1,0:T(8,128)(2,1)}, bf16[160,2048]{1,0:T(8,128)(2,1)}, u32[]{:S(2)}, u32[]{:S(2)}) collective-permute-start(bf16[160,2048]{1,0:T(8,128)(2,1)} %get-tuple-element.199), channel_id=1, source_target_pairs={{0,1},{1,0},{2,3},{3,2},{4,5},{5,4},{6,7},{7,6},{8,9},{9,8},{10,11... | collective-permute-start | bytes 1966088 | tf_op jit(solution)/shard_map/ppermute | solution.py:30
  649.7 30.9 %collective-permute-start.68 = (bf16[160,2048]{1,0:T(8,128)(2,1)}, bf16[160,2048]{1,0:T(8,128)(2,1)}, u32[]{:S(2)}, u32[]{:S(2)}) collective-permute-start(bf16[160,2048]{1,0:T(8,128)(2,1)} %get-tuple-element.200), channel_id=1, source_target_pairs={{0,2},{1,3},{2,0},{3,1},{4,6},{5,7},{6,4},{7,5},{8,10},{9,11},{10,... | collective-permute-start | bytes 1966088 | tf_op jit(solution)/shard_map/ppermute | solution.py:30
  651.2 29.5 %collective-permute-start.69 = (bf16[160,2048]{1,0:T(8,128)(2,1)}, bf16[160,2048]{1,0:T(8,128)(2,1)}, u32[]{:S(2)}, u32[]{:S(2)}) collective-permute-start(bf16[160,2048]{1,0:T(8,128)(2,1)} %get-tuple-element.201), channel_id=1, source_target_pairs={{0,3},{1,2},{2,1},{3,0},{4,7},{5,6},{6,5},{7,4},{8,11},{9,10},{10,... | collective-permute-start | bytes 1966088 | tf_op jit(solution)/shard_map/ppermute | solution.py:30
  664.3 173.6 %reduce-scatter.13.cloned.1.call-start = ((), (), s32[]{:S(2)}) async-start(), calls=%async_computation.13 | async-start | bytes 3604480 | tf_op jit(solution)/shard_map/reduce_scatter | solution.py:189
  664.9 59.4 %collective-permute-start.78 = (bf16[640,1408]{1,0:T(8,128)(2,1)}, bf16[640,1408]{1,0:T(8,128)(2,1)}, u32[]{:S(2)}, u32[]{:S(2)}) collective-permute-start(bf16[640,1408]{1,0:T(8,128)(2,1)} %get-tuple-element.154.refs_0_), channel_id=1, source_target_pairs={{0,4},{4,0},{1,5},{5,1},{2,6},{6,2},{3,7},{7,3},{8,12},{12,8},{9,1... | collective-permute-start | bytes 5406728 | tf_op jit(solution)/shard_map/ppermute | solution.py:34
  688.9 29.8 %collective-permute-start.76 = (bf16[160,2048]{1,0:T(8,128)(2,1)S(1)}, bf16[160,2048]{1,0:T(8,128)(2,1)S(1)}, u32[]{:S(2)}, u32[]{:S(2)}) collective-permute-start(bf16[160,2048]{1,0:T(8,128)(2,1)S(1)} %get-tuple-element.209.refs_2_.refs_0_), channel_id=1, source_target_pairs={{0,2},{1,3},{2,0},{3,1},{4,6},{5,7},{6,4},{7,5},{8,10},{9,11},{10,... | collective-permute-start | bytes 1966088 | tf_op jit(solution)/shard_map/ppermute | solution.py:30
  689.8 29.7 %collective-permute-start.77 = (bf16[160,2048]{1,0:T(8,128)(2,1)S(1)}, bf16[160,2048]{1,0:T(8,128)(2,1)}, u32[]{:S(2)}, u32[]{:S(2)}) collective-permute-start(bf16[160,2048]{1,0:T(8,128)(2,1)S(1)} %get-tuple-element.209.refs_2_.refs_0_), channel_id=1, source_target_pairs={{0,3},{1,2},{2,1},{3,0},{4,7},{5,6},{6,5},{7,4},{8,11},{9,10},{10,... | collective-permute-start | bytes 1966088 | tf_op jit(solution)/shard_map/ppermute | solution.py:30
  691.2 33.6 %collective-permute-start.79 = (bf16[160,2048]{1,0:T(8,128)(2,1)S(1)}, bf16[160,2048]{1,0:T(8,128)(2,1)}, u32[]{:S(2)}, u32[]{:S(2)}) collective-permute-start(bf16[160,2048]{1,0:T(8,128)(2,1)S(1)} %get-tuple-element.209.refs_2_.refs_0_), channel_id=1, source_target_pairs={{0,4},{4,0},{1,5},{5,1},{2,6},{6,2},{3,7},{7,3},{8,12},{12,8},{9,1... | collective-permute-start | bytes 1966088 | tf_op jit(solution)/shard_map/ppermute | solution.py:34
  724.3 25.2 %collective-permute-start.88 = (bf16[160,2048]{1,0:T(8,128)(2,1)S(1)}, bf16[160,2048]{1,0:T(8,128)(2,1)}, u32[]{:S(2)}, u32[]{:S(2)}) collective-permute-start(bf16[160,2048]{1,0:T(8,128)(2,1)S(1)} %copy-done.5), channel_id=1, source_target_pairs={{0,4},{4,0},{1,5},{5,1},{2,6},{6,2},{3,7},{7,3},{8,12},{12,8},{9,1... | collective-permute-start | bytes 1966088 | tf_op jit(solution)/shard_map/ppermute | solution.py:34
  724.8 37.6 %collective-permute-start.89 = (bf16[160,2048]{1,0:T(8,128)(2,1)S(1)}, bf16[160,2048]{1,0:T(8,128)(2,1)}, u32[]{:S(2)}, u32[]{:S(2)}) collective-permute-start(bf16[160,2048]{1,0:T(8,128)(2,1)S(1)} %copy-done.23), channel_id=1, source_target_pairs={{0,4},{4,0},{1,5},{5,1},{2,6},{6,2},{3,7},{7,3},{8,12},{12,8},{9,1... | collective-permute-start | bytes 1966088 | tf_op jit(solution)/shard_map/ppermute | solution.py:34
  724.9 38.3 %collective-permute-start.90 = (bf16[160,2048]{1,0:T(8,128)(2,1)S(1)}, bf16[160,2048]{1,0:T(8,128)(2,1)}, u32[]{:S(2)}, u32[]{:S(2)}) collective-permute-start(bf16[160,2048]{1,0:T(8,128)(2,1)S(1)} %copy-done.25), channel_id=1, source_target_pairs={{0,4},{4,0},{1,5},{5,1},{2,6},{6,2},{3,7},{7,3},{8,12},{12,8},{9,1... | collective-permute-start | bytes 1966088 | tf_op jit(solution)/shard_map/ppermute | solution.py:34
  725.3 38.2 %collective-permute-start.91 = (bf16[160,2048]{1,0:T(8,128)(2,1)}, bf16[160,2048]{1,0:T(8,128)(2,1)}, u32[]{:S(2)}, u32[]{:S(2)}) collective-permute-start(bf16[160,2048]{1,0:T(8,128)(2,1)} %copy-done.141), channel_id=1, source_target_pairs={{0,4},{4,0},{1,5},{5,1},{2,6},{6,2},{3,7},{7,3},{8,12},{12,8},{9,1... | collective-permute-start | bytes 1966088 | tf_op jit(solution)/shard_map/ppermute | solution.py:34
  749.2 185.3 %reduce-scatter.15.cloned.1.call-start = ((), (), s32[]{:S(2)}) async-start(), calls=%async_computation.14 | async-start | bytes 7208960 | tf_op jit(solution)/shard_map/reduce_scatter | solution.py:189
  762.4 20.2 %collective-permute-start.83 = (bf16[160,2048]{1,0:T(8,128)(2,1)}, bf16[160,2048]{1,0:T(8,128)(2,1)}, u32[]{:S(2)}, u32[]{:S(2)}) collective-permute-start(bf16[160,2048]{1,0:T(8,128)(2,1)} %get-tuple-element.220), channel_id=1, source_target_pairs={{0,1},{1,0},{2,3},{3,2},{4,5},{5,4},{6,7},{7,6},{8,9},{9,8},{10,11... | collective-permute-start | bytes 1966088 | tf_op jit(solution)/shard_map/ppermute | solution.py:30
  763.2 31.1 %collective-permute-start.84 = (bf16[160,2048]{1,0:T(8,128)(2,1)}, bf16[160,2048]{1,0:T(8,128)(2,1)}, u32[]{:S(2)}, u32[]{:S(2)}) collective-permute-start(bf16[160,2048]{1,0:T(8,128)(2,1)} %get-tuple-element.221), channel_id=1, source_target_pairs={{0,2},{1,3},{2,0},{3,1},{4,6},{5,7},{6,4},{7,5},{8,10},{9,11},{10,... | collective-permute-start | bytes 1966088 | tf_op jit(solution)/shard_map/ppermute | solution.py:30
  763.5 30.7 %collective-permute-start.85 = (bf16[160,2048]{1,0:T(8,128)(2,1)}, bf16[160,2048]{1,0:T(8,128)(2,1)}, u32[]{:S(2)}, u32[]{:S(2)}) collective-permute-start(bf16[160,2048]{1,0:T(8,128)(2,1)} %get-tuple-element.222), channel_id=1, source_target_pairs={{0,3},{1,2},{2,1},{3,0},{4,7},{5,6},{6,5},{7,4},{8,11},{9,10},{10,... | collective-permute-start | bytes 1966088 | tf_op jit(solution)/shard_map/ppermute | solution.py:30
  782.4 209.5 %reduce-scatter.17.cloned.1.call-start = ((), (), s32[]{:S(2)}) async-start(), calls=%async_computation.15 | async-start | bytes 5242880 | tf_op jit(solution)/shard_map/reduce_scatter | solution.py:189
  804.5 31.7 %collective-permute-start.95 = (bf16[160,2048]{1,0:T(8,128)(2,1)S(1)}, bf16[160,2048]{1,0:T(8,128)(2,1)S(1)}, u32[]{:S(2)}, u32[]{:S(2)}) collective-permute-start(bf16[160,2048]{1,0:T(8,128)(2,1)S(1)} %get-tuple-element.329.refs_0_.refs_12_), channel_id=1, source_target_pairs={{0,1},{1,0},{2,3},{3,2},{4,5},{5,4},{6,7},{7,6},{8,9},{9,8},{10,11... | collective-permute-start | bytes 1966088 | tf_op jit(solution)/shard_map/ppermute | solution.py:30
  805.4 31.8 %collective-permute-start.96 = (bf16[160,2048]{1,0:T(8,128)(2,1)S(1)}, bf16[160,2048]{1,0:T(8,128)(2,1)S(1)}, u32[]{:S(2)}, u32[]{:S(2)}) collective-permute-start(bf16[160,2048]{1,0:T(8,128)(2,1)S(1)} %get-tuple-element.329.refs_0_.refs_12_), channel_id=1, source_target_pairs={{0,2},{1,3},{2,0},{3,1},{4,6},{5,7},{6,4},{7,5},{8,10},{9,11},{10,... | collective-permute-start | bytes 1966088 | tf_op jit(solution)/shard_map/ppermute | solution.py:30
  806.8 31.1 %collective-permute-start.97 = (bf16[160,2048]{1,0:T(8,128)(2,1)S(1)}, bf16[160,2048]{1,0:T(8,128)(2,1)}, u32[]{:S(2)}, u32[]{:S(2)}) collective-permute-start(bf16[160,2048]{1,0:T(8,128)(2,1)S(1)} %get-tuple-element.329.refs_0_.refs_12_), channel_id=1, source_target_pairs={{0,3},{1,2},{2,1},{3,0},{4,7},{5,6},{6,5},{7,4},{8,11},{9,10},{10,... | collective-permute-start | bytes 1966088 | tf_op jit(solution)/shard_map/ppermute | solution.py:30
  815.1 19.4 %collective-permute-start.99 = (f32[160]{0:T(256)S(1)}, f32[160]{0:T(256)S(1)}, u32[]{:S(2)}, u32[]{:S(2)}) collective-permute-start(f32[160]{0:T(256)S(1)} %multiply_reduce_fusion.3), channel_id=1, source_target_pairs={{0,2},{1,3},{2,0},{3,1},{4,6},{5,7},{6,4},{7,5},{8,10},{9,11},{10,... | collective-permute-start | bytes 1928 | tf_op jit(solution)/shard_map/ppermute | solution.py:30
  817.4 37.9 %collective-permute-start.92 = (bf16[160,2048]{1,0:T(8,128)(2,1)}, bf16[160,2048]{1,0:T(8,128)(2,1)S(1)}, u32[]{:S(2)}, u32[]{:S(2)}) collective-permute-start(bf16[160,2048]{1,0:T(8,128)(2,1)} %get-tuple-element.350), channel_id=1, source_target_pairs={{0,1},{1,0},{2,3},{3,2},{4,5},{5,4},{6,7},{7,6},{8,9},{9,8},{10,11... | collective-permute-start | bytes 1966088 | tf_op jit(solution)/shard_map/ppermute | solution.py:30
  834.4 28.2 %collective-permute-start.93 = (bf16[160,2048]{1,0:T(8,128)(2,1)}, bf16[160,2048]{1,0:T(8,128)(2,1)S(1)}, u32[]{:S(2)}, u32[]{:S(2)}) collective-permute-start(bf16[160,2048]{1,0:T(8,128)(2,1)} %get-tuple-element.352), channel_id=1, source_target_pairs={{0,2},{1,3},{2,0},{3,1},{4,6},{5,7},{6,4},{7,5},{8,10},{9,11},{10,... | collective-permute-start | bytes 1966088 | tf_op jit(solution)/shard_map/ppermute | solution.py:30
  836.2 26.5 %collective-permute-start.94 = (bf16[160,2048]{1,0:T(8,128)(2,1)}, bf16[160,2048]{1,0:T(8,128)(2,1)}, u32[]{:S(2)}, u32[]{:S(2)}) collective-permute-start(bf16[160,2048]{1,0:T(8,128)(2,1)} %get-tuple-element.351), channel_id=1, source_target_pairs={{0,3},{1,2},{2,1},{3,0},{4,7},{5,6},{6,5},{7,4},{8,11},{9,10},{10,... | collective-permute-start | bytes 1966088 | tf_op jit(solution)/shard_map/ppermute | solution.py:30
  901.8 17.9 %collective-permute-start.110 = (bf16[160,2048]{1,0:T(8,128)(2,1)}, bf16[160,2048]{1,0:T(8,128)(2,1)}, u32[]{:S(2)}, u32[]{:S(2)}) collective-permute-start(bf16[160,2048]{1,0:T(8,128)(2,1)} %get-tuple-element.245), channel_id=1, source_target_pairs={{0,1},{1,0},{2,3},{3,2},{4,5},{5,4},{6,7},{7,6},{8,9},{9,8},{10,11... | collective-permute-start | bytes 1966088 | tf_op jit(solution)/shard_map/ppermute | solution.py:30
  903.4 31.1 %collective-permute-start.111 = (bf16[160,2048]{1,0:T(8,128)(2,1)}, bf16[160,2048]{1,0:T(8,128)(2,1)}, u32[]{:S(2)}, u32[]{:S(2)}) collective-permute-start(bf16[160,2048]{1,0:T(8,128)(2,1)} %get-tuple-element.246), channel_id=1, source_target_pairs={{0,2},{1,3},{2,0},{3,1},{4,6},{5,7},{6,4},{7,5},{8,10},{9,11},{10,... | collective-permute-start | bytes 1966088 | tf_op jit(solution)/shard_map/ppermute | solution.py:30
  904.1 30.4 %collective-permute-start.112 = (bf16[160,2048]{1,0:T(8,128)(2,1)}, bf16[160,2048]{1,0:T(8,128)(2,1)}, u32[]{:S(2)}, u32[]{:S(2)}) collective-permute-start(bf16[160,2048]{1,0:T(8,128)(2,1)} %get-tuple-element.247), channel_id=1, source_target_pairs={{0,3},{1,2},{2,1},{3,0},{4,7},{5,6},{6,5},{7,4},{8,11},{9,10},{10,... | collective-permute-start | bytes 1966088 | tf_op jit(solution)/shard_map/ppermute | solution.py:30
  (233 other events, 4092.5 us)
Sparse Core Ops, SparseCore 0:
  11.4 84.7 all-gather.6
  98.3 154.6 all-gather.8
  255.2 80.9 all-gather.10
  337.7 106.7 all-gather.12
  446.4 59.1 all-gather.14
  508.4 54.3 reduce-scatter.6
  565.1 102.3 reduce-scatter.8
  669.8 77.2 reduce-scatter.10
  750.1 56.6 reduce-scatter.12
  809.1 102.3 reduce-scatter.14
  913.9 77.9 reduce-scatter.16

commit v7 on v6

--- a/solution.py
+++ b/solution.py
@@ -211,9 +211,42 @@
         out_specs=[pl.BlockSpec((1, *shape), lambda j: (layer, 0, 0)) for shape in shapes],
         out_shape=[jax.ShapeDtypeStruct((layers, *shape), f32) for shape in shapes],
         input_output_aliases={k + 1: k for k in range(len(before))},
-        compiler_params=pltpu.CompilerParams(vmem_limit_bytes=VMEM),
+        compiler_params=pltpu.CompilerParams(vmem_limit_bytes=60 * 1000 * 1000),
         cost_estimate=pl.CostEstimate(flops=0, bytes_accessed=0, transcendentals=0),
     )(shard, *before)
+
+
+def beside(matrices, turned):
+    depth, width = matrices[0].shape[1:]
+    count = len(matrices)
+
+    def kernel(*refs):
+        sources, (out, held, arrived) = refs[: count + 1], refs[count + 1 :]
+        copies = [
+            pltpu.make_async_copy(
+                sources[k].at[0], out.at[:, k * width : (k + 1) * width], arrived.at[k]
+            )
+            for k in range(count)
+        ]
+        copies.append(pltpu.make_async_copy(sources[count].at[0], held, arrived.at[count]))
+        for copy in copies:
+            copy.start()
+        for copy in copies:
+            copy.wait()
+        out[:, count * width :] = held[...].T
+
+    operands = (*matrices, turned)
+    return pl.pallas_call(
+        kernel,
+        in_specs=[pl.BlockSpec(memory_space=pl.ANY)] * len(operands),
+        out_specs=pl.BlockSpec(memory_space=pltpu.VMEM),
+        out_shape=jax.ShapeDtypeStruct((depth, width * len(operands)), bf16),
+        scratch_shapes=[
+            pltpu.VMEM(turned.shape[1:], bf16), pltpu.SemaphoreType.DMA((len(operands),)),
+        ],
+        compiler_params=pltpu.CompilerParams(vmem_limit_bytes=60 * 1000 * 1000),
+        cost_estimate=pl.CostEstimate(flops=0, bytes_accessed=0, transcendentals=0),
+    )(*operands)
 
 
 def rows_at(matrix, at, rows, tile):
@@ -548,7 +581,7 @@
     def tall(*shards):
         return lax.all_gather(jnp.concatenate(shards, axis=0), SEQ, axis=1, tiled=True)
 
-    mixes, boths, downs = [side(w_input[0], w_forget[0], w_gate[0], w_out[0].T)], [], []
+    mixes, boths, downs = [side(beside((w_input, w_forget, w_gate), w_out))], [], []
     for layer in range(LAYERS):
         if layer > 0:
             mixes.append(tall(w_input[layer].T, w_forget[layer].T, w_gate[layer].T, w_out[layer]))

time: 1010 us -> 1010 us (level)
    unnamed x330 -> x321, local copies, waits for them, and re-layouts: 36.5 us -> 33.7 us
  transfers between devices with their start and end apart: 138 -> 138, of which waited for: 55 -> 56; matrix products, arithmetic and copies ran while one was open for 15% -> 15% of each run, Pallas kernels for 19% -> 19%
where the time goes in v7:
time: 1010 us; the launch traced here: 1000 us
  waiting for transfers between devices  502 us (50%)
  Pallas kernels  192 us (19%)
  starting transfers between devices  115 us (11%)
  local copies, waits for them, and re-layouts  63.5 us (6%)
  matrix products  58.7 us (6%)
  other arithmetic  52.2 us (5%)
  between operations  16.5 us (2%)
    ppermute x66, waiting for transfers between devices, exchange(): return lax.ppermute(values, 'fsdp', [(i, i ^ step) for i in range(size)])  355 us
    pallas_call x16, Pallas kernels, call(): pl.pallas_call(kernel, grid_spec=pltpu.PrefetchScalarGridSpec(num_scalar_...  185 us
    all_gather x4, waiting for transfers between devices, tall(): lax.all_gather(jnp.concatenate(shards, axis=0), SEQ, axis=1, tiled=True)  91.4 us
    ppermute x66, starting transfers between devices, exchange(): return lax.ppermute(values, 'fsdp', [(i, i ^ step) for i in range(size)])  80.8 us
    dot_general x6, matrix products, dot(): return jnp.dot(left, right, preferred_element_type=f32)  48.2 us
    unnamed x321, local copies, waits for them, and re-layouts  33.7 us
    ppermute x12, starting transfers between devices, entering_of(): lax.ppermute(pair, SEQ, [(i, i + sign * 2 * hop) for i in range(length) i...  21.4 us
  transfers between devices with their start and end apart: 138, of which 56 were waited for; matrix products, arithmetic and copies ran while one was open for 15% of the time, Pallas kernels for 19%

profile of v7, /device:TPU:0, one launch (start us, length us, event | category | flops | bytes accessed | tf_op | source)
XLA Modules:
  0.0 1000.1 jit_solution(9661004021852780162)
XLA Ops:
  28.4 13.7 %collective-permute-done.refs_1_.refs_5_ = bf16[160,2048]{1,0:T(8,128)(2,1)S(1)} collective-permute-done((bf16[160,2048]{1,0:T(8,128)(2,1)S(1)}, bf16[160,2048]{1,0:T(8,128)(2,1)S(1)}, u32[]{:S(2)}, u32[]{:S(2)}) %collective-permute-start) | collective-permute-done | bytes 655392 | tf_op jit(solution)/shard_map/ppermute | solution.py:30
  42.1 14.7 %collective-permute-done.1.refs_2_.refs_6_ = bf16[160,2048]{1,0:T(8,128)(2,1)S(1)} collective-permute-done((bf16[160,2048]{1,0:T(8,128)(2,1)S(1)}, bf16[160,2048]{1,0:T(8,128)(2,1)S(1)}, u32[]{:S(2)}, u32[]{:S(2)}) %collective-permute-start.1) | collective-permute-done | bytes 655392 | tf_op jit(solution)/shard_map/ppermute | solution.py:30
  62.7 12.6 %collective-permute-done.3.refs_3_.refs_1_ = bf16[160,2048]{1,0:T(8,128)(2,1)S(1)} collective-permute-done((bf16[160,2048]{1,0:T(8,128)(2,1)S(1)}, bf16[160,2048]{1,0:T(8,128)(2,1)S(1)}, u32[]{:S(2)}, u32[]{:S(2)}) %collective-permute-start.3) | collective-permute-done | bytes 655392 | tf_op jit(solution)/shard_map/ppermute | solution.py:30
  75.4 10.9 %collective-permute-done.4.refs_4_.refs_2_ = bf16[160,2048]{1,0:T(8,128)(2,1)} collective-permute-done((bf16[160,2048]{1,0:T(8,128)(2,1)S(1)}, bf16[160,2048]{1,0:T(8,128)(2,1)}, u32[]{:S(2)}, u32[]{:S(2)}) %collective-permute-start.4) | collective-permute-done | bytes 655392 | tf_op jit(solution)/shard_map/ppermute | solution.py:30
  88.2 6.7 all-gather.7.cloned.1.call-done.refs_4_.refs_5_.refs_6_
  95.0 13.3 %shard_map.238 = (f32[640,512]{1,0:T(8,128)}, f32[640,512]{1,0:T(8,128)}, f32[640,512]{1,0:T(8,128)}, f32[640,512]{1,0:T(8,128)}, f32[640,512]{1,0:T(8,128)}) custom-call(s32[1]{0:T(128)} %bitcast.place_ref, bf16[160,2048]{1,0:T(8,128)(2,1)S(1)} %fusion.38.refs_0_.refs_4_, bf16[160,2048]{1,0:T(8,128)(2,1)S(1)} %collective-permute-done.refs_1_.refs_5_, ...), custom_call_target="tpu_custom_call" | custom-call | flops 22145925120 | bytes 7864320 | tf_op jit(solution)/shard_map/pallas_call | solution.py:106
  111.6 3.7 collective-permute-start.8
  123.8 3.2 convolution_convert_fusion.2
  133.0 14.0 %collective-permute-done.10 = bf16[160,2048]{1,0:T(8,128)(2,1)S(1)} collective-permute-done((bf16[160,2048]{1,0:T(8,128)(2,1)}, bf16[160,2048]{1,0:T(8,128)(2,1)S(1)}, u32[]{:S(2)}, u32[]{:S(2)}) %collective-permute-start.10) | collective-permute-done | bytes 655392 | tf_op jit(solution)/shard_map/ppermute | solution.py:30
  147.0 13.3 %collective-permute-done.11 = bf16[160,2048]{1,0:T(8,128)(2,1)S(1)} collective-permute-done((bf16[160,2048]{1,0:T(8,128)(2,1)}, bf16[160,2048]{1,0:T(8,128)(2,1)S(1)}, u32[]{:S(2)}, u32[]{:S(2)}) %collective-permute-start.11) | collective-permute-done | bytes 655392 | tf_op jit(solution)/shard_map/ppermute | solution.py:30
  167.4 14.2 %collective-permute-done.16.refs_1_.refs_5_ = bf16[160,2048]{1,0:T(8,128)(2,1)S(1)} collective-permute-done((bf16[160,2048]{1,0:T(8,128)(2,1)S(1)}, bf16[160,2048]{1,0:T(8,128)(2,1)S(1)}, u32[]{:S(2)}, u32[]{:S(2)}) %collective-permute-start.16) | collective-permute-done | bytes 655392 | tf_op jit(solution)/shard_map/ppermute | solution.py:30
  181.5 11.6 %collective-permute-done.17.refs_2_.refs_6_ = bf16[160,2048]{1,0:T(8,128)(2,1)S(1)} collective-permute-done((bf16[160,2048]{1,0:T(8,128)(2,1)S(1)}, bf16[160,2048]{1,0:T(8,128)(2,1)S(1)}, u32[]{:S(2)}, u32[]{:S(2)}) %collective-permute-start.17) | collective-permute-done | bytes 655392 | tf_op jit(solution)/shard_map/ppermute | solution.py:30
  193.2 58.7 %all-gather.9.cloned.1.call-done.refs_4_.refs_5_ = bf16[4224,2048]{1,0:T(8,128)(2,1)} async-done(((bf16[4224,256]{1,0:T(8,128)(2,1)}), bf16[4224,2048]{1,0:T(8,128)(2,1)}) %all-gather.9.cloned.1.call-update) | async-done | bytes 17301520 | tf_op jit(solution)/shard_map/all_gather | solution.py:582
  251.9 15.1 %shard_map.239 = (bf16[640,1408]{1,0:T(8,128)(2,1)}, bf16[640,1408]{1,0:T(8,128)(2,1)}, bf16[640,1408]{1,0:T(8,128)(2,1)}) custom-call(bf16[160,2048]{1,0:T(8,128)(2,1)S(1)} %multiply_convert_fusion.3.refs_0_.refs_4_, bf16[160,2048]{1,0:T(8,128)(2,1)S(1)} %collective-permute-done.16.refs_1_.refs_5_, ...), custom_call_target="tpu_custom_call" | custom-call | flops 40600862720 | bytes 14417920 | tf_op jit(solution)/shard_map/pallas_call | solution.py:106
  267.0 7.4 fusion.18
  278.1 14.1 %collective-permute-done.19 = bf16[160,2048]{1,0:T(8,128)(2,1)S(1)} collective-permute-done((bf16[160,2048]{1,0:T(8,128)(2,1)S(1)}, bf16[160,2048]{1,0:T(8,128)(2,1)S(1)}, u32[]{:S(2)}, u32[]{:S(2)}) %collective-permute-start.19) | collective-permute-done | bytes 655392 | tf_op jit(solution)/shard_map/ppermute | solution.py:30
  292.2 14.6 %collective-permute-done.20 = bf16[160,2048]{1,0:T(8,128)(2,1)S(1)} collective-permute-done((bf16[160,2048]{1,0:T(8,128)(2,1)S(1)}, bf16[160,2048]{1,0:T(8,128)(2,1)S(1)}, u32[]{:S(2)}, u32[]{:S(2)}) %collective-permute-start.20) | collective-permute-done | bytes 655392 | tf_op jit(solution)/shard_map/ppermute | solution.py:30
  311.2 14.2 %collective-permute-done.22.refs_1_.refs_5_ = bf16[160,2048]{1,0:T(8,128)(2,1)S(1)} collective-permute-done((bf16[160,2048]{1,0:T(8,128)(2,1)S(1)}, bf16[160,2048]{1,0:T(8,128)(2,1)S(1)}, u32[]{:S(2)}, u32[]{:S(2)}) %collective-permute-start.22) | collective-permute-done | bytes 655392 | tf_op jit(solution)/shard_map/ppermute | solution.py:30
  325.4 13.4 %collective-permute-done.23.refs_2_.refs_6_ = bf16[160,2048]{1,0:T(8,128)(2,1)S(1)} collective-permute-done((bf16[160,2048]{1,0:T(8,128)(2,1)S(1)}, bf16[160,2048]{1,0:T(8,128)(2,1)S(1)}, u32[]{:S(2)}, u32[]{:S(2)}) %collective-permute-start.23) | collective-permute-done | bytes 655392 | tf_op jit(solution)/shard_map/ppermute | solution.py:30
  339.7 13.8 %shard_map.240 = (f32[640,512]{1,0:T(8,128)}, f32[640,512]{1,0:T(8,128)}, f32[640,512]{1,0:T(8,128)}, f32[640,512]{1,0:T(8,128)}, f32[640,512]{1,0:T(8,128)}) custom-call(s32[1]{0:T(128)} %bitcast.place_ref, bf16[160,2048]{1,0:T(8,128)(2,1)S(1)} %multiply_convert_fusion.2.refs_0_.refs_4_, bf16[160,2048]{1,0:T(8,128)(2,1)S(1)} %collective-permute-done.22.refs_1_.refs_5_, ...), custom_call_target="tpu_custom_call" | custom-call | flops 22145925120 | bytes 7864320 | tf_op jit(solution)/shard_map/pallas_call | solution.py:106
  357.5 3.8 collective-permute-start.27
  369.5 3.6 convolution_convert_fusion.1
  379.1 14.0 %collective-permute-done.29 = bf16[160,2048]{1,0:T(8,128)(2,1)S(1)} collective-permute-done((bf16[160,2048]{1,0:T(8,128)(2,1)}, bf16[160,2048]{1,0:T(8,128)(2,1)S(1)}, u32[]{:S(2)}, u32[]{:S(2)}) %collective-permute-start.29) | collective-permute-done | bytes 655392 | tf_op jit(solution)/shard_map/ppermute | solution.py:30
  393.1 11.8 %collective-permute-done.30 = bf16[160,2048]{1,0:T(8,128)(2,1)S(1)} collective-permute-done((bf16[160,2048]{1,0:T(8,128)(2,1)}, bf16[160,2048]{1,0:T(8,128)(2,1)S(1)}, u32[]{:S(2)}, u32[]{:S(2)}) %collective-permute-start.30) | collective-permute-done | bytes 655392 | tf_op jit(solution)/shard_map/ppermute | solution.py:30
  410.9 14.2 %collective-permute-done.35.refs_1_.refs_5_ = bf16[160,2048]{1,0:T(8,128)(2,1)S(1)} collective-permute-done((bf16[160,2048]{1,0:T(8,128)(2,1)S(1)}, bf16[160,2048]{1,0:T(8,128)(2,1)S(1)}, u32[]{:S(2)}, u32[]{:S(2)}) %collective-permute-start.35) | collective-permute-done | bytes 655392 | tf_op jit(solution)/shard_map/ppermute | solution.py:30
  425.1 11.4 %collective-permute-done.36.refs_2_.refs_6_ = bf16[160,2048]{1,0:T(8,128)(2,1)S(1)} collective-permute-done((bf16[160,2048]{1,0:T(8,128)(2,1)S(1)}, bf16[160,2048]{1,0:T(8,128)(2,1)S(1)}, u32[]{:S(2)}, u32[]{:S(2)}) %collective-permute-start.36) | collective-permute-done | bytes 655392 | tf_op jit(solution)/shard_map/ppermute | solution.py:30
  437.3 5.9 all-gather.13.cloned.1.call-done.refs_4_.refs_5_
  444.3 15.1 %shard_map.241 = (bf16[640,1408]{1,0:T(8,128)(2,1)}, bf16[640,1408]{1,0:T(8,128)(2,1)}, bf16[640,1408]{1,0:T(8,128)(2,1)}) custom-call(bf16[160,2048]{1,0:T(8,128)(2,1)S(1)} %multiply_convert_fusion.refs_0_.refs_4_, bf16[160,2048]{1,0:T(8,128)(2,1)S(1)} %collective-permute-done.35.refs_1_.refs_5_, bf16[160,2048]{1,0:T(8,128)(2,1)S(1)} %copy-done.31, ...), custom_call_target="tpu_custom_call" | custom-call | flops 40600862720 | bytes 14417920 | tf_op jit(solution)/shard_map/pallas_call | solution.py:106
  468.3 9.1 shard_map.242
  477.7 26.8 %all-gather.15.cloned.1.call-done = bf16[1,1408,2048]{2,1,0:T(8,128)(2,1)} async-done(((bf16[1,1408,256]{2,1,0:T(8,128)(2,1)}), bf16[1,1408,2048]{2,1,0:T(8,128)(2,1)}) %all-gather.15.cloned.1.call-update) | async-done | bytes 5767184 | tf_op jit(solution)/shard_map/all_gather | solution.py:582
  504.5 10.6 %shard_map.243 = (bf16[640,1408]{1,0:T(8,128)(2,1)}, bf16[640,1408]{1,0:T(8,128)(2,1)}) custom-call(bf16[160,2048]{1,0:T(8,128)(2,1)S(1)} %copy-done.1, bf16[160,2048]{1,0:T(8,128)(2,1)S(1)} %copy-done.27, bf16[160,2048]{1,0:T(8,128)(2,1)} %collective-permute-done.4.refs_4_.refs_2_, bf16[160,2048]{1,0:T(8,128)(2,1)} %collective-permute-done.5.refs_5_.refs_3_, ...), custom_call_target="tpu_custom_call" | custom-call | flops 20300431360 | bytes 7208960 | tf_op jit(solution)/shard_map/pallas_call | solution.py:106
  515.5 11.5 %fusion.15 = bf16[640,2048]{1,0:T(8,128)(2,1)S(1)} fusion(bf16[2816,2048]{1,0:T(8,128)(2,1)} %all-gather.13.cloned.1.call-done.refs_4_.refs_5_, bf16[640,1408]{1,0:T(8,128)(2,1)} %get-tuple-element.172.refs_2_, bf16[640,1408]{1,0:T(8,128)(2,1)} %get-tuple-element.178), kind=kOutput, calls=%fused_computation.15 | convolution fusion | flops 7390494720 | bytes 17760256 | tf_op jit(solution)/shard_map/dot_general | solution.py:94
  534.5 15.2 %shard_map.244 = bf16[2816,1024]{1,0:T(8,128)(2,1)} custom-call(s32[1]{0:T(128)} %bitcast.27.core_ref, bf16[640,1408]{1,0:T(8,128)(2,1)} %get-tuple-element.178, bf16[640,1408]{1,0:T(8,128)(2,1)} %copy-done.131, bf16[640,1408]{1,0:T(8,128)(2,1)} %get-tuple-element.172.refs_2_, bf16[640,1408]{1,0:T(8,128)(2,1)} %copy-done.132, ...), custom_call_target="tpu_custom_call" | custom-call | flops 81201725440 | bytes 28835840 | tf_op jit(solution)/shard_map/pallas_call | solution.py:106
  549.8 11.0 %collective-permute-done.44 = bf16[160,2048]{1,0:T(8,128)(2,1)} collective-permute-done((bf16[160,2048]{1,0:T(8,128)(2,1)}, bf16[160,2048]{1,0:T(8,128)(2,1)}, u32[]{:S(2)}, u32[]{:S(2)}) %collective-permute-start.44) | collective-permute-done | bytes 655392 | tf_op jit(solution)/shard_map/ppermute | solution.py:30
  575.2 20.9 %collective-permute-done.55 = f32[160]{0:T(256)S(1)} collective-permute-done((f32[160]{0:T(256)S(1)}, f32[160]{0:T(256)S(1)}, u32[]{:S(2)}, u32[]{:S(2)}) %collective-permute-start.55) | collective-permute-done | bytes 672 | tf_op jit(solution)/shard_map/ppermute | solution.py:30
  600.8 11.2 %shard_map.245 = (f32[640,512]{1,0:T(8,128)}, f32[640,512]{1,0:T(8,128)}, bf16[640,512]{1,0:T(8,128)(2,1)S(1)}, bf16[640,512]{1,0:T(8,128)(2,1)}, f32[1,512]{1,0:T(1,128)S(1)}) custom-call(s32[1]{0:T(128)} %bitcast.place_ref, bf16[160,2048]{1,0:T(8,128)(2,1)} %copy-done.58, bf16[160,2048]{1,0:T(8,128)(2,1)} %collective-permute-done.52.refs_1_.refs_13_, ...), custom_call_target="tpu_custom_call" | custom-call | flops 180224000 | bytes 64000 | tf_op jit(solution)/shard_map/pallas_call | solution.py:106
  620.2 4.0 collective-permute-done.59
  630.0 5.6 shard_map.246
  638.4 7.2 fusion.21
  650.9 12.3 %shard_map.247 = bf16[2048,1024]{1,0:T(8,128)(2,1)} custom-call(s32[1]{0:T(128)} %bitcast.27.core_ref, bf16[640,1536]{1,0:T(8,128)(2,1)} %copy-done.89, bf16[640,1536]{1,0:T(8,128)(2,1)} %collective-permute-done.70.refs_1_, bf16[640,512]{1,0:T(8,128)(2,1)S(1)} %copy-done.29, bf16[640,512]{1,0:T(8,128)(2,1)S(1)} %collective-permute-done.66.refs_3_, ...), custom_call_target="tpu_custom_call" | custom-call | flops 59055800320 | bytes 20971520 | tf_op jit(solution)/shard_map/pallas_call | solution.py:106
  665.0 14.5 %collective-permute-done.68 = bf16[160,2048]{1,0:T(8,128)(2,1)} collective-permute-done((bf16[160,2048]{1,0:T(8,128)(2,1)}, bf16[160,2048]{1,0:T(8,128)(2,1)}, u32[]{:S(2)}, u32[]{:S(2)}) %collective-permute-start.68) | collective-permute-done | bytes 655392 | tf_op jit(solution)/shard_map/ppermute | solution.py:30
  682.8 3.8 fusion.78
  690.2 14.2 %collective-permute-done.75.refs_3_.refs_1_ = bf16[160,2048]{1,0:T(8,128)(2,1)S(1)} collective-permute-done((bf16[160,2048]{1,0:T(8,128)(2,1)S(1)}, bf16[160,2048]{1,0:T(8,128)(2,1)S(1)}, u32[]{:S(2)}, u32[]{:S(2)}) %collective-permute-start.75) | collective-permute-done | bytes 655392 | tf_op jit(solution)/shard_map/ppermute | solution.py:30
  704.3 13.2 %collective-permute-done.76.refs_4_.refs_2_ = bf16[160,2048]{1,0:T(8,128)(2,1)S(1)} collective-permute-done((bf16[160,2048]{1,0:T(8,128)(2,1)S(1)}, bf16[160,2048]{1,0:T(8,128)(2,1)S(1)}, u32[]{:S(2)}, u32[]{:S(2)}) %collective-permute-start.76) | collective-permute-done | bytes 655392 | tf_op jit(solution)/shard_map/ppermute | solution.py:30
  726.5 9.0 shard_map.248
  737.7 10.0 shard_map.249
  748.5 11.5 %fusion.27 = bf16[640,2048]{1,0:T(8,128)(2,1)S(1)} fusion(bf16[4224,2048]{1,0:T(8,128)(2,1)} %all-gather.9.cloned.1.call-done.refs_4_.refs_5_, bf16[640,1408]{1,0:T(8,128)(2,1)} %get-tuple-element.218.refs_2_, bf16[640,1408]{1,0:T(8,128)(2,1)} %get-tuple-element.223.refs_0_), kind=kOutput, calls=%fused_computation.19 | convolution fusion | flops 7390494720 | bytes 17760256 | tf_op jit(solution)/shard_map/dot_general | solution.py:94
  766.1 15.1 %shard_map.250 = bf16[2816,1024]{1,0:T(8,128)(2,1)} custom-call(s32[1]{0:T(128)} %bitcast.27.core_ref, bf16[640,1408]{1,0:T(8,128)(2,1)} %get-tuple-element.223.refs_0_, bf16[640,1408]{1,0:T(8,128)(2,1)} %collective-permute-done.86.refs_1_, bf16[640,1408]{1,0:T(8,128)(2,1)} %get-tuple-element.218.refs_2_, bf16[640,1408]{1,0:T(8,128)(2,1)} %copy-done.133, ...), custom_call_target="tpu_custom_call" | custom-call | flops 81201725440 | bytes 28835840 | tf_op jit(solution)/shard_map/pallas_call | solution.py:106
  781.5 11.6 %collective-permute-done.84 = bf16[160,2048]{1,0:T(8,128)(2,1)} collective-permute-done((bf16[160,2048]{1,0:T(8,128)(2,1)}, bf16[160,2048]{1,0:T(8,128)(2,1)}, u32[]{:S(2)}, u32[]{:S(2)}) %collective-permute-start.84) | collective-permute-done | bytes 655392 | tf_op jit(solution)/shard_map/ppermute | solution.py:30
  795.4 3.4 fusion.77
  806.9 7.0 convolution_convert_fusion
  817.7 15.6 %collective-permute-done.99 = f32[160]{0:T(256)S(1)} collective-permute-done((f32[160]{0:T(256)S(1)}, f32[160]{0:T(256)S(1)}, u32[]{:S(2)}, u32[]{:S(2)}) %collective-permute-start.99) | collective-permute-done | bytes 672 | tf_op jit(solution)/shard_map/ppermute | solution.py:30
  836.9 11.3 %shard_map.251 = (f32[640,512]{1,0:T(8,128)}, f32[640,512]{1,0:T(8,128)}, bf16[640,512]{1,0:T(8,128)(2,1)S(1)}, bf16[640,512]{1,0:T(8,128)(2,1)}, f32[1,512]{1,0:T(1,128)S(1)}) custom-call(s32[1]{0:T(128)} %bitcast.place_ref, bf16[160,2048]{1,0:T(8,128)(2,1)} %copy-done.56, bf16[160,2048]{1,0:T(8,128)(2,1)} %copy-done.85, bf16[160,2048]{1,0:T(8,128)(2,1)} %copy-done.87, ...), custom_call_target="tpu_custom_call" | custom-call | flops 180224000 | bytes 64000 | tf_op jit(solution)/shard_map/pallas_call | solution.py:106
  855.8 5.7 collective-permute-done.93
  868.6 5.9 shard_map.252
  877.2 7.3 fusion.24
  887.3 12.3 %shard_map.253 = bf16[2048,1024]{1,0:T(8,128)(2,1)} custom-call(s32[1]{0:T(128)} %bitcast.27.core_ref, bf16[640,1536]{1,0:T(8,128)(2,1)} %copy-done.77, bf16[640,1536]{1,0:T(8,128)(2,1)} %collective-permute-done.113.refs_1_, bf16[640,512]{1,0:T(8,128)(2,1)S(1)} %copy-done.28, bf16[640,512]{1,0:T(8,128)(2,1)S(1)} %collective-permute-done.109.refs_3_, ...), custom_call_target="tpu_custom_call" | custom-call | flops 59055800320 | bytes 20971520 | tf_op jit(solution)/shard_map/pallas_call | solution.py:106
  909.0 8.7 collective-permute-done.110
  917.7 14.5 %collective-permute-done.111 = bf16[160,2048]{1,0:T(8,128)(2,1)} collective-permute-done((bf16[160,2048]{1,0:T(8,128)(2,1)}, bf16[160,2048]{1,0:T(8,128)(2,1)}, u32[]{:S(2)}, u32[]{:S(2)}) %collective-permute-start.111) | collective-permute-done | bytes 655392 | tf_op jit(solution)/shard_map/ppermute | solution.py:30
  941.2 3.4 fusion.42
  944.8 4.7 collective-permute-done.122
  950.7 5.1 collective-permute-done.123
  961.3 3.4 copy.111
  973.4 17.3 %reduce-scatter.17.cloned.1.call-done.ref = bf16[2048,256]{1,0:T(8,128)(2,1)} async-done(((bf16[2048,1024]{1,0:T(8,128)(2,1)}), bf16[2048,256]{1,0:T(8,128)(2,1)}) %reduce-scatter.17.cloned.1.call-update) | async-done | bytes 1048592 | tf_op jit(solution)/shard_map/reduce_scatter | solution.py:189
  (724 shorter events, 247.0 us)
Async XLA Ops:
  7.2 87.8 %all-gather.7.cloned.1.call-start = ((), (), s32[]{:S(2)}) async-start(), calls=%async_computation.6 | async-start | bytes 9437184 | tf_op jit(solution)/shard_map/all_gather | solution.py:579
  9.7 242.2 %all-gather.9.cloned.1.call-start = ((), (), s32[]{:S(2)}) async-start(), calls=%async_computation.7 | async-start | bytes 19464192 | tf_op jit(solution)/shard_map/all_gather | solution.py:582
  17.7 322.0 %all-gather.11.cloned.1.call-start = ((), (), s32[]{:S(2)}) async-start(), calls=%async_computation.8 | async-start | bytes 9437184 | tf_op jit(solution)/shard_map/all_gather | solution.py:582
  20.1 423.1 %all-gather.13.cloned.1.call-start = ((), (), s32[]{:S(2)}) async-start(), calls=%async_computation.9 | async-start | bytes 12976128 | tf_op jit(solution)/shard_map/all_gather | solution.py:582
  22.0 482.5 %all-gather.15.cloned.1.call-start = ((), (), s32[]{:S(2)}) async-start(), calls=%async_computation.16 | async-start | bytes 6488064 | tf_op jit(solution)/shard_map/all_gather | solution.py:582
  23.7 18.4 %collective-permute-start = (bf16[160,2048]{1,0:T(8,128)(2,1)S(1)}, bf16[160,2048]{1,0:T(8,128)(2,1)S(1)}, u32[]{:S(2)}, u32[]{:S(2)}) collective-permute-start(bf16[160,2048]{1,0:T(8,128)(2,1)S(1)} %fusion.38.refs_0_.refs_4_), channel_id=1, source_target_pairs={{0,1},{1,0},{2,3},{3,2},{4,5},{5,4},{6,7},{7,6},{8,9},{9,8},{10,11... | collective-permute-start | bytes 1966088 | tf_op jit(solution)/shard_map/ppermute | solution.py:30
  26.6 30.3 %collective-permute-start.1 = (bf16[160,2048]{1,0:T(8,128)(2,1)S(1)}, bf16[160,2048]{1,0:T(8,128)(2,1)S(1)}, u32[]{:S(2)}, u32[]{:S(2)}) collective-permute-start(bf16[160,2048]{1,0:T(8,128)(2,1)S(1)} %fusion.38.refs_0_.refs_4_), channel_id=1, source_target_pairs={{0,2},{1,3},{2,0},{3,1},{4,6},{5,7},{6,4},{7,5},{8,10},{9,11},{10,... | collective-permute-start | bytes 1966088 | tf_op jit(solution)/shard_map/ppermute | solution.py:30
  28.1 29.6 %collective-permute-start.2 = (bf16[160,2048]{1,0:T(8,128)(2,1)S(1)}, bf16[160,2048]{1,0:T(8,128)(2,1)}, u32[]{:S(2)}, u32[]{:S(2)}) collective-permute-start(bf16[160,2048]{1,0:T(8,128)(2,1)S(1)} %fusion.38.refs_0_.refs_4_), channel_id=1, source_target_pairs={{0,3},{1,2},{2,1},{3,0},{4,7},{5,6},{6,5},{7,4},{8,11},{9,10},{10,... | collective-permute-start | bytes 1966088 | tf_op jit(solution)/shard_map/ppermute | solution.py:30
  58.2 28.1 %collective-permute-start.4 = (bf16[160,2048]{1,0:T(8,128)(2,1)S(1)}, bf16[160,2048]{1,0:T(8,128)(2,1)}, u32[]{:S(2)}, u32[]{:S(2)}) collective-permute-start(bf16[160,2048]{1,0:T(8,128)(2,1)S(1)} %copy-done), channel_id=1, source_target_pairs={{0,2},{1,3},{2,0},{3,1},{4,6},{5,7},{6,4},{7,5},{8,10},{9,11},{10,... | collective-permute-start | bytes 1966088 | tf_op jit(solution)/shard_map/ppermute | solution.py:30
  59.8 28.5 %collective-permute-start.5 = (bf16[160,2048]{1,0:T(8,128)(2,1)S(1)}, bf16[160,2048]{1,0:T(8,128)(2,1)}, u32[]{:S(2)}, u32[]{:S(2)}) collective-permute-start(bf16[160,2048]{1,0:T(8,128)(2,1)S(1)} %copy-done), channel_id=1, source_target_pairs={{0,3},{1,2},{2,1},{3,0},{4,7},{5,6},{6,5},{7,4},{8,11},{9,10},{10,... | collective-permute-start | bytes 1966088 | tf_op jit(solution)/shard_map/ppermute | solution.py:30
  130.8 29.5 %collective-permute-start.11 = (bf16[160,2048]{1,0:T(8,128)(2,1)}, bf16[160,2048]{1,0:T(8,128)(2,1)S(1)}, u32[]{:S(2)}, u32[]{:S(2)}) collective-permute-start(bf16[160,2048]{1,0:T(8,128)(2,1)} %get-tuple-element.373), channel_id=1, source_target_pairs={{0,2},{1,3},{2,0},{3,1},{4,6},{5,7},{6,4},{7,5},{8,10},{9,11},{10,... | collective-permute-start | bytes 1966088 | tf_op jit(solution)/shard_map/ppermute | solution.py:30
  132.3 28.0 %collective-permute-start.12 = (bf16[160,2048]{1,0:T(8,128)(2,1)}, bf16[160,2048]{1,0:T(8,128)(2,1)S(1)}, u32[]{:S(2)}, u32[]{:S(2)}) collective-permute-start(bf16[160,2048]{1,0:T(8,128)(2,1)} %get-tuple-element.372), channel_id=1, source_target_pairs={{0,3},{1,2},{2,1},{3,0},{4,7},{5,6},{6,5},{7,4},{8,11},{9,10},{10,... | collective-permute-start | bytes 1966088 | tf_op jit(solution)/shard_map/ppermute | solution.py:30
  164.8 28.4 %collective-permute-start.17 = (bf16[160,2048]{1,0:T(8,128)(2,1)S(1)}, bf16[160,2048]{1,0:T(8,128)(2,1)S(1)}, u32[]{:S(2)}, u32[]{:S(2)}) collective-permute-start(bf16[160,2048]{1,0:T(8,128)(2,1)S(1)} %multiply_convert_fusion.3.refs_0_.refs_4_), channel_id=1, source_target_pairs={{0,2},{1,3},{2,0},{3,1},{4,6},{5,7},{6,4},{7,5},{8,10},{9,11},{10,... | collective-permute-start | bytes 1966088 | tf_op jit(solution)/shard_map/ppermute | solution.py:30
  165.9 27.3 %collective-permute-start.18 = (bf16[160,2048]{1,0:T(8,128)(2,1)S(1)}, bf16[160,2048]{1,0:T(8,128)(2,1)S(1)}, u32[]{:S(2)}, u32[]{:S(2)}) collective-permute-start(bf16[160,2048]{1,0:T(8,128)(2,1)S(1)} %multiply_convert_fusion.3.refs_0_.refs_4_), channel_id=1, source_target_pairs={{0,3},{1,2},{2,1},{3,0},{4,7},{5,6},{6,5},{7,4},{8,11},{9,10},{10,... | collective-permute-start | bytes 1966088 | tf_op jit(solution)/shard_map/ppermute | solution.py:30
  276.2 30.6 %collective-permute-start.20 = (bf16[160,2048]{1,0:T(8,128)(2,1)S(1)}, bf16[160,2048]{1,0:T(8,128)(2,1)S(1)}, u32[]{:S(2)}, u32[]{:S(2)}) collective-permute-start(bf16[160,2048]{1,0:T(8,128)(2,1)S(1)} %get-tuple-element.370), channel_id=1, source_target_pairs={{0,2},{1,3},{2,0},{3,1},{4,6},{5,7},{6,4},{7,5},{8,10},{9,11},{10,... | collective-permute-start | bytes 1966088 | tf_op jit(solution)/shard_map/ppermute | solution.py:30
  277.6 29.2 %collective-permute-start.21 = (bf16[160,2048]{1,0:T(8,128)(2,1)S(1)}, bf16[160,2048]{1,0:T(8,128)(2,1)S(1)}, u32[]{:S(2)}, u32[]{:S(2)}) collective-permute-start(bf16[160,2048]{1,0:T(8,128)(2,1)S(1)} %get-tuple-element.369), channel_id=1, source_target_pairs={{0,3},{1,2},{2,1},{3,0},{4,7},{5,6},{6,5},{7,4},{8,11},{9,10},{10,... | collective-permute-start | bytes 1966088 | tf_op jit(solution)/shard_map/ppermute | solution.py:30
  308.9 29.9 %collective-permute-start.23 = (bf16[160,2048]{1,0:T(8,128)(2,1)S(1)}, bf16[160,2048]{1,0:T(8,128)(2,1)S(1)}, u32[]{:S(2)}, u32[]{:S(2)}) collective-permute-start(bf16[160,2048]{1,0:T(8,128)(2,1)S(1)} %multiply_convert_fusion.2.refs_0_.refs_4_), channel_id=1, source_target_pairs={{0,2},{1,3},{2,0},{3,1},{4,6},{5,7},{6,4},{7,5},{8,10},{9,11},{10,... | collective-permute-start | bytes 1966088 | tf_op jit(solution)/shard_map/ppermute | solution.py:30
  309.7 29.9 %collective-permute-start.24 = (bf16[160,2048]{1,0:T(8,128)(2,1)S(1)}, bf16[160,2048]{1,0:T(8,128)(2,1)}, u32[]{:S(2)}, u32[]{:S(2)}) collective-permute-start(bf16[160,2048]{1,0:T(8,128)(2,1)S(1)} %multiply_convert_fusion.2.refs_0_.refs_4_), channel_id=1, source_target_pairs={{0,3},{1,2},{2,1},{3,0},{4,7},{5,6},{6,5},{7,4},{8,11},{9,10},{10,... | collective-permute-start | bytes 1966088 | tf_op jit(solution)/shard_map/ppermute | solution.py:30
  362.6 199.0 %reduce-scatter.7.cloned.1.call-start = ((), (), s32[]{:S(2)}) async-start(), calls=%async_computation.10 | async-start | bytes 3604480 | tf_op jit(solution)/shard_map/reduce_scatter | solution.py:189
  375.9 29.0 %collective-permute-start.30 = (bf16[160,2048]{1,0:T(8,128)(2,1)}, bf16[160,2048]{1,0:T(8,128)(2,1)S(1)}, u32[]{:S(2)}, u32[]{:S(2)}) collective-permute-start(bf16[160,2048]{1,0:T(8,128)(2,1)} %get-tuple-element.367), channel_id=1, source_target_pairs={{0,2},{1,3},{2,0},{3,1},{4,6},{5,7},{6,4},{7,5},{8,10},{9,11},{10,... | collective-permute-start | bytes 1966088 | tf_op jit(solution)/shard_map/ppermute | solution.py:30
  377.5 27.4 %collective-permute-start.31 = (bf16[160,2048]{1,0:T(8,128)(2,1)}, bf16[160,2048]{1,0:T(8,128)(2,1)}, u32[]{:S(2)}, u32[]{:S(2)}) collective-permute-start(bf16[160,2048]{1,0:T(8,128)(2,1)} %get-tuple-element.366), channel_id=1, source_target_pairs={{0,3},{1,2},{2,1},{3,0},{4,7},{5,6},{6,5},{7,4},{8,11},{9,10},{10,... | collective-permute-start | bytes 1966088 | tf_op jit(solution)/shard_map/ppermute | solution.py:30
  408.6 27.9 %collective-permute-start.36 = (bf16[160,2048]{1,0:T(8,128)(2,1)S(1)}, bf16[160,2048]{1,0:T(8,128)(2,1)S(1)}, u32[]{:S(2)}, u32[]{:S(2)}) collective-permute-start(bf16[160,2048]{1,0:T(8,128)(2,1)S(1)} %multiply_convert_fusion.refs_0_.refs_4_), channel_id=1, source_target_pairs={{0,2},{1,3},{2,0},{3,1},{4,6},{5,7},{6,4},{7,5},{8,10},{9,11},{10,... | collective-permute-start | bytes 1966088 | tf_op jit(solution)/shard_map/ppermute | solution.py:30
  409.4 27.9 %collective-permute-start.37 = (bf16[160,2048]{1,0:T(8,128)(2,1)S(1)}, bf16[160,2048]{1,0:T(8,128)(2,1)}, u32[]{:S(2)}, u32[]{:S(2)}) collective-permute-start(bf16[160,2048]{1,0:T(8,128)(2,1)S(1)} %multiply_convert_fusion.refs_0_.refs_4_), channel_id=1, source_target_pairs={{0,3},{1,2},{2,1},{3,0},{4,7},{5,6},{6,5},{7,4},{8,11},{9,10},{10,... | collective-permute-start | bytes 1966088 | tf_op jit(solution)/shard_map/ppermute | solution.py:30
  465.0 50.2 %collective-permute-start.48 = (bf16[160,2048]{1,0:T(8,128)(2,1)S(1)}, bf16[160,2048]{1,0:T(8,128)(2,1)}, u32[]{:S(2)}, u32[]{:S(2)}) collective-permute-start(bf16[160,2048]{1,0:T(8,128)(2,1)S(1)} %multiply_convert_fusion.refs_0_.refs_4_), channel_id=1, source_target_pairs={{0,4},{4,0},{1,5},{5,1},{2,6},{6,2},{3,7},{7,3},{8,12},{12,8},{9,1... | collective-permute-start | bytes 1966088 | tf_op jit(solution)/shard_map/ppermute | solution.py:34
  467.4 61.0 %collective-permute-start.49 = (bf16[160,2048]{1,0:T(8,128)(2,1)S(1)}, bf16[160,2048]{1,0:T(8,128)(2,1)}, u32[]{:S(2)}, u32[]{:S(2)}) collective-permute-start(bf16[160,2048]{1,0:T(8,128)(2,1)S(1)} %collective-permute-done.35.refs_1_.refs_5_), channel_id=1, source_target_pairs={{0,4},{4,0},{1,5},{5,1},{2,6},{6,2},{3,7},{7,3},{8,12},{12,8},{9,1... | collective-permute-start | bytes 1966088 | tf_op jit(solution)/shard_map/ppermute | solution.py:34
  467.8 61.9 %collective-permute-start.50 = (bf16[160,2048]{1,0:T(8,128)(2,1)}, bf16[160,2048]{1,0:T(8,128)(2,1)}, u32[]{:S(2)}, u32[]{:S(2)}) collective-permute-start(bf16[160,2048]{1,0:T(8,128)(2,1)} %copy-done.30), channel_id=1, source_target_pairs={{0,4},{4,0},{1,5},{5,1},{2,6},{6,2},{3,7},{7,3},{8,12},{12,8},{9,1... | collective-permute-start | bytes 1966088 | tf_op jit(solution)/shard_map/ppermute | solution.py:34
  467.9 63.2 %collective-permute-start.51 = (bf16[160,2048]{1,0:T(8,128)(2,1)}, bf16[160,2048]{1,0:T(8,128)(2,1)}, u32[]{:S(2)}, u32[]{:S(2)}) collective-permute-start(bf16[160,2048]{1,0:T(8,128)(2,1)} %collective-permute-done.37.refs_3_.refs_7_), channel_id=1, source_target_pairs={{0,4},{4,0},{1,5},{5,1},{2,6},{6,2},{3,7},{7,3},{8,12},{12,8},{9,1... | collective-permute-start | bytes 1966088 | tf_op jit(solution)/shard_map/ppermute | solution.py:34
  477.4 240.9 %reduce-scatter.9.cloned.1.call-start = ((), (), s32[]{:S(2)}) async-start(), calls=%async_computation.11 | async-start | bytes 7208960 | tf_op jit(solution)/shard_map/reduce_scatter | solution.py:189
  528.5 21.3 %collective-permute-start.43 = (bf16[160,2048]{1,0:T(8,128)(2,1)}, bf16[160,2048]{1,0:T(8,128)(2,1)}, u32[]{:S(2)}, u32[]{:S(2)}) collective-permute-start(bf16[160,2048]{1,0:T(8,128)(2,1)} %get-tuple-element.174), channel_id=1, source_target_pairs={{0,1},{1,0},{2,3},{3,2},{4,5},{5,4},{6,7},{7,6},{8,9},{9,8},{10,11... | collective-permute-start | bytes 1966088 | tf_op jit(solution)/shard_map/ppermute | solution.py:30
  529.7 31.1 %collective-permute-start.44 = (bf16[160,2048]{1,0:T(8,128)(2,1)}, bf16[160,2048]{1,0:T(8,128)(2,1)}, u32[]{:S(2)}, u32[]{:S(2)}) collective-permute-start(bf16[160,2048]{1,0:T(8,128)(2,1)} %get-tuple-element.175), channel_id=1, source_target_pairs={{0,2},{1,3},{2,0},{3,1},{4,6},{5,7},{6,4},{7,5},{8,10},{9,11},{10,... | collective-permute-start | bytes 1966088 | tf_op jit(solution)/shard_map/ppermute | solution.py:30
  531.1 29.6 %collective-permute-start.45 = (bf16[160,2048]{1,0:T(8,128)(2,1)}, bf16[160,2048]{1,0:T(8,128)(2,1)}, u32[]{:S(2)}, u32[]{:S(2)}) collective-permute-start(bf16[160,2048]{1,0:T(8,128)(2,1)} %get-tuple-element.176), channel_id=1, source_target_pairs={{0,3},{1,2},{2,1},{3,0},{4,7},{5,6},{6,5},{7,4},{8,11},{9,10},{10,... | collective-permute-start | bytes 1966088 | tf_op jit(solution)/shard_map/ppermute | solution.py:30
  549.7 198.6 %reduce-scatter.11.cloned.1.call-start = ((), (), s32[]{:S(2)}) async-start(), calls=%async_computation.12 | async-start | bytes 5242880 | tf_op jit(solution)/shard_map/reduce_scatter | solution.py:189
  565.6 35.2 %collective-permute-start.52 = (bf16[160,2048]{1,0:T(8,128)(2,1)S(1)}, bf16[160,2048]{1,0:T(8,128)(2,1)}, u32[]{:S(2)}, u32[]{:S(2)}) collective-permute-start(bf16[160,2048]{1,0:T(8,128)(2,1)S(1)} %fusion.75.refs_0_.refs_12_), channel_id=1, source_target_pairs={{0,1},{1,0},{2,3},{3,2},{4,5},{5,4},{6,7},{7,6},{8,9},{9,8},{10,11... | collective-permute-start | bytes 1966088 | tf_op jit(solution)/shard_map/ppermute | solution.py:30
  567.2 33.6 %collective-permute-start.53 = (bf16[160,2048]{1,0:T(8,128)(2,1)S(1)}, bf16[160,2048]{1,0:T(8,128)(2,1)}, u32[]{:S(2)}, u32[]{:S(2)}) collective-permute-start(bf16[160,2048]{1,0:T(8,128)(2,1)S(1)} %fusion.75.refs_0_.refs_12_), channel_id=1, source_target_pairs={{0,2},{1,3},{2,0},{3,1},{4,6},{5,7},{6,4},{7,5},{8,10},{9,11},{10,... | collective-permute-start | bytes 1966088 | tf_op jit(solution)/shard_map/ppermute | solution.py:30
  568.6 32.2 %collective-permute-start.54 = (bf16[160,2048]{1,0:T(8,128)(2,1)S(1)}, bf16[160,2048]{1,0:T(8,128)(2,1)}, u32[]{:S(2)}, u32[]{:S(2)}) collective-permute-start(bf16[160,2048]{1,0:T(8,128)(2,1)S(1)} %fusion.75.refs_0_.refs_12_), channel_id=1, source_target_pairs={{0,3},{1,2},{2,1},{3,0},{4,7},{5,6},{6,5},{7,4},{8,11},{9,10},{10,... | collective-permute-start | bytes 1966088 | tf_op jit(solution)/shard_map/ppermute | solution.py:30
  571.4 24.7 %collective-permute-start.55 = (f32[160]{0:T(256)S(1)}, f32[160]{0:T(256)S(1)}, u32[]{:S(2)}, u32[]{:S(2)}) collective-permute-start(f32[160]{0:T(256)S(1)} %multiply_reduce_fusion.6), channel_id=1, source_target_pairs={{0,1},{1,0},{2,3},{3,2},{4,5},{5,4},{6,7},{7,6},{8,9},{9,8},{10,11... | collective-permute-start | bytes 1928 | tf_op jit(solution)/shard_map/ppermute | solution.py:30
  573.6 24.8 %collective-permute-start.56 = (f32[160]{0:T(256)S(1)}, f32[160]{0:T(256)S(1)}, u32[]{:S(2)}, u32[]{:S(2)}) collective-permute-start(f32[160]{0:T(256)S(1)} %multiply_reduce_fusion.6), channel_id=1, source_target_pairs={{0,2},{1,3},{2,0},{3,1},{4,6},{5,7},{6,4},{7,5},{8,10},{9,11},{10,... | collective-permute-start | bytes 1928 | tf_op jit(solution)/shard_map/ppermute | solution.py:30
  647.1 17.9 %collective-permute-start.67 = (bf16[160,2048]{1,0:T(8,128)(2,1)}, bf16[160,2048]{1,0:T(8,128)(2,1)}, u32[]{:S(2)}, u32[]{:S(2)}) collective-permute-start(bf16[160,2048]{1,0:T(8,128)(2,1)} %get-tuple-element.199), channel_id=1, source_target_pairs={{0,1},{1,0},{2,3},{3,2},{4,5},{5,4},{6,7},{7,6},{8,9},{9,8},{10,11... | collective-permute-start | bytes 1966088 | tf_op jit(solution)/shard_map/ppermute | solution.py:30
  648.6 30.9 %collective-permute-start.68 = (bf16[160,2048]{1,0:T(8,128)(2,1)}, bf16[160,2048]{1,0:T(8,128)(2,1)}, u32[]{:S(2)}, u32[]{:S(2)}) collective-permute-start(bf16[160,2048]{1,0:T(8,128)(2,1)} %get-tuple-element.200), channel_id=1, source_target_pairs={{0,2},{1,3},{2,0},{3,1},{4,6},{5,7},{6,4},{7,5},{8,10},{9,11},{10,... | collective-permute-start | bytes 1966088 | tf_op jit(solution)/shard_map/ppermute | solution.py:30
  650.0 29.5 %collective-permute-start.69 = (bf16[160,2048]{1,0:T(8,128)(2,1)}, bf16[160,2048]{1,0:T(8,128)(2,1)}, u32[]{:S(2)}, u32[]{:S(2)}) collective-permute-start(bf16[160,2048]{1,0:T(8,128)(2,1)} %get-tuple-element.201), channel_id=1, source_target_pairs={{0,3},{1,2},{2,1},{3,0},{4,7},{5,6},{6,5},{7,4},{8,11},{9,10},{10,... | collective-permute-start | bytes 1966088 | tf_op jit(solution)/shard_map/ppermute | solution.py:30
  663.2 173.7 %reduce-scatter.13.cloned.1.call-start = ((), (), s32[]{:S(2)}) async-start(), calls=%async_computation.13 | async-start | bytes 3604480 | tf_op jit(solution)/shard_map/reduce_scatter | solution.py:189
  663.8 59.4 %collective-permute-start.78 = (bf16[640,1408]{1,0:T(8,128)(2,1)}, bf16[640,1408]{1,0:T(8,128)(2,1)}, u32[]{:S(2)}, u32[]{:S(2)}) collective-permute-start(bf16[640,1408]{1,0:T(8,128)(2,1)} %get-tuple-element.154.refs_0_), channel_id=1, source_target_pairs={{0,4},{4,0},{1,5},{5,1},{2,6},{6,2},{3,7},{7,3},{8,12},{12,8},{9,1... | collective-permute-start | bytes 5406728 | tf_op jit(solution)/shard_map/ppermute | solution.py:34
  687.8 29.8 %collective-permute-start.76 = (bf16[160,2048]{1,0:T(8,128)(2,1)S(1)}, bf16[160,2048]{1,0:T(8,128)(2,1)S(1)}, u32[]{:S(2)}, u32[]{:S(2)}) collective-permute-start(bf16[160,2048]{1,0:T(8,128)(2,1)S(1)} %get-tuple-element.209.refs_2_.refs_0_), channel_id=1, source_target_pairs={{0,2},{1,3},{2,0},{3,1},{4,6},{5,7},{6,4},{7,5},{8,10},{9,11},{10,... | collective-permute-start | bytes 1966088 | tf_op jit(solution)/shard_map/ppermute | solution.py:30
  688.7 29.7 %collective-permute-start.77 = (bf16[160,2048]{1,0:T(8,128)(2,1)S(1)}, bf16[160,2048]{1,0:T(8,128)(2,1)}, u32[]{:S(2)}, u32[]{:S(2)}) collective-permute-start(bf16[160,2048]{1,0:T(8,128)(2,1)S(1)} %get-tuple-element.209.refs_2_.refs_0_), channel_id=1, source_target_pairs={{0,3},{1,2},{2,1},{3,0},{4,7},{5,6},{6,5},{7,4},{8,11},{9,10},{10,... | collective-permute-start | bytes 1966088 | tf_op jit(solution)/shard_map/ppermute | solution.py:30
  690.2 33.5 %collective-permute-start.79 = (bf16[160,2048]{1,0:T(8,128)(2,1)S(1)}, bf16[160,2048]{1,0:T(8,128)(2,1)}, u32[]{:S(2)}, u32[]{:S(2)}) collective-permute-start(bf16[160,2048]{1,0:T(8,128)(2,1)S(1)} %get-tuple-element.209.refs_2_.refs_0_), channel_id=1, source_target_pairs={{0,4},{4,0},{1,5},{5,1},{2,6},{6,2},{3,7},{7,3},{8,12},{12,8},{9,1... | collective-permute-start | bytes 1966088 | tf_op jit(solution)/shard_map/ppermute | solution.py:34
  723.2 25.2 %collective-permute-start.88 = (bf16[160,2048]{1,0:T(8,128)(2,1)S(1)}, bf16[160,2048]{1,0:T(8,128)(2,1)}, u32[]{:S(2)}, u32[]{:S(2)}) collective-permute-start(bf16[160,2048]{1,0:T(8,128)(2,1)S(1)} %copy-done.3), channel_id=1, source_target_pairs={{0,4},{4,0},{1,5},{5,1},{2,6},{6,2},{3,7},{7,3},{8,12},{12,8},{9,1... | collective-permute-start | bytes 1966088 | tf_op jit(solution)/shard_map/ppermute | solution.py:34
  723.7 37.6 %collective-permute-start.89 = (bf16[160,2048]{1,0:T(8,128)(2,1)S(1)}, bf16[160,2048]{1,0:T(8,128)(2,1)}, u32[]{:S(2)}, u32[]{:S(2)}) collective-permute-start(bf16[160,2048]{1,0:T(8,128)(2,1)S(1)} %copy-done.21), channel_id=1, source_target_pairs={{0,4},{4,0},{1,5},{5,1},{2,6},{6,2},{3,7},{7,3},{8,12},{12,8},{9,1... | collective-permute-start | bytes 1966088 | tf_op jit(solution)/shard_map/ppermute | solution.py:34
  723.8 38.3 %collective-permute-start.90 = (bf16[160,2048]{1,0:T(8,128)(2,1)S(1)}, bf16[160,2048]{1,0:T(8,128)(2,1)}, u32[]{:S(2)}, u32[]{:S(2)}) collective-permute-start(bf16[160,2048]{1,0:T(8,128)(2,1)S(1)} %copy-done.23), channel_id=1, source_target_pairs={{0,4},{4,0},{1,5},{5,1},{2,6},{6,2},{3,7},{7,3},{8,12},{12,8},{9,1... | collective-permute-start | bytes 1966088 | tf_op jit(solution)/shard_map/ppermute | solution.py:34
  724.2 38.2 %collective-permute-start.91 = (bf16[160,2048]{1,0:T(8,128)(2,1)}, bf16[160,2048]{1,0:T(8,128)(2,1)}, u32[]{:S(2)}, u32[]{:S(2)}) collective-permute-start(bf16[160,2048]{1,0:T(8,128)(2,1)} %copy-done.136), channel_id=1, source_target_pairs={{0,4},{4,0},{1,5},{5,1},{2,6},{6,2},{3,7},{7,3},{8,12},{12,8},{9,1... | collective-permute-start | bytes 1966088 | tf_op jit(solution)/shard_map/ppermute | solution.py:34
  748.1 184.1 %reduce-scatter.15.cloned.1.call-start = ((), (), s32[]{:S(2)}) async-start(), calls=%async_computation.14 | async-start | bytes 7208960 | tf_op jit(solution)/shard_map/reduce_scatter | solution.py:189
  761.3 20.2 %collective-permute-start.83 = (bf16[160,2048]{1,0:T(8,128)(2,1)}, bf16[160,2048]{1,0:T(8,128)(2,1)}, u32[]{:S(2)}, u32[]{:S(2)}) collective-permute-start(bf16[160,2048]{1,0:T(8,128)(2,1)} %get-tuple-element.220), channel_id=1, source_target_pairs={{0,1},{1,0},{2,3},{3,2},{4,5},{5,4},{6,7},{7,6},{8,9},{9,8},{10,11... | collective-permute-start | bytes 1966088 | tf_op jit(solution)/shard_map/ppermute | solution.py:30
  762.0 31.1 %collective-permute-start.84 = (bf16[160,2048]{1,0:T(8,128)(2,1)}, bf16[160,2048]{1,0:T(8,128)(2,1)}, u32[]{:S(2)}, u32[]{:S(2)}) collective-permute-start(bf16[160,2048]{1,0:T(8,128)(2,1)} %get-tuple-element.221), channel_id=1, source_target_pairs={{0,2},{1,3},{2,0},{3,1},{4,6},{5,7},{6,4},{7,5},{8,10},{9,11},{10,... | collective-permute-start | bytes 1966088 | tf_op jit(solution)/shard_map/ppermute | solution.py:30
  762.4 30.7 %collective-permute-start.85 = (bf16[160,2048]{1,0:T(8,128)(2,1)}, bf16[160,2048]{1,0:T(8,128)(2,1)}, u32[]{:S(2)}, u32[]{:S(2)}) collective-permute-start(bf16[160,2048]{1,0:T(8,128)(2,1)} %get-tuple-element.222), channel_id=1, source_target_pairs={{0,3},{1,2},{2,1},{3,0},{4,7},{5,6},{6,5},{7,4},{8,11},{9,10},{10,... | collective-permute-start | bytes 1966088 | tf_op jit(solution)/shard_map/ppermute | solution.py:30
  781.2 209.4 %reduce-scatter.17.cloned.1.call-start = ((), (), s32[]{:S(2)}) async-start(), calls=%async_computation.15 | async-start | bytes 5242880 | tf_op jit(solution)/shard_map/reduce_scatter | solution.py:189
  803.4 31.7 %collective-permute-start.95 = (bf16[160,2048]{1,0:T(8,128)(2,1)S(1)}, bf16[160,2048]{1,0:T(8,128)(2,1)S(1)}, u32[]{:S(2)}, u32[]{:S(2)}) collective-permute-start(bf16[160,2048]{1,0:T(8,128)(2,1)S(1)} %get-tuple-element.329.refs_0_.refs_12_), channel_id=1, source_target_pairs={{0,1},{1,0},{2,3},{3,2},{4,5},{5,4},{6,7},{7,6},{8,9},{9,8},{10,11... | collective-permute-start | bytes 1966088 | tf_op jit(solution)/shard_map/ppermute | solution.py:30
  804.3 31.7 %collective-permute-start.96 = (bf16[160,2048]{1,0:T(8,128)(2,1)S(1)}, bf16[160,2048]{1,0:T(8,128)(2,1)S(1)}, u32[]{:S(2)}, u32[]{:S(2)}) collective-permute-start(bf16[160,2048]{1,0:T(8,128)(2,1)S(1)} %get-tuple-element.329.refs_0_.refs_12_), channel_id=1, source_target_pairs={{0,2},{1,3},{2,0},{3,1},{4,6},{5,7},{6,4},{7,5},{8,10},{9,11},{10,... | collective-permute-start | bytes 1966088 | tf_op jit(solution)/shard_map/ppermute | solution.py:30
  805.7 31.2 %collective-permute-start.97 = (bf16[160,2048]{1,0:T(8,128)(2,1)S(1)}, bf16[160,2048]{1,0:T(8,128)(2,1)}, u32[]{:S(2)}, u32[]{:S(2)}) collective-permute-start(bf16[160,2048]{1,0:T(8,128)(2,1)S(1)} %get-tuple-element.329.refs_0_.refs_12_), channel_id=1, source_target_pairs={{0,3},{1,2},{2,1},{3,0},{4,7},{5,6},{6,5},{7,4},{8,11},{9,10},{10,... | collective-permute-start | bytes 1966088 | tf_op jit(solution)/shard_map/ppermute | solution.py:30
  814.0 19.3 %collective-permute-start.99 = (f32[160]{0:T(256)S(1)}, f32[160]{0:T(256)S(1)}, u32[]{:S(2)}, u32[]{:S(2)}) collective-permute-start(f32[160]{0:T(256)S(1)} %multiply_reduce_fusion.3), channel_id=1, source_target_pairs={{0,2},{1,3},{2,0},{3,1},{4,6},{5,7},{6,4},{7,5},{8,10},{9,11},{10,... | collective-permute-start | bytes 1928 | tf_op jit(solution)/shard_map/ppermute | solution.py:30
  816.3 38.0 %collective-permute-start.92 = (bf16[160,2048]{1,0:T(8,128)(2,1)}, bf16[160,2048]{1,0:T(8,128)(2,1)S(1)}, u32[]{:S(2)}, u32[]{:S(2)}) collective-permute-start(bf16[160,2048]{1,0:T(8,128)(2,1)} %get-tuple-element.350), channel_id=1, source_target_pairs={{0,1},{1,0},{2,3},{3,2},{4,5},{5,4},{6,7},{7,6},{8,9},{9,8},{10,11... | collective-permute-start | bytes 1966088 | tf_op jit(solution)/shard_map/ppermute | solution.py:30
  833.3 28.2 %collective-permute-start.93 = (bf16[160,2048]{1,0:T(8,128)(2,1)}, bf16[160,2048]{1,0:T(8,128)(2,1)S(1)}, u32[]{:S(2)}, u32[]{:S(2)}) collective-permute-start(bf16[160,2048]{1,0:T(8,128)(2,1)} %get-tuple-element.352), channel_id=1, source_target_pairs={{0,2},{1,3},{2,0},{3,1},{4,6},{5,7},{6,4},{7,5},{8,10},{9,11},{10,... | collective-permute-start | bytes 1966088 | tf_op jit(solution)/shard_map/ppermute | solution.py:30
  835.1 26.5 %collective-permute-start.94 = (bf16[160,2048]{1,0:T(8,128)(2,1)}, bf16[160,2048]{1,0:T(8,128)(2,1)}, u32[]{:S(2)}, u32[]{:S(2)}) collective-permute-start(bf16[160,2048]{1,0:T(8,128)(2,1)} %get-tuple-element.351), channel_id=1, source_target_pairs={{0,3},{1,2},{2,1},{3,0},{4,7},{5,6},{6,5},{7,4},{8,11},{9,10},{10,... | collective-permute-start | bytes 1966088 | tf_op jit(solution)/shard_map/ppermute | solution.py:30
  899.8 18.0 %collective-permute-start.110 = (bf16[160,2048]{1,0:T(8,128)(2,1)}, bf16[160,2048]{1,0:T(8,128)(2,1)}, u32[]{:S(2)}, u32[]{:S(2)}) collective-permute-start(bf16[160,2048]{1,0:T(8,128)(2,1)} %get-tuple-element.245), channel_id=1, source_target_pairs={{0,1},{1,0},{2,3},{3,2},{4,5},{5,4},{6,7},{7,6},{8,9},{9,8},{10,11... | collective-permute-start | bytes 1966088 | tf_op jit(solution)/shard_map/ppermute | solution.py:30
  901.3 30.8 %collective-permute-start.111 = (bf16[160,2048]{1,0:T(8,128)(2,1)}, bf16[160,2048]{1,0:T(8,128)(2,1)}, u32[]{:S(2)}, u32[]{:S(2)}) collective-permute-start(bf16[160,2048]{1,0:T(8,128)(2,1)} %get-tuple-element.246), channel_id=1, source_target_pairs={{0,2},{1,3},{2,0},{3,1},{4,6},{5,7},{6,4},{7,5},{8,10},{9,11},{10,... | collective-permute-start | bytes 1966088 | tf_op jit(solution)/shard_map/ppermute | solution.py:30
  902.1 30.1 %collective-permute-start.112 = (bf16[160,2048]{1,0:T(8,128)(2,1)}, bf16[160,2048]{1,0:T(8,128)(2,1)}, u32[]{:S(2)}, u32[]{:S(2)}) collective-permute-start(bf16[160,2048]{1,0:T(8,128)(2,1)} %get-tuple-element.247), channel_id=1, source_target_pairs={{0,3},{1,2},{2,1},{3,0},{4,7},{5,6},{6,5},{7,4},{8,11},{9,10},{10,... | collective-permute-start | bytes 1966088 | tf_op jit(solution)/shard_map/ppermute | solution.py:30
  (232 other events, 4127.0 us)
Sparse Core Ops, SparseCore 0:
  10.2 84.7 all-gather.6
  97.1 154.6 all-gather.8
  254.0 80.9 all-gather.10
  336.5 106.7 all-gather.12
  445.2 59.1 all-gather.14
  507.2 54.3 reduce-scatter.6
  563.9 102.3 reduce-scatter.8
  668.6 77.2 reduce-scatter.10
  748.9 56.6 reduce-scatter.12
  807.9 102.3 reduce-scatter.14
  912.7 77.9 reduce-scatter.16
